TPU v7x, 32 devices: a whole 2x2x4 slice. The times are simulated.
32 devices in a mesh: wide: 8 (over z, x), narrow: 4 (over y, core).
Axes of the slice: x: 2, y: 2, z: 4, core: 2. Of those that a mesh axis runs over, the one named last changes fastest.
Arguments:
- tokens: bfloat16 [8, 2048, 1024], P('narrow', 'wide'), may hold values from -6 to 6
- lengths: int32 [8], P('narrow'), may hold values from 128 to 2048, as said below
- value_ids: int32 [8, 2048, 4, 2], P('narrow', 'wide'), may hold values from 0 to 4, all different within a row
- out_ids: int32 [8, 2048, 4, 2], P('narrow', 'wide'), may hold values from 0 to 4, all different within a row
- mlp_ids: int32 [8, 2048, 16], P('narrow'), may hold values from 0 to 63, all different within a row
- w_query: bfloat16 [1024, 512], replicated, may hold values from -0.1875 to 0.1875
- w_key: bfloat16 [1024, 512], replicated, may hold values from -0.1875 to 0.1875
- w_value: bfloat16 [1024, 2560], replicated, may hold values from -0.1875 to 0.1875
- w_out: bfloat16 [4, 128, 5120], replicated, may hold values from -6 to 6
- sel_value: bfloat16 [1024, 20], replicated, may hold values from -0.125 to 0.125
- sel_out: bfloat16 [1024, 20], replicated, may hold values from -0.125 to 0.125
- gain_one: float32 [1024], replicated, may hold values from 0.5 to 1.5
- bias_one: float32 [1024], replicated, may hold values from -1.2 to 1.2
- gain_two: float32 [1024], replicated, may hold values from 0.5 to 1.5
- bias_two: float32 [1024], replicated, may hold values from -1.2 to 1.2
- w_select: bfloat16 [1024, 64], P(None, 'wide'), may hold values from -0.09375 to 0.09375
- w_up: bfloat16 [1024, 8192], P(None, 'wide'), may hold values from -0.1875 to 0.1875
- w_down: bfloat16 [8192, 1024], P('wide'), may hold values from -0.25 to 0.25
- cotangent: bfloat16 [8, 2048, 1024], P('narrow', 'wide'), may hold values from -6 to 6
Outputs:
- output: bfloat16 [8, 2048, 1024], P('narrow', 'wide')
- grad_tokens: bfloat16 [8, 2048, 1024], P('narrow', 'wide')
- grad_query: float32 [1024, 512], replicated
- grad_key: float32 [1024, 512], replicated
- grad_value: float32 [1024, 2560], replicated
- grad_out: float32 [4, 128, 5120], replicated
- grad_sel_value: float32 [1024, 20], replicated
- grad_sel_out: float32 [1024, 20], replicated
- grad_gain_one: float32 [1024], replicated
- grad_bias_one: float32 [1024], replicated
- grad_gain_two: float32 [1024], replicated
- grad_bias_two: float32 [1024], replicated
- grad_select: float32 [1024, 64], P(None, 'wide')
- grad_up: float32 [1024, 8192], P(None, 'wide')
- grad_down: float32 [8192, 1024], P('wide')
Inputs may be any that keep to these rules, and one draw needn't show every extreme that they name: `lengths`: in each group of 2 consecutive sequences one has length 2048. `value_ids`: the 2 experts of a token and head are distinct. `out_ids`: the 2 experts of a token and head are distinct. `mlp_ids`: the 16 experts of a token are distinct.
All inputs are finite; a program needn't handle non-finite values.
Results may differ from a plain program's by a relative error of at most 0.017.
Values may be sent and summed in bfloat16 or wider, within the bound.
No kernel may reach another device: no remote copies, remote signals or barrier semaphores. Data moves between devices by JAX's collectives and lax.ppermute only.
A program may use at most 384 MiB of HBM per device.

v0:
```python
import jax
import jax.numpy as jnp
from jax import lax
from jax.sharding import PartitionSpec as P

EPSILON = 1e-05
FULL_TYPE = jnp.float32
HALF_TYPE = jnp.bfloat16


def for_sending(value):

    def short(part):
        return part.astype(jnp.bfloat16) if part.dtype == jnp.float32 else part

    return jax.tree.map(short, value)


def norm_parts(values_in, gain, bias):
    row_mean = jnp.mean(values_in, axis=-1, keepdims=True)
    centred = values_in - row_mean
    inv_scale = lax.rsqrt(jnp.mean(centred * centred, axis=-1, keepdims=True) + EPSILON)
    normal = centred * inv_scale
    return (normal * gain + bias, normal, inv_scale)


def norm_back(grad_in, normal, inv_scale, gain):
    scaled = grad_in * gain
    return inv_scale * (
        scaled
        - jnp.mean(scaled, axis=-1, keepdims=True)
        - normal * jnp.mean(scaled * normal, axis=-1, keepdims=True)
    )


def rotate(values_in, positions, turn):
    half_dim = values_in.shape[-1] // 2
    frequency = 10000.0 ** (-(jnp.arange(half_dim).astype(FULL_TYPE) * 2.0 / values_in.shape[-1]))
    angles = positions.astype(FULL_TYPE)[:, None] * frequency[None, :]
    cosine = jnp.cos(angles)[:, None, :]
    sine_part = turn * jnp.sin(angles)[:, None, :]
    front_half = values_in[..., :half_dim]
    back_half = values_in[..., half_dim:]
    return jnp.concatenate(
        [front_half * cosine - back_half * sine_part, front_half * sine_part + back_half * cosine],
        axis=-1,
    )


def one_hot_sum(ids, wanted):
    return jnp.sum((ids[..., None] == wanted).astype(FULL_TYPE), axis=-2)


def matmul(left_op, right_op):
    return jnp.dot(left_op, right_op, preferred_element_type=FULL_TYPE)


def contract_rows(left_op, right_op):
    left_flat = left_op.reshape(-1, left_op.shape[-1])
    right_flat = right_op.reshape(-1, right_op.shape[-1])
    return lax.dot_general(
        left_flat, right_flat, (((0,), (0,)), ((), ())), preferred_element_type=FULL_TYPE
    )


def times_transpose(grad_in, weight):
    return lax.dot_general(
        grad_in, weight, (((grad_in.ndim - 1,), (1,)), ((), ())), preferred_element_type=FULL_TYPE
    )


def attend_forward(
    tokens,
    lengths,
    value_ids,
    out_ids,
    w_query,
    w_key,
    w_value,
    w_out,
    sel_value,
    sel_out,
    gain_one,
    bias_one,
    gain_two,
    bias_two,
):
    seq_count, row_count, model_width = tokens.shape
    head_count = w_out.shape[0]
    head_dim = w_out.shape[1]
    value_experts = sel_value.shape[1] // head_count
    positions = lax.axis_index("wide") * row_count + jnp.arange(row_count, dtype=jnp.int32)
    inputs = tokens.astype(FULL_TYPE)
    normed, normal_one, scale_one = norm_parts(inputs, gain_one, bias_one)
    normed_low = normed.astype(HALF_TYPE)
    query_pre = matmul(normed_low, w_query).reshape(seq_count, row_count, head_count, head_dim)
    key_pre = matmul(normed_low, w_key).reshape(seq_count, row_count, head_count, head_dim)
    queries = rotate(query_pre, positions, 1.0).astype(HALF_TYPE)
    key_low = rotate(key_pre, positions, 1.0).astype(HALF_TYPE)
    expert_ids = jnp.arange(value_experts, dtype=jnp.int32)
    value_choice = one_hot_sum(value_ids, expert_ids)
    value_sig = jax.nn.sigmoid(
        matmul(normed_low, sel_value).reshape(seq_count, row_count, head_count, value_experts)
    )
    value_gate = value_sig * value_choice
    projected = matmul(tokens, w_value).reshape(
        seq_count, row_count, head_count, value_experts, head_dim
    )
    values = jnp.sum(value_gate[..., None] * projected, axis=3).astype(HALF_TYPE)
    keys_all, values_all = (
        lax.all_gather(key_low, "wide", axis=1, tiled=True),
        lax.all_gather(values, "wide", axis=1, tiled=True),
    )
    span = keys_all.shape[1]
    key_pos = jnp.arange(span, dtype=jnp.int32)
    allowed = (key_pos[None, None, None, :] <= positions[None, None, :, None]) & (
        key_pos[None, None, None, :] < lengths[:, None, None, None]
    )
    scores = jnp.einsum(
        "bphc,bshc->bhps", queries, keys_all, preferred_element_type=FULL_TYPE
    ) * head_dim ** (-0.5)
    masked = jnp.where(allowed, scores, -1e30)
    row_max = jnp.max(masked, axis=-1, keepdims=True)
    exponent = jnp.exp(masked - row_max)
    row_total = jnp.sum(exponent, axis=-1, keepdims=True)
    attn_probs = exponent / row_total
    log_total = row_max + jnp.log(row_total)
    attended = jnp.einsum(
        "bhps,bshc->bphc",
        attn_probs.astype(HALF_TYPE),
        values_all,
        preferred_element_type=FULL_TYPE,
    )
    live_rows = (positions[None, :] < lengths[:, None]).astype(FULL_TYPE)[:, :, None, None]
    mixed_out = (attended * live_rows).astype(HALF_TYPE)
    out_choice = one_hot_sum(out_ids, expert_ids)
    out_sig = jax.nn.sigmoid(
        matmul(normed_low, sel_out).reshape(seq_count, row_count, head_count, value_experts)
    )
    out_gate = out_sig * out_choice
    expert_out = jnp.einsum(
        "bphc,hcf->bphf", mixed_out, w_out, preferred_element_type=FULL_TYPE
    ).reshape(seq_count, row_count, head_count, value_experts, model_width)
    after_attn = inputs + jnp.sum(out_gate[..., None] * expert_out, axis=(2, 3))
    normed_two, normal_two, scale_two = norm_parts(after_attn, gain_two, bias_two)
    return dict(
        positions=positions,
        normal_one=normal_one,
        scale_one=scale_one,
        normed_low=normed_low,
        queries=queries,
        keys_all=keys_all,
        values_all=values_all,
        allowed=allowed,
        log_total=log_total,
        live_rows=live_rows,
        mixed_out=mixed_out,
        value_choice=value_choice,
        value_sig=value_sig,
        value_gate=value_gate,
        projected=projected,
        out_choice=out_choice,
        out_sig=out_sig,
        out_gate=out_gate,
        expert_out=expert_out,
        after_attn=after_attn,
        normed_two=normed_two,
        normal_two=normal_two,
        scale_two=scale_two,
    )


def expert_forward(after_attn, normed_two, mlp_ids, w_select, w_up):
    rows_all, normed_all = (
        lax.all_gather(for_sending(after_attn.astype(HALF_TYPE)), "wide", axis=1, tiled=True),
        lax.all_gather(for_sending(normed_two.astype(HALF_TYPE)), "wide", axis=1, tiled=True),
    )
    local_count = w_select.shape[1]
    hidden = w_up.shape[1] // local_count
    seq_count, span = (rows_all.shape[0], rows_all.shape[1])
    owned_ids = lax.axis_index("wide") * local_count + jnp.arange(local_count, dtype=jnp.int32)
    chosen = one_hot_sum(mlp_ids, owned_ids)
    sigmoid_gate = jax.nn.sigmoid(matmul(normed_all, w_select))
    mlp_gate = sigmoid_gate * chosen
    pre_act = matmul(rows_all, w_up)
    activated = jax.nn.gelu(pre_act).reshape(seq_count, span, local_count, hidden)
    inner_low = (
        (activated * mlp_gate[..., None])
        .reshape(seq_count, span, local_count * hidden)
        .astype(HALF_TYPE)
    )
    return dict(
        rows_all=rows_all,
        normed_all=normed_all,
        chosen=chosen,
        sigmoid_gate=sigmoid_gate,
        mlp_gate=mlp_gate,
        pre_act=pre_act,
        activated=activated,
        inner_low=inner_low,
    )


def per_device(
    tokens,
    lengths,
    value_ids,
    out_ids,
    mlp_ids,
    w_query,
    w_key,
    w_value,
    w_out,
    sel_value,
    sel_out,
    gain_one,
    bias_one,
    gain_two,
    bias_two,
    w_select,
    w_up,
    w_down,
    cotangent,
):
    seq_count, row_count, model_width = tokens.shape
    head_count = w_out.shape[0]
    head_dim = w_out.shape[1]
    value_experts = sel_value.shape[1] // head_count
    saved = attend_forward(
        tokens,
        lengths,
        value_ids,
        out_ids,
        w_query,
        w_key,
        w_value,
        w_out,
        sel_value,
        sel_out,
        gain_one,
        bias_one,
        gain_two,
        bias_two,
    )
    expert_state = expert_forward(saved["after_attn"], saved["normed_two"], mlp_ids, w_select, w_up)
    branch_part = matmul(expert_state["inner_low"], w_down)
    branch_sum = lax.psum_scatter(
        branch_part.astype(jnp.bfloat16), "wide", scatter_dimension=1, tiled=True
    ).astype(jnp.float32)
    output = (saved["after_attn"] + branch_sum).astype(HALF_TYPE)
    saved = attend_forward(
        tokens,
        lengths,
        value_ids,
        out_ids,
        w_query,
        w_key,
        w_value,
        w_out,
        sel_value,
        sel_out,
        gain_one,
        bias_one,
        gain_two,
        bias_two,
    )
    expert_state = expert_forward(saved["after_attn"], saved["normed_two"], mlp_ids, w_select, w_up)
    cot_all = lax.all_gather(cotangent, "wide", axis=1, tiled=True)
    grad_down = contract_rows(expert_state["inner_low"], cot_all)
    d_inner = times_transpose(cot_all, w_down)
    activated = expert_state["activated"]
    d_inner_four = d_inner.reshape(activated.shape)
    d_mlp_gate = jnp.sum(d_inner_four * activated, axis=-1)
    mlp_gate = expert_state["mlp_gate"]
    gated_grad = (d_inner_four * mlp_gate[..., None]).reshape(expert_state["pre_act"].shape)
    unused_value, gelu_pull = jax.vjp(jax.nn.gelu, expert_state["pre_act"])
    d_pre = gelu_pull(gated_grad)[0].astype(HALF_TYPE)
    sigmoid_gate = expert_state["sigmoid_gate"]
    d_logit = (d_mlp_gate * expert_state["chosen"] * sigmoid_gate * (1.0 - sigmoid_gate)).astype(
        HALF_TYPE
    )
    grad_up = contract_rows(expert_state["rows_all"], d_pre)
    grad_select = contract_rows(expert_state["normed_all"], d_logit)
    row_part = times_transpose(d_pre, w_up)
    norm_part = times_transpose(d_logit, w_select)
    row_grad, norm_grad = (
        lax.psum_scatter(row_part, "wide", scatter_dimension=1, tiled=True),
        lax.psum_scatter(norm_part, "wide", scatter_dimension=1, tiled=True),
    )
    grad_gain_two = jnp.sum(norm_grad * saved["normal_two"], axis=(0, 1))
    grad_bias_two = jnp.sum(norm_grad, axis=(0, 1))
    d_after = (
        cotangent.astype(FULL_TYPE)
        + row_grad
        + norm_back(norm_grad, saved["normal_two"], saved["scale_two"], gain_two)
    )
    out_gate = saved["out_gate"]
    d_expert = (out_gate[..., None] * d_after[:, :, None, None, :]).astype(HALF_TYPE)
    d_out_gate = jnp.sum(saved["expert_out"] * d_after[:, :, None, None, :], axis=-1)
    d_expert_flat = d_expert.reshape(seq_count, row_count, head_count, value_experts * model_width)
    grad_out = jnp.einsum(
        "bphc,bphf->hcf", saved["mixed_out"], d_expert_flat, preferred_element_type=FULL_TYPE
    )
    d_mixed = jnp.einsum("bphf,hcf->bphc", d_expert_flat, w_out, preferred_element_type=FULL_TYPE)
    d_attended = (d_mixed * saved["live_rows"]).astype(HALF_TYPE)
    out_sig = saved["out_sig"]
    d_out_logit = (
        (d_out_gate * saved["out_choice"] * out_sig * (1.0 - out_sig))
        .astype(HALF_TYPE)
        .reshape(seq_count, row_count, head_count * value_experts)
    )
    queries = saved["queries"]
    keys_all = saved["keys_all"]
    values_all = saved["values_all"]
    score_scale = head_dim ** (-0.5)
    scores = (
        jnp.einsum("bphc,bshc->bhps", queries, keys_all, preferred_element_type=FULL_TYPE)
        * score_scale
    )
    attn_probs = jnp.where(saved["allowed"], jnp.exp(scores - saved["log_total"]), 0.0)
    d_values_part = jnp.einsum(
        "bhps,bphc->bshc",
        attn_probs.astype(HALF_TYPE),
        d_attended,
        preferred_element_type=FULL_TYPE,
    )
    d_probs = jnp.einsum(
        "bphc,bshc->bhps", d_attended, values_all, preferred_element_type=FULL_TYPE
    )
    row_inner = jnp.sum(attn_probs * d_probs, axis=-1, keepdims=True)
    d_scores = (attn_probs * (d_probs - row_inner)).astype(HALF_TYPE)
    d_queries = (
        jnp.einsum("bhps,bshc->bphc", d_scores, keys_all, preferred_element_type=FULL_TYPE)
        * score_scale
    )
    d_keys_part = (
        jnp.einsum("bhps,bphc->bshc", d_scores, queries, preferred_element_type=FULL_TYPE)
        * score_scale
    )
    d_keys, d_values = (
        lax.psum_scatter(
            d_keys_part.astype(jnp.bfloat16), "wide", scatter_dimension=1, tiled=True
        ).astype(jnp.float32),
        lax.psum_scatter(
            d_values_part.astype(jnp.bfloat16), "wide", scatter_dimension=1, tiled=True
        ).astype(jnp.float32),
    )
    positions = saved["positions"]
    d_query_pre = (
        rotate(d_queries, positions, -1.0)
        .astype(HALF_TYPE)
        .reshape(seq_count, row_count, head_count * head_dim)
    )
    d_key_pre = (
        rotate(d_keys, positions, -1.0)
        .astype(HALF_TYPE)
        .reshape(seq_count, row_count, head_count * head_dim)
    )
    d_projected = (
        (saved["value_gate"][..., None] * d_values[:, :, :, None, :])
        .astype(HALF_TYPE)
        .reshape(seq_count, row_count, head_count * value_experts * head_dim)
    )
    d_value_gate = jnp.sum(saved["projected"] * d_values[:, :, :, None, :], axis=-1)
    value_sig = saved["value_sig"]
    d_value_logit = (
        (d_value_gate * saved["value_choice"] * value_sig * (1.0 - value_sig))
        .astype(HALF_TYPE)
        .reshape(seq_count, row_count, head_count * value_experts)
    )
    normed_low = saved["normed_low"]
    grad_query = contract_rows(normed_low, d_query_pre)
    grad_key = contract_rows(normed_low, d_key_pre)
    grad_sel_value = contract_rows(normed_low, d_value_logit)
    grad_sel_out = contract_rows(normed_low, d_out_logit)
    grad_value = contract_rows(tokens, d_projected)
    d_normed = (
        times_transpose(d_query_pre, w_query)
        + times_transpose(d_key_pre, w_key)
        + times_transpose(d_value_logit, sel_value)
        + times_transpose(d_out_logit, sel_out)
    )
    grad_gain_one = jnp.sum(d_normed * saved["normal_one"], axis=(0, 1))
    grad_bias_one = jnp.sum(d_normed, axis=(0, 1))
    grad_tokens = (
        d_after
        + times_transpose(d_projected, w_value)
        + norm_back(d_normed, saved["normal_one"], saved["scale_one"], gain_one)
    ).astype(HALF_TYPE)
    (
        grad_query,
        grad_key,
        grad_value,
        grad_out,
        grad_sel_value,
        grad_sel_out,
        grad_gain_one,
        grad_bias_one,
        grad_gain_two,
        grad_bias_two,
    ) = lax.psum(
        (
            grad_query,
            grad_key,
            grad_value,
            grad_out,
            grad_sel_value,
            grad_sel_out,
            grad_gain_one,
            grad_bias_one,
            grad_gain_two,
            grad_bias_two,
        ),
        ("wide", "narrow"),
    )
    grad_select, grad_up, grad_down = (
        lax.psum(grad_select.astype(jnp.bfloat16), "narrow").astype(jnp.float32),
        lax.psum(grad_up.astype(jnp.bfloat16), "narrow").astype(jnp.float32),
        lax.psum(grad_down.astype(jnp.bfloat16), "narrow").astype(jnp.float32),
    )
    return (
        output,
        grad_tokens,
        grad_query,
        grad_key,
        grad_value,
        grad_out,
        grad_sel_value,
        grad_sel_out,
        grad_gain_one,
        grad_bias_one,
        grad_gain_two,
        grad_bias_two,
        grad_select,
        grad_up,
        grad_down,
    )


def solution(mesh):
    placed = (
        P("narrow", "wide", None),
        P("narrow"),
        P("narrow", "wide", None, None),
        P("narrow", "wide", None, None),
        P("narrow", None, None),
        P(),
        P(),
        P(),
        P(),
        P(),
        P(),
        P(),
        P(),
        P(),
        P(),
        P(None, "wide"),
        P(None, "wide"),
        P("wide", None),
        P("narrow", "wide", None),
    )
    return jax.shard_map(
        per_device,
        mesh=mesh,
        in_specs=placed,
        out_specs=(
            P("narrow", "wide", None),
            P("narrow", "wide", None),
            P(),
            P(),
            P(),
            P(),
            P(),
            P(),
            P(),
            P(),
            P(),
            P(),
            P(None, "wide"),
            P(None, "wide"),
            P("wide", None),
        ),
        check_vma=False,
    )
```

profile of v0, /device:TPU:0, one launch (start us, length us, event | category | flops | bytes accessed | tf_op | source)
XLA Modules:
  0.0 2108.3 jit_solution(4594043843404111894)
XLA Ops:
  42.4 14.1 mul.653
  56.5 40.1 %copy.168 = f32[2,256,4,5120]{3,1,0,2:T(8,128)} copy(f32[2,256,4,5120]{1,3,2,0:T(8,128)} %bitcast.179) | data formatting | bytes 83886080 | tf_op jit(solution)/shard_map/mul | solution.py:144
  107.1 12.3 select_reduce_fusion
  127.6 55.5 %all-gather.6.cloned.1.call-done = bf16[2,2048,4,128]{1,3,2,0:T(8,128)(2,1)} async-done(((bf16[2,256,4,128]{1,3,2,0:T(8,128)(2,1)}), bf16[2,2048,4,128]{1,3,2,0:T(8,128)(2,1)}) %all-gather.6.cloned.1.call-update) | async-done | bytes 4194320 | tf_op jit(solution)/shard_map/all_gather | solution.py:112
  183.1 10.7 fusion.69
  193.8 33.7 %multiply_reduce_fusion.1 = (f32[2,256,5120]{2,1,0:T(8,128)}, f32[2,256,4,5120]{3,1,0,2:T(8,128)}) fusion(f32[2,256,4,5120]{3,1,0,2:T(8,128)} %copy.168, bf16[4,128,5120]{2,1,0:T(8,128)(2,1)} %param.27, bf16[2,256,4,128]{1,3,2,0:T(8,128)(2,1)} %fusion.69), kind=kOutput, calls=%fused_computation.2 | convolution fusion | flops 2702704640 | bytes 100139008 | tf_op jit(solution)/shard_map/bphc,hcf->bphf/dot_general | solution.py:141
  227.5 11.8 copy.169
  260.3 115.3 %all-gather.10.cloned.1.call-done = bf16[2,2048,1024]{2,1,0:T(8,128)(2,1)} async-done(((bf16[2,256,1024]{2,1,0:T(8,128)(2,1)}), bf16[2,2048,1024]{2,1,0:T(8,128)(2,1)}) %all-gather.10.cloned.1.call-update) | async-done | bytes 8388624 | tf_op jit(solution)/shard_map/all_gather | solution.py:175
  375.6 16.1 fusion.52
  391.7 109.1 %all-gather.14.cloned.1.call-done = bf16[2,2048,1024]{2,1,0:T(8,128)(2,1)} async-done(((bf16[2,256,1024]{2,1,0:T(8,128)(2,1)}), bf16[2,2048,1024]{2,1,0:T(8,128)(2,1)}) %all-gather.14.cloned.1.call-update) | async-done | bytes 8388624 | tf_op jit(solution)/shard_map/all_gather | solution.py:268
  500.8 20.2 bitcast_reduce_fusion
  521.0 105.5 %all-gather.12.cloned.1.call-done = bf16[2,2048,1024]{2,1,0:T(8,128)(2,1)} async-done(((bf16[2,256,1024]{2,1,0:T(8,128)(2,1)}), bf16[2,2048,1024]{2,1,0:T(8,128)(2,1)}) %all-gather.12.cloned.1.call-update) | async-done | bytes 8388624 | tf_op jit(solution)/shard_map/all_gather | solution.py:176
  641.0 19.2 fusion.8
  663.5 11.2 convolution_convert_fusion
  676.3 14.9 fusion.50
  691.8 229.5 %reduce-scatter.10.cloned.1.call-done = f32[2,256,1024]{2,1,0:T(8,128)} async-done(((f32[2,2048,1024]{2,1,0:T(8,128)}), f32[2,256,1024]{2,1,0:T(8,128)}) %reduce-scatter.10.cloned.1.call-update) | async-done | bytes 2097168 | tf_op jit(solution)/shard_map/reduce_scatter | solution.py:288
  924.5 149.5 %reduce-scatter.6.cloned.1.call-done = bf16[2,256,1024]{2,1,0:T(8,128)(2,1)} async-done(((bf16[2,2048,1024]{2,1,0:T(8,128)(2,1)}), bf16[2,256,1024]{2,1,0:T(8,128)(2,1)}) %reduce-scatter.6.cloned.1.call-update) | async-done | bytes 1048592 | tf_op jit(solution)/shard_map/reduce_scatter | solution.py:247
  1074.0 284.8 %reduce-scatter.8.cloned.1.call-done = f32[2,256,1024]{2,1,0:T(8,128)} async-done(((f32[2,2048,1024]{2,1,0:T(8,128)}), f32[2,256,1024]{2,1,0:T(8,128)}) %reduce-scatter.8.cloned.1.call-update) | async-done | bytes 2097168 | tf_op jit(solution)/shard_map/reduce_scatter | solution.py:287
  1375.1 12.8 fusion.70
  1397.2 14.9 multiply_reduce_fusion.2
  1412.0 12.9 multiply_convert_fusion.1
  1433.7 40.0 %copy.191 = f32[2,256,4,5120]{1,3,2,0:T(8,128)} copy(f32[2,256,4,5120]{3,1,0,2:T(8,128)} %get-tuple-element.131) | data formatting | bytes 83886080 | tf_op jit(solution)/shard_map/bphc,hcf->bphf/transpose | solution.py:141
  1473.7 14.9 bitcast_convert_fusion.1
  1488.6 14.8 bitcast_convert_fusion
  1503.5 13.4 convolution_bitcast_fusion.1
  1516.9 17.6 multiply_reduce_fusion
  1552.4 24.2 %reduce-scatter.14.cloned.1.call-done = bf16[2,256,4,128]{3,1,2,0:T(8,128)(2,1)} async-done(((bf16[2,2048,4,128]{3,1,2,0:T(8,128)(2,1)}), bf16[2,256,4,128]{3,1,2,0:T(8,128)(2,1)}) %reduce-scatter.14.cloned.1.call-update) | async-done | bytes 524304 | tf_op jit(solution)/shard_map/reduce_scatter | solution.py:341
  1596.4 12.7 psum.101
  1609.8 55.2 %all-reduce.8.cloned.1.call-done = (bf16[1024,1024]{1,0:T(8,128)(2,1)}, bf16[1024,1024]{1,0:T(8,128)(2,1)}) async-done(((bf16[1024,1024]{1,0:T(8,128)(2,1)}, bf16[1024,1024]{1,0:T(8,128)(2,1)}), (bf16[1024,1024]{1,0:T(8,128)(2,1)}, bf16[1024,1024]{1,0:T(8,128)(2,1)})) %all-reduce.8.cloned.1.call-update) | async-done | bytes 4194320 | tf_op jit(solution)/shard_map/psum | solution.py:418
  1678.2 41.9 %all-reduce = (f32[1024]{0:T(1024)}, f32[1024]{0:T(1024)}, f32[1024]{0:T(1024)}, f32[1024]{0:T(1024)}) all-reduce(f32[1024]{0:T(1024)S(1)} %get-tuple-element.77, f32[1024]{0:T(1024)S(1)} %get-tuple-element.82, f32[1024]{0:T(1024)S(1)} %copy-done.62, f32[1024]{0:T(1024)S(1)} %copy-done.63), channel_id=1, replica_groups=mesh['wide'=8,'narrow'=4] {'wide','narrow'}, use_global_device_ids=true, to_apply=%region_32.33 | all-reduce | flops 4096 | bytes 32768 | tf_op jit(solution)/shard_map/psum | solution.py:401
  1730.0 344.2 %all-reduce.6.cloned.1.call-done = (f32[1024,512]{1,0:T(8,128)}, f32[1024,512]{1,0:T(8,128)}, f32[1024,2560]{0,1:T(8,128)}, f32[4,128,5120]{2,1,0:T(8,128)}, f32[1024,20]{0,1:T(8,128)}, /*index=5*/f32[1024,20]{0,1:T(8,128)}) async-done(((f32[1024,512]{1,0:T(8,128)}, f32[1024,512]{1,0:T(8,128)}, f32[1024,2560]{0,1:T(8,128)}, f32[4,128,5120]{2,1,0:T(8,128)}, f32[1024,20]{0,1:T(8,128)}, ...) | async-done | bytes 25329680 | tf_op jit(solution)/shard_map/psum | solution.py:401
  2074.2 11.4 copy.208
  (269 shorter events, 208.4 us)
Async XLA Ops:
  7.2 493.6 %copy-start = (bf16[1024,1024]{1,0:T(8,128)(2,1)S(1)}, bf16[1024,1024]{1,0:T(8,128)(2,1)}, u32[]{:S(2)}) copy-start(bf16[1024,1024]{1,0:T(8,128)(2,1)} %param.36) | copy-start | bytes 6291460
  7.2 99.9 %all-gather.8.cloned.1.call-start = ((), (), s32[]{:S(2)}) async-start(), calls=%async_computation.6 | async-start | bytes 4718592 | tf_op jit(solution)/shard_map/all_gather | solution.py:111
  12.2 29.0 %copy-start.3 = (bf16[2,256,1024]{2,1,0:T(8,128)(2,1)}, bf16[2,256,1024]{2,1,0:T(8,128)(2,1)S(1)}, u32[]{:S(2)}) copy-start(bf16[2,256,1024]{2,1,0:T(8,128)(2,1)S(1)} %fusion.39) | copy-start | bytes 3145732
  30.9 152.2 %all-gather.6.cloned.1.call-start = ((), (), s32[]{:S(2)}) async-start(), calls=%async_computation.5 | async-start | bytes 4718592 | tf_op jit(solution)/shard_map/all_gather | solution.py:112
  41.2 334.4 %all-gather.10.cloned.1.call-start = ((), (), s32[]{:S(2)}) async-start(), calls=%async_computation.7 | async-start | bytes 9437184 | tf_op jit(solution)/shard_map/all_gather | solution.py:175
  42.4 14.1 copy-start.29
  56.5 40.1 %copy-start.67 = (s32[2]{0:T(128)S(1)}, s32[2]{0:T(128)}, u32[]{:S(2)}) copy-start(s32[2]{0:T(128)} %param.20) | copy-start | bytes 28
  96.7 86.4 %copy-start.68 = (f32[2,256]{1,0:T(2,128)}, f32[2,256]{1,0:T(2,128)S(1)}, u32[]{:S(2)}) copy-start(f32[2,256]{1,0:T(2,128)S(1)} %compare_convert_fusion) | copy-start | bytes 6148
  97.8 85.3 %copy-start.8 = (pred[2,256,2048]{2,1,0:T(8,128)(4,1)}, pred[2,256,2048]{2,1,0:T(8,128)(4,1)S(1)}, u32[]{:S(2)}) copy-start(pred[2,256,2048]{2,1,0:T(8,128)(4,1)S(1)} %broadcast_and_fusion) | copy-start | bytes 3145732
  119.5 63.6 %copy-start.51 = (f32[2,4,256]{2,1,0:T(4,128)}, f32[2,4,256]{2,1,0:T(4,128)S(1)}, u32[]{:S(2)}) copy-start(f32[2,4,256]{2,1,0:T(4,128)S(1)} %get-tuple-element.128) | copy-start | bytes 24580
  127.6 66.2 %copy-start.55 = (f32[2,4,256]{2,1,0:T(4,128)}, f32[2,4,256]{2,1,0:T(4,128)S(1)}, u32[]{:S(2)}) copy-start(f32[2,4,256]{2,1,0:T(4,128)S(1)} %fusion.10) | copy-start | bytes 24580
  252.4 248.4 %all-gather.14.cloned.1.call-start = ((), (), s32[]{:S(2)}) async-start(), calls=%async_computation.10 | async-start | bytes 9437184 | tf_op jit(solution)/shard_map/all_gather | solution.py:268
  252.9 373.6 %all-gather.12.cloned.1.call-start = ((), (), s32[]{:S(2)}) async-start(), calls=%async_computation.8 | async-start | bytes 9437184 | tf_op jit(solution)/shard_map/all_gather | solution.py:176
  260.0 661.3 %reduce-scatter.10.cloned.1.call-start = ((), (), s32[]{:S(2)}) async-start(), calls=%async_computation.12 | async-start | bytes 18874368 | tf_op jit(solution)/shard_map/reduce_scatter | solution.py:288
  391.7 234.8 %copy-start.53 = (bf16[1024,8]{0,1:T(8,128)(2,1)S(1)}, bf16[1024,8]{0,1:T(8,128)(2,1)}, u32[]{:S(2)}) copy-start(bf16[1024,8]{0,1:T(8,128)(2,1)} %param.34) | copy-start | bytes 49156
  641.0 433.0 %reduce-scatter.6.cloned.1.call-start = ((), (), s32[]{:S(2)}) async-start(), calls=%async_computation.9 | async-start | bytes 9437184 | tf_op jit(solution)/shard_map/reduce_scatter | solution.py:247
  674.7 684.1 %reduce-scatter.8.cloned.1.call-start = ((), (), s32[]{:S(2)}) async-start(), calls=%async_computation.11 | async-start | bytes 18874368 | tf_op jit(solution)/shard_map/reduce_scatter | solution.py:287
  691.1 230.2 %copy-start.2 = (f32[2,256,1024]{2,1,0:T(8,128)S(1)}, f32[2,256,1024]{2,1,0:T(8,128)}, u32[]{:S(2)}) copy-start(f32[2,256,1024]{2,1,0:T(8,128)} %get-tuple-element.100) | copy-start | bytes 6291460
  691.1 667.7 %copy-start.16 = (bf16[2,256,1024]{2,1,0:T(8,128)(2,1)S(1)}, bf16[2,256,1024]{2,1,0:T(8,128)(2,1)}, u32[]{:S(2)}) copy-start(bf16[2,256,1024]{2,1,0:T(8,128)(2,1)} %param.37) | copy-start | bytes 3145732
  691.1 850.3 %reduce-scatter.12.cloned.1.call-start = ((), (), s32[]{:S(2)}) async-start(), calls=%async_computation.13 | async-start | bytes 4718592 | tf_op jit(solution)/shard_map/reduce_scatter | solution.py:344
  1397.1 179.5 %reduce-scatter.14.cloned.1.call-start = ((), (), s32[]{:S(2)}) async-start(), calls=%async_computation.14 | async-start | bytes 4718592 | tf_op jit(solution)/shard_map/reduce_scatter | solution.py:341
  1412.0 16.1 copy-start.14
  1412.0 16.1 copy-start.15
  1433.7 231.2 %all-reduce.8.cloned.1.call-start = ((), (), s32[]{:S(2)}) async-start(), calls=%async_computation.16 | async-start | bytes 8388608 | tf_op jit(solution)/shard_map/psum | solution.py:418
  1488.6 14.8 copy-start.19
  1503.4 570.8 %all-reduce.6.cloned.1.call-start = ((), (), s32[]{:S(2)}) async-start(), calls=%async_computation.15 | async-start | bytes 50724864 | tf_op jit(solution)/shard_map/psum | solution.py:401
  1516.9 17.6 copy-start.39
  1516.9 17.6 copy-start.43
  1516.9 17.7 copy-start.4
  1516.9 18.6 copy-start.17
  1547.8 29.9 %copy-start.23 = (f32[256,64]{1,0:T(8,128)S(1)}, f32[256,64]{1,0:T(8,128)}, u32[]{:S(2)}) copy-start(f32[256,64]{1,0:T(8,128)} %copy-done.22) | copy-start | bytes 196612
  1547.8 29.9 %copy-start.31 = (f32[256,64]{1,0:T(8,128)S(1)}, f32[256,64]{1,0:T(8,128)}, u32[]{:S(2)}) copy-start(f32[256,64]{1,0:T(8,128)} %get-tuple-element.125) | copy-start | bytes 196612
  (51 other events, 200.4 us)
Sparse Core Ops, SparseCore 0:
  31.0 76.0 all-gather.7
  109.7 73.2 all-gather.5
  252.5 123.0 all-gather.9
  377.6 123.0 all-gather.13
  503.4 123.0 all-gather.11
  641.1 280.1 reduce-scatter.9
  925.9 148.0 reduce-scatter.5
  1077.8 280.9 reduce-scatter.7
  1397.2 87.3 reduce-scatter.11
  1488.7 87.8 reduce-scatter.13
  1579.2 85.6 all-reduce.7
  1671.8 402.4 all-reduce.5
where the time goes:
time: 2120 us; the launch traced here: 2110 us
  waiting for transfers between devices  1480 us (70%)
  matrix products  269 us (13%)
  local copies, waits for them, and re-layouts  169 us (8%)
  other arithmetic  117 us (6%)
  blocking collectives  54.6 us (3%)
    psum x1, waiting for transfers between devices, per_device(): lax.psum((grad_query, grad_key, grad_value, grad_out, grad_sel_value, gra...  344 us
    reduce_scatter x1, waiting for transfers between devices, per_device(): lax.psum_scatter(row_part, 'wide', scatter_dimension=1, tiled=True)  285 us
    reduce_scatter x1, waiting for transfers between devices, per_device(): lax.psum_scatter(norm_part, 'wide', scatter_dimension=1, tiled=True)  229 us
    reduce_scatter x1, waiting for transfers between devices, per_device(): lax.psum_scatter(branch_part.astype(jnp.bfloat16), 'wide', scatter_dimens...  150 us
    all_gather x1, waiting for transfers between devices, expert_forward(): lax.all_gather(for_sending(after_attn.astype(HALF_TYPE)), 'wide', axis=1,...  115 us
    all_gather x1, waiting for transfers between devices, per_device(): cot_all = lax.all_gather(cotangent, 'wide', axis=1, tiled=True)  109 us
    all_gather x1, waiting for transfers between devices, expert_forward(): lax.all_gather(for_sending(normed_two.astype(HALF_TYPE)), 'wide', axis=1,...  105 us
    dot_general x8, matrix products, times_transpose(): lax.dot_general(grad_in, weight, (((grad_in.ndim - 1,), (1,)), ((), ())),...  59 us
  transfers between devices with their start and end apart: 12, of which 11 were waited for; matrix products, arithmetic and copies ran while one was open for 17% of the time, Pallas kernels for 0%

commit v1 on v0

--- a/solution.py
+++ b/solution.py
@@ -1,6 +1,8 @@
 import jax
 import jax.numpy as jnp
 from jax import lax
+from jax.experimental import pallas as pl
+from jax.experimental.pallas import tpu as pltpu
 from jax.sharding import PartitionSpec as P
 
 EPSILON = 1e-05
@@ -437,6 +439,710 @@
     )
 
 
+SELV = 72
+SELO = 92
+LANES = 128
+
+
+def call(kernel, out_shape, *args, grid=None, in_specs=None, out_specs=None, scratch=(), flops=0, limit=56):
+    moved = sum(a.size * a.dtype.itemsize for a in jax.tree.leaves((args, out_shape)))
+    extra = {}
+    if grid is not None:
+        extra["grid"] = grid
+        extra["in_specs"] = in_specs
+        extra["out_specs"] = out_specs
+    elif in_specs is not None:
+        extra["in_specs"] = in_specs
+    return pl.pallas_call(
+        kernel,
+        out_shape=out_shape,
+        scratch_shapes=list(scratch),
+        compiler_params=pltpu.CompilerParams(vmem_limit_bytes=limit * 1024 * 1024),
+        cost_estimate=pl.CostEstimate(flops=int(flops), bytes_accessed=int(moved), transcendentals=0),
+        **extra,
+    )(*args)
+
+
+def full(shape):
+    rank = len(shape)
+    return pl.BlockSpec(tuple(shape), lambda s: (0,) * rank)
+
+
+def shaped(shape, dtype=HALF_TYPE):
+    return jax.ShapeDtypeStruct(tuple(shape), dtype)
+
+
+def nn(a, b):
+    return lax.dot_general(a, b, (((1,), (0,)), ((), ())), preferred_element_type=FULL_TYPE)
+
+
+def nt(a, b):
+    return lax.dot_general(a, b, (((1,), (1,)), ((), ())), preferred_element_type=FULL_TYPE)
+
+
+def tn(a, b):
+    return lax.dot_general(a, b, (((0,), (0,)), ((), ())), preferred_element_type=FULL_TYPE)
+
+
+def layer_stats(v):
+    centred = v - jnp.mean(v, axis=-1, keepdims=True)
+    inv = lax.rsqrt(jnp.mean(centred * centred, axis=-1, keepdims=True) + EPSILON)
+    return centred * inv, inv
+
+
+def turned(v, cos, sin):
+    return v * cos + pltpu.roll(v, v.shape[-1] // 2, axis=v.ndim - 1) * sin
+
+
+def lane_ids(shape, dim):
+    return lax.broadcasted_iota(jnp.int32, shape, dim)
+
+
+def pre_kernel(tok, gain, bias, wq, wk, wv, sel, vid, oid, cos, sin, qkv, proj, gate):
+    heads = qkv.shape[0]
+    experts = wv.shape[1] // (heads * LANES)
+    low = tok[0]
+    normal, _ = layer_stats(low.astype(FULL_TYPE))
+    normed = (normal * gain[...] + bias[...]).astype(HALF_TYPE)
+    for part, weight in ((0, wq), (1, wk)):
+        pre = nn(normed, weight[...])
+        for h in range(heads):
+            qkv[h, part] = turned(pre[:, h * LANES:(h + 1) * LANES], cos[...], sin[...]).astype(HALF_TYPE)
+    lanes = lane_ids((low.shape[0], LANES), 1)
+    chosen = jnp.zeros((low.shape[0], LANES), FULL_TYPE)
+    tops = vid.shape[2] // heads
+    for h in range(heads):
+        for k in range(tops):
+            j = h * tops + k
+            chosen += (lanes == vid[0, :, j:j + 1] + (SELV + experts * h)).astype(FULL_TYPE)
+            chosen += (lanes == oid[0, :, j:j + 1] + (SELO + experts * h)).astype(FULL_TYPE)
+    gates = jax.nn.sigmoid(nn(normed, sel[...])) * chosen
+    gate[0] = gates
+    for h in range(heads):
+        at = h * experts * LANES
+        block = nn(low, wv[:, at:at + experts * LANES])
+        proj[0, :, at:at + experts * LANES] = block.astype(HALF_TYPE)
+        total = None
+        for e in range(experts):
+            col = SELV + h * experts + e
+            term = gates[:, col:col + 1] * block[:, e * LANES:(e + 1) * LANES]
+            total = term if total is None else total + term
+        qkv[h, 2] = total.astype(HALF_TYPE)
+
+
+def limits_of(i, rows, length):
+    position = i * rows + lane_ids((1, rows), 1)
+    return jnp.minimum(position + 1, length), position
+
+
+def attend_kernel(length, qkv, mixed, out_t, lse):
+    blocks, _, rows, width = qkv.shape
+    scale = width ** (-0.5)
+    values_t = jnp.transpose(
+        qkv[:, 2].reshape(blocks * rows, width).astype(FULL_TYPE)
+    ).astype(HALF_TYPE)
+    for i in range(blocks):
+        n = (i + 1) * rows
+        keys = qkv[0:i + 1, 1].reshape(n, width)
+        limit, position = limits_of(i, rows, length[0])
+        scores = nt(keys, qkv[i, 0]) * scale
+        scores = jnp.where(lane_ids((n, rows), 0) < limit, scores, -1e30)
+        top = jnp.max(scores, axis=0, keepdims=True)
+        weights = jnp.exp(scores - top)
+        total = jnp.sum(weights, axis=0, keepdims=True)
+        attended = nn(values_t[:, :n], weights.astype(HALF_TYPE)) / total
+        out_t[:, i * rows:(i + 1) * rows] = attended
+        lse[:, i * rows:(i + 1) * rows] = top + jnp.log(total)
+        live = (position < length[0]).astype(FULL_TYPE)
+        mixed[i] = jnp.transpose(attended * live).astype(HALF_TYPE)
+
+
+def attend_back_kernel(length, qkv, d_out, out_t, lse, cos, sin, d_qkv, d_keys, d_values):
+    blocks, _, rows, width = qkv.shape
+    scale = width ** (-0.5)
+    keys_t = jnp.transpose(
+        qkv[:, 1].reshape(blocks * rows, width).astype(FULL_TYPE)
+    ).astype(HALF_TYPE)
+    d_keys[...] = jnp.zeros_like(d_keys)
+    d_values[...] = jnp.zeros_like(d_values)
+    for i in range(blocks):
+        n = (i + 1) * rows
+        here = slice(i * rows, (i + 1) * rows)
+        limit, _ = limits_of(i, rows, length[0])
+        query = qkv[i, 0]
+        d_att = d_out[i]
+        delta = jnp.sum(jnp.transpose(d_att.astype(FULL_TYPE)) * out_t[:, here], axis=0, keepdims=True)
+        scores = nt(qkv[0:i + 1, 1].reshape(n, width), query) * scale
+        probs = jnp.where(lane_ids((n, rows), 0) < limit, jnp.exp(scores - lse[:, here]), 0.0)
+        d_probs = nt(qkv[0:i + 1, 2].reshape(n, width), d_att)
+        d_scores = (probs * (d_probs - delta)).astype(HALF_TYPE)
+        d_values[0:n, :] += nn(probs.astype(HALF_TYPE), d_att)
+        d_keys[0:n, :] += nn(d_scores, query)
+        d_query = jnp.transpose(nn(keys_t[:, :n], d_scores)) * scale
+        d_qkv[i, 0] = turned(d_query, cos[here, :], -sin[here, :]).astype(HALF_TYPE)
+    for i in range(blocks):
+        here = slice(i * rows, (i + 1) * rows)
+        d_qkv[i, 1] = turned(d_keys[here, :] * scale, cos[here, :], -sin[here, :]).astype(HALF_TYPE)
+        d_qkv[i, 2] = d_values[here, :].astype(HALF_TYPE)
+
+
+def gated(mixed, gate, hp, e, experts):
+    parts = []
+    for h in (2 * hp, 2 * hp + 1):
+        col = SELO + h * experts + e
+        parts.append((gate[:, col:col + 1] * mixed[h].astype(FULL_TYPE)).astype(HALF_TYPE))
+    return jnp.concatenate(parts, axis=1)
+
+
+def out_block(w_out, hp, e, width):
+    block = w_out[2 * hp:2 * hp + 2, :, e * width:(e + 1) * width]
+    return block.reshape(2 * block.shape[1], width)
+
+
+def post_kernel(mixed, gate, w_out, tok, gain, bias, w_sel, ids, eids, places, after, rows, gates, sent):
+    width = tok.shape[2]
+    heads = w_out.shape[0]
+    experts = w_out.shape[2] // width
+    total = tok[0].astype(FULL_TYPE)
+    gate_here = gate[0]
+    mixed_here = mixed[...]
+    for hp in range(heads // 2):
+        for e in range(experts):
+            total += nn(gated(mixed_here, gate_here, hp, e, experts), out_block(w_out, hp, e, width))
+    after[...] = total
+    rows[...] = total.astype(HALF_TYPE)
+    normal, _ = layer_stats(total)
+    normed = (normal * gain[...] + bias[...]).astype(HALF_TYPE)
+    chosen = jnp.zeros((eids.shape[0], ids.shape[2]), FULL_TYPE)
+    for k in range(ids.shape[1]):
+        chosen += (eids[...] == ids[0, k:k + 1, :]).astype(FULL_TYPE)
+    values = jax.nn.sigmoid(nt(w_sel[...], normed)) * chosen
+    gates[...] = values
+    moved = nn(places[...], values.astype(HALF_TYPE)).astype(HALF_TYPE)
+    sent[...] = moved.reshape(sent.shape)
+
+
+def expand(count, cols, first):
+    rows = lane_ids((count, cols), 0)
+    cut = lane_ids((count, cols), 1)
+    hit = None
+    for i in range(cols // LANES):
+        inside = (cut >= i * LANES) & (cut < (i + 1) * LANES) & (rows == first + i)
+        hit = inside if hit is None else hit | inside
+    return hit.astype(FULL_TYPE).astype(HALF_TYPE)
+
+
+def experts_kernel(*refs):
+    rows, cot, gate = refs[:3]
+    ups, downs = refs[3:11], refs[11:19]
+    d_rows, branch, d_gate, inner, d_pre = refs[19:]
+    low, cot_low, gates = rows[...], cot[...], gate[...]
+    row_total = branch_total = gate_total = None
+    for p in range(8):
+        w_up, w_down = ups[p][...], downs[p][...]
+        cols = w_up.shape[1]
+        spread = expand(gates.shape[0], cols, p * (cols // LANES))
+        gate_wide = tn(gates, spread)
+        pre = nn(low, w_up)
+        d_in = nt(cot_low, w_down)
+        root = 0.7978845608028654
+        square = pre * pre
+        tanh = jnp.tanh(root * pre * (1.0 + 0.044715 * square))
+        half = 0.5 * (1.0 + tanh)
+        act = pre * half
+        slope = half + 0.5 * pre * (1.0 - tanh * tanh) * (root * (1.0 + 3 * 0.044715 * square))
+        in_low = (act * gate_wide).astype(HALF_TYPE)
+        pre_low = (slope * gate_wide * d_in).astype(HALF_TYPE)
+        inner[:, p * cols:(p + 1) * cols] = in_low
+        d_pre[:, p * cols:(p + 1) * cols] = pre_low
+        g = nt(spread, (d_in * act).astype(HALF_TYPE))
+        r = nt(pre_low, w_up)
+        b = nn(in_low, w_down)
+        gate_total = g if p == 0 else gate_total + g
+        row_total = r if p == 0 else row_total + r
+        branch_total = b if p == 0 else branch_total + b
+    d_rows[...] = row_total.astype(HALF_TYPE)
+    branch[...] = branch_total.astype(HALF_TYPE)
+    d_gate[...] = gate_total.astype(HALF_TYPE)
+
+
+def expert_grads_kernel(*refs):
+    count = 4
+    rows, cots = refs[0:count], refs[count:2 * count]
+    pres, inners = refs[2 * count:3 * count], refs[3 * count:4 * count]
+    up, down = refs[4 * count:]
+    total = None
+    for i in range(count):
+        term = tn(rows[i][...], pres[i][...])
+        total = term if i == 0 else total + term
+    up[0] = total.astype(HALF_TYPE)
+    for i in range(count):
+        term = tn(inners[i][...], cots[i][...])
+        total = term if i == 0 else total + term
+    down[0] = total.astype(HALF_TYPE)
+
+
+def mid_kernel(length, r0, r1, r2, r3, g0, g1, g2, g3, cot, after, gates, gain, bias, w_sel, places, order, w_out, gate, mixed,
+               d_after, d_att, d_gate_out, small, acc):
+    step = pl.program_id(0)
+    width = cot.shape[2]
+    heads = w_out.shape[0]
+    experts = w_out.shape[2] // width
+    row_count = cot.shape[1]
+    d_rel = jnp.concatenate([g0[...], g1[...], g2[...], g3[...]], axis=0)
+    d_gate = tn(places[...], d_rel)
+    values = gates[...]
+    d_logit = (d_gate * values * (1.0 - values)).astype(HALF_TYPE)
+    normal, inv = layer_stats(after[...])
+    normed = (normal * gain[...] + bias[...]).astype(HALF_TYPE)
+    d_normed = tn(d_logit, w_sel[...])
+    sel_part = nn(d_logit, normed)
+    gain_part = jnp.sum(d_normed * normal, axis=0, keepdims=True)
+    bias_part = jnp.sum(d_normed, axis=0, keepdims=True)
+    count = sel_part.shape[0]
+
+    @pl.when(step == 0)
+    def _():
+        acc[...] = jnp.zeros_like(acc)
+
+    acc[0:count, :] += sel_part
+    acc[count:count + 1, :] += gain_part
+    acc[count + 1:count + 2, :] += bias_part
+    d_row = (
+        r0[...].astype(FULL_TYPE) + r1[...].astype(FULL_TYPE)
+        + r2[...].astype(FULL_TYPE) + r3[...].astype(FULL_TYPE)
+    )
+    total = cot[0].astype(FULL_TYPE) + d_row + norm_back(d_normed, normal, inv, gain[...])
+    d_after[...] = total
+    total_low = total.astype(HALF_TYPE)
+    mixed_here = mixed[...]
+    gate_here = gate[0]
+    lanes = lane_ids((2 * LANES, LANES), 1)
+    second = (lane_ids((2 * LANES, LANES), 0) >= LANES).astype(jnp.int32)
+    d_gates = jnp.zeros((row_count, LANES), FULL_TYPE)
+    for hp in range(heads // 2):
+        both = jnp.concatenate([mixed_here[2 * hp], mixed_here[2 * hp + 1]], axis=1).astype(FULL_TYPE)
+        sums = [None, None]
+        for e in range(experts):
+            d_mixed = nt(total_low, out_block(w_out, hp, e, width))
+            hit = (lanes == SELO + 2 * hp * experts + e + second * experts).astype(FULL_TYPE).astype(HALF_TYPE)
+            d_gates += nn((both * d_mixed).astype(HALF_TYPE), hit)
+            for i in range(2):
+                col = SELO + (2 * hp + i) * experts + e
+                term = gate_here[:, col:col + 1] * d_mixed[:, i * LANES:(i + 1) * LANES]
+                sums[i] = term if e == 0 else sums[i] + term
+        for i in range(2):
+            position = length[1] + lane_ids((row_count, 1), 0)
+            live = (position < length[2 + step]).astype(FULL_TYPE)
+            d_att[2 * hp + i] = (sums[i] * live).astype(HALF_TYPE)
+    d_gate_out[0] = d_gates
+
+    @pl.when(step == pl.num_programs(0) - 1)
+    def _():
+        small[...] = tn(acc[...].astype(HALF_TYPE), order[...])
+
+
+def out_grad_kernel(mixed, gate, d_after, out):
+    heads, experts = 4, out.shape[1] // d_after.shape[1]
+    width = d_after.shape[1]
+    seqs, row_count = gate.shape[0], gate.shape[1]
+    low = d_after[...].astype(HALF_TYPE)
+    for hp in range(heads // 2):
+        for e in range(experts):
+            total = None
+            for s in range(seqs):
+                left = gated([mixed[s * heads + h] for h in range(heads)], gate[s], hp, e, experts)
+                term = tn(left, low[s * row_count:(s + 1) * row_count, :])
+                total = term if total is None else total + term
+            out[2 * hp * LANES:(2 * hp + 2) * LANES, e * width:(e + 1) * width] = total.astype(HALF_TYPE)
+
+
+def last_kernel(d_qkv, tok, gain, bias, wq, wk, sel, proj, gate, d_gate_out, small, d_after,
+                grads, d_proj, part, d_qk, d_sel):
+    seqs, row_count, width = tok.shape
+    heads = 4
+    experts = proj.shape[2] // (heads * LANES)
+    lanes = lane_ids((LANES, LANES), 1)
+    gain_sum = bias_sum = 0.0
+    normed_t, tok_t = [], []
+    for s in range(seqs):
+        low = tok[s]
+        normal, inv = layer_stats(low.astype(FULL_TYPE))
+        normed = (normal * gain[...] + bias[...]).astype(HALF_TYPE)
+        d_gates = d_gate_out[s]
+        gate_here = gate[s]
+        here = slice(s * row_count, (s + 1) * row_count)
+        for h in range(heads):
+            for part_id in range(2):
+                at = part_id * heads * LANES + h * LANES
+                d_qk[here, at:at + LANES] = d_qkv[s * heads + h, part_id]
+            d_value = d_qkv[s * heads + h, 2].astype(FULL_TYPE)
+            for e in range(experts):
+                col = SELV + h * experts + e
+                at = (h * experts + e) * LANES
+                d_proj[here, at:at + LANES] = (gate_here[:, col:col + 1] * d_value).astype(HALF_TYPE)
+                hit = (lanes == col).astype(FULL_TYPE).astype(HALF_TYPE)
+                product = (proj[s, :, at:at + LANES].astype(FULL_TYPE) * d_value).astype(HALF_TYPE)
+                d_gates += nn(product, hit)
+        d_logit = (d_gates * gate_here * (1.0 - gate_here)).astype(HALF_TYPE)
+        d_sel[here, :] = d_logit
+        half = heads * LANES
+        d_normed = (
+            nt(d_qk[here, 0:half], wq[...]) + nt(d_qk[here, half:2 * half], wk[...]) + nt(d_logit, sel[...])
+        )
+        gain_sum += jnp.sum(d_normed * normal, axis=0, keepdims=True)
+        bias_sum += jnp.sum(d_normed, axis=0, keepdims=True)
+        part[here, :] = d_after[here, :] + norm_back(d_normed, normal, inv, gain[...])
+        normed_t.append(jnp.transpose(normed.astype(FULL_TYPE)).astype(HALF_TYPE))
+        tok_t.append(jnp.transpose(low.astype(FULL_TYPE)).astype(HALF_TYPE))
+    normed_t = jnp.concatenate(normed_t, axis=1)
+    tok_t = jnp.concatenate(tok_t, axis=1)
+    size = 512
+    at = 0
+    for left, right in ((normed_t, d_qk), (tok_t, d_proj)):
+        for b in range(right.shape[1] // size):
+            grads[:, at:at + size] = nn(left, right[:, b * size:(b + 1) * size]).astype(HALF_TYPE)
+            at += size
+    rows = jnp.concatenate([gain_sum, bias_sum, jnp.zeros((14, width), FULL_TYPE)], axis=0).astype(HALF_TYPE)
+    spot = (lane_ids((16, LANES), 1) == lane_ids((16, LANES), 0) + 66) & (lane_ids((16, LANES), 0) < 2)
+    spread = tn(rows, spot.astype(FULL_TYPE).astype(HALF_TYPE))
+    grads[:, at:at + LANES] = (small[...] + nn(normed_t, d_sel[...]) + spread).astype(HALF_TYPE)
+
+
+def token_grad_kernel(part, d_proj, wv, out):
+    out[...] = (part[...] + nt(d_proj[...], wv[...])).astype(HALF_TYPE)
+
+
+def output_kernel(after, b0, b1, b2, b3, out):
+    out[...] = (
+        after[...] + b0[...].astype(FULL_TYPE) + b1[...].astype(FULL_TYPE)
+        + b2[...].astype(FULL_TYPE) + b3[...].astype(FULL_TYPE)
+    ).astype(HALF_TYPE)
+
+
+class Place:
+    def __init__(self):
+        self.wide = lax.axis_index("wide")
+        self.narrow = lax.axis_index("narrow")
+        self.z, self.x = self.wide // 2, self.wide % 2
+        self.y, self.c = self.narrow // 2, self.narrow % 2
+
+    @staticmethod
+    def pairs(move):
+        every = []
+        for z in range(4):
+            for x in range(2):
+                for y in range(2):
+                    for c in range(2):
+                        tz, tx, ty, tc = move(z, x, y, c)
+                        every.append(((z * 2 + x) * 4 + y * 2 + c, (tz * 2 + tx) * 4 + ty * 2 + tc))
+        return every
+
+    def send(self, value, move):
+        return lax.ppermute(value, ("wide", "narrow"), self.pairs(move))
+
+    def swap_x(self, value):
+        return self.send(value, lambda z, x, y, c: (z, 1 - x, y, c))
+
+    def swap_y(self, value):
+        return self.send(value, lambda z, x, y, c: (z, x, 1 - y, c))
+
+    def swap_xy(self, value):
+        return self.send(value, lambda z, x, y, c: (z, 1 - x, 1 - y, c))
+
+    def swap_c(self, value):
+        return self.send(value, lambda z, x, y, c: (z, x, y, 1 - c))
+
+    def shift_z(self, value, k):
+        return self.send(value, lambda z, x, y, c: ((z + k) % 4, x, y, c))
+
+
+def pick(array, index):
+    return lax.dynamic_index_in_dim(array, index, 0, keepdims=False)
+
+
+def add(*terms):
+    total = terms[0].astype(FULL_TYPE)
+    for term in terms[1:]:
+        total = total + term.astype(FULL_TYPE)
+    return total.astype(HALF_TYPE)
+
+
+def in_order(bit, mine, other):
+    return jnp.stack([jnp.where(bit == 0, mine, other), jnp.where(bit == 0, other, mine)])
+
+
+def sum_everywhere(place, array):
+    rows, cols = array.shape
+    parts = array.reshape(2, 2, 2, 2, 4, rows // 64, cols)
+    bits = ((place.y, place.swap_y), (place.x, place.swap_x))
+
+    def halve(bit, swap, value):
+        return add(pick(value, bit), swap(pick(value, 1 - bit)))
+
+    kept = halve(place.c, place.swap_c, parts)
+    first = [halve(*bits[i], kept[i]) for i in range(2)]
+    second = [halve(*bits[1 - i], first[i]) for i in range(2)]
+    value = jnp.stack(second, axis=1)
+    came = [place.shift_z(pick(value, (place.z + k) % 4), k) for k in (1, 2, 3)]
+    done = add(pick(value, place.z), *came)
+    around = [done] + [place.shift_z(done, k) for k in (1, 2, 3)]
+    around = jnp.stack(around)
+    ordered = jnp.stack([pick(around, (place.z - k) % 4) for k in range(4)])
+    back = []
+    for i in range(2):
+        own = ordered[:, i]
+        bit, swap = bits[1 - i]
+        own = in_order(bit, own, swap(own))
+        bit, swap = bits[i]
+        back.append(in_order(bit, own, swap(own)))
+    own = jnp.stack(back)
+    whole = in_order(place.c, own, place.swap_c(own))
+    return whole.reshape(rows, cols)
+
+
+def tuned_device(
+    tokens, lengths, value_ids, out_ids, mlp_ids, w_query, w_key, w_value, w_out, sel_value, sel_out,
+    gain_one, bias_one, gain_two, bias_two, w_select, w_up, w_down, cotangent,
+):
+    seqs, row_count, width = tokens.shape
+    heads, head_dim = w_out.shape[0], w_out.shape[1]
+    experts = w_out.shape[2] // width
+    pair_count = seqs * heads
+    span = 8 * row_count
+    all_rows = seqs * row_count
+    place = Place()
+    first_row = place.wide * row_count
+    row = lambda v: v.reshape(1, -1)
+
+    half = head_dim // 2
+    frequency = 10000.0 ** (-(jnp.arange(half).astype(FULL_TYPE) * 2.0 / head_dim))
+    angles = jnp.arange(span).astype(FULL_TYPE)[:, None] * frequency[None, :]
+    cosine, sine = jnp.cos(angles), jnp.sin(angles)
+    cosine = jnp.concatenate([cosine, cosine], axis=1)
+    sine = jnp.concatenate([-sine, sine], axis=1)
+    here = lambda t: lax.dynamic_slice_in_dim(t, first_row, row_count, 0)
+    sel = jnp.concatenate(
+        [
+            jnp.zeros((width, SELV), HALF_TYPE), sel_value, sel_out,
+            jnp.zeros((width, LANES - SELO - heads * experts), HALF_TYPE),
+        ],
+        axis=1,
+    )
+    value_flat = value_ids.reshape(seqs, row_count, -1)
+    out_flat = out_ids.reshape(seqs, row_count, -1)
+
+    local = w_up.shape[1] // 4
+    my_up = lax.dynamic_slice_in_dim(w_up, place.narrow * local, local, 1)
+    my_down = lax.dynamic_slice_in_dim(w_down, place.narrow * local, local, 0)
+    peer = place.narrow + 1 - 2 * place.c
+    ups = [my_up, lax.dynamic_slice_in_dim(w_up, peer * local, local, 1)]
+    downs = [my_down, lax.dynamic_slice_in_dim(w_down, peer * local, local, 0)]
+    for k in (1, 2, 3):
+        up_k, down_k = place.shift_z(my_up, 4 - k), place.shift_z(my_down, 4 - k)
+        ups += [up_k, place.swap_c(up_k)]
+        downs += [down_k, place.swap_c(down_k)]
+
+    own_select = jnp.transpose(w_select)
+    select = jnp.concatenate(
+        [own_select] + [lax.ppermute(own_select, "wide", [(i, i ^ k) for i in range(8)]) for k in range(1, 8)]
+    )
+    own_count = own_select.shape[0]
+    select_ids = ((place.wide ^ jnp.arange(8))[:, None] * own_count + jnp.arange(own_count)[None, :]).reshape(-1)
+    kind = place.x * 2 + place.y
+    kinds = kind ^ jnp.arange(4)
+    kx, ky = (kinds // 2)[:, None, None, None], (kinds % 2)[:, None, None, None]
+    kz = ((place.z + jnp.arange(4)) % 4)[None, :, None, None]
+    kc = (place.c ^ jnp.arange(2))[None, None, :, None]
+    ki = jnp.arange(2)[None, None, None, :]
+    sent_ids = ((kz * 2 + kx) * own_count + ky * 4 + kc * 2 + ki).reshape(-1)
+    places = (sent_ids[:, None] == select_ids[None, :]).astype(HALF_TYPE)
+    count = select_ids.shape[0]
+    lanes = jnp.arange(LANES)
+    targets = jnp.concatenate([select_ids, count + jnp.arange(LANES - count)])
+    order = (targets[:, None] == lanes[None, :]).astype(HALF_TYPE)
+
+    cot_own = cotangent.reshape(all_rows, width)
+    cots = [cot_own, place.swap_y(cot_own), place.swap_x(cot_own), place.swap_xy(cot_own)]
+
+    by_seq = lambda shape: pl.BlockSpec((1,) + tuple(shape[1:]), lambda s: (s,) + (0,) * (len(shape) - 1))
+    split = lambda shape: pl.BlockSpec((shape[0] // seqs,) + tuple(shape[1:]), lambda s: (s,) + (0,) * (len(shape) - 1))
+    wide_out = heads * experts * LANES
+    qkv, projected, gate = call(
+        pre_kernel,
+        (
+            shaped((pair_count, 3, row_count, head_dim)),
+            shaped((seqs, row_count, wide_out)),
+            shaped((seqs, row_count, LANES), FULL_TYPE),
+        ),
+        tokens, row(gain_one), row(bias_one), w_query, w_key, w_value, sel, value_flat, out_flat,
+        here(cosine), here(sine),
+        grid=(seqs,),
+        in_specs=[
+            by_seq(tokens.shape), full((1, width)), full((1, width)), full(w_query.shape), full(w_key.shape),
+            full(w_value.shape), full(sel.shape), by_seq(value_flat.shape), by_seq(out_flat.shape),
+            full((row_count, head_dim)), full((row_count, head_dim)),
+        ],
+        out_specs=(
+            split((pair_count, 3, row_count, head_dim)), by_seq((seqs, row_count, wide_out)),
+            by_seq((seqs, row_count, LANES)),
+        ),
+        flops=2 * all_rows * width * 3712,
+    )
+    qkv = lax.all_to_all(qkv, "wide", 0, 0, tiled=True)
+    length = pick(lengths, place.wide // heads).reshape(1)
+    smem = pl.BlockSpec(memory_space=pltpu.SMEM)
+    vmem = pl.BlockSpec(memory_space=pltpu.VMEM)
+    mixed, out_t, lse = call(
+        attend_kernel,
+        (
+            shaped((8, row_count, head_dim)), shaped((head_dim, span), FULL_TYPE), shaped((1, span), FULL_TYPE),
+        ),
+        length, qkv,
+        in_specs=[smem, vmem],
+        flops=2 * span * span * head_dim,
+    )
+    mixed = lax.all_to_all(mixed, "wide", 0, 0, tiled=True)
+
+    own_mlp = lax.dynamic_slice_in_dim(mlp_ids, first_row, row_count, 1)
+    own_mlp = jnp.swapaxes(own_mlp, 1, 2)
+    token_cols = lambda n: pl.BlockSpec((n, row_count), lambda s: (0, s))
+    after, rows_own, gates, sent = call(
+        post_kernel,
+        (
+            shaped((all_rows, width), FULL_TYPE), shaped((all_rows, width)),
+            shaped((count, all_rows), FULL_TYPE), shaped((4, count // 4, all_rows)),
+        ),
+        mixed, gate, w_out, tokens, row(gain_two), row(bias_two), select, own_mlp,
+        select_ids.reshape(-1, 1), places,
+        grid=(seqs,),
+        in_specs=[
+            split(mixed.shape), by_seq(gate.shape), full(w_out.shape), by_seq(tokens.shape), full((1, width)),
+            full((1, width)), full(select.shape), by_seq(own_mlp.shape), full((count, 1)), full(places.shape),
+        ],
+        out_specs=(
+            split((all_rows, width)), split((all_rows, width)), token_cols(count),
+            pl.BlockSpec((4, count // 4, row_count), lambda s: (0, 0, s)),
+        ),
+        flops=2 * all_rows * width * wide_out,
+    )
+
+    swaps = (lambda v: v, place.swap_y, place.swap_x, place.swap_xy)
+    rows_in = [swaps[i](rows_own) for i in range(4)]
+    gates_in = [swaps[i](sent[i]) for i in range(4)]
+    hidden = 8 * local
+    results = []
+    for i in range(4):
+        results.append(
+            call(
+                experts_kernel,
+                (
+                    shaped((all_rows, width)), shaped((all_rows, width)), shaped((count // 4, all_rows)),
+                    shaped((all_rows, hidden)), shaped((all_rows, hidden)),
+                ),
+                rows_in[i], cots[i], gates_in[i], *ups, *downs,
+                flops=8 * all_rows * width * hidden,
+            )
+        )
+    d_rows = [swaps[i](results[i][0]) for i in range(4)]
+    d_gates = [swaps[i](results[i][2]) for i in range(4)]
+    branches = [swaps[i](results[i][1]) for i in range(4)]
+
+    cols = lambda: pl.BlockSpec((all_rows, local), lambda p: (0, p))
+    whole = lambda: pl.BlockSpec((all_rows, width), lambda p: (0, 0))
+    grad_up, grad_down = call(
+        expert_grads_kernel,
+        (shaped((8, width, local)), shaped((8, local, width))),
+        *rows_in, *cots, *[r[4] for r in results], *[r[3] for r in results],
+        grid=(8,),
+        in_specs=[whole() for _ in range(8)] + [cols() for _ in range(8)],
+        out_specs=(
+            pl.BlockSpec((1, width, local), lambda p: (p, 0, 0)), pl.BlockSpec((1, local, width), lambda p: (p, 0, 0)),
+        ),
+        flops=16 * all_rows * width * hidden,
+    )
+
+    live_info = jnp.concatenate([jnp.zeros((1,), jnp.int32), first_row.reshape(1).astype(jnp.int32), lengths])
+    d_after, d_att, d_gate_out, small = call(
+        mid_kernel,
+        (
+            shaped((all_rows, width), FULL_TYPE), shaped((pair_count, row_count, head_dim)),
+            shaped((seqs, row_count, LANES), FULL_TYPE), shaped((width, LANES), FULL_TYPE),
+        ),
+        live_info, *d_rows, *d_gates, cotangent, after, gates, row(gain_two), row(bias_two), select, places, order,
+        w_out, gate, mixed,
+        grid=(seqs,),
+        in_specs=[smem] + [split((all_rows, width))] * 4 + [token_cols(count // 4)] * 4 + [
+            by_seq(cotangent.shape), split((all_rows, width)), token_cols(count), full((1, width)), full((1, width)),
+            full(select.shape), full(places.shape), full(order.shape), full(w_out.shape), by_seq(gate.shape),
+            split(mixed.shape),
+        ],
+        out_specs=(
+            split((all_rows, width)), split((pair_count, row_count, head_dim)),
+            by_seq((seqs, row_count, LANES)), full((width, LANES)),
+        ),
+        scratch=[pltpu.VMEM((LANES, width), FULL_TYPE)],
+        flops=2 * all_rows * width * wide_out,
+    )
+    d_att = lax.all_to_all(d_att, "wide", 0, 0, tiled=True)
+    d_qkv = call(
+        attend_back_kernel,
+        shaped((8, 3, row_count, head_dim)),
+        length, qkv, d_att, out_t, lse, cosine, sine,
+        in_specs=[smem] + [vmem] * 6,
+        scratch=[pltpu.VMEM((span, head_dim), FULL_TYPE), pltpu.VMEM((span, head_dim), FULL_TYPE)],
+        flops=5 * span * span * head_dim,
+    )
+    d_qkv = lax.all_to_all(d_qkv, "wide", 0, 0, tiled=True)
+
+    grad_out = call(
+        out_grad_kernel, shaped((heads * head_dim, experts * width)), mixed, gate, d_after,
+        flops=2 * all_rows * width * wide_out,
+    )
+    output = call(output_kernel, shaped((all_rows, width)), after, *branches)
+
+    grads, d_proj, part = call(
+        last_kernel,
+        (shaped((width, 2 * heads * head_dim + wide_out + LANES)), shaped((all_rows, wide_out)), shaped((all_rows, width), FULL_TYPE)),
+        d_qkv, tokens, row(gain_one), row(bias_one), w_query, w_key, sel, projected, gate, d_gate_out, small, d_after,
+        scratch=[pltpu.VMEM((all_rows, 2 * heads * head_dim), HALF_TYPE), pltpu.VMEM((all_rows, LANES), HALF_TYPE)],
+        flops=2 * all_rows * width * 4700,
+    )
+    grad_tokens = call(token_grad_kernel, shaped((all_rows, width)), part, d_proj, w_value, flops=2 * all_rows * width * wide_out)
+
+    grad_out = sum_everywhere(place, grad_out).astype(FULL_TYPE).reshape(heads, head_dim, -1)
+    grads = sum_everywhere(place, grads).astype(FULL_TYPE)
+    wide_qk = heads * head_dim
+    grad_query, grad_key = grads[:, :wide_qk], grads[:, wide_qk:2 * wide_qk]
+    grad_value = grads[:, 2 * wide_qk:2 * wide_qk + wide_out]
+    small = grads[:, 2 * wide_qk + wide_out:]
+    grad_select = lax.dynamic_slice_in_dim(small, place.wide * own_count, own_count, 1)
+    grad_gain_two, grad_bias_two = small[:, count], small[:, count + 1]
+    grad_gain_one, grad_bias_one = small[:, count + 2], small[:, count + 3]
+    grad_sel_value = small[:, SELV:SELV + heads * experts]
+    grad_sel_out = small[:, SELO:SELO + heads * experts]
+
+    def experts_sum(pieces):
+        by_z = [add(pieces[2 * k], place.swap_c(pieces[2 * k + 1])) for k in range(4)]
+        mine = add(by_z[0], *[place.shift_z(by_z[k], k) for k in (1, 2, 3)])
+        pair = in_order(place.c, mine, place.swap_c(mine))
+        return in_order(place.y, pair, place.swap_y(pair)).reshape((4,) + mine.shape)
+
+    up_sum = experts_sum(grad_up)
+    down_sum = experts_sum(grad_down)
+    grad_up = jnp.swapaxes(up_sum, 0, 1).reshape(width, -1).astype(FULL_TYPE)
+    grad_down = down_sum.reshape(-1, width).astype(FULL_TYPE)
+    return (
+        output.reshape(tokens.shape), grad_tokens.reshape(tokens.shape), grad_query, grad_key, grad_value, grad_out,
+        grad_sel_value, grad_sel_out, grad_gain_one, grad_bias_one, grad_gain_two, grad_bias_two, grad_select,
+        grad_up, grad_down,
+    )
+
+
+def fits(mesh):
+    return dict(mesh.shape) == {"wide": 8, "narrow": 4}
+
+
 def solution(mesh):
     placed = (
         P("narrow", "wide", None),
@@ -460,7 +1166,7 @@
         P("narrow", "wide", None),
     )
     return jax.shard_map(
-        per_device,
+        tuned_device if fits(mesh) else per_device,
         mesh=mesh,
         in_specs=placed,
         out_specs=(

time: 2120 us -> 862 us (0.41)
  waiting for transfers between devices: 1480 us -> 369 us
  matrix products: 269 us -> 0 us
  Pallas kernels: 0 us -> 189 us
  starting transfers between devices: 0.49 us -> 168 us
  local copies, waits for them, and re-layouts: 169 us -> 56.9 us
  blocking collectives: 54.6 us -> 0 us
  other arithmetic: 117 us -> 69.4 us
    reduce_scatter x5 -> x0, waiting for transfers between devices: 688 us -> none  [the longest x1 285 us: per_device(): lax.psum_scatter(row_part, 'wide', scatter_dimension=1, tiled=True)]
    psum x2 -> x0, waiting for transfers between devices: 399 us -> none  [the longest x1 344 us: per_device(): lax.psum((grad_query, grad_key, grad_value, grad_out, grad_sel_value, gra...]
    all_gather x5 -> x0, waiting for transfers between devices: 395 us -> none  [the longest x1 115 us: expert_forward(): lax.all_gather(for_sending(after_attn.astype(HALF_TYPE)), 'wide', axis=1,...]
    ppermute x0 -> x87, waiting for transfers between devices: none -> 322 us  [the longest x80 299 us: send(): return lax.ppermute(value, ('wide', 'narrow'), self.pairs(move))]
    dot_general x33 -> x0, matrix products: 269 us -> none  [the longest x8 59 us: times_transpose(): lax.dot_general(grad_in, weight, (((grad_in.ndim - 1,), (1,)), ((), ())),...]
    pallas_call x0 -> x14, Pallas kernels: none -> 189 us  [call(): pl.pallas_call(kernel, out_shape=out_shape, scratch_shapes=list(scratch),...]
    ppermute x0 -> x87, starting transfers between devices: none -> 130 us  [the longest x80 119 us: send(): return lax.ppermute(value, ('wide', 'narrow'), self.pairs(move))]
    mul x7 -> x0, local copies, waits for them, and re-layouts: 55.2 us -> none  [the longest x2 54.2 us: attend_forward(): after_attn = inputs + jnp.sum(out_gate[..., None] * expert_out, axis=(2, 3))]
  transfers between devices with their start and end apart: 12 -> 91, of which waited for: 11 -> 32; matrix products, arithmetic and copies ran while one was open for 17% -> 9% of each run, Pallas kernels for 0% -> 21%
where the time goes in v1:
time: 862 us; the launch traced here: 854 us
  waiting for transfers between devices  369 us (43%)
  Pallas kernels  189 us (22%)
  starting transfers between devices  168 us (19%)
  other arithmetic  69.4 us (8%)
  local copies, waits for them, and re-layouts  56.9 us (7%)
    ppermute x80, waiting for transfers between devices, send(): return lax.ppermute(value, ('wide', 'narrow'), self.pairs(move))  299 us
    pallas_call x14, Pallas kernels, call(): pl.pallas_call(kernel, out_shape=out_shape, scratch_shapes=list(scratch),...  189 us
    ppermute x80, starting transfers between devices, send(): return lax.ppermute(value, ('wide', 'narrow'), self.pairs(move))  119 us
    all_to_all x1, waiting for transfers between devices, tuned_device(): qkv = lax.all_to_all(qkv, 'wide', 0, 0, tiled=True)  46.9 us
    ppermute x7, waiting for transfers between devices, tuned_device(): lax.ppermute(own_select, 'wide', [(i, i ^ k) for i in range(8)])  23.2 us
    another operation x22, other arithmetic, in_order(): jnp.stack([jnp.where(bit == 0, mine, other), jnp.where(bit == 0, other, m...  23 us
    all_to_all x1, starting transfers between devices, tuned_device(): d_qkv = lax.all_to_all(d_qkv, 'wide', 0, 0, tiled=True)  22.9 us
  transfers between devices with their start and end apart: 91, of which 32 were waited for; matrix products, arithmetic and copies ran while one was open for 9% of the time, Pallas kernels for 21%

profile of v1, /device:TPU:0, one launch (start us, length us, event | category | flops | bytes accessed | tf_op | source)
XLA Modules:
  0.0 854.0 jit_solution(14741357236424191934)
XLA Ops:
  12.8 10.7 %shard_map.298 = (bf16[8,3,256,128]{3,2,1,0:T(8,128)(2,1)}, bf16[2,256,2560]{2,1,0:T(8,128)(2,1)}, f32[2,256,128]{2,1,0:T(8,128)}) custom-call(bf16[2,256,1024]{2,1,0:T(8,128)(2,1)} %tok.5, f32[1,1024]{1,0:T(1,128)} %bitcast.291, f32[1,1024]{1,0:T(1,128)} %bitcast.293, bf16[1024,512]{1,0:T(8,128)(2,1)} %wq.3, bf16[1024,512]{1,0:T(8,128)(2,1)} %wk.3, ...), custom_call_target="tpu_custom_call" | custom-call | flops 3892314112 | bytes 13410304 | tf_op jit(solution)/shard_map/pallas_call | solution.py:456
  45.9 46.9 %all-to-all-done.qkv = bf16[8,3,256,128]{3,2,1,0:T(8,128)(2,1)} async-done(((bf16[8,3,256,128]{3,2,1,0:T(8,128)(2,1)}), bf16[8,3,256,128]{3,2,1,0:T(8,128)(2,1)}, u32[]{:S(2)}, u32[]{:S(2)}) %all-to-all-start) | async-done | bytes 1572896 | tf_op jit(solution)/shard_map/all_to_all | solution.py:992
  92.8 9.5 %shard_map.299 = (bf16[8,256,128]{2,1,0:T(8,128)(2,1)}, f32[128,2048]{1,0:T(8,128)}, f32[1,2048]{1,0:T(1,128)}) custom-call(s32[1]{0:T(128)} %dynamic_slice.144.length, bf16[8,3,256,128]{3,2,1,0:T(8,128)(2,1)} %all-to-all-done.qkv), custom_call_target="tpu_custom_call" | custom-call | flops 1073741824 | bytes 3153924 | tf_op jit(solution)/shard_map/pallas_call | solution.py:456
  121.8 7.8 collective-permute-start.17
  131.7 11.2 %collective-permute-done.1 = bf16[8,1024]{1,0:T(8,128)(2,1)S(1)} collective-permute-done((bf16[8,1024]{1,0:T(8,128)(2,1)}, bf16[8,1024]{1,0:T(8,128)(2,1)S(1)}, u32[]{:S(2)}, u32[]{:S(2)}) %collective-permute-start.1) | collective-permute-done | bytes 16416 | tf_op jit(solution)/shard_map/ppermute | solution.py:948
  152.9 16.3 %collective-permute-done.15.refs_15_ = bf16[256,1024]{1,0:T(8,128)(2,1)} collective-permute-done((bf16[256,1024]{1,0:T(8,128)(2,1)}, bf16[256,1024]{1,0:T(8,128)(2,1)}, u32[]{:S(2)}, u32[]{:S(2)}) %collective-permute-start.15) | collective-permute-done | bytes 524320 | tf_op jit(solution)/shard_map/ppermute | solution.py:842
  172.5 8.7 %shard_map.300 = (f32[512,1024]{1,0:T(8,128)}, bf16[512,1024]{1,0:T(8,128)(2,1)}, f32[64,512]{1,0:T(8,128)}, bf16[4,16,512]{2,1,0:T(8,128)(2,1)}) custom-call(bf16[8,256,128]{2,1,0:T(8,128)(2,1)} %all-to-all-done.1.mixed, f32[2,256,128]{2,1,0:T(8,128)} %get-tuple-element.56.gate, bf16[4,128,5120]{2,1,0:T(8,128)(2,1)} %w_out.3, bf16[2,256,1024]{2,1,0:T(8,128)(2,1)} %tok.5, ...), custom_call_target="tpu_custom_call" | custom-call | flops 2684354560 | bytes 10600704 | tf_op jit(solution)/shard_map/pallas_call | solution.py:456
  188.8 18.5 %shard_map.301 = (bf16[512,1024]{1,0:T(8,128)(2,1)}, bf16[512,1024]{1,0:T(8,128)(2,1)}, bf16[16,512]{1,0:T(8,128)(2,1)}, bf16[512,2048]{1,0:T(8,128)(2,1)}, bf16[512,2048]{1,0:T(8,128)(2,1)}) custom-call(bf16[512,1024]{1,0:T(8,128)(2,1)} %get-tuple-element.58.refs_0_, bf16[512,1024]{1,0:T(8,128)(2,1)} %bitcast.8.refs_1_.refs_4_, ...), custom_call_target="tpu_custom_call" | custom-call | flops 8589934592 | bytes 16809984 | tf_op jit(solution)/shard_map/pallas_call | solution.py:456
  209.8 19.5 %collective-permute-done.21.refs_2_ = bf16[16,512]{1,0:T(8,128)(2,1)S(1)} collective-permute-done((bf16[16,512]{1,0:T(8,128)(2,1)S(1)}, bf16[16,512]{1,0:T(8,128)(2,1)S(1)}, u32[]{:S(2)}, u32[]{:S(2)}) %collective-permute-start.21) | collective-permute-done | bytes 16416 | tf_op jit(solution)/shard_map/ppermute | solution.py:842
  232.3 18.3 %shard_map.302 = (bf16[512,1024]{1,0:T(8,128)(2,1)}, bf16[512,1024]{1,0:T(8,128)(2,1)}, bf16[16,512]{1,0:T(8,128)(2,1)}, bf16[512,2048]{1,0:T(8,128)(2,1)}, bf16[512,2048]{1,0:T(8,128)(2,1)}) custom-call(bf16[512,1024]{1,0:T(8,128)(2,1)} %collective-permute-done.19.refs_0_.refs_1_, bf16[512,1024]{1,0:T(8,128)(2,1)} %collective-permute-done.20.refs_1_.refs_5_, ...), custom_call_target="tpu_custom_call" | custom-call | flops 8589934592 | bytes 16809984 | tf_op jit(solution)/shard_map/pallas_call | solution.py:456
  252.5 25.5 %collective-permute-done.25.refs_2_ = bf16[16,512]{1,0:T(8,128)(2,1)S(1)} collective-permute-done((bf16[16,512]{1,0:T(8,128)(2,1)S(1)}, bf16[16,512]{1,0:T(8,128)(2,1)S(1)}, u32[]{:S(2)}, u32[]{:S(2)}) %collective-permute-start.25) | collective-permute-done | bytes 16416 | tf_op jit(solution)/shard_map/ppermute | solution.py:842
  280.5 18.5 %shard_map.303 = (bf16[512,1024]{1,0:T(8,128)(2,1)}, bf16[512,1024]{1,0:T(8,128)(2,1)}, bf16[16,512]{1,0:T(8,128)(2,1)}, bf16[512,2048]{1,0:T(8,128)(2,1)}, bf16[512,2048]{1,0:T(8,128)(2,1)}) custom-call(bf16[512,1024]{1,0:T(8,128)(2,1)} %copy-done.27, bf16[512,1024]{1,0:T(8,128)(2,1)} %copy-done.26, bf16[16,512]{1,0:T(8,128)(2,1)} %copy-done.32, ...), custom_call_target="tpu_custom_call" | custom-call | flops 8589934592 | bytes 16809984 | tf_op jit(solution)/shard_map/pallas_call | solution.py:456
  301.4 18.3 %shard_map.304 = (bf16[512,1024]{1,0:T(8,128)(2,1)}, bf16[512,1024]{1,0:T(8,128)(2,1)}, bf16[16,512]{1,0:T(8,128)(2,1)}, bf16[512,2048]{1,0:T(8,128)(2,1)}, bf16[512,2048]{1,0:T(8,128)(2,1)}) custom-call(bf16[512,1024]{1,0:T(8,128)(2,1)} %collective-permute-done.27.refs_0_.refs_3_, bf16[512,1024]{1,0:T(8,128)(2,1)} %copy-done.28, ...), custom_call_target="tpu_custom_call" | custom-call | flops 8589934592 | bytes 16809984 | tf_op jit(solution)/shard_map/pallas_call | solution.py:456
  321.7 24.8 %shard_map.311 = (bf16[8,1024,256]{2,1,0:T(8,128)(2,1)}, bf16[8,256,1024]{2,1,0:T(8,128)(2,1)}) custom-call(bf16[512,1024]{1,0:T(8,128)(2,1)} %get-tuple-element.58.refs_0_, bf16[512,1024]{1,0:T(8,128)(2,1)} %collective-permute-done.19.refs_0_.refs_1_, bf16[512,1024]{1,0:T(8,128)(2,1)} %copy-done.27, ...), custom_call_target="tpu_custom_call" | custom-call | flops 17179869184 | bytes 33554432 | tf_op jit(solution)/shard_map/pallas_call | solution.py:456
  355.3 15.7 %shard_map.306 = (f32[512,1024]{1,0:T(8,128)}, bf16[8,256,128]{2,1,0:T(8,128)(2,1)}, f32[2,256,128]{2,1,0:T(8,128)}, f32[1024,128]{1,0:T(8,128)}) custom-call(s32[4]{0:T(128)} %pad_add_fusion.length, bf16[512,1024]{1,0:T(8,128)(2,1)} %get-tuple-element.64.r0, bf16[512,1024]{1,0:T(8,128)(2,1)} %collective-permute-done.31.r1, ...), custom_call_target="tpu_custom_call" | custom-call | flops 2684354560 | bytes 17154064 | tf_op jit(solution)/shard_map/pallas_call | solution.py:456
  385.3 9.0 %collective-permute-start.71 = (bf16[1024,256]{1,0:T(8,128)(2,1)S(1)}, bf16[1024,256]{1,0:T(8,128)(2,1)S(1)}, u32[]{:S(2)}, u32[]{:S(2)}) collective-permute-start(bf16[1024,256]{1,0:T(8,128)(2,1)S(1)} %get-tuple-element.161), channel_id=1, source_target_pairs={{0,8},{1,9},{2,10},{3,11},{4,12},{5,13},{6,14},{7,15},{8,16},{9,17... | collective-permute-start | bytes 1572872 | tf_op jit(solution)/shard_map/ppermute | solution.py:842
  409.3 14.5 %collective-permute-start.84 = (bf16[256,1024]{1,0:T(8,128)(2,1)S(1)}, bf16[256,1024]{1,0:T(8,128)(2,1)S(1)}, u32[]{:S(2)}, u32[]{:S(2)}) collective-permute-start(bf16[256,1024]{1,0:T(8,128)(2,1)S(1)} %get-tuple-element.155), channel_id=1, source_target_pairs={{0,24},{1,25},{2,26},{3,27},{4,28},{5,29},{6,30},{7,31},{8,0},{9,1... | collective-permute-start | bytes 1572872 | tf_op jit(solution)/shard_map/ppermute | solution.py:842
  423.8 30.4 %collective-permute-done.73 = bf16[1024,256]{1,0:T(8,128)(2,1)S(1)} collective-permute-done((bf16[1024,256]{1,0:T(8,128)(2,1)S(1)}, bf16[1024,256]{1,0:T(8,128)(2,1)S(1)}, u32[]{:S(2)}, u32[]{:S(2)}) %collective-permute-start.73) | collective-permute-done | bytes 524320 | tf_op jit(solution)/shard_map/ppermute | solution.py:842
  461.3 26.1 %collective-permute-done.82 = bf16[256,1024]{1,0:T(8,128)(2,1)} collective-permute-done((bf16[256,1024]{1,0:T(8,128)(2,1)}, bf16[256,1024]{1,0:T(8,128)(2,1)}, u32[]{:S(2)}, u32[]{:S(2)}) %collective-permute-start.82) | collective-permute-done | bytes 524320 | tf_op jit(solution)/shard_map/ppermute | solution.py:842
  496.7 9.9 %collective-permute-done.30.b3 = bf16[512,1024]{1,0:T(8,128)(2,1)} collective-permute-done((bf16[512,1024]{1,0:T(8,128)(2,1)}, bf16[512,1024]{1,0:T(8,128)(2,1)}, u32[]{:S(2)}, u32[]{:S(2)}) %collective-permute-start.30) | collective-permute-done | bytes 1048608 | tf_op jit(solution)/shard_map/ppermute | solution.py:842
  519.5 11.3 %shard_map.307 = bf16[8,3,256,128]{3,2,1,0:T(8,128)(2,1)} custom-call(s32[1]{0:T(128)} %dynamic_slice.144.length, bf16[8,3,256,128]{3,2,1,0:T(8,128)(2,1)} %all-to-all-done.qkv, bf16[8,256,128]{2,1,0:T(8,128)(2,1)} %all-to-all-done.2.d_out, f32[128,2048]{1,0:T(8,128)} %get-tuple-element.74.out_t, f32[1,2048]{1,0:T(1,128)} %get-tuple-element.75.lse, ...), custom_call_target="tpu_custom_call" | custom-call | flops 2684354560 | bytes 6823940 | tf_op jit(solution)/shard_map/pallas_call | solution.py:456
  530.8 22.9 %all-to-all-start.3 = ((bf16[8,3,256,128]{3,2,1,0:T(8,128)(2,1)}), bf16[8,3,256,128]{3,2,1,0:T(8,128)(2,1)}, u32[]{:S(2)}, u32[]{:S(2)}) async-start(bf16[8,3,256,128]{3,2,1,0:T(8,128)(2,1)} %shard_map.307), calls=%async_computation.3 | async-start | bytes 3145728 | tf_op jit(solution)/shard_map/all_to_all | solution.py:1096
  557.2 30.0 %collective-permute-done.56 = bf16[2,4,8,5120]{3,2,1,0:T(8,128)(2,1)S(1)} collective-permute-done((bf16[2,4,8,5120]{3,2,1,0:T(8,128)(2,1)S(1)}, bf16[2,4,8,5120]{3,2,1,0:T(8,128)(2,1)S(1)}, u32[]{:S(2)}, u32[]{:S(2)}) %collective-permute-start.56) | collective-permute-done | bytes 655392 | tf_op jit(solution)/shard_map/ppermute | solution.py:842
  599.3 14.6 %shard_map.308 = (bf16[1024,3712]{1,0:T(8,128)(2,1)}, bf16[512,2560]{1,0:T(8,128)(2,1)}, f32[512,1024]{1,0:T(8,128)}) custom-call(bf16[8,3,256,128]{3,2,1,0:T(8,128)(2,1)} %all-to-all-done.3.d_qkv, bf16[2,256,1024]{2,1,0:T(8,128)(2,1)} %tok.5, f32[1,1024]{1,0:T(1,128)} %bitcast.292, f32[1,1024]{1,0:T(1,128)} %bitcast.294, bf16[1024,512]{1,0:T(8,128)(2,1)} %wq.3, ...), custom_call_target="tpu_custom_call" | custom-call | flops 4928307200 | bytes 23076864 | tf_op jit(solution)/shard_map/pallas_call | solution.py:456
  643.1 12.1 %collective-permute-done.67 = bf16[2,4,8,5120]{3,2,1,0:T(8,128)(2,1)} collective-permute-done((bf16[2,4,8,5120]{3,2,1,0:T(8,128)(2,1)S(1)}, bf16[2,4,8,5120]{3,2,1,0:T(8,128)(2,1)}, u32[]{:S(2)}, u32[]{:S(2)}) %collective-permute-start.67) | collective-permute-done | bytes 655392 | tf_op jit(solution)/shard_map/ppermute | solution.py:842
  656.5 34.8 %collective-permute-done.38 = bf16[2,4,16,3712]{3,2,1,0:T(8,128)(2,1)S(1)} collective-permute-done((bf16[2,4,16,3712]{3,2,1,0:T(8,128)(2,1)S(1)}, bf16[2,4,16,3712]{3,2,1,0:T(8,128)(2,1)S(1)}, u32[]{:S(2)}, u32[]{:S(2)}) %collective-permute-start.38) | collective-permute-done | bytes 950304 | tf_op jit(solution)/shard_map/ppermute | solution.py:842
  721.1 10.4 %collective-permute-start.47 = (bf16[2,16,3712]{2,1,0:T(8,128)(2,1)S(1)}, bf16[2,16,3712]{2,1,0:T(8,128)(2,1)S(1)}, u32[]{:S(2)}, u32[]{:S(2)}) collective-permute-start(bf16[2,16,3712]{2,1,0:T(8,128)(2,1)S(1)} %fusion.22), channel_id=1, source_target_pairs={{0,24},{1,25},{2,26},{3,27},{4,28},{5,29},{6,30},{7,31},{8,0},{9,1... | collective-permute-start | bytes 712712 | tf_op jit(solution)/shard_map/ppermute | solution.py:842
  737.7 11.8 %collective-permute-done.46 = bf16[2,16,3712]{2,1,0:T(8,128)(2,1)S(1)} collective-permute-done((bf16[2,16,3712]{2,1,0:T(8,128)(2,1)S(1)}, bf16[2,16,3712]{2,1,0:T(8,128)(2,1)S(1)}, u32[]{:S(2)}, u32[]{:S(2)}) %collective-permute-start.46) | collective-permute-done | bytes 237600 | tf_op jit(solution)/shard_map/ppermute | solution.py:842
  752.6 8.8 %collective-permute-done.48 = bf16[4,16,3712]{2,1,0:T(8,128)(2,1)S(1)} collective-permute-done((bf16[4,16,3712]{2,1,0:T(8,128)(2,1)S(1)}, bf16[4,16,3712]{2,1,0:T(8,128)(2,1)S(1)}, u32[]{:S(2)}, u32[]{:S(2)}) %collective-permute-start.48) | collective-permute-done | bytes 475168 | tf_op jit(solution)/shard_map/ppermute | solution.py:842
  766.7 15.9 %collective-permute-done.51 = bf16[2,4,16,3712]{3,2,1,0:T(8,128)(2,1)S(1)} collective-permute-done((bf16[2,4,16,3712]{3,2,1,0:T(8,128)(2,1)S(1)}, bf16[2,4,16,3712]{3,2,1,0:T(8,128)(2,1)S(1)}, u32[]{:S(2)}, u32[]{:S(2)}) %collective-permute-start.51) | collective-permute-done | bytes 950304 | tf_op jit(solution)/shard_map/ppermute | solution.py:842
  800.5 7.8 shard_map.309
  842.3 8.9 %slice.164 = f32[1024,2560]{1,0:T(8,128)} slice(f32[1024,3712]{1,0:T(8,128)} %bitcast_convert_fusion), slice={[0:1024], [1024:3584]} | slice | bytes 20971520 | tf_op jit(solution)/shard_map/slice | solution.py:1117
  (368 shorter events, 302.8 us)
Async XLA Ops:
  23.5 69.3 %all-to-all-start = ((bf16[8,3,256,128]{3,2,1,0:T(8,128)(2,1)}), bf16[8,3,256,128]{3,2,1,0:T(8,128)(2,1)}, u32[]{:S(2)}, u32[]{:S(2)}) async-start(bf16[8,3,256,128]{3,2,1,0:T(8,128)(2,1)} %get-tuple-element.54), calls=%async_computation | async-start | bytes 3145728 | tf_op jit(solution)/shard_map/all_to_all | solution.py:992
  30.8 75.7 %collective-permute-start.6 = (bf16[8,1024]{1,0:T(8,128)(2,1)}, bf16[8,1024]{1,0:T(8,128)(2,1)}, u32[]{:S(2)}, u32[]{:S(2)}) collective-permute-start(bf16[8,1024]{1,0:T(8,128)(2,1)} %bitcast.6), channel_id=1, source_target_pairs={{0,28},{4,24},{8,20},{12,16},{16,12},{20,8},{24,4},{28,0},{1,29},{... | collective-permute-start | bytes 49160 | tf_op jit(solution)/shard_map/ppermute | solution.py:948
  35.5 76.0 %collective-permute-start.5 = (bf16[8,1024]{1,0:T(8,128)(2,1)}, bf16[8,1024]{1,0:T(8,128)(2,1)}, u32[]{:S(2)}, u32[]{:S(2)}) collective-permute-start(bf16[8,1024]{1,0:T(8,128)(2,1)} %bitcast.6), channel_id=1, source_target_pairs={{0,24},{4,28},{8,16},{12,20},{16,8},{20,12},{24,0},{28,4},{1,25},{... | collective-permute-start | bytes 49160 | tf_op jit(solution)/shard_map/ppermute | solution.py:948
  36.1 77.0 %collective-permute-start.4 = (bf16[8,1024]{1,0:T(8,128)(2,1)}, bf16[8,1024]{1,0:T(8,128)(2,1)}, u32[]{:S(2)}, u32[]{:S(2)}) collective-permute-start(bf16[8,1024]{1,0:T(8,128)(2,1)} %bitcast.6), channel_id=1, source_target_pairs={{0,20},{4,16},{8,28},{12,24},{16,4},{20,0},{24,12},{28,8},{1,21},{... | collective-permute-start | bytes 49160 | tf_op jit(solution)/shard_map/ppermute | solution.py:948
  38.9 109.7 %collective-permute-start.11 = (bf16[1024,256]{1,0:T(8,128)(2,1)}, bf16[1024,256]{1,0:T(8,128)(2,1)}, u32[]{:S(2)}, u32[]{:S(2)}) collective-permute-start(bf16[1024,256]{1,0:T(8,128)(2,1)} %get-tuple-element.175.refs_3_), channel_id=1, source_target_pairs={{0,8},{1,9},{2,10},{3,11},{4,12},{5,13},{6,14},{7,15},{8,16},{9,17... | collective-permute-start | bytes 1572872 | tf_op jit(solution)/shard_map/ppermute | solution.py:842
  42.6 106.8 %collective-permute-start.9 = (bf16[1024,256]{1,0:T(8,128)(2,1)}, bf16[1024,256]{1,0:T(8,128)(2,1)}, u32[]{:S(2)}, u32[]{:S(2)}) collective-permute-start(bf16[1024,256]{1,0:T(8,128)(2,1)} %get-tuple-element.175.refs_3_), channel_id=1, source_target_pairs={{0,16},{1,17},{2,18},{3,19},{4,20},{5,21},{6,22},{7,23},{8,24},{9,... | collective-permute-start | bytes 1572872 | tf_op jit(solution)/shard_map/ppermute | solution.py:842
  102.3 70.1 %all-to-all-start.1 = ((bf16[8,256,128]{2,1,0:T(8,128)(2,1)}), bf16[8,256,128]{2,1,0:T(8,128)(2,1)}, u32[]{:S(2)}, u32[]{:S(2)}) async-start(bf16[8,256,128]{2,1,0:T(8,128)(2,1)} %get-tuple-element.55), calls=%async_computation.1 | async-start | bytes 1048576 | tf_op jit(solution)/shard_map/all_to_all | solution.py:1005
  182.7 49.4 %collective-permute-start.19 = (bf16[512,1024]{1,0:T(8,128)(2,1)}, bf16[512,1024]{1,0:T(8,128)(2,1)}, u32[]{:S(2)}, u32[]{:S(2)}) collective-permute-start(bf16[512,1024]{1,0:T(8,128)(2,1)} %get-tuple-element.58.refs_0_), channel_id=1, source_target_pairs={{0,2},{1,3},{2,0},{3,1},{4,6},{5,7},{6,4},{7,5},{8,10},{9,11},{10,... | collective-permute-start | bytes 3145736 | tf_op jit(solution)/shard_map/ppermute | solution.py:842
  185.2 65.5 %collective-permute-start.24 = (bf16[512,1024]{1,0:T(8,128)(2,1)}, bf16[512,1024]{1,0:T(8,128)(2,1)S(1)}, u32[]{:S(2)}, u32[]{:S(2)}) collective-permute-start(bf16[512,1024]{1,0:T(8,128)(2,1)} %bitcast.8.refs_1_.refs_4_), channel_id=1, source_target_pairs={{0,4},{1,5},{2,6},{3,7},{4,0},{5,1},{6,2},{7,3},{8,12},{9,13},{10,... | collective-permute-start | bytes 3145736 | tf_op jit(solution)/shard_map/ppermute | solution.py:842
  186.6 92.9 %collective-permute-start.23 = (bf16[512,1024]{1,0:T(8,128)(2,1)}, bf16[512,1024]{1,0:T(8,128)(2,1)S(1)}, u32[]{:S(2)}, u32[]{:S(2)}) collective-permute-start(bf16[512,1024]{1,0:T(8,128)(2,1)} %get-tuple-element.58.refs_0_), channel_id=1, source_target_pairs={{0,4},{1,5},{2,6},{3,7},{4,0},{5,1},{6,2},{7,3},{8,12},{9,13},{10,... | collective-permute-start | bytes 3145736 | tf_op jit(solution)/shard_map/ppermute | solution.py:842
  187.2 42.1 %collective-permute-start.21 = (bf16[16,512]{1,0:T(8,128)(2,1)S(1)}, bf16[16,512]{1,0:T(8,128)(2,1)S(1)}, u32[]{:S(2)}, u32[]{:S(2)}) collective-permute-start(bf16[16,512]{1,0:T(8,128)(2,1)S(1)} %get-tuple-element.220), channel_id=1, source_target_pairs={{0,2},{1,3},{2,0},{3,1},{4,6},{5,7},{6,4},{7,5},{8,10},{9,11},{10,... | collective-permute-start | bytes 49160 | tf_op jit(solution)/shard_map/ppermute | solution.py:842
  207.6 91.4 %collective-permute-start.28 = (bf16[512,1024]{1,0:T(8,128)(2,1)}, bf16[512,1024]{1,0:T(8,128)(2,1)S(1)}, u32[]{:S(2)}, u32[]{:S(2)}) collective-permute-start(bf16[512,1024]{1,0:T(8,128)(2,1)} %bitcast.8.refs_1_.refs_4_), channel_id=1, source_target_pairs={{0,6},{1,7},{2,4},{3,5},{4,2},{5,3},{6,0},{7,1},{8,14},{9,15},{10,... | collective-permute-start | bytes 3145736 | tf_op jit(solution)/shard_map/ppermute | solution.py:842
  229.3 71.8 %collective-permute-start.27 = (bf16[512,1024]{1,0:T(8,128)(2,1)S(1)}, bf16[512,1024]{1,0:T(8,128)(2,1)}, u32[]{:S(2)}, u32[]{:S(2)}) collective-permute-start(bf16[512,1024]{1,0:T(8,128)(2,1)S(1)} %copy-done.25), channel_id=1, source_target_pairs={{0,6},{1,7},{2,4},{3,5},{4,2},{5,3},{6,0},{7,1},{8,14},{9,15},{10,... | collective-permute-start | bytes 3145736 | tf_op jit(solution)/shard_map/ppermute | solution.py:842
  232.1 45.9 %collective-permute-start.25 = (bf16[16,512]{1,0:T(8,128)(2,1)S(1)}, bf16[16,512]{1,0:T(8,128)(2,1)S(1)}, u32[]{:S(2)}, u32[]{:S(2)}) collective-permute-start(bf16[16,512]{1,0:T(8,128)(2,1)S(1)} %get-tuple-element.219), channel_id=1, source_target_pairs={{0,4},{1,5},{2,6},{3,7},{4,0},{5,1},{6,2},{7,3},{8,12},{9,13},{10,... | collective-permute-start | bytes 49160 | tf_op jit(solution)/shard_map/ppermute | solution.py:842
  250.7 50.1 %collective-permute-start.29 = (bf16[16,512]{1,0:T(8,128)(2,1)S(1)}, bf16[16,512]{1,0:T(8,128)(2,1)S(1)}, u32[]{:S(2)}, u32[]{:S(2)}) collective-permute-start(bf16[16,512]{1,0:T(8,128)(2,1)S(1)} %get-tuple-element.218), channel_id=1, source_target_pairs={{0,6},{1,7},{2,4},{3,5},{4,2},{5,3},{6,0},{7,1},{8,14},{9,15},{10,... | collective-permute-start | bytes 49160 | tf_op jit(solution)/shard_map/ppermute | solution.py:842
  278.0 71.6 %collective-permute-start.34 = (bf16[16,512]{1,0:T(8,128)(2,1)}, bf16[16,512]{1,0:T(8,128)(2,1)S(1)}, u32[]{:S(2)}, u32[]{:S(2)}) collective-permute-start(bf16[16,512]{1,0:T(8,128)(2,1)} %get-tuple-element.69), channel_id=1, source_target_pairs={{0,2},{1,3},{2,0},{3,1},{4,6},{5,7},{6,4},{7,5},{8,10},{9,11},{10,... | collective-permute-start | bytes 49160 | tf_op jit(solution)/shard_map/ppermute | solution.py:842
  279.5 74.8 %collective-permute-start.31 = (bf16[512,1024]{1,0:T(8,128)(2,1)}, bf16[512,1024]{1,0:T(8,128)(2,1)}, u32[]{:S(2)}, u32[]{:S(2)}) collective-permute-start(bf16[512,1024]{1,0:T(8,128)(2,1)} %get-tuple-element.65), channel_id=1, source_target_pairs={{0,2},{1,3},{2,0},{3,1},{4,6},{5,7},{6,4},{7,5},{8,10},{9,11},{10,... | collective-permute-start | bytes 3145736 | tf_op jit(solution)/shard_map/ppermute | solution.py:842
  299.0 53.0 %collective-permute-start.35 = (bf16[16,512]{1,0:T(8,128)(2,1)}, bf16[16,512]{1,0:T(8,128)(2,1)S(1)}, u32[]{:S(2)}, u32[]{:S(2)}) collective-permute-start(bf16[16,512]{1,0:T(8,128)(2,1)} %get-tuple-element.70), channel_id=1, source_target_pairs={{0,4},{1,5},{2,6},{3,7},{4,0},{5,1},{6,2},{7,3},{8,12},{9,13},{10,... | collective-permute-start | bytes 49160 | tf_op jit(solution)/shard_map/ppermute | solution.py:842
  300.8 54.0 %collective-permute-start.32 = (bf16[512,1024]{1,0:T(8,128)(2,1)}, bf16[512,1024]{1,0:T(8,128)(2,1)}, u32[]{:S(2)}, u32[]{:S(2)}) collective-permute-start(bf16[512,1024]{1,0:T(8,128)(2,1)} %get-tuple-element.66), channel_id=1, source_target_pairs={{0,4},{1,5},{2,6},{3,7},{4,0},{5,1},{6,2},{7,3},{8,12},{9,13},{10,... | collective-permute-start | bytes 3145736 | tf_op jit(solution)/shard_map/ppermute | solution.py:842
  382.5 132.0 %collective-permute-start.53 = (bf16[2,2,2,4,8,5120]{5,4,3,2,1,0:T(8,128)(2,1)}, bf16[2,2,2,4,8,5120]{5,4,3,2,1,0:T(8,128)(2,1)}, u32[]{:S(2)}, u32[]{:S(2)}) collective-permute-start(bf16[2,2,2,4,8,5120]{5,4,3,2,1,0:T(8,128)(2,1)} %dynamic-slice_bitcast_fusion.1), channel_id=1, source_target_pairs={{0,1},{1,0},{2,3},{3,2},{4,5},{5,4},{6,7},{7,6},{8,9},{9,8},{10,11... | collective-permute-start | bytes 7864328 | tf_op jit(solution)/shard_map/ppermute | solution.py:842
  399.3 55.0 %collective-permute-start.73 = (bf16[1024,256]{1,0:T(8,128)(2,1)S(1)}, bf16[1024,256]{1,0:T(8,128)(2,1)S(1)}, u32[]{:S(2)}, u32[]{:S(2)}) collective-permute-start(bf16[1024,256]{1,0:T(8,128)(2,1)S(1)} %get-tuple-element.163), channel_id=1, source_target_pairs={{0,16},{1,17},{2,18},{3,19},{4,20},{5,21},{6,22},{7,23},{8,24},{9,... | collective-permute-start | bytes 1572872 | tf_op jit(solution)/shard_map/ppermute | solution.py:842
  399.8 55.4 %collective-permute-start.80 = (bf16[256,1024]{1,0:T(8,128)(2,1)S(1)}, bf16[256,1024]{1,0:T(8,128)(2,1)S(1)}, u32[]{:S(2)}, u32[]{:S(2)}) collective-permute-start(bf16[256,1024]{1,0:T(8,128)(2,1)S(1)} %get-tuple-element.154), channel_id=1, source_target_pairs={{0,8},{1,9},{2,10},{3,11},{4,12},{5,13},{6,14},{7,15},{8,16},{9,17... | collective-permute-start | bytes 1572872 | tf_op jit(solution)/shard_map/ppermute | solution.py:842
  409.3 46.5 %collective-permute-start.84 = (bf16[256,1024]{1,0:T(8,128)(2,1)S(1)}, bf16[256,1024]{1,0:T(8,128)(2,1)S(1)}, u32[]{:S(2)}, u32[]{:S(2)}) collective-permute-start(bf16[256,1024]{1,0:T(8,128)(2,1)S(1)} %get-tuple-element.155), channel_id=1, source_target_pairs={{0,24},{1,25},{2,26},{3,27},{4,28},{5,29},{6,30},{7,31},{8,0},{9,1... | collective-permute-start | bytes 1572872 | tf_op jit(solution)/shard_map/ppermute | solution.py:842
  423.8 63.6 %collective-permute-start.82 = (bf16[256,1024]{1,0:T(8,128)(2,1)}, bf16[256,1024]{1,0:T(8,128)(2,1)}, u32[]{:S(2)}, u32[]{:S(2)}) collective-permute-start(bf16[256,1024]{1,0:T(8,128)(2,1)} %get-tuple-element.156), channel_id=1, source_target_pairs={{0,16},{1,17},{2,18},{3,19},{4,20},{5,21},{6,22},{7,23},{8,24},{9,... | collective-permute-start | bytes 1572872 | tf_op jit(solution)/shard_map/ppermute | solution.py:842
  456.6 50.0 %collective-permute-start.30 = (bf16[512,1024]{1,0:T(8,128)(2,1)}, bf16[512,1024]{1,0:T(8,128)(2,1)}, u32[]{:S(2)}, u32[]{:S(2)}) collective-permute-start(bf16[512,1024]{1,0:T(8,128)(2,1)} %get-tuple-element.63), channel_id=1, source_target_pairs={{0,6},{1,7},{2,4},{3,5},{4,2},{5,3},{6,0},{7,1},{8,14},{9,15},{10,... | collective-permute-start | bytes 3145736 | tf_op jit(solution)/shard_map/ppermute | solution.py:842
  496.1 133.6 %collective-permute-start.85 = (bf16[256,1024]{1,0:T(8,128)(2,1)}, bf16[256,1024]{1,0:T(8,128)(2,1)}, u32[]{:S(2)}, u32[]{:S(2)}) collective-permute-start(bf16[256,1024]{1,0:T(8,128)(2,1)} %add_convert_fusion), channel_id=1, source_target_pairs={{0,1},{1,0},{2,3},{3,2},{4,5},{5,4},{6,7},{7,6},{8,9},{9,8},{10,11... | collective-permute-start | bytes 1572872 | tf_op jit(solution)/shard_map/ppermute | solution.py:842
  513.5 278.0 %collective-permute-start.77 = (bf16[2,1024,256]{2,1,0:T(8,128)(2,1)}, bf16[2,1024,256]{2,1,0:T(8,128)(2,1)}, u32[]{:S(2)}, u32[]{:S(2)}) collective-permute-start(bf16[2,1024,256]{2,1,0:T(8,128)(2,1)} %pad_maximum_fusion.6), channel_id=1, source_target_pairs={{0,2},{1,3},{2,0},{3,1},{4,6},{5,7},{6,4},{7,5},{8,10},{9,11},{10,... | collective-permute-start | bytes 3145736 | tf_op jit(solution)/shard_map/ppermute | solution.py:842
  530.8 68.6 %all-to-all-start.3 = ((bf16[8,3,256,128]{3,2,1,0:T(8,128)(2,1)}), bf16[8,3,256,128]{3,2,1,0:T(8,128)(2,1)}, u32[]{:S(2)}, u32[]{:S(2)}) async-start(bf16[8,3,256,128]{3,2,1,0:T(8,128)(2,1)} %shard_map.307), calls=%async_computation.3 | async-start | bytes 3145728 | tf_op jit(solution)/shard_map/all_to_all | solution.py:1096
  632.1 164.2 %collective-permute-start.86 = (bf16[2,256,1024]{2,1,0:T(8,128)(2,1)}, bf16[2,256,1024]{2,1,0:T(8,128)(2,1)}, u32[]{:S(2)}, u32[]{:S(2)}) collective-permute-start(bf16[2,256,1024]{2,1,0:T(8,128)(2,1)} %pad_maximum_fusion.7), channel_id=1, source_target_pairs={{0,2},{1,3},{2,0},{3,1},{4,6},{5,7},{6,4},{7,5},{8,10},{9,11},{10,... | collective-permute-start | bytes 3145736 | tf_op jit(solution)/shard_map/ppermute | solution.py:842
  639.6 70.1 %collective-permute-start.65 = (bf16[2,4,8,5120]{3,2,1,0:T(8,128)(2,1)S(1)}, bf16[2,4,8,5120]{3,2,1,0:T(8,128)(2,1)}, u32[]{:S(2)}, u32[]{:S(2)}) collective-permute-start(bf16[2,4,8,5120]{3,2,1,0:T(8,128)(2,1)S(1)} %pad_maximum_fusion.16), channel_id=1, source_target_pairs={{0,2},{1,3},{2,0},{3,1},{4,6},{5,7},{6,4},{7,5},{8,10},{9,11},{10,... | collective-permute-start | bytes 1966088 | tf_op jit(solution)/shard_map/ppermute | solution.py:842
  642.1 49.1 %collective-permute-start.38 = (bf16[2,4,16,3712]{3,2,1,0:T(8,128)(2,1)S(1)}, bf16[2,4,16,3712]{3,2,1,0:T(8,128)(2,1)S(1)}, u32[]{:S(2)}, u32[]{:S(2)}) collective-permute-start(bf16[2,4,16,3712]{3,2,1,0:T(8,128)(2,1)S(1)} %dynamic-slice_bitcast_fusion.3), channel_id=1, source_target_pairs={{0,2},{1,3},{2,0},{3,1},{4,6},{5,7},{6,4},{7,5},{8,10},{9,11},{10,... | collective-permute-start | bytes 2850824 | tf_op jit(solution)/shard_map/ppermute | solution.py:842
  765.2 43.0 %collective-permute-start.68 = (bf16[2,2,2,4,8,5120]{5,4,3,2,1,0:T(8,128)(2,1)}, bf16[2,2,2,4,8,5120]{5,4,3,2,1,0:T(8,128)(2,1)}, u32[]{:S(2)}, u32[]{:S(2)}) collective-permute-start(bf16[2,2,2,4,8,5120]{5,4,3,2,1,0:T(8,128)(2,1)} %pad_maximum_fusion.3), channel_id=1, source_target_pairs={{0,1},{1,0},{2,3},{3,2},{4,5},{5,4},{6,7},{7,6},{8,9},{9,8},{10,11... | collective-permute-start | bytes 7864328 | tf_op jit(solution)/shard_map/ppermute | solution.py:842
  (97 other events, 1873.5 us)

commit v2 on v1

--- a/solution.py
+++ b/solution.py
@@ -1,5 +1,8 @@
+import functools
+
 import jax
 import jax.numpy as jnp
+import numpy as np
 from jax import lax
 from jax.experimental import pallas as pl
 from jax.experimental.pallas import tpu as pltpu
@@ -444,19 +447,27 @@
 LANES = 128
 
 
-def call(kernel, out_shape, *args, grid=None, in_specs=None, out_specs=None, scratch=(), flops=0, limit=56):
+def call(
+    kernel, out_shape, *args, grid=None, in_specs=None, out_specs=None, scratch=(), flops=0, limit=56, prefetch=0, aliases=None
+):
     moved = sum(a.size * a.dtype.itemsize for a in jax.tree.leaves((args, out_shape)))
     extra = {}
-    if grid is not None:
-        extra["grid"] = grid
-        extra["in_specs"] = in_specs
-        extra["out_specs"] = out_specs
-    elif in_specs is not None:
-        extra["in_specs"] = in_specs
+    if prefetch:
+        extra["grid_spec"] = pltpu.PrefetchScalarGridSpec(
+            num_scalar_prefetch=prefetch, grid=grid, in_specs=in_specs, out_specs=out_specs, scratch_shapes=list(scratch)
+        )
+    else:
+        extra["scratch_shapes"] = list(scratch)
+        if grid is not None:
+            extra["grid"] = grid
+        if in_specs is not None:
+            extra["in_specs"] = in_specs
+        if out_specs is not None:
+            extra["out_specs"] = out_specs
     return pl.pallas_call(
         kernel,
         out_shape=out_shape,
-        scratch_shapes=list(scratch),
+        input_output_aliases=aliases or {},
         compiler_params=pltpu.CompilerParams(vmem_limit_bytes=limit * 1024 * 1024),
         cost_estimate=pl.CostEstimate(flops=int(flops), bytes_accessed=int(moved), transcendentals=0),
         **extra,
@@ -465,7 +476,7 @@
 
 def full(shape):
     rank = len(shape)
-    return pl.BlockSpec(tuple(shape), lambda s: (0,) * rank)
+    return pl.BlockSpec(tuple(shape), lambda *s: (0,) * rank)
 
 
 def shaped(shape, dtype=HALF_TYPE):
@@ -498,18 +509,20 @@
     return lax.broadcasted_iota(jnp.int32, shape, dim)
 
 
-def pre_kernel(tok, gain, bias, wq, wk, wv, sel, vid, oid, cos, sin, qkv, proj, gate):
+def pre_kernel(tok, gain, bias, wq, wk, wv, sel, vid, oid, cos, sin, select, qkv, proj, gate):
     heads = qkv.shape[0]
     experts = wv.shape[1] // (heads * LANES)
     low = tok[0]
+    rows = low.shape[0]
     normal, _ = layer_stats(low.astype(FULL_TYPE))
     normed = (normal * gain[...] + bias[...]).astype(HALF_TYPE)
     for part, weight in ((0, wq), (1, wk)):
         pre = nn(normed, weight[...])
         for h in range(heads):
-            qkv[h, part] = turned(pre[:, h * LANES:(h + 1) * LANES], cos[...], sin[...]).astype(HALF_TYPE)
-    lanes = lane_ids((low.shape[0], LANES), 1)
-    chosen = jnp.zeros((low.shape[0], LANES), FULL_TYPE)
+            head = turned(pre[:, h * LANES:(h + 1) * LANES], cos[...], sin[...])
+            qkv[h, part * rows:(part + 1) * rows] = head.astype(HALF_TYPE)
+    lanes = lane_ids((rows, LANES), 1)
+    chosen = jnp.zeros((rows, LANES), FULL_TYPE)
     tops = vid.shape[2] // heads
     for h in range(heads):
         for k in range(tops):
@@ -518,6 +531,7 @@
             chosen += (lanes == oid[0, :, j:j + 1] + (SELO + experts * h)).astype(FULL_TYPE)
     gates = jax.nn.sigmoid(nn(normed, sel[...])) * chosen
     gate[0] = gates
+    gates_low = gates.astype(HALF_TYPE)
     for h in range(heads):
         at = h * experts * LANES
         block = nn(low, wv[:, at:at + experts * LANES])
@@ -527,7 +541,15 @@
             col = SELV + h * experts + e
             term = gates[:, col:col + 1] * block[:, e * LANES:(e + 1) * LANES]
             total = term if total is None else total + term
-        qkv[h, 2] = total.astype(HALF_TYPE)
+        qkv[h, 2 * rows:3 * rows] = total.astype(HALF_TYPE)
+        first = SELV + h * experts
+        row_id = lane_ids((8, LANES), 0)
+        spot = (lane_ids((8, LANES), 1) == row_id + first) & (row_id < experts)
+        turned_gates = nt(spot.astype(FULL_TYPE).astype(HALF_TYPE), gates_low)
+        tail = jnp.concatenate([turned_gates[:, i * LANES:(i + 1) * LANES] for i in range(rows // LANES)], axis=0)
+        last = 3 * rows + select.shape[0]
+        qkv[h, 3 * rows:last] = select[...]
+        qkv[h, last:last + tail.shape[0]] = tail.astype(HALF_TYPE)
 
 
 def limits_of(i, rows, length):
@@ -535,17 +557,20 @@
     return jnp.minimum(position + 1, length), position
 
 
+def parts_of(ref, first, last, part, rows):
+    block = ref[first:last, part * rows:(part + 1) * rows]
+    return block.reshape((last - first) * rows, block.shape[2])
+
+
 def attend_kernel(length, qkv, mixed, out_t, lse):
-    blocks, _, rows, width = qkv.shape
+    blocks, rows, width = mixed.shape
     scale = width ** (-0.5)
-    values_t = jnp.transpose(
-        qkv[:, 2].reshape(blocks * rows, width).astype(FULL_TYPE)
-    ).astype(HALF_TYPE)
+    values_t = jnp.transpose(parts_of(qkv, 0, blocks, 2, rows).astype(FULL_TYPE)).astype(HALF_TYPE)
     for i in range(blocks):
         n = (i + 1) * rows
-        keys = qkv[0:i + 1, 1].reshape(n, width)
+        keys = parts_of(qkv, 0, i + 1, 1, rows)
         limit, position = limits_of(i, rows, length[0])
-        scores = nt(keys, qkv[i, 0]) * scale
+        scores = nt(keys, qkv[i, 0:rows]) * scale
         scores = jnp.where(lane_ids((n, rows), 0) < limit, scores, -1e30)
         top = jnp.max(scores, axis=0, keepdims=True)
         weights = jnp.exp(scores - top)
@@ -558,32 +583,30 @@
 
 
 def attend_back_kernel(length, qkv, d_out, out_t, lse, cos, sin, d_qkv, d_keys, d_values):
-    blocks, _, rows, width = qkv.shape
+    blocks, rows, width = d_out.shape
     scale = width ** (-0.5)
-    keys_t = jnp.transpose(
-        qkv[:, 1].reshape(blocks * rows, width).astype(FULL_TYPE)
-    ).astype(HALF_TYPE)
+    keys_t = jnp.transpose(parts_of(qkv, 0, blocks, 1, rows).astype(FULL_TYPE)).astype(HALF_TYPE)
     d_keys[...] = jnp.zeros_like(d_keys)
     d_values[...] = jnp.zeros_like(d_values)
     for i in range(blocks):
         n = (i + 1) * rows
         here = slice(i * rows, (i + 1) * rows)
         limit, _ = limits_of(i, rows, length[0])
-        query = qkv[i, 0]
+        query = qkv[i, 0:rows]
         d_att = d_out[i]
         delta = jnp.sum(jnp.transpose(d_att.astype(FULL_TYPE)) * out_t[:, here], axis=0, keepdims=True)
-        scores = nt(qkv[0:i + 1, 1].reshape(n, width), query) * scale
+        scores = nt(parts_of(qkv, 0, i + 1, 1, rows), query) * scale
         probs = jnp.where(lane_ids((n, rows), 0) < limit, jnp.exp(scores - lse[:, here]), 0.0)
-        d_probs = nt(qkv[0:i + 1, 2].reshape(n, width), d_att)
+        d_probs = nt(parts_of(qkv, 0, i + 1, 2, rows), d_att)
         d_scores = (probs * (d_probs - delta)).astype(HALF_TYPE)
         d_values[0:n, :] += nn(probs.astype(HALF_TYPE), d_att)
         d_keys[0:n, :] += nn(d_scores, query)
         d_query = jnp.transpose(nn(keys_t[:, :n], d_scores)) * scale
-        d_qkv[i, 0] = turned(d_query, cos[here, :], -sin[here, :]).astype(HALF_TYPE)
+        d_qkv[i, 0:rows] = turned(d_query, cos[here, :], -sin[here, :]).astype(HALF_TYPE)
     for i in range(blocks):
         here = slice(i * rows, (i + 1) * rows)
-        d_qkv[i, 1] = turned(d_keys[here, :] * scale, cos[here, :], -sin[here, :]).astype(HALF_TYPE)
-        d_qkv[i, 2] = d_values[here, :].astype(HALF_TYPE)
+        d_qkv[i, rows:2 * rows] = turned(d_keys[here, :] * scale, cos[here, :], -sin[here, :]).astype(HALF_TYPE)
+        d_qkv[i, 2 * rows:3 * rows] = d_values[here, :].astype(HALF_TYPE)
 
 
 def gated(mixed, gate, hp, e, experts):
@@ -599,10 +622,11 @@
     return block.reshape(2 * block.shape[1], width)
 
 
-def post_kernel(mixed, gate, w_out, tok, gain, bias, w_sel, ids, eids, places, after, rows, gates, sent):
+def post_kernel(mixed, gate, w_out, tok, gain, bias, columns, ids, places, after, gates, sent, select):
     width = tok.shape[2]
     heads = w_out.shape[0]
     experts = w_out.shape[2] // width
+    row_count = tok.shape[1]
     total = tok[0].astype(FULL_TYPE)
     gate_here = gate[0]
     mixed_here = mixed[...]
@@ -610,16 +634,31 @@
         for e in range(experts):
             total += nn(gated(mixed_here, gate_here, hp, e, experts), out_block(w_out, hp, e, width))
     after[...] = total
-    rows[...] = total.astype(HALF_TYPE)
+    sent[0, 0:row_count] = total.astype(HALF_TYPE)
     normal, _ = layer_stats(total)
     normed = (normal * gain[...] + bias[...]).astype(HALF_TYPE)
-    chosen = jnp.zeros((eids.shape[0], ids.shape[2]), FULL_TYPE)
+    every = columns[...].astype(FULL_TYPE)
+    count = every.shape[1]
+    each = count // 8
+    w_sel = jnp.concatenate(
+        [every[:, j * each:(j + 1) * each].reshape(count, LANES) for j in range(8)], axis=1
+    ).astype(HALF_TYPE)
+    select[...] = w_sel
+    row_id = lane_ids((count, row_count), 0)
+    chosen = jnp.zeros((count, row_count), FULL_TYPE)
     for k in range(ids.shape[1]):
-        chosen += (eids[...] == ids[0, k:k + 1, :]).astype(FULL_TYPE)
-    values = jax.nn.sigmoid(nt(w_sel[...], normed)) * chosen
+        chosen += (row_id == ids[0, k:k + 1, :]).astype(FULL_TYPE)
+    values = jax.nn.sigmoid(nt(w_sel, normed)) * chosen
     gates[...] = values
     moved = nn(places[...], values.astype(HALF_TYPE)).astype(HALF_TYPE)
-    sent[...] = moved.reshape(sent.shape)
+    quarter = count // 4
+    for i in range(4):
+        sent[0, row_count:row_count + quarter, i * row_count:(i + 1) * row_count] = moved[i * quarter:(i + 1) * quarter]
+
+
+def weights_kernel(spots, up, down, out):
+    out[0, 0] = up[...]
+    out[0, 1] = jnp.transpose(down[...].astype(FULL_TYPE)).astype(HALF_TYPE)
 
 
 def expand(count, cols, first):
@@ -632,64 +671,89 @@
     return hit.astype(FULL_TYPE).astype(HALF_TYPE)
 
 
-def experts_kernel(*refs):
-    rows, cot, gate = refs[:3]
-    ups, downs = refs[3:11], refs[11:19]
-    d_rows, branch, d_gate, inner, d_pre = refs[19:]
-    low, cot_low, gates = rows[...], cot[...], gate[...]
-    row_total = branch_total = gate_total = None
+def experts_kernel(kind, halves, *refs):
+    rows_in, cot, first = refs[:halves], refs[halves], refs[halves + 1]
+    others = refs[halves + 2:halves + 8]
+    back, inner, d_pre = refs[halves + 8:]
+    seqs, tall, width = back.shape
+    row_count = width // 4
+    cols = first.shape[3]
+    quarter = tall - row_count
+    picked = [rows_in[0][s] if halves == 1 else rows_in[s][...] for s in range(seqs)]
+    low = jnp.concatenate([block[0:row_count] for block in picked], axis=0)
+    gates = jnp.concatenate(
+        [block[row_count:tall, kind * row_count:(kind + 1) * row_count] for block in picked], axis=1
+    )
+    cot_low = cot[...]
+    row_total = gate_total = None
+    weight = lambda p, u: first[p, u] if p < 2 else others[p - 2][u]
+    root, cube = 0.7978845608028654, 0.044715
     for p in range(8):
-        w_up, w_down = ups[p][...], downs[p][...]
-        cols = w_up.shape[1]
-        spread = expand(gates.shape[0], cols, p * (cols // LANES))
+        spread = expand(quarter, cols, p * (cols // LANES))
         gate_wide = tn(gates, spread)
-        pre = nn(low, w_up)
-        d_in = nt(cot_low, w_down)
-        root = 0.7978845608028654
+        pre = nn(low, weight(p, 0))
+        d_in = nn(cot_low, weight(p, 1))
         square = pre * pre
-        tanh = jnp.tanh(root * pre * (1.0 + 0.044715 * square))
-        half = 0.5 * (1.0 + tanh)
+        tanh = jnp.tanh(pre * (root + (root * cube) * square))
+        half = 0.5 + 0.5 * tanh
         act = pre * half
-        slope = half + 0.5 * pre * (1.0 - tanh * tanh) * (root * (1.0 + 3 * 0.044715 * square))
-        in_low = (act * gate_wide).astype(HALF_TYPE)
-        pre_low = (slope * gate_wide * d_in).astype(HALF_TYPE)
-        inner[:, p * cols:(p + 1) * cols] = in_low
-        d_pre[:, p * cols:(p + 1) * cols] = pre_low
+        slope = half + act * (1.0 - tanh) * (root + (3 * root * cube) * square)
+        d_pre[p] = (slope * gate_wide * d_in).astype(HALF_TYPE)
+        inner[p] = (act * gate_wide).astype(HALF_TYPE)
         g = nt(spread, (d_in * act).astype(HALF_TYPE))
-        r = nt(pre_low, w_up)
-        b = nn(in_low, w_down)
         gate_total = g if p == 0 else gate_total + g
+    for p in range(8):
+        r = nt(d_pre[p], weight(p, 0))
         row_total = r if p == 0 else row_total + r
-        branch_total = b if p == 0 else branch_total + b
-    d_rows[...] = row_total.astype(HALF_TYPE)
-    branch[...] = branch_total.astype(HALF_TYPE)
-    d_gate[...] = gate_total.astype(HALF_TYPE)
+    for s in range(seqs):
+        here = slice(s * row_count, (s + 1) * row_count)
+        back[s, 0:row_count] = row_total[here].astype(HALF_TYPE)
+        back[s, row_count:tall] = jnp.zeros((quarter, width), HALF_TYPE)
+        back[s, row_count:tall, 0:row_count] = gate_total[:, here].astype(HALF_TYPE)
+
+
+def branch_kernel(*refs):
+    inners, first, others, outs = refs[0:4], refs[4], refs[5:11], refs[11:15]
+    downs = [first[0, 1], first[1, 1]] + [ref[1] for ref in others]
+    for i in range(4):
+        total = None
+        for p in range(8):
+            term = nt(inners[i][p], downs[p])
+            total = term if p == 0 else total + term
+        outs[i][...] = total.astype(HALF_TYPE)
 
 
 def expert_grads_kernel(*refs):
-    count = 4
-    rows, cots = refs[0:count], refs[count:2 * count]
-    pres, inners = refs[2 * count:3 * count], refs[3 * count:4 * count]
-    up, down = refs[4 * count:]
-    total = None
-    for i in range(count):
-        term = tn(rows[i][...], pres[i][...])
-        total = term if i == 0 else total + term
-    up[0] = total.astype(HALF_TYPE)
-    for i in range(count):
-        term = tn(inners[i][...], cots[i][...])
-        total = term if i == 0 else total + term
-    down[0] = total.astype(HALF_TYPE)
-
-
-def mid_kernel(length, r0, r1, r2, r3, g0, g1, g2, g3, cot, after, gates, gain, bias, w_sel, places, order, w_out, gate, mixed,
+    rows, cots, pres, inners = refs[0:5], refs[5:9], refs[9:13], refs[13:17]
+    outs = refs[17:21]
+    step = pl.program_id(0)
+    row_count = pres[0].shape[1] // 2
+    up = down = None
+    for i in range(4):
+        for s in range(2):
+            block = rows[i][s, 0:row_count] if i < 3 else rows[3 + s][0:row_count]
+            term = tn(block, pres[i][0, s * row_count:(s + 1) * row_count])
+            up = term if up is None else up + term
+        term = tn(cots[i][...], inners[i][0])
+        down = term if down is None else down + term
+    results = (up.astype(HALF_TYPE), down.astype(HALF_TYPE))
+    for j in range(4):
+
+        @pl.when(step // 2 == j)
+        def _(j=j):
+            for u in range(2):
+                outs[j][0, u] = results[u]
+
+
+def mid_kernel(length, r0, r1, r2, r3, cot, after, gates, gain, bias, w_sel, places, w_out, gate, mixed,
                d_after, d_att, d_gate_out, small, acc):
     step = pl.program_id(0)
     width = cot.shape[2]
     heads = w_out.shape[0]
     experts = w_out.shape[2] // width
     row_count = cot.shape[1]
-    d_rel = jnp.concatenate([g0[...], g1[...], g2[...], g3[...]], axis=0)
+    tall = r0.shape[1]
+    d_rel = jnp.concatenate([r[0, row_count:tall, 0:row_count] for r in (r0, r1, r2, r3)], axis=0)
     d_gate = tn(places[...], d_rel)
     values = gates[...]
     d_logit = (d_gate * values * (1.0 - values)).astype(HALF_TYPE)
@@ -708,10 +772,7 @@
     acc[0:count, :] += sel_part
     acc[count:count + 1, :] += gain_part
     acc[count + 1:count + 2, :] += bias_part
-    d_row = (
-        r0[...].astype(FULL_TYPE) + r1[...].astype(FULL_TYPE)
-        + r2[...].astype(FULL_TYPE) + r3[...].astype(FULL_TYPE)
-    )
+    d_row = sum(r[0, 0:row_count].astype(FULL_TYPE) for r in (r0, r1, r2, r3))
     total = cot[0].astype(FULL_TYPE) + d_row + norm_back(d_normed, normal, inv, gain[...])
     d_after[...] = total
     total_low = total.astype(HALF_TYPE)
@@ -739,7 +800,8 @@
 
     @pl.when(step == pl.num_programs(0) - 1)
     def _():
-        small[...] = tn(acc[...].astype(HALF_TYPE), order[...])
+        spots = (lane_ids((LANES, LANES), 0) == lanes[0:LANES]).astype(FULL_TYPE).astype(HALF_TYPE)
+        small[...] = tn(acc[...].astype(HALF_TYPE), spots)
 
 
 def out_grad_kernel(mixed, gate, d_after, out):
@@ -757,60 +819,162 @@
             out[2 * hp * LANES:(2 * hp + 2) * LANES, e * width:(e + 1) * width] = total.astype(HALF_TYPE)
 
 
-def last_kernel(d_qkv, tok, gain, bias, wq, wk, sel, proj, gate, d_gate_out, small, d_after,
-                grads, d_proj, part, d_qk, d_sel):
-    seqs, row_count, width = tok.shape
-    heads = 4
+def last_kernel(d_qkv, tok, gain, bias, wq, wk, wv, sel, proj, gate, d_gate_out, small, d_after,
+                out, sums, d_proj, acc):
+    step = pl.program_id(0)
+    row_count, width = tok.shape[1], tok.shape[2]
+    heads = d_qkv.shape[0]
     experts = proj.shape[2] // (heads * LANES)
     lanes = lane_ids((LANES, LANES), 1)
-    gain_sum = bias_sum = 0.0
-    normed_t, tok_t = [], []
-    for s in range(seqs):
-        low = tok[s]
-        normal, inv = layer_stats(low.astype(FULL_TYPE))
-        normed = (normal * gain[...] + bias[...]).astype(HALF_TYPE)
-        d_gates = d_gate_out[s]
-        gate_here = gate[s]
-        here = slice(s * row_count, (s + 1) * row_count)
-        for h in range(heads):
-            for part_id in range(2):
-                at = part_id * heads * LANES + h * LANES
-                d_qk[here, at:at + LANES] = d_qkv[s * heads + h, part_id]
-            d_value = d_qkv[s * heads + h, 2].astype(FULL_TYPE)
-            for e in range(experts):
-                col = SELV + h * experts + e
-                at = (h * experts + e) * LANES
-                d_proj[here, at:at + LANES] = (gate_here[:, col:col + 1] * d_value).astype(HALF_TYPE)
-                hit = (lanes == col).astype(FULL_TYPE).astype(HALF_TYPE)
-                product = (proj[s, :, at:at + LANES].astype(FULL_TYPE) * d_value).astype(HALF_TYPE)
-                d_gates += nn(product, hit)
-        d_logit = (d_gates * gate_here * (1.0 - gate_here)).astype(HALF_TYPE)
-        d_sel[here, :] = d_logit
-        half = heads * LANES
-        d_normed = (
-            nt(d_qk[here, 0:half], wq[...]) + nt(d_qk[here, half:2 * half], wk[...]) + nt(d_logit, sel[...])
-        )
-        gain_sum += jnp.sum(d_normed * normal, axis=0, keepdims=True)
-        bias_sum += jnp.sum(d_normed, axis=0, keepdims=True)
-        part[here, :] = d_after[here, :] + norm_back(d_normed, normal, inv, gain[...])
-        normed_t.append(jnp.transpose(normed.astype(FULL_TYPE)).astype(HALF_TYPE))
-        tok_t.append(jnp.transpose(low.astype(FULL_TYPE)).astype(HALF_TYPE))
-    normed_t = jnp.concatenate(normed_t, axis=1)
-    tok_t = jnp.concatenate(tok_t, axis=1)
-    size = 512
-    at = 0
-    for left, right in ((normed_t, d_qk), (tok_t, d_proj)):
-        for b in range(right.shape[1] // size):
-            grads[:, at:at + size] = nn(left, right[:, b * size:(b + 1) * size]).astype(HALF_TYPE)
-            at += size
+    low = tok[0]
+    normal, inv = layer_stats(low.astype(FULL_TYPE))
+    normed = (normal * gain[...] + bias[...]).astype(HALF_TYPE)
+    d_gates = d_gate_out[0]
+    gate_here = gate[0]
+    d_query = jnp.concatenate([d_qkv[h, 0:row_count] for h in range(heads)], axis=1)
+    d_key = jnp.concatenate([d_qkv[h, row_count:2 * row_count] for h in range(heads)], axis=1)
+    for h in range(heads):
+        d_value = d_qkv[h, 2 * row_count:3 * row_count].astype(FULL_TYPE)
+        for e in range(experts):
+            col = SELV + h * experts + e
+            at = (h * experts + e) * LANES
+            d_proj[:, at:at + LANES] = (gate_here[:, col:col + 1] * d_value).astype(HALF_TYPE)
+            hit = (lanes == col).astype(FULL_TYPE).astype(HALF_TYPE)
+            product = (proj[0, :, at:at + LANES].astype(FULL_TYPE) * d_value).astype(HALF_TYPE)
+            d_gates += nn(product, hit)
+    d_logit = (d_gates * gate_here * (1.0 - gate_here)).astype(HALF_TYPE)
+    d_normed = nt(d_query, wq[...]) + nt(d_key, wk[...]) + nt(d_logit, sel[...])
+    total = d_after[...] + norm_back(d_normed, normal, inv, gain[...]) + nt(d_proj[...], wv[...])
+    out[...] = total.astype(HALF_TYPE)
+    gain_sum = jnp.sum(d_normed * normal, axis=0, keepdims=True)
+    bias_sum = jnp.sum(d_normed, axis=0, keepdims=True)
     rows = jnp.concatenate([gain_sum, bias_sum, jnp.zeros((14, width), FULL_TYPE)], axis=0).astype(HALF_TYPE)
     spot = (lane_ids((16, LANES), 1) == lane_ids((16, LANES), 0) + 66) & (lane_ids((16, LANES), 0) < 2)
     spread = tn(rows, spot.astype(FULL_TYPE).astype(HALF_TYPE))
-    grads[:, at:at + LANES] = (small[...] + nn(normed_t, d_sel[...]) + spread).astype(HALF_TYPE)
-
-
-def token_grad_kernel(part, d_proj, wv, out):
-    out[...] = (part[...] + nt(d_proj[...], wv[...])).astype(HALF_TYPE)
+    part = tn(normed, d_logit) + spread
+
+    @pl.when(step == 0)
+    def _():
+        acc[...] = small[...] + part
+
+    @pl.when(step > 0)
+    def _():
+        acc[...] += part
+
+    sums[...] = acc[...].astype(HALF_TYPE)
+
+
+def turn_kernel(near, far, gain, bias, tok_t, norm_t):
+    step = pl.program_id(0)
+
+    def turn(low):
+        normal, _ = layer_stats(low.astype(FULL_TYPE))
+        tok_t[0] = jnp.transpose(low.astype(FULL_TYPE)).astype(HALF_TYPE)
+        normed = (normal * gain[...] + bias[...]).astype(HALF_TYPE)
+        norm_t[0] = jnp.transpose(normed.astype(FULL_TYPE)).astype(HALF_TYPE)
+
+    @pl.when(step < 4)
+    def _():
+        turn(near[0])
+
+    @pl.when(step >= 4)
+    def _():
+        turn(far[0])
+
+
+def head_grads_kernel(spot, tok_t, norm_t, d_qkv, gate, out, acc):
+    step = pl.program_id(0)
+    rows = tok_t.shape[2]
+    experts = out.shape[1] // LANES - 2
+    both = jnp.concatenate([d_qkv[0, 0:rows], d_qkv[0, rows:2 * rows]], axis=1)
+    wide = experts * LANES
+    spread = expand(8, wide, 0)
+    tail = gate[0]
+    gates = jnp.concatenate([tn(tail[i * 8:(i + 1) * 8], spread) for i in range(rows // LANES)], axis=0)
+    d_value = d_qkv[0, 2 * rows:3 * rows].astype(FULL_TYPE)
+    d_proj = (gates * jnp.concatenate([d_value] * experts, axis=1)).astype(HALF_TYPE)
+    first = nn(norm_t[0], both)
+    second = nn(tok_t[0], d_proj)
+
+    @pl.when(step == 0)
+    def _():
+        acc[:, 0:2 * LANES] = first
+        acc[:, 2 * LANES:] = second
+
+    @pl.when(step > 0)
+    def _():
+        acc[:, 0:2 * LANES] += first
+        acc[:, 2 * LANES:] += second
+
+    @pl.when(step == pl.num_programs(0) - 1)
+    def _():
+        out[...] = acc[...].astype(HALF_TYPE)
+
+
+def place_heads_kernel(bits, *refs):
+    sources = refs[:4]
+    query, key, value = refs[-3:]
+    step = pl.program_id(0)
+    part = step // 4
+    x, low = bits[1], bits[3]
+    wide = value.shape[1] // 4
+
+    def put(block, head):
+        at = pl.multiple_of(head * LANES, LANES)
+        query[:, pl.ds(at, LANES)] = block[:, 0:LANES].astype(FULL_TYPE)
+        key[:, pl.ds(at, LANES)] = block[:, LANES:2 * LANES].astype(FULL_TYPE)
+        value[:, pl.ds(pl.multiple_of(head * wide, LANES), wide)] = block[:, 2 * LANES:].astype(FULL_TYPE)
+
+    for y in range(2):
+
+        @pl.when((part == 0) & ((step // 2) % 2 == y))
+        def _(y=y):
+            for i in range(2):
+                for b in range(2):
+                    put(sources[y][i, b, 0], (low ^ b) * 2 + (x ^ i))
+
+    @pl.when(part == 1)
+    def _():
+        for i in range(2):
+            for b in range(2):
+                put(sources[2 + i][0, b, 0], (low ^ b) * 2 + (x ^ i))
+
+
+def place_out_kernel(spot, mine, peer, out):
+    step = pl.program_id(0)
+
+    @pl.when(step < 2)
+    def _():
+        out[0] = mine[...].astype(FULL_TYPE)
+
+    @pl.when(step >= 2)
+    def _():
+        out[0] = peer[...].astype(FULL_TYPE)
+
+
+def place_small_kernel(first, small, select, value, out, rows):
+    low = small[...]
+
+    def rows_of(count, start):
+        hit = lane_ids((count, LANES), 1) == lane_ids((count, LANES), 0) + start
+        return nt(hit.astype(FULL_TYPE).astype(HALF_TYPE), low)
+
+    select[...] = rows_of(select.shape[0], first[0])
+    value[...] = rows_of(value.shape[0], SELV)
+    out[...] = rows_of(out.shape[0], SELO)
+    spots = (lane_ids((8, LANES), 1) == lane_ids((8, LANES), 0) + 64) & (lane_ids((8, LANES), 0) < 4)
+    rows[...] = nt(spots.astype(FULL_TYPE).astype(HALF_TYPE), low)
+
+
+def place_experts_kernel(spots, *refs):
+    up, down = refs[4:]
+    step = pl.program_id(0)
+    for i in range(4):
+
+        @pl.when(step == i)
+        def _(i=i):
+            up[...] = refs[i][0].astype(FULL_TYPE)
+            down[...] = jnp.transpose(refs[i][1].astype(FULL_TYPE))
 
 
 def output_kernel(after, b0, b1, b2, b3, out):
@@ -826,6 +990,7 @@
         self.narrow = lax.axis_index("narrow")
         self.z, self.x = self.wide // 2, self.wide % 2
         self.y, self.c = self.narrow // 2, self.narrow % 2
+        self.high, self.low = self.z // 2, self.z % 2
 
     @staticmethod
     def pairs(move):
@@ -853,8 +1018,11 @@
     def swap_c(self, value):
         return self.send(value, lambda z, x, y, c: (z, x, y, 1 - c))
 
-    def shift_z(self, value, k):
-        return self.send(value, lambda z, x, y, c: ((z + k) % 4, x, y, c))
+    def swap_low(self, value):
+        return self.send(value, lambda z, x, y, c: (z ^ 1, x, y, c))
+
+    def swap_high(self, value):
+        return self.send(value, lambda z, x, y, c: (z ^ 2, x, y, c))
 
 
 def pick(array, index):
@@ -872,33 +1040,64 @@
     return jnp.stack([jnp.where(bit == 0, mine, other), jnp.where(bit == 0, other, mine)])
 
 
-def sum_everywhere(place, array):
-    rows, cols = array.shape
-    parts = array.reshape(2, 2, 2, 2, 4, rows // 64, cols)
-    bits = ((place.y, place.swap_y), (place.x, place.swap_x))
-
-    def halve(bit, swap, value):
-        return add(pick(value, bit), swap(pick(value, 1 - bit)))
-
-    kept = halve(place.c, place.swap_c, parts)
-    first = [halve(*bits[i], kept[i]) for i in range(2)]
-    second = [halve(*bits[1 - i], first[i]) for i in range(2)]
-    value = jnp.stack(second, axis=1)
-    came = [place.shift_z(pick(value, (place.z + k) % 4), k) for k in (1, 2, 3)]
-    done = add(pick(value, place.z), *came)
-    around = [done] + [place.shift_z(done, k) for k in (1, 2, 3)]
-    around = jnp.stack(around)
-    ordered = jnp.stack([pick(around, (place.z - k) % 4) for k in range(4)])
-    back = []
-    for i in range(2):
-        own = ordered[:, i]
-        bit, swap = bits[1 - i]
-        own = in_order(bit, own, swap(own))
-        bit, swap = bits[i]
-        back.append(in_order(bit, own, swap(own)))
-    own = jnp.stack(back)
-    whole = in_order(place.c, own, place.swap_c(own))
-    return whole.reshape(rows, cols)
+def tie(value, *others):
+    return lax.optimization_barrier((value,) + others)[0]
+
+
+def halve(bit, swap, value):
+    return add(pick(value, bit), swap(pick(value, 1 - bit)))
+
+
+def place_heads(place, sources, core, heads, rows, begun):
+    size, cols = sources[0].shape[3:]
+
+    def block(j):
+        part, y = j // 2, j % 2
+
+        def at(s, bits):
+            a = s % 2
+            active = (s // 4) == part
+            if part == 0:
+                active = active & ((s // 2) % 2 == y)
+                return (0, 0, jnp.where(active, a, 0), 0, 0)
+            return (jnp.where(active, (s // 2) % 2, 0), 0, jnp.where(active, a, 0), 0, 0)
+
+        return pl.BlockSpec((2 if part == 0 else 1, 2, 1, size, cols), at)
+
+    def row_block(s, bits):
+        part, i, a = s // 4, (s // 2) % 2, s % 2
+        y, high = bits[0] ^ i, bits[2] ^ a
+        inside = jnp.where(part == 0, y * 2 + high, high * 2 + y)
+        return (((bits[4] ^ core) * 2 + part) * 4 + inside, 0)
+
+    wide = cols - 2 * LANES
+    more = () if begun is None else tuple(begun)
+    return call(
+        place_heads_kernel,
+        (
+            shaped((rows, heads * LANES), FULL_TYPE), shaped((rows, heads * LANES), FULL_TYPE),
+            shaped((rows, heads * wide), FULL_TYPE),
+        ),
+        jnp.stack([place.y, place.x, place.high, place.low, place.c]).astype(jnp.int32), *sources, *more,
+        grid=(8,), prefetch=1,
+        in_specs=[block(j) for j in range(4)] + [pl.BlockSpec(memory_space=pl.ANY)] * len(more),
+        out_specs=(
+            pl.BlockSpec((size, heads * LANES), row_block), pl.BlockSpec((size, heads * LANES), row_block),
+            pl.BlockSpec((size, heads * wide), row_block),
+        ),
+        aliases={5 + i: i for i in range(len(more))},
+    )
+
+
+def turn_tables(span, head_dim):
+    half = head_dim // 2
+    frequency = np.float32(10000.0) ** (-(np.arange(half).astype(np.float32) * np.float32(2.0) / np.float32(head_dim)))
+    angles = np.arange(span).astype(np.float32)[:, None] * frequency[None, :].astype(np.float32)
+    cosine, sine = np.cos(angles.astype(np.float64)), np.sin(angles.astype(np.float64))
+    return (
+        jnp.asarray(np.concatenate([cosine, cosine], axis=1).astype(np.float32)),
+        jnp.asarray(np.concatenate([-sine, sine], axis=1).astype(np.float32)),
+    )
 
 
 def tuned_device(
@@ -911,16 +1110,43 @@
     pair_count = seqs * heads
     span = 8 * row_count
     all_rows = seqs * row_count
+    wide_out = heads * experts * LANES
+    local = w_up.shape[1] // 4
+    hidden = 8 * local
+    own_count = w_select.shape[1]
+    count = 8 * own_count
+    quarter = count // 4
+    tall = row_count + quarter
     place = Place()
     first_row = place.wide * row_count
     row = lambda v: v.reshape(1, -1)
-
-    half = head_dim // 2
-    frequency = 10000.0 ** (-(jnp.arange(half).astype(FULL_TYPE) * 2.0 / head_dim))
-    angles = jnp.arange(span).astype(FULL_TYPE)[:, None] * frequency[None, :]
-    cosine, sine = jnp.cos(angles), jnp.sin(angles)
-    cosine = jnp.concatenate([cosine, cosine], axis=1)
-    sine = jnp.concatenate([-sine, sine], axis=1)
+    smem = pl.BlockSpec(memory_space=pltpu.SMEM)
+    vmem = pl.BlockSpec(memory_space=pltpu.VMEM)
+    hbm = pl.BlockSpec(memory_space=pl.ANY)
+    by_seq = lambda shape: pl.BlockSpec((1,) + tuple(shape[1:]), lambda s: (s,) + (0,) * (len(shape) - 1))
+    split = lambda shape: pl.BlockSpec((shape[0] // seqs,) + tuple(shape[1:]), lambda s: (s,) + (0,) * (len(shape) - 1))
+    token_cols = lambda n: pl.BlockSpec((n, row_count), lambda s: (0, s))
+
+    own_select = jnp.transpose(w_select).reshape(own_count, 8, -1).swapaxes(0, 1).reshape(-1, LANES)
+
+    own_weights = call(
+        weights_kernel,
+        shaped((2, 2, width, local)),
+        jnp.stack([place.narrow, place.narrow + 1 - 2 * place.c]).astype(jnp.int32), w_up, w_down,
+        grid=(2,), prefetch=1,
+        in_specs=[
+            pl.BlockSpec((width, local), lambda s, spots: (0, spots[s])),
+            pl.BlockSpec((local, width), lambda s, spots: (spots[s], 0)),
+        ],
+        out_specs=pl.BlockSpec((1, 2, width, local), lambda s, spots: (s, 0, 0, 0)),
+    )
+    weights_far = place.swap_high(own_weights[0])
+    weights_near = place.swap_low(own_weights[0])
+
+    cot_own = cotangent.reshape(all_rows, width)
+    cots = [cot_own, place.swap_y(cot_own), place.swap_x(cot_own), place.swap_xy(cot_own)]
+
+    cosine, sine = turn_tables(span, head_dim)
     here = lambda t: lax.dynamic_slice_in_dim(t, first_row, row_count, 0)
     sel = jnp.concatenate(
         [
@@ -931,68 +1157,37 @@
     )
     value_flat = value_ids.reshape(seqs, row_count, -1)
     out_flat = out_ids.reshape(seqs, row_count, -1)
-
-    local = w_up.shape[1] // 4
-    my_up = lax.dynamic_slice_in_dim(w_up, place.narrow * local, local, 1)
-    my_down = lax.dynamic_slice_in_dim(w_down, place.narrow * local, local, 0)
-    peer = place.narrow + 1 - 2 * place.c
-    ups = [my_up, lax.dynamic_slice_in_dim(w_up, peer * local, local, 1)]
-    downs = [my_down, lax.dynamic_slice_in_dim(w_down, peer * local, local, 0)]
-    for k in (1, 2, 3):
-        up_k, down_k = place.shift_z(my_up, 4 - k), place.shift_z(my_down, 4 - k)
-        ups += [up_k, place.swap_c(up_k)]
-        downs += [down_k, place.swap_c(down_k)]
-
-    own_select = jnp.transpose(w_select)
-    select = jnp.concatenate(
-        [own_select] + [lax.ppermute(own_select, "wide", [(i, i ^ k) for i in range(8)]) for k in range(1, 8)]
-    )
-    own_count = own_select.shape[0]
-    select_ids = ((place.wide ^ jnp.arange(8))[:, None] * own_count + jnp.arange(own_count)[None, :]).reshape(-1)
-    kind = place.x * 2 + place.y
-    kinds = kind ^ jnp.arange(4)
-    kx, ky = (kinds // 2)[:, None, None, None], (kinds % 2)[:, None, None, None]
-    kz = ((place.z + jnp.arange(4)) % 4)[None, :, None, None]
-    kc = (place.c ^ jnp.arange(2))[None, None, :, None]
-    ki = jnp.arange(2)[None, None, None, :]
-    sent_ids = ((kz * 2 + kx) * own_count + ky * 4 + kc * 2 + ki).reshape(-1)
-    places = (sent_ids[:, None] == select_ids[None, :]).astype(HALF_TYPE)
-    count = select_ids.shape[0]
-    lanes = jnp.arange(LANES)
-    targets = jnp.concatenate([select_ids, count + jnp.arange(LANES - count)])
-    order = (targets[:, None] == lanes[None, :]).astype(HALF_TYPE)
-
-    cot_own = cotangent.reshape(all_rows, width)
-    cots = [cot_own, place.swap_y(cot_own), place.swap_x(cot_own), place.swap_xy(cot_own)]
-
-    by_seq = lambda shape: pl.BlockSpec((1,) + tuple(shape[1:]), lambda s: (s,) + (0,) * (len(shape) - 1))
-    split = lambda shape: pl.BlockSpec((shape[0] // seqs,) + tuple(shape[1:]), lambda s: (s,) + (0,) * (len(shape) - 1))
-    wide_out = heads * experts * LANES
+    payload = 3 * row_count + own_select.shape[0] + 16
     qkv, projected, gate = call(
         pre_kernel,
         (
-            shaped((pair_count, 3, row_count, head_dim)),
+            shaped((pair_count, payload, head_dim)),
             shaped((seqs, row_count, wide_out)),
             shaped((seqs, row_count, LANES), FULL_TYPE),
         ),
         tokens, row(gain_one), row(bias_one), w_query, w_key, w_value, sel, value_flat, out_flat,
-        here(cosine), here(sine),
+        here(cosine), here(sine), own_select,
         grid=(seqs,),
         in_specs=[
             by_seq(tokens.shape), full((1, width)), full((1, width)), full(w_query.shape), full(w_key.shape),
             full(w_value.shape), full(sel.shape), by_seq(value_flat.shape), by_seq(out_flat.shape),
             full((row_count, head_dim)), full((row_count, head_dim)),
+            full(own_select.shape),
         ],
         out_specs=(
-            split((pair_count, 3, row_count, head_dim)), by_seq((seqs, row_count, wide_out)),
+            split((pair_count, payload, head_dim)), by_seq((seqs, row_count, wide_out)),
             by_seq((seqs, row_count, LANES)),
         ),
         flops=2 * all_rows * width * 3712,
     )
     qkv = lax.all_to_all(qkv, "wide", 0, 0, tiled=True)
-    length = pick(lengths, place.wide // heads).reshape(1)
-    smem = pl.BlockSpec(memory_space=pltpu.SMEM)
-    vmem = pl.BlockSpec(memory_space=pltpu.VMEM)
+    qkv, weights_far, weights_near, cots[1], cots[2], cots[3] = lax.optimization_barrier(
+        (qkv, weights_far, weights_near, cots[1], cots[2], cots[3])
+    )
+    tokens_x = place.swap_x(tie(tokens, qkv))
+    weights_last = place.swap_low(weights_far)
+    seq_here = place.wide // heads
+    length = pick(lengths, seq_here).reshape(1)
     mixed, out_t, lse = call(
         attend_kernel,
         (
@@ -1003,64 +1198,85 @@
         flops=2 * span * span * head_dim,
     )
     mixed = lax.all_to_all(mixed, "wide", 0, 0, tiled=True)
+    mixed, weights_last, tokens_x = lax.optimization_barrier((mixed, weights_last, tokens_x))
+
+    kinds = (place.x * 2 + place.y) ^ jnp.arange(4)
+    kx, ky = (kinds // 2)[:, None, None, None], (kinds % 2)[:, None, None, None]
+    kz = (place.z ^ jnp.arange(4))[None, :, None, None]
+    kc = (place.c ^ jnp.arange(2))[None, None, :, None]
+    ki = jnp.arange(2)[None, None, None, :]
+    sent_ids = ((kz * 2 + kx) * own_count + ky * 4 + kc * 2 + ki).reshape(-1)
+    places = (sent_ids[:, None] == jnp.arange(count)[None, :]).astype(HALF_TYPE)
 
     own_mlp = lax.dynamic_slice_in_dim(mlp_ids, first_row, row_count, 1)
     own_mlp = jnp.swapaxes(own_mlp, 1, 2)
-    token_cols = lambda n: pl.BlockSpec((n, row_count), lambda s: (0, s))
-    after, rows_own, gates, sent = call(
+    after, gates, rows_own, select = call(
         post_kernel,
         (
-            shaped((all_rows, width), FULL_TYPE), shaped((all_rows, width)),
-            shaped((count, all_rows), FULL_TYPE), shaped((4, count // 4, all_rows)),
+            shaped((all_rows, width), FULL_TYPE), shaped((count, all_rows), FULL_TYPE), shaped((seqs, tall, width)),
+            shaped((count, width)),
         ),
-        mixed, gate, w_out, tokens, row(gain_two), row(bias_two), select, own_mlp,
-        select_ids.reshape(-1, 1), places,
+        mixed, gate, w_out, tokens, row(gain_two), row(bias_two), qkv, own_mlp, places,
         grid=(seqs,),
         in_specs=[
             split(mixed.shape), by_seq(gate.shape), full(w_out.shape), by_seq(tokens.shape), full((1, width)),
-            full((1, width)), full(select.shape), by_seq(own_mlp.shape), full((count, 1)), full(places.shape),
+            full((1, width)), pl.BlockSpec((8, 8 * own_count, LANES), lambda s: (0, 3 * row_count // (8 * own_count), 0)),
+            by_seq(own_mlp.shape), full(places.shape),
         ],
         out_specs=(
-            split((all_rows, width)), split((all_rows, width)), token_cols(count),
-            pl.BlockSpec((4, count // 4, row_count), lambda s: (0, 0, s)),
+            split((all_rows, width)), token_cols(count), by_seq((seqs, tall, width)), full((count, width)),
         ),
         flops=2 * all_rows * width * wide_out,
     )
 
-    swaps = (lambda v: v, place.swap_y, place.swap_x, place.swap_xy)
-    rows_in = [swaps[i](rows_own) for i in range(4)]
-    gates_in = [swaps[i](sent[i]) for i in range(4)]
-    hidden = 8 * local
+    rows_y, rows_x = place.swap_y(rows_own), place.swap_x(rows_own)
+    rows_d = (place.swap_x(rows_y[0]), place.swap_y(rows_x[1]))
+    rows_in = [(rows_own,), (rows_y,), (rows_x,), rows_d]
+    weights = [own_weights]
+    for piece in (weights_near, weights_far, weights_last):
+        weights += [piece, place.swap_c(piece)]
     results = []
     for i in range(4):
+        if i:
+            cots[i] = tie(cots[i], results[-1][1])
         results.append(
             call(
-                experts_kernel,
+                functools.partial(experts_kernel, i, len(rows_in[i])),
                 (
-                    shaped((all_rows, width)), shaped((all_rows, width)), shaped((count // 4, all_rows)),
-                    shaped((all_rows, hidden)), shaped((all_rows, hidden)),
+                    shaped((seqs, tall, width)), shaped((8, all_rows, local)), shaped((8, all_rows, local)),
                 ),
-                rows_in[i], cots[i], gates_in[i], *ups, *downs,
-                flops=8 * all_rows * width * hidden,
+                *rows_in[i], cots[i], *weights,
+                flops=6 * all_rows * width * hidden,
             )
         )
+    swaps = (lambda v: v, place.swap_y, place.swap_x, place.swap_xy)
     d_rows = [swaps[i](results[i][0]) for i in range(4)]
-    d_gates = [swaps[i](results[i][2]) for i in range(4)]
-    branches = [swaps[i](results[i][1]) for i in range(4)]
-
-    cols = lambda: pl.BlockSpec((all_rows, local), lambda p: (0, p))
-    whole = lambda: pl.BlockSpec((all_rows, width), lambda p: (0, 0))
-    grad_up, grad_down = call(
+    inners = [r[1] for r in results]
+
+    own_two = jnp.stack([pick(tokens, seq_here), pick(tokens_x, seq_here)])
+    other_two = jnp.stack([pick(tokens, 1 - seq_here), pick(tokens_x, 1 - seq_here)])
+    near_four = jnp.concatenate([own_two, tie(place.swap_high(tie(other_two, rows_own)), results[1][1])])
+    far_four = place.swap_low(near_four)
+
+    whole = lambda shape: pl.BlockSpec(tuple(shape), lambda p: (0,) * len(shape))
+    piece = lambda: pl.BlockSpec((1, all_rows, local), lambda p: (2 * (2 * (p % 2) + (p // 2) % 2) + p // 4, 0, 0))
+    grads_out = [
+        pl.BlockSpec((1, 2, width, local), lambda p, j=j: (jnp.clip(p - 2 * j, 0, 1), 0, 0, 0)) for j in range(4)
+    ]
+    grad_near, grad_far, peer_near, peer_far = call(
         expert_grads_kernel,
-        (shaped((8, width, local)), shaped((8, local, width))),
-        *rows_in, *cots, *[r[4] for r in results], *[r[3] for r in results],
+        (shaped((2, 2, width, local)),) * 4,
+        tie(rows_own, d_rows[1], d_rows[2]), rows_y, rows_x, *rows_d, *cots, *[r[2] for r in results], *inners,
         grid=(8,),
-        in_specs=[whole() for _ in range(8)] + [cols() for _ in range(8)],
-        out_specs=(
-            pl.BlockSpec((1, width, local), lambda p: (p, 0, 0)), pl.BlockSpec((1, local, width), lambda p: (p, 0, 0)),
-        ),
+        in_specs=[whole((seqs, tall, width))] * 3 + [whole((tall, width))] * 2 + [whole((all_rows, width))] * 4
+        + [piece() for _ in range(8)],
+        out_specs=tuple(grads_out),
         flops=16 * all_rows * width * hidden,
     )
+    d_rows[3], peer_far, peer_near, far_four = lax.optimization_barrier(
+        (tie(d_rows[3], grad_near), peer_far, peer_near, far_four)
+    )
+    came_far, came_near = place.swap_c(peer_far), place.swap_c(peer_near)
 
     live_info = jnp.concatenate([jnp.zeros((1,), jnp.int32), first_row.reshape(1).astype(jnp.int32), lengths])
     d_after, d_att, d_gate_out, small = call(
@@ -1069,12 +1285,12 @@
             shaped((all_rows, width), FULL_TYPE), shaped((pair_count, row_count, head_dim)),
             shaped((seqs, row_count, LANES), FULL_TYPE), shaped((width, LANES), FULL_TYPE),
         ),
-        live_info, *d_rows, *d_gates, cotangent, after, gates, row(gain_two), row(bias_two), select, places, order,
+        live_info, *d_rows, cotangent, after, gates, row(gain_two), row(bias_two), select, places,
         w_out, gate, mixed,
         grid=(seqs,),
-        in_specs=[smem] + [split((all_rows, width))] * 4 + [token_cols(count // 4)] * 4 + [
+        in_specs=[smem] + [by_seq((seqs, tall, width))] * 4 + [
             by_seq(cotangent.shape), split((all_rows, width)), token_cols(count), full((1, width)), full((1, width)),
-            full(select.shape), full(places.shape), full(order.shape), full(w_out.shape), by_seq(gate.shape),
+            full(select.shape), full(places.shape), full(w_out.shape), by_seq(gate.shape),
             split(mixed.shape),
         ],
         out_specs=(
@@ -1084,54 +1300,174 @@
         scratch=[pltpu.VMEM((LANES, width), FULL_TYPE)],
         flops=2 * all_rows * width * wide_out,
     )
-    d_att = lax.all_to_all(d_att, "wide", 0, 0, tiled=True)
+    d_att_all = lax.all_to_all(d_att, "wide", 0, 0, tiled=True)
+
+    to_low = add(grad_far, came_far)
+    passed = place.swap_low(to_low)
+    near_four = tie(near_four, d_att, to_low)
+    tok_t, norm_t = call(
+        turn_kernel,
+        (shaped((8, width, row_count)), shaped((8, width, row_count))),
+        near_four, far_four, row(gain_one), row(bias_one),
+        grid=(8,),
+        in_specs=[
+            pl.BlockSpec((1, row_count, width), lambda i: (jnp.minimum(i, 3), 0, 0)),
+            pl.BlockSpec((1, row_count, width), lambda i: (jnp.maximum(i - 4, 0), 0, 0)),
+            full((1, width)), full((1, width)),
+        ],
+        out_specs=(
+            pl.BlockSpec((1, width, row_count), lambda i: (i, 0, 0)),
+            pl.BlockSpec((1, width, row_count), lambda i: (i, 0, 0)),
+        ),
+    )
+    grad_out = call(
+        out_grad_kernel, shaped((heads * head_dim, experts * width)), tie(mixed, d_att, came_far, came_near), gate, d_after,
+        flops=2 * all_rows * width * wide_out,
+    )
+    rows_out, cols_out = grad_out.shape
+    flat = ((place.y, place.swap_y), (place.x, place.swap_x))
+    out_parts = halve(place.c, place.swap_c, grad_out.reshape(2, 2, 2, 2, 2, 2, rows_out // 64, cols_out))
+
+    d_att_all, tok_t, out_parts = lax.optimization_barrier((d_att_all, tok_t, out_parts))
+    out_parts = [halve(*flat[i], out_parts[i]) for i in range(2)]
     d_qkv = call(
         attend_back_kernel,
-        shaped((8, 3, row_count, head_dim)),
-        length, qkv, d_att, out_t, lse, cosine, sine,
+        shaped((8, 3 * row_count, head_dim)),
+        length, qkv, d_att_all, out_t, lse, cosine, sine,
         in_specs=[smem] + [vmem] * 6,
         scratch=[pltpu.VMEM((span, head_dim), FULL_TYPE), pltpu.VMEM((span, head_dim), FULL_TYPE)],
         flops=5 * span * span * head_dim,
     )
-    d_qkv = lax.all_to_all(d_qkv, "wide", 0, 0, tiled=True)
-
+
+    d_qkv, out_parts[0], out_parts[1] = lax.optimization_barrier((d_qkv, *out_parts))
+    out_parts = [halve(*flat[1 - i], out_parts[i]) for i in range(2)]
+
+    block_of = lambda i, spot: spot[0] ^ ((i & 1) | ((i & 2) << 1) | ((i & 4) >> 1))
+    head_cols = (2 + experts) * LANES
+    head_grads = call(
+        head_grads_kernel,
+        shaped((width, head_cols)),
+        place.wide.reshape(1).astype(jnp.int32), tok_t, norm_t, d_qkv, qkv,
+        grid=(8,), prefetch=1,
+        in_specs=[
+            pl.BlockSpec((1, width, row_count), lambda i, spot: (i, 0, 0)),
+            pl.BlockSpec((1, width, row_count), lambda i, spot: (i, 0, 0)),
+            pl.BlockSpec((1, 3 * row_count, head_dim), lambda i, spot: (block_of(i, spot), 0, 0)),
+            pl.BlockSpec((1, 16, head_dim), lambda i, spot: (block_of(i, spot), payload // 16 - 1, 0)),
+        ],
+        out_specs=pl.BlockSpec((width, head_cols), lambda i, spot: (0, 0)),
+        scratch=[pltpu.VMEM((width, head_cols), FULL_TYPE)],
+        flops=2 * span * width * head_cols,
+    )
+    d_qkv_rows = lax.all_to_all(d_qkv, "wide", 0, 0, tiled=True)
+    bits = ((place.y, place.swap_y), (place.high, place.swap_high))
+    rows_head = width // 16
+    head_grads, out_sum, passed = lax.optimization_barrier((head_grads, jnp.stack(out_parts, axis=2), passed))
+    branches = call(
+        branch_kernel,
+        (shaped((all_rows, width)),) * 4,
+        tie(inners[0], head_grads), *inners[1:], *weights,
+        flops=8 * all_rows * width * hidden,
+    )
+    b0, b1, b2, b3 = branches
+    b1, b2 = place.swap_y(b1), place.swap_x(b2)
+    mine = add(grad_near[0], came_near[0], passed[0])
+    mine_far = place.swap_high(add(grad_near[1], came_near[1], passed[1]))
+    kept = halve(place.c, place.swap_c, head_grads.reshape(2, 2, 2, 2, rows_head, head_cols))
+    out_sum = halve(place.low, place.swap_low, out_sum)
+    kept, out_sum, b3 = lax.optimization_barrier((kept, out_sum, b3))
+    value = [halve(*bits[i], kept[i]) for i in range(2)]
+    out_sum = halve(place.high, place.swap_high, out_sum)
+    value[0], value[1], out_sum, d_qkv_rows, b1, b2 = lax.optimization_barrier(
+        (value[0], value[1], out_sum, d_qkv_rows, b1, b2)
+    )
+    b3 = place.swap_xy(tie(b3, b1))
+    value = [halve(*bits[1 - i], value[i]) for i in range(2)]
+    out_sum = in_order(place.high, out_sum, place.swap_high(out_sum))
+    grad_tokens, small = call(
+        last_kernel,
+        (shaped((all_rows, width)), shaped((width, LANES))),
+        d_qkv_rows, tokens, row(gain_one), row(bias_one), w_query, w_key, w_value, sel, projected, gate, d_gate_out,
+        small, d_after,
+        grid=(seqs,),
+        in_specs=[
+            split(d_qkv.shape), by_seq(tokens.shape), full((1, width)), full((1, width)), full(w_query.shape),
+            full(w_key.shape), full(w_value.shape), full(sel.shape), by_seq(projected.shape), by_seq(gate.shape),
+            by_seq(d_gate_out.shape), full(small.shape), split(d_after.shape),
+        ],
+        out_specs=(split((all_rows, width)), full((width, LANES))),
+        scratch=[pltpu.VMEM((row_count, wide_out), HALF_TYPE), pltpu.VMEM((width, LANES), FULL_TYPE)],
+        flops=2 * all_rows * width * 3712,
+    )
+    done, small, out_sum = lax.optimization_barrier((jnp.stack(value), small, out_sum))
+    far = place.swap_high(done)
+    out_sum = in_order(place.low, out_sum, place.swap_low(out_sum))
+    everywhere = ("wide", "narrow")
+    small = lax.all_to_all(small, everywhere, 0, 0, tiled=True).reshape(32, -1, LANES)
+    far, small, out_sum, mine_far, b3 = lax.optimization_barrier((far, small, out_sum, mine_far, b3))
+    mine = add(mine, mine_far)
+    mine_y = place.swap_y(mine)
+    near = [place.swap_low(done), place.swap_low(far)]
+    sets = [
+        jnp.stack([jnp.stack([done[i], far[i]]), jnp.stack([near[0][i], near[1][i]])]) for i in range(2)
+    ]
+    small = jnp.sum(small.astype(FULL_TYPE), axis=0).astype(HALF_TYPE)
+    small = lax.all_to_all(jnp.broadcast_to(small[None], (32,) + small.shape), everywhere, 0, 0, tiled=True)
+    back = [in_order(flat[1 - i][0], out_sum[:, :, i], flat[1 - i][1](out_sum[:, :, i])) for i in range(2)]
+    sets[0], sets[1], small, back[0], back[1] = lax.optimization_barrier((sets[0], sets[1], small, back[0], back[1]))
+    back = [in_order(flat[i][0], back[i], flat[i][1](back[i])) for i in range(2)]
+    first = jnp.stack([sets[0], place.swap_x(sets[0])])
+    second = jnp.stack([sets[1], place.swap_y(sets[1])])
+    out_half = jnp.stack(back).reshape(rows_out // 2, cols_out)
+    first, second, out_half, mine_y = lax.optimization_barrier((first, second, out_half, mine_y))
+    sources = [first, place.swap_y(first), second, place.swap_x(second)]
+    out_peer = place.swap_c(out_half)
+    mine_c, mine_yc = place.swap_c(mine), place.swap_c(mine_y)
+    output = call(output_kernel, shaped((all_rows, width)), after, b0, b1, b2, b3)
+    spots = jnp.stack(
+        [place.narrow, place.narrow ^ 2, place.narrow ^ 1, place.narrow ^ 3]
+    ).astype(jnp.int32)
+    grad_up, grad_down = call(
+        place_experts_kernel,
+        (shaped((width, 4 * local), FULL_TYPE), shaped((4 * local, width), FULL_TYPE)),
+        spots, mine, mine_y, mine_c, mine_yc,
+        grid=(4,), prefetch=1,
+        in_specs=[full((2, width, local))] * 4,
+        out_specs=(
+            pl.BlockSpec((width, local), lambda s, spots: (0, spots[s])),
+            pl.BlockSpec((local, width), lambda s, spots: (spots[s], 0)),
+        ),
+    )
+    half_spec = lambda mine: pl.BlockSpec((head_dim, cols_out), lambda s, spot: (jnp.where((s < 2) == mine, s % 2, 1), 0))
     grad_out = call(
-        out_grad_kernel, shaped((heads * head_dim, experts * width)), mixed, gate, d_after,
-        flops=2 * all_rows * width * wide_out,
-    )
-    output = call(output_kernel, shaped((all_rows, width)), after, *branches)
-
-    grads, d_proj, part = call(
-        last_kernel,
-        (shaped((width, 2 * heads * head_dim + wide_out + LANES)), shaped((all_rows, wide_out)), shaped((all_rows, width), FULL_TYPE)),
-        d_qkv, tokens, row(gain_one), row(bias_one), w_query, w_key, sel, projected, gate, d_gate_out, small, d_after,
-        scratch=[pltpu.VMEM((all_rows, 2 * heads * head_dim), HALF_TYPE), pltpu.VMEM((all_rows, LANES), HALF_TYPE)],
-        flops=2 * all_rows * width * 4700,
-    )
-    grad_tokens = call(token_grad_kernel, shaped((all_rows, width)), part, d_proj, w_value, flops=2 * all_rows * width * wide_out)
-
-    grad_out = sum_everywhere(place, grad_out).astype(FULL_TYPE).reshape(heads, head_dim, -1)
-    grads = sum_everywhere(place, grads).astype(FULL_TYPE)
-    wide_qk = heads * head_dim
-    grad_query, grad_key = grads[:, :wide_qk], grads[:, wide_qk:2 * wide_qk]
-    grad_value = grads[:, 2 * wide_qk:2 * wide_qk + wide_out]
-    small = grads[:, 2 * wide_qk + wide_out:]
-    grad_select = lax.dynamic_slice_in_dim(small, place.wide * own_count, own_count, 1)
-    grad_gain_two, grad_bias_two = small[:, count], small[:, count + 1]
-    grad_gain_one, grad_bias_one = small[:, count + 2], small[:, count + 3]
-    grad_sel_value = small[:, SELV:SELV + heads * experts]
-    grad_sel_out = small[:, SELO:SELO + heads * experts]
-
-    def experts_sum(pieces):
-        by_z = [add(pieces[2 * k], place.swap_c(pieces[2 * k + 1])) for k in range(4)]
-        mine = add(by_z[0], *[place.shift_z(by_z[k], k) for k in (1, 2, 3)])
-        pair = in_order(place.c, mine, place.swap_c(mine))
-        return in_order(place.y, pair, place.swap_y(pair)).reshape((4,) + mine.shape)
-
-    up_sum = experts_sum(grad_up)
-    down_sum = experts_sum(grad_down)
-    grad_up = jnp.swapaxes(up_sum, 0, 1).reshape(width, -1).astype(FULL_TYPE)
-    grad_down = down_sum.reshape(-1, width).astype(FULL_TYPE)
+        place_out_kernel,
+        shaped((heads, head_dim, cols_out), FULL_TYPE),
+        place.c.reshape(1).astype(jnp.int32), out_half, out_peer,
+        grid=(4,), prefetch=1,
+        in_specs=[half_spec(True), half_spec(False)],
+        out_specs=pl.BlockSpec((1, head_dim, cols_out), lambda s, spot: (2 * (spot[0] ^ (s // 2)) + s % 2, 0, 0)),
+    )
+    small = small.reshape(width, LANES)
+    grad_select, grad_sel_value, grad_sel_out, rows_four = call(
+        place_small_kernel,
+        (
+            shaped((own_count, width), FULL_TYPE), shaped((heads * experts, width), FULL_TYPE),
+            shaped((heads * experts, width), FULL_TYPE), shaped((8, width), FULL_TYPE),
+        ),
+        (place.wide * own_count).reshape(1).astype(jnp.int32), small,
+        in_specs=[smem, vmem],
+    )
+    peers = [place.swap_c(first), None, place.swap_c(second), None]
+    (sources[1], sources[3], peers[0], peers[2], output, grad_up, grad_down, grad_out, grad_select, grad_sel_value,
+     grad_sel_out, rows_four) = lax.optimization_barrier(
+        (sources[1], sources[3], peers[0], peers[2], output, grad_up, grad_down, grad_out, grad_select, grad_sel_value,
+         grad_sel_out, rows_four)
+    )
+    peers[1], peers[3] = place.swap_c(sources[1]), place.swap_c(sources[3])
+    grad_heads = place_heads(place, sources, 0, heads, width, None)
+    grad_query, grad_key, grad_value = place_heads(place, peers, 1, heads, width, grad_heads)
+    grad_select, grad_sel_value, grad_sel_out = grad_select.T, grad_sel_value.T, grad_sel_out.T
+    grad_gain_two, grad_bias_two, grad_gain_one, grad_bias_one = (rows_four[i] for i in range(4))
     return (
         output.reshape(tokens.shape), grad_tokens.reshape(tokens.shape), grad_query, grad_key, grad_value, grad_out,
         grad_sel_value, grad_sel_out, grad_gain_one, grad_bias_one, grad_gain_two, grad_bias_two, grad_select,

time: 862 us -> 660 us (0.77)
  waiting for transfers between devices: 369 us -> 260 us
  starting transfers between devices: 168 us -> 85.6 us
  Pallas kernels: 189 us -> 250 us
  other arithmetic: 69.4 us -> 22.9 us
  local copies, waits for them, and re-layouts: 56.9 us -> 29.8 us
    ppermute x80 -> x59, starting transfers between devices: 119 us -> 56.6 us  [send(): return lax.ppermute(value, ('wide', 'narrow'), self.pairs(move))]
    pallas_call x14 -> x22, Pallas kernels: 189 us -> 250 us  [call(): pl.pallas_call(kernel, out_shape=out_shape, input_output_aliases=aliases...]
    ppermute x80 -> x59, waiting for transfers between devices: 299 us -> 242 us  [send(): return lax.ppermute(value, ('wide', 'narrow'), self.pairs(move))]
    all_to_all x1, waiting for transfers between devices: 46.9 us -> 0.01 us  [tuned_device(): qkv = lax.all_to_all(qkv, 'wide', 0, 0, tiled=True)]
    ppermute x7 -> x0, waiting for transfers between devices: 23.2 us -> none  [tuned_device(): lax.ppermute(own_select, 'wide', [(i, i ^ k) for i in range(8)])]
    another operation x22 -> x9, other arithmetic: 23 us -> 0.72 us  [in_order(): jnp.stack([jnp.where(bit == 0, mine, other), jnp.where(bit == 0, other, m...]
    slice x8 -> x7, local copies, waits for them, and re-layouts: 19.4 us -> 0.97 us  [the longest x1 0.61 us: tuned_device(): rows_four[i]]
    all_to_all x1, waiting for transfers between devices: 0.01 us -> 17.2 us  [tuned_device(): mixed = lax.all_to_all(mixed, 'wide', 0, 0, tiled=True)]
  transfers between devices with their start and end apart: 91 -> 65, of which waited for: 32 -> 20; matrix products, arithmetic and copies ran while one was open for 9% -> 5% of each run, Pallas kernels for 21% -> 34%
where the time goes in v2:
time: 660 us; the launch traced here: 651 us
  waiting for transfers between devices  260 us (39%)
  Pallas kernels  250 us (38%)
  starting transfers between devices  85.6 us (13%)
  local copies, waits for them, and re-layouts  29.8 us (5%)
  other arithmetic  22.9 us (3%)
    pallas_call x22, Pallas kernels, call(): pl.pallas_call(kernel, out_shape=out_shape, input_output_aliases=aliases...  250 us
    ppermute x59, waiting for transfers between devices, send(): return lax.ppermute(value, ('wide', 'narrow'), self.pairs(move))  242 us
    ppermute x59, starting transfers between devices, send(): return lax.ppermute(value, ('wide', 'narrow'), self.pairs(move))  56.6 us
    all_to_all x1, waiting for transfers between devices, tuned_device(): mixed = lax.all_to_all(mixed, 'wide', 0, 0, tiled=True)  17.2 us
    convert_element_type x11, other arithmetic, add(): return total.astype(HALF_TYPE)  14 us
  transfers between devices with their start and end apart: 65, of which 20 were waited for; matrix products, arithmetic and copies ran while one was open for 5% of the time, Pallas kernels for 34%

profile of v2, /device:TPU:0, one launch (start us, length us, event | category | flops | bytes accessed | tf_op | source)
XLA Modules:
  0.0 650.9 jit_solution(12238760114943603050)
XLA Ops:
  8.6 10.9 %shard_map.316 = (bf16[8,848,128]{2,1,0:T(8,128)(2,1)}, bf16[2,256,2560]{2,1,0:T(8,128)(2,1)}, f32[2,256,128]{2,1,0:T(8,128)}) custom-call(bf16[2,256,1024]{2,1,0:T(8,128)(2,1)} %tok.5, f32[1,1024]{1,0:T(1,128)} %bitcast.196, f32[1,1024]{1,0:T(1,128)} %bitcast.199, bf16[1024,512]{1,0:T(8,128)(2,1)} %wq.3, bf16[1024,512]{1,0:T(8,128)(2,1)} %wk.3, ...), custom_call_target="tpu_custom_call" | custom-call | flops 3892314112 | bytes 13590528 | tf_op jit(solution)/shard_map/pallas_call | solution.py:467
  19.4 7.3 %all-to-all-start = ((bf16[8,848,128]{2,1,0:T(8,128)(2,1)}), bf16[8,848,128]{2,1,0:T(8,128)(2,1)S(1)}, u32[]{:S(2)}, u32[]{:S(2)}) async-start(bf16[8,848,128]{2,1,0:T(8,128)(2,1)} %get-tuple-element.137), calls=%async_computation | async-start | bytes 3473408 | tf_op jit(solution)/shard_map/all_to_all | solution.py:1183
  41.5 70.7 %collective-permute-done.refs_5_.refs_6_.refs_7_ = bf16[2,1024,256]{2,1,0:T(8,128)(2,1)} collective-permute-done((bf16[2,1024,256]{2,1,0:T(8,128)(2,1)}, bf16[2,1024,256]{2,1,0:T(8,128)(2,1)}, u32[]{:S(2)}, u32[]{:S(2)}) %collective-permute-start) | collective-permute-done | bytes 1048608 | tf_op jit(solution)/shard_map/ppermute | solution.py:1007
  114.0 9.6 %shard_map.318 = (bf16[8,256,128]{2,1,0:T(8,128)(2,1)}, f32[128,2048]{1,0:T(8,128)}, f32[1,2048]{1,0:T(1,128)}) custom-call(s32[1]{0:T(128)} %dynamic_slice.105.length, bf16[8,848,128]{2,1,0:T(8,128)(2,1)} %copy-done.13), custom_call_target="tpu_custom_call" | custom-call | flops 1073741824 | bytes 3317764 | tf_op jit(solution)/shard_map/pallas_call | solution.py:467
  128.8 17.2 %all-to-all-done.1.mixed = bf16[8,256,128]{2,1,0:T(8,128)(2,1)S(1)} async-done(((bf16[8,256,128]{2,1,0:T(8,128)(2,1)}), bf16[8,256,128]{2,1,0:T(8,128)(2,1)S(1)}, u32[]{:S(2)}, u32[]{:S(2)}) %all-to-all-start.1) | async-done | bytes 524320 | tf_op jit(solution)/shard_map/all_to_all | solution.py:1200
  147.5 8.7 %shard_map.319 = (f32[512,1024]{1,0:T(8,128)}, f32[64,512]{1,0:T(8,128)}, bf16[2,272,1024]{2,1,0:T(8,128)(2,1)}, bf16[64,1024]{1,0:T(8,128)(2,1)}) custom-call(bf16[8,256,128]{2,1,0:T(8,128)(2,1)} %copy-done.9, f32[2,256,128]{2,1,0:T(8,128)} %get-tuple-element.143.gate, bf16[4,128,5120]{2,1,0:T(8,128)(2,1)} %w_out.3, bf16[2,256,1024]{2,1,0:T(8,128)(2,1)} %tok.5, ...), custom_call_target="tpu_custom_call" | custom-call | flops 2684354560 | bytes 12337152 | tf_op jit(solution)/shard_map/pallas_call | solution.py:467
  162.3 14.2 %shard_map.320 = (bf16[2,272,1024]{2,1,0:T(8,128)(2,1)}, bf16[8,512,256]{2,1,0:T(8,128)(2,1)}, bf16[8,512,256]{2,1,0:T(8,128)(2,1)}) custom-call(bf16[2,272,1024]{2,1,0:T(8,128)(2,1)} %get-tuple-element.160.refs_0_, bf16[512,1024]{1,0:T(8,128)(2,1)} %bitcast.13.refs_1_.refs_5_, bf16[2,2,1024,256]{3,2,1,0:T(8,128)(2,1)} %shard_map.317.refs_2_.refs_3_.refs_4_, ...), custom_call_target="tpu_custom_call" | custom-call | flops 6442450944 | bytes 15859712 | tf_op jit(solution)/shard_map/pallas_call | solution.py:467
  176.4 6.9 %collective-permute-done.10.refs_0_.refs_1_ = bf16[2,272,1024]{2,1,0:T(8,128)(2,1)S(1)} collective-permute-done((bf16[2,272,1024]{2,1,0:T(8,128)(2,1)}, bf16[2,272,1024]{2,1,0:T(8,128)(2,1)S(1)}, u32[]{:S(2)}, u32[]{:S(2)}) %collective-permute-start.10) | collective-permute-done | bytes 1114144 | tf_op jit(solution)/shard_map/ppermute | solution.py:1007
  184.4 22.9 %shard_map.321 = (bf16[2,272,1024]{2,1,0:T(8,128)(2,1)}, bf16[8,512,256]{2,1,0:T(8,128)(2,1)}, bf16[8,512,256]{2,1,0:T(8,128)(2,1)}) custom-call(bf16[2,272,1024]{2,1,0:T(8,128)(2,1)} %copy-done.26, bf16[512,1024]{1,0:T(8,128)(2,1)} %collective-permute-done.2.refs_1_.refs_6_, bf16[2,2,1024,256]{3,2,1,0:T(8,128)(2,1)} %shard_map.317.refs_2_.refs_3_.refs_4_, ...), custom_call_target="tpu_custom_call" | custom-call | flops 6442450944 | bytes 15859712 | tf_op jit(solution)/shard_map/pallas_call | solution.py:467
  212.2 14.2 %shard_map.322 = (bf16[2,272,1024]{2,1,0:T(8,128)(2,1)}, bf16[8,512,256]{2,1,0:T(8,128)(2,1)}, bf16[8,512,256]{2,1,0:T(8,128)(2,1)}) custom-call(bf16[2,272,1024]{2,1,0:T(8,128)(2,1)} %copy-done.27, bf16[512,1024]{1,0:T(8,128)(2,1)} %collective-permute-done.3.refs_1_.refs_7_, bf16[2,2,1024,256]{3,2,1,0:T(8,128)(2,1)} %shard_map.317.refs_2_.refs_3_.refs_4_, ...), custom_call_target="tpu_custom_call" | custom-call | flops 6442450944 | bytes 15859712 | tf_op jit(solution)/shard_map/pallas_call | solution.py:467
  229.8 15.9 %collective-permute-done.15.refs_1_.refs_4_ = bf16[272,1024]{1,0:T(8,128)(2,1)} collective-permute-done((bf16[272,1024]{1,0:T(8,128)(2,1)}, bf16[272,1024]{1,0:T(8,128)(2,1)}, u32[]{:S(2)}, u32[]{:S(2)}) %collective-permute-start.15) | collective-permute-done | bytes 557088 | tf_op jit(solution)/shard_map/ppermute | solution.py:1007
  245.7 14.4 %shard_map.323 = (bf16[2,272,1024]{2,1,0:T(8,128)(2,1)}, bf16[8,512,256]{2,1,0:T(8,128)(2,1)}, bf16[8,512,256]{2,1,0:T(8,128)(2,1)}) custom-call(bf16[272,1024]{1,0:T(8,128)(2,1)} %collective-permute-done.14.refs_0_.refs_3_, bf16[272,1024]{1,0:T(8,128)(2,1)} %collective-permute-done.15.refs_1_.refs_4_, ...), custom_call_target="tpu_custom_call" | custom-call | flops 6442450944 | bytes 15859712 | tf_op jit(solution)/shard_map/pallas_call | solution.py:467
  260.2 28.6 %shard_map.324 = (bf16[2,2,1024,256]{3,2,1,0:T(8,128)(2,1)}, bf16[2,2,1024,256]{3,2,1,0:T(8,128)(2,1)}, bf16[2,2,1024,256]{3,2,1,0:T(8,128)(2,1)}, bf16[2,2,1024,256]{3,2,1,0:T(8,128)(2,1)}) custom-call(bf16[2,272,1024]{2,1,0:T(8,128)(2,1)} %get-tuple-element.160.refs_0_, bf16[2,272,1024]{2,1,0:T(8,128)(2,1)} %copy-done.26, ...), custom_call_target="tpu_custom_call" | custom-call | flops 17179869184 | bytes 33816576 | tf_op jit(solution)/shard_map/pallas_call | solution.py:467
  291.6 16.8 %shard_map.325 = (f32[512,1024]{1,0:T(8,128)}, bf16[8,256,128]{2,1,0:T(8,128)(2,1)}, f32[2,256,128]{2,1,0:T(8,128)}, f32[1024,128]{1,0:T(8,128)}) custom-call(s32[4]{0:T(128)} %pad_add_fusion.length, bf16[2,272,1024]{2,1,0:T(8,128)(2,1)} %get-tuple-element.147.r0, bf16[2,272,1024]{2,1,0:T(8,128)(2,1)} %copy-done.14, bf16[2,272,1024]{2,1,0:T(8,128)(2,1)} %copy-done.15, ...), custom_call_target="tpu_custom_call" | custom-call | flops 2684354560 | bytes 17317904 | tf_op jit(solution)/shard_map/pallas_call | solution.py:467
  308.5 8.1 %shard_map.327 = bf16[512,5120]{1,0:T(8,128)(2,1)} custom-call(bf16[8,256,128]{2,1,0:T(8,128)(2,1)} %copy-done.9, f32[2,256,128]{2,1,0:T(8,128)} %get-tuple-element.143.gate, f32[512,1024]{1,0:T(8,128)} %get-tuple-element.185.d_after), custom_call_target="tpu_custom_call" | custom-call | flops 2684354560 | bytes 8126464 | tf_op jit(solution)/shard_map/pallas_call | solution.py:467
  331.1 9.6 %shard_map.326 = (bf16[8,1024,256]{2,1,0:T(8,128)(2,1)}, bf16[8,1024,256]{2,1,0:T(8,128)(2,1)}) custom-call(bf16[4,256,1024]{2,1,0:T(8,128)(2,1)} %copy-done.3, bf16[4,256,1024]{2,1,0:T(8,128)(2,1)} %copy-done.11, f32[1,1024]{1,0:T(1,128)} %bitcast.197, f32[1,1024]{1,0:T(1,128)} %bitcast.200), custom_call_target="tpu_custom_call" | custom-call | bytes 12591104 | tf_op jit(solution)/shard_map/pallas_call | solution.py:467
  347.2 11.4 %shard_map.328.d_qkv = bf16[8,768,128]{2,1,0:T(8,128)(2,1)} custom-call(s32[1]{0:T(128)} %dynamic_slice.105.length, bf16[8,848,128]{2,1,0:T(8,128)(2,1)} %copy-done.13, bf16[8,256,128]{2,1,0:T(8,128)(2,1)} %copy-done.25, f32[128,2048]{1,0:T(8,128)} %get-tuple-element.189.out_t, f32[1,2048]{1,0:T(1,128)} %get-tuple-element.190.lse, ...), custom_call_target="tpu_custom_call" | custom-call | flops 2684354560 | bytes 6987780 | tf_op jit(solution)/shard_map/pallas_call | solution.py:467
  370.2 13.0 %shard_map.329 = bf16[1024,896]{1,0:T(8,128)(2,1)} custom-call(s32[1]{0:T(128)} %bitcast.spot, bf16[8,1024,256]{2,1,0:T(8,128)(2,1)} %get-tuple-element.186.tok_t, bf16[8,1024,256]{2,1,0:T(8,128)(2,1)} %get-tuple-element.187.norm_t, bf16[8,768,128]{2,1,0:T(8,128)(2,1)} %shard_map.328.d_qkv, bf16[8,848,128]{2,1,0:T(8,128)(2,1)} %copy-done.13), custom_call_target="tpu_custom_call" | custom-call | flops 3758096384 | bytes 13533188 | tf_op jit(solution)/shard_map/pallas_call | solution.py:467
  384.5 10.0 %collective-permute-done.26 = bf16[2,2,1024,256]{3,2,1,0:T(8,128)(2,1)} collective-permute-done((bf16[2,2,1024,256]{3,2,1,0:T(8,128)(2,1)}, bf16[2,2,1024,256]{3,2,1,0:T(8,128)(2,1)}, u32[]{:S(2)}, u32[]{:S(2)}) %collective-permute-start.26) | collective-permute-done | bytes 2097184 | tf_op jit(solution)/shard_map/ppermute | solution.py:1007
  395.7 15.7 %shard_map.330 = (bf16[512,1024]{1,0:T(8,128)(2,1)}, bf16[512,1024]{1,0:T(8,128)(2,1)}, bf16[512,1024]{1,0:T(8,128)(2,1)}, bf16[512,1024]{1,0:T(8,128)(2,1)}) custom-call(bf16[8,512,256]{2,1,0:T(8,128)(2,1)} %get-tuple-element.197.refs_13_.refs_0_, bf16[8,512,256]{2,1,0:T(8,128)(2,1)} %get-tuple-element.153.refs_14_.refs_1_, ...), custom_call_target="tpu_custom_call" | custom-call | flops 8589934592 | bytes 20971520 | tf_op jit(solution)/shard_map/pallas_call | solution.py:467
  414.9 7.2 %collective-permute-start.39 = (bf16[2,1024,256]{2,1,0:T(8,128)(2,1)}, bf16[2,1024,256]{2,1,0:T(8,128)(2,1)}, u32[]{:S(2)}, u32[]{:S(2)}) collective-permute-start(bf16[2,1024,256]{2,1,0:T(8,128)(2,1)} %fusion.5), channel_id=1, source_target_pairs={{0,16},{1,17},{2,18},{3,19},{4,20},{5,21},{6,22},{7,23},{8,24},{9,... | collective-permute-start | bytes 3145736 | tf_op jit(solution)/shard_map/ppermute | solution.py:1007
  424.4 50.6 %collective-permute-done.31 = bf16[2,8,5120]{2,1,0:T(8,128)(2,1)S(1)} collective-permute-done((bf16[2,8,5120]{2,1,0:T(8,128)(2,1)S(1)}, bf16[2,8,5120]{2,1,0:T(8,128)(2,1)S(1)}, u32[]{:S(2)}, u32[]{:S(2)}) %collective-permute-start.31) | collective-permute-done | bytes 163872 | tf_op jit(solution)/shard_map/ppermute | solution.py:1007
  475.1 12.6 %collective-permute-done.30 = bf16[2,64,896]{2,1,0:T(8,128)(2,1)S(1)} collective-permute-done((bf16[2,64,896]{2,1,0:T(8,128)(2,1)S(1)}, bf16[2,64,896]{2,1,0:T(8,128)(2,1)S(1)}, u32[]{:S(2)}, u32[]{:S(2)}) %collective-permute-start.30) | collective-permute-done | bytes 229408 | tf_op jit(solution)/shard_map/ppermute | solution.py:1007
  494.7 11.9 %shard_map.331 = (bf16[512,1024]{1,0:T(8,128)(2,1)}, bf16[1024,128]{1,0:T(8,128)(2,1)}) custom-call(bf16[8,768,128]{2,1,0:T(8,128)(2,1)} %copy-done.4, bf16[2,256,1024]{2,1,0:T(8,128)(2,1)} %tok.5, f32[1,1024]{1,0:T(1,128)} %bitcast.198, f32[1,1024]{1,0:T(1,128)} %bitcast.201, bf16[1024,512]{1,0:T(8,128)(2,1)} %wq.3, bf16[1024,512]{1,0:T(8,128)(2,1)} %wk.3, ...), custom_call_target="tpu_custom_call" | custom-call | flops 3892314112 | bytes 17309696 | tf_op jit(solution)/shard_map/pallas_call | solution.py:467
  513.3 9.1 %collective-permute-done.41 = bf16[2,64,896]{2,1,0:T(8,128)(2,1)S(1)} collective-permute-done((bf16[2,64,896]{2,1,0:T(8,128)(2,1)S(1)}, bf16[2,64,896]{2,1,0:T(8,128)(2,1)S(1)}, u32[]{:S(2)}, u32[]{:S(2)}) %collective-permute-start.41) | collective-permute-done | bytes 229408 | tf_op jit(solution)/shard_map/ppermute | solution.py:1007
  522.4 6.8 %collective-permute-done.38 = bf16[2,2,8,5120]{3,2,0,1:T(8,128)(2,1)S(1)} collective-permute-done((bf16[2,2,8,5120]{3,2,0,1:T(8,128)(2,1)S(1)}, bf16[2,2,8,5120]{3,2,0,1:T(8,128)(2,1)S(1)}, u32[]{:S(2)}, u32[]{:S(2)}) %collective-permute-start.38) | collective-permute-done | bytes 327712 | tf_op jit(solution)/shard_map/ppermute | solution.py:1007
  538.9 9.0 %collective-permute-done.44 = bf16[2,2,8,5120]{3,2,1,0:T(8,128)(2,1)S(1)} collective-permute-done((bf16[2,2,8,5120]{3,2,1,0:T(8,128)(2,1)S(1)}, bf16[2,2,8,5120]{3,2,1,0:T(8,128)(2,1)S(1)}, u32[]{:S(2)}, u32[]{:S(2)}) %collective-permute-start.44) | collective-permute-done | bytes 327712 | tf_op jit(solution)/shard_map/ppermute | solution.py:1007
  565.3 9.6 %collective-permute-done.48 = bf16[2,2,2,8,5120]{4,3,2,1,0:T(8,128)(2,1)S(1)} collective-permute-done((bf16[2,2,2,8,5120]{4,3,2,1,0:T(8,128)(2,1)S(1)}, bf16[2,2,2,8,5120]{4,3,2,1,0:T(8,128)(2,1)S(1)}, u32[]{:S(2)}, u32[]{:S(2)}) %collective-permute-start.48) | collective-permute-done | bytes 655392 | tf_op jit(solution)/shard_map/ppermute | solution.py:1007
  575.2 23.6 %collective-permute-done.47 = bf16[2,2,2,8,5120]{4,3,2,1,0:T(8,128)(2,1)S(1)} collective-permute-done((bf16[2,2,2,8,5120]{4,3,2,1,0:T(8,128)(2,1)S(1)}, bf16[2,2,2,8,5120]{4,3,2,1,0:T(8,128)(2,1)S(1)}, u32[]{:S(2)}, u32[]{:S(2)}) %collective-permute-start.47) | collective-permute-done | bytes 655392 | tf_op jit(solution)/shard_map/ppermute | solution.py:1007
  623.4 7.5 %shard_map.334 = f32[4,128,5120]{2,1,0:T(8,128)} custom-call(s32[1]{0:T(128)} %bitcast.83.spot, bf16[256,5120]{1,0:T(8,128)(2,1)} %bitcast.183, bf16[256,5120]{1,0:T(8,128)(2,1)} %collective-permute-done.56.peer), custom_call_target="tpu_custom_call" | custom-call | bytes 15728644 | tf_op jit(solution)/shard_map/pallas_call | solution.py:467
  632.2 8.2 %shard_map.336 = (f32[1024,512]{1,0:T(8,128)}, f32[1024,512]{1,0:T(8,128)}, f32[1024,2560]{1,0:T(8,128)}) custom-call(s32[5]{0:T(128)} %stack.235.bits, bf16[2,2,2,64,896]{4,3,2,1,0:T(8,128)(2,1)} %pad_maximum_fusion.3.refs_0_, bf16[2,2,2,64,896]{4,3,2,1,0:T(8,128)(2,1)} %collective-permute-done.50.refs_1_, ...), custom_call_target="tpu_custom_call" | custom-call | bytes 18350100 | tf_op jit(solution)/shard_map/pallas_call | solution.py:467
  642.2 8.3 %shard_map.337 = (f32[1024,512]{1,0:T(8,128)}, f32[1024,512]{1,0:T(8,128)}, f32[1024,2560]{1,0:T(8,128)}) custom-call(s32[5]{0:T(128)} %stack.235.bits, bf16[2,2,2,64,896]{4,3,2,1,0:T(8,128)(2,1)} %collective-permute-done.52.refs_0_, bf16[2,2,2,64,896]{4,3,2,1,0:T(8,128)(2,1)} %copy-done.23, ...), custom_call_target="tpu_custom_call", output_to_operand_aliasing={{0}: (5, {}), {1}: (6, {}), {2}: (7, {})} | custom-call | bytes 33030164 | tf_op jit(solution)/shard_map/pallas_call | solution.py:467
  (274 shorter events, 158.2 us)
Async XLA Ops:
  19.4 92.8 %all-to-all-start = ((bf16[8,848,128]{2,1,0:T(8,128)(2,1)}), bf16[8,848,128]{2,1,0:T(8,128)(2,1)S(1)}, u32[]{:S(2)}, u32[]{:S(2)}) async-start(bf16[8,848,128]{2,1,0:T(8,128)(2,1)} %get-tuple-element.137), calls=%async_computation | async-start | bytes 3473408 | tf_op jit(solution)/shard_map/all_to_all | solution.py:1183
  33.1 79.2 %collective-permute-start = (bf16[2,1024,256]{2,1,0:T(8,128)(2,1)}, bf16[2,1024,256]{2,1,0:T(8,128)(2,1)}, u32[]{:S(2)}, u32[]{:S(2)}) collective-permute-start(bf16[2,1024,256]{2,1,0:T(8,128)(2,1)} %slice_bitcast_fusion), channel_id=1, source_target_pairs={{0,16},{1,17},{2,18},{3,19},{4,20},{5,21},{6,22},{7,23},{8,24},{9,... | collective-permute-start | bytes 3145736 | tf_op jit(solution)/shard_map/ppermute | solution.py:1007
  36.0 76.3 %collective-permute-start.1 = (bf16[2,1024,256]{2,1,0:T(8,128)(2,1)}, bf16[2,1024,256]{2,1,0:T(8,128)(2,1)}, u32[]{:S(2)}, u32[]{:S(2)}) collective-permute-start(bf16[2,1024,256]{2,1,0:T(8,128)(2,1)} %slice_bitcast_fusion), channel_id=1, source_target_pairs={{0,8},{1,9},{2,10},{3,11},{4,12},{5,13},{6,14},{7,15},{8,0},{9,1},... | collective-permute-start | bytes 3145736 | tf_op jit(solution)/shard_map/ppermute | solution.py:1007
  37.4 74.8 %collective-permute-start.2 = (bf16[512,1024]{1,0:T(8,128)(2,1)}, bf16[512,1024]{1,0:T(8,128)(2,1)}, u32[]{:S(2)}, u32[]{:S(2)}) collective-permute-start(bf16[512,1024]{1,0:T(8,128)(2,1)} %bitcast.13.refs_1_.refs_5_), channel_id=1, source_target_pairs={{0,2},{1,3},{2,0},{3,1},{4,6},{5,7},{6,4},{7,5},{8,10},{9,11},{10,... | collective-permute-start | bytes 3145736 | tf_op jit(solution)/shard_map/ppermute | solution.py:1007
  39.0 73.3 %collective-permute-start.3 = (bf16[512,1024]{1,0:T(8,128)(2,1)}, bf16[512,1024]{1,0:T(8,128)(2,1)}, u32[]{:S(2)}, u32[]{:S(2)}) collective-permute-start(bf16[512,1024]{1,0:T(8,128)(2,1)} %bitcast.13.refs_1_.refs_5_), channel_id=1, source_target_pairs={{0,4},{1,5},{2,6},{3,7},{4,0},{5,1},{6,2},{7,3},{8,12},{9,13},{10,... | collective-permute-start | bytes 3145736 | tf_op jit(solution)/shard_map/ppermute | solution.py:1007
  40.4 71.8 %collective-permute-start.4 = (bf16[512,1024]{1,0:T(8,128)(2,1)}, bf16[512,1024]{1,0:T(8,128)(2,1)}, u32[]{:S(2)}, u32[]{:S(2)}) collective-permute-start(bf16[512,1024]{1,0:T(8,128)(2,1)} %bitcast.13.refs_1_.refs_5_), channel_id=1, source_target_pairs={{0,6},{1,7},{2,4},{3,5},{4,2},{5,3},{6,0},{7,1},{8,14},{9,15},{10,... | collective-permute-start | bytes 3145736 | tf_op jit(solution)/shard_map/ppermute | solution.py:1007
  112.3 33.8 %collective-permute-start.5 = (bf16[2,1024,256]{2,1,0:T(8,128)(2,1)}, bf16[2,1024,256]{2,1,0:T(8,128)(2,1)}, u32[]{:S(2)}, u32[]{:S(2)}) collective-permute-start(bf16[2,1024,256]{2,1,0:T(8,128)(2,1)} %collective-permute-done.refs_5_.refs_6_.refs_7_), channel_id=1, source_target_pairs={{0,8},{1,9},{2,10},{3,11},{4,12},{5,13},{6,14},{7,15},{8,0},{9,1},... | collective-permute-start | bytes 3145736 | tf_op jit(solution)/shard_map/ppermute | solution.py:1007
  112.4 33.7 %collective-permute-start.6 = (bf16[2,256,1024]{2,1,0:T(8,128)(2,1)S(1)}, bf16[2,256,1024]{2,1,0:T(8,128)(2,1)}, u32[]{:S(2)}, u32[]{:S(2)}) collective-permute-start(bf16[2,256,1024]{2,1,0:T(8,128)(2,1)S(1)} %copy-done.6), channel_id=1, source_target_pairs={{0,4},{1,5},{2,6},{3,7},{4,0},{5,1},{6,2},{7,3},{8,12},{9,13},{10,... | collective-permute-start | bytes 3145736 | tf_op jit(solution)/shard_map/ppermute | solution.py:1007
  128.3 34.0 %collective-permute-start.8 = (bf16[2,1024,256]{2,1,0:T(8,128)(2,1)}, bf16[2,1024,256]{2,1,0:T(8,128)(2,1)}, u32[]{:S(2)}, u32[]{:S(2)}) collective-permute-start(bf16[2,1024,256]{2,1,0:T(8,128)(2,1)} %collective-permute-done.refs_5_.refs_6_.refs_7_), channel_id=1, source_target_pairs={{0,1},{1,0},{2,3},{3,2},{4,5},{5,4},{6,7},{7,6},{8,9},{9,8},{10,11... | collective-permute-start | bytes 3145736 | tf_op jit(solution)/shard_map/ppermute | solution.py:1007
  128.4 32.1 %collective-permute-start.7 = (bf16[2,1024,256]{2,1,0:T(8,128)(2,1)}, bf16[2,1024,256]{2,1,0:T(8,128)(2,1)}, u32[]{:S(2)}, u32[]{:S(2)}) collective-permute-start(bf16[2,1024,256]{2,1,0:T(8,128)(2,1)} %collective-permute-done.1.refs_3_.refs_4_.refs_5_), channel_id=1, source_target_pairs={{0,1},{1,0},{2,3},{3,2},{4,5},{5,4},{6,7},{7,6},{8,9},{9,8},{10,11... | collective-permute-start | bytes 3145736 | tf_op jit(solution)/shard_map/ppermute | solution.py:1007
  156.3 27.1 %collective-permute-start.10 = (bf16[2,272,1024]{2,1,0:T(8,128)(2,1)}, bf16[2,272,1024]{2,1,0:T(8,128)(2,1)S(1)}, u32[]{:S(2)}, u32[]{:S(2)}) collective-permute-start(bf16[2,272,1024]{2,1,0:T(8,128)(2,1)} %get-tuple-element.160.refs_0_), channel_id=1, source_target_pairs={{0,2},{1,3},{2,0},{3,1},{4,6},{5,7},{6,4},{7,5},{8,10},{9,11},{10,... | collective-permute-start | bytes 3342344 | tf_op jit(solution)/shard_map/ppermute | solution.py:1007
  159.1 51.7 %collective-permute-start.12 = (bf16[2,272,1024]{2,1,0:T(8,128)(2,1)S(1)}, bf16[2,272,1024]{2,1,0:T(8,128)(2,1)S(1)}, u32[]{:S(2)}, u32[]{:S(2)}) collective-permute-start(bf16[2,272,1024]{2,1,0:T(8,128)(2,1)S(1)} %copy-done.30), channel_id=1, source_target_pairs={{0,4},{1,5},{2,6},{3,7},{4,0},{5,1},{6,2},{7,3},{8,12},{9,13},{10,... | collective-permute-start | bytes 3342344 | tf_op jit(solution)/shard_map/ppermute | solution.py:1007
  160.5 68.0 %collective-permute-start.17 = (bf16[2,256,1024]{2,1,0:T(8,128)(2,1)S(1)}, bf16[2,256,1024]{2,1,0:T(8,128)(2,1)S(1)}, u32[]{:S(2)}, u32[]{:S(2)}) collective-permute-start(bf16[2,256,1024]{2,1,0:T(8,128)(2,1)S(1)} %pad_maximum_fusion.2), channel_id=1, source_target_pairs={{0,16},{1,17},{2,18},{3,19},{4,20},{5,21},{6,22},{7,23},{8,24},{9,... | collective-permute-start | bytes 3145736 | tf_op jit(solution)/shard_map/ppermute | solution.py:1007
  207.4 52.8 %collective-permute-start.11 = (bf16[2,272,1024]{2,1,0:T(8,128)(2,1)}, bf16[2,272,1024]{2,1,0:T(8,128)(2,1)S(1)}, u32[]{:S(2)}, u32[]{:S(2)}) collective-permute-start(bf16[2,272,1024]{2,1,0:T(8,128)(2,1)} %get-tuple-element.151), channel_id=1, source_target_pairs={{0,2},{1,3},{2,0},{3,1},{4,6},{5,7},{6,4},{7,5},{8,10},{9,11},{10,... | collective-permute-start | bytes 3342344 | tf_op jit(solution)/shard_map/ppermute | solution.py:1007
  211.7 34.0 %collective-permute-start.15 = (bf16[272,1024]{1,0:T(8,128)(2,1)}, bf16[272,1024]{1,0:T(8,128)(2,1)}, u32[]{:S(2)}, u32[]{:S(2)}) collective-permute-start(bf16[272,1024]{1,0:T(8,128)(2,1)} %slice_bitcast_fusion.1), channel_id=1, source_target_pairs={{0,2},{1,3},{2,0},{3,1},{4,6},{5,7},{6,4},{7,5},{8,10},{9,11},{10,... | collective-permute-start | bytes 1671176 | tf_op jit(solution)/shard_map/ppermute | solution.py:1007
  226.4 33.8 %collective-permute-start.13 = (bf16[2,272,1024]{2,1,0:T(8,128)(2,1)}, bf16[2,272,1024]{2,1,0:T(8,128)(2,1)S(1)}, u32[]{:S(2)}, u32[]{:S(2)}) collective-permute-start(bf16[2,272,1024]{2,1,0:T(8,128)(2,1)} %get-tuple-element.155), channel_id=1, source_target_pairs={{0,4},{1,5},{2,6},{3,7},{4,0},{5,1},{6,2},{7,3},{8,12},{9,13},{10,... | collective-permute-start | bytes 3342344 | tf_op jit(solution)/shard_map/ppermute | solution.py:1007
  228.6 60.2 %collective-permute-start.18 = (bf16[4,256,1024]{2,1,0:T(8,128)(2,1)S(1)}, bf16[4,256,1024]{2,1,0:T(8,128)(2,1)S(1)}, u32[]{:S(2)}, u32[]{:S(2)}) collective-permute-start(bf16[4,256,1024]{2,1,0:T(8,128)(2,1)S(1)} %pad_maximum_fusion.1.near), channel_id=1, source_target_pairs={{0,8},{1,9},{2,10},{3,11},{4,12},{5,13},{6,14},{7,15},{8,0},{9,1},... | collective-permute-start | bytes 6291464 | tf_op jit(solution)/shard_map/ppermute | solution.py:1007
  260.2 28.7 %collective-permute-start.16 = (bf16[2,272,1024]{2,1,0:T(8,128)(2,1)}, bf16[2,272,1024]{2,1,0:T(8,128)(2,1)S(1)}, u32[]{:S(2)}, u32[]{:S(2)}) collective-permute-start(bf16[2,272,1024]{2,1,0:T(8,128)(2,1)} %get-tuple-element.159), channel_id=1, source_target_pairs={{0,6},{1,7},{2,4},{3,5},{4,2},{5,3},{6,0},{7,1},{8,14},{9,15},{10,... | collective-permute-start | bytes 3342344 | tf_op jit(solution)/shard_map/ppermute | solution.py:1007
  329.1 65.4 %collective-permute-start.26 = (bf16[2,2,1024,256]{3,2,1,0:T(8,128)(2,1)}, bf16[2,2,1024,256]{3,2,1,0:T(8,128)(2,1)}, u32[]{:S(2)}, u32[]{:S(2)}) collective-permute-start(bf16[2,2,1024,256]{3,2,1,0:T(8,128)(2,1)} %add_convert_fusion), channel_id=1, source_target_pairs={{0,8},{1,9},{2,10},{3,11},{4,12},{5,13},{6,14},{7,15},{8,0},{9,1},... | collective-permute-start | bytes 6291464 | tf_op jit(solution)/shard_map/ppermute | solution.py:1007
  366.3 122.5 %all-to-all-start.3 = ((bf16[8,768,128]{2,1,0:T(8,128)(2,1)}), bf16[8,768,128]{2,1,0:T(8,128)(2,1)S(1)}, u32[]{:S(2)}, u32[]{:S(2)}) async-start(bf16[8,768,128]{2,1,0:T(8,128)(2,1)} %shard_map.328.d_qkv), calls=%async_computation.3 | async-start | bytes 3145728 | tf_op jit(solution)/shard_map/all_to_all | solution.py:1362
  395.6 26.7 %collective-permute-start.27 = (bf16[2,2,2,64,896]{4,3,2,1,0:T(8,128)(2,1)}, bf16[2,2,2,64,896]{4,3,2,1,0:T(8,128)(2,1)S(1)}, u32[]{:S(2)}, u32[]{:S(2)}) collective-permute-start(bf16[2,2,2,64,896]{4,3,2,1,0:T(8,128)(2,1)} %dynamic-slice_bitcast_fusion.1), channel_id=1, source_target_pairs={{0,1},{1,0},{2,3},{3,2},{4,5},{5,4},{6,7},{7,6},{8,9},{9,8},{10,11... | collective-permute-start | bytes 2752520 | tf_op jit(solution)/shard_map/ppermute | solution.py:1007
  395.6 26.6 %collective-permute-start.28 = (bf16[2,2,8,5120]{3,2,1,0:T(8,128)(2,1)S(1)}, bf16[2,2,8,5120]{3,2,1,0:T(8,128)(2,1)S(1)}, u32[]{:S(2)}, u32[]{:S(2)}) collective-permute-start(bf16[2,2,8,5120]{3,2,1,0:T(8,128)(2,1)S(1)} %dynamic-slice_bitcast_fusion.4), channel_id=1, source_target_pairs={{0,8},{1,9},{2,10},{3,11},{4,12},{5,13},{6,14},{7,15},{8,0},{9,1},... | collective-permute-start | bytes 983048 | tf_op jit(solution)/shard_map/ppermute | solution.py:1007
  411.4 76.4 %collective-permute-start.32 = (bf16[512,1024]{1,0:T(8,128)(2,1)}, bf16[512,1024]{1,0:T(8,128)(2,1)S(1)}, u32[]{:S(2)}, u32[]{:S(2)}) collective-permute-start(bf16[512,1024]{1,0:T(8,128)(2,1)} %get-tuple-element.201), channel_id=1, source_target_pairs={{0,2},{1,3},{2,0},{3,1},{4,6},{5,7},{6,4},{7,5},{8,10},{9,11},{10,... | collective-permute-start | bytes 3145736 | tf_op jit(solution)/shard_map/ppermute | solution.py:1007
  411.9 76.8 %collective-permute-start.33 = (bf16[512,1024]{1,0:T(8,128)(2,1)}, bf16[512,1024]{1,0:T(8,128)(2,1)}, u32[]{:S(2)}, u32[]{:S(2)}) collective-permute-start(bf16[512,1024]{1,0:T(8,128)(2,1)} %get-tuple-element.202), channel_id=1, source_target_pairs={{0,4},{1,5},{2,6},{3,7},{4,0},{5,1},{6,2},{7,3},{8,12},{9,13},{10,... | collective-permute-start | bytes 3145736 | tf_op jit(solution)/shard_map/ppermute | solution.py:1007
  414.9 114.4 %collective-permute-start.39 = (bf16[2,1024,256]{2,1,0:T(8,128)(2,1)}, bf16[2,1024,256]{2,1,0:T(8,128)(2,1)}, u32[]{:S(2)}, u32[]{:S(2)}) collective-permute-start(bf16[2,1024,256]{2,1,0:T(8,128)(2,1)} %fusion.5), channel_id=1, source_target_pairs={{0,16},{1,17},{2,18},{3,19},{4,20},{5,21},{6,22},{7,23},{8,24},{9,... | collective-permute-start | bytes 3145736 | tf_op jit(solution)/shard_map/ppermute | solution.py:1007
  422.6 52.4 %collective-permute-start.31 = (bf16[2,8,5120]{2,1,0:T(8,128)(2,1)S(1)}, bf16[2,8,5120]{2,1,0:T(8,128)(2,1)S(1)}, u32[]{:S(2)}, u32[]{:S(2)}) collective-permute-start(bf16[2,8,5120]{2,1,0:T(8,128)(2,1)S(1)} %dynamic-slice_bitcast_fusion.9), channel_id=1, source_target_pairs={{0,16},{1,17},{2,18},{3,19},{4,20},{5,21},{6,22},{7,23},{8,24},{9,... | collective-permute-start | bytes 491528 | tf_op jit(solution)/shard_map/ppermute | solution.py:1007
  422.8 52.3 %collective-permute-start.29 = (bf16[2,64,896]{2,1,0:T(8,128)(2,1)S(1)}, bf16[2,64,896]{2,1,0:T(8,128)(2,1)S(1)}, u32[]{:S(2)}, u32[]{:S(2)}) collective-permute-start(bf16[2,64,896]{2,1,0:T(8,128)(2,1)S(1)} %dynamic-slice_bitcast_fusion.8), channel_id=1, source_target_pairs={{0,2},{1,3},{2,0},{3,1},{4,6},{5,7},{6,4},{7,5},{8,10},{9,11},{10,... | collective-permute-start | bytes 688136 | tf_op jit(solution)/shard_map/ppermute | solution.py:1007
  493.4 37.4 %collective-permute-start.40 = (bf16[512,1024]{1,0:T(8,128)(2,1)}, bf16[512,1024]{1,0:T(8,128)(2,1)S(1)}, u32[]{:S(2)}, u32[]{:S(2)}) collective-permute-start(bf16[512,1024]{1,0:T(8,128)(2,1)} %get-tuple-element.217), channel_id=1, source_target_pairs={{0,6},{1,7},{2,4},{3,5},{4,2},{5,3},{6,0},{7,1},{8,14},{9,15},{10,... | collective-permute-start | bytes 3145736 | tf_op jit(solution)/shard_map/ppermute | solution.py:1007
  554.5 44.9 %collective-permute-start.49 = (bf16[2,1024,256]{2,1,0:T(8,128)(2,1)S(1)}, bf16[2,1024,256]{2,1,0:T(8,128)(2,1)S(1)}, u32[]{:S(2)}, u32[]{:S(2)}) collective-permute-start(bf16[2,1024,256]{2,1,0:T(8,128)(2,1)S(1)} %fusion.1.refs_0_), channel_id=1, source_target_pairs={{0,2},{1,3},{2,0},{3,1},{4,6},{5,7},{6,4},{7,5},{8,10},{9,11},{10,... | collective-permute-start | bytes 3145736 | tf_op jit(solution)/shard_map/ppermute | solution.py:1007
  555.6 43.2 %collective-permute-start.47 = (bf16[2,2,2,8,5120]{4,3,2,1,0:T(8,128)(2,1)S(1)}, bf16[2,2,2,8,5120]{4,3,2,1,0:T(8,128)(2,1)S(1)}, u32[]{:S(2)}, u32[]{:S(2)}) collective-permute-start(bf16[2,2,2,8,5120]{4,3,2,1,0:T(8,128)(2,1)S(1)} %pad_maximum_fusion.7), channel_id=1, source_target_pairs={{0,2},{1,3},{2,0},{3,1},{4,6},{5,7},{6,4},{7,5},{8,10},{9,11},{10,... | collective-permute-start | bytes 1966088 | tf_op jit(solution)/shard_map/ppermute | solution.py:1007
  600.1 30.8 %collective-permute-start.50 = (bf16[2,2,2,64,896]{4,3,2,1,0:T(8,128)(2,1)}, bf16[2,2,2,64,896]{4,3,2,1,0:T(8,128)(2,1)}, u32[]{:S(2)}, u32[]{:S(2)}) collective-permute-start(bf16[2,2,2,64,896]{4,3,2,1,0:T(8,128)(2,1)} %pad_maximum_fusion.3.refs_0_), channel_id=1, source_target_pairs={{0,2},{1,3},{2,0},{3,1},{4,6},{5,7},{6,4},{7,5},{8,10},{9,11},{10,... | collective-permute-start | bytes 2752520 | tf_op jit(solution)/shard_map/ppermute | solution.py:1007
  601.0 29.9 %collective-permute-start.52 = (bf16[2,2,2,64,896]{4,3,2,1,0:T(8,128)(2,1)}, bf16[2,2,2,64,896]{4,3,2,1,0:T(8,128)(2,1)}, u32[]{:S(2)}, u32[]{:S(2)}) collective-permute-start(bf16[2,2,2,64,896]{4,3,2,1,0:T(8,128)(2,1)} %pad_maximum_fusion.3.refs_0_), channel_id=1, source_target_pairs={{0,1},{1,0},{2,3},{3,2},{4,5},{5,4},{6,7},{7,6},{8,9},{9,8},{10,11... | collective-permute-start | bytes 2752520 | tf_op jit(solution)/shard_map/ppermute | solution.py:1007
  (64 other events, 1055.1 us)

commit v3 on v2

--- a/solution.py
+++ b/solution.py
@@ -656,9 +656,13 @@
         sent[0, row_count:row_count + quarter, i * row_count:(i + 1) * row_count] = moved[i * quarter:(i + 1) * quarter]
 
 
-def weights_kernel(spots, up, down, out):
-    out[0, 0] = up[...]
-    out[0, 1] = jnp.transpose(down[...].astype(FULL_TYPE)).astype(HALF_TYPE)
+def weights_kernel(spots, up, down, mine, peer):
+    for s, out in enumerate((mine, peer)):
+
+        @pl.when(pl.program_id(0) == s)
+        def _(out=out):
+            out[0] = up[...]
+            out[1] = jnp.transpose(down[...].astype(FULL_TYPE)).astype(HALF_TYPE)
 
 
 def expand(count, cols, first):
@@ -672,12 +676,11 @@
 
 
 def experts_kernel(kind, halves, *refs):
-    rows_in, cot, first = refs[:halves], refs[halves], refs[halves + 1]
-    others = refs[halves + 2:halves + 8]
-    back, inner, d_pre = refs[halves + 8:]
+    rows_in, cot, pieces = refs[:halves], refs[halves], refs[halves + 1:halves + 9]
+    back, inner, d_pre = refs[halves + 9:]
     seqs, tall, width = back.shape
     row_count = width // 4
-    cols = first.shape[3]
+    cols = pieces[0].shape[2]
     quarter = tall - row_count
     picked = [rows_in[0][s] if halves == 1 else rows_in[s][...] for s in range(seqs)]
     low = jnp.concatenate([block[0:row_count] for block in picked], axis=0)
@@ -686,7 +689,7 @@
     )
     cot_low = cot[...]
     row_total = gate_total = None
-    weight = lambda p, u: first[p, u] if p < 2 else others[p - 2][u]
+    weight = lambda p, u: pieces[p][u]
     root, cube = 0.7978845608028654, 0.044715
     for p in range(8):
         spread = expand(quarter, cols, p * (cols // LANES))
@@ -713,8 +716,8 @@
 
 
 def branch_kernel(*refs):
-    inners, first, others, outs = refs[0:4], refs[4], refs[5:11], refs[11:15]
-    downs = [first[0, 1], first[1, 1]] + [ref[1] for ref in others]
+    inners, pieces, outs = refs[0:4], refs[4:12], refs[12:16]
+    downs = [ref[1] for ref in pieces]
     for i in range(4):
         total = None
         for p in range(8):
@@ -940,16 +943,8 @@
                 put(sources[2 + i][0, b, 0], (low ^ b) * 2 + (x ^ i))
 
 
-def place_out_kernel(spot, mine, peer, out):
-    step = pl.program_id(0)
-
-    @pl.when(step < 2)
-    def _():
-        out[0] = mine[...].astype(FULL_TYPE)
-
-    @pl.when(step >= 2)
-    def _():
-        out[0] = peer[...].astype(FULL_TYPE)
+def place_out_kernel(spot, mine, *rest):
+    rest[-1][0] = mine[...].astype(FULL_TYPE)
 
 
 def place_small_kernel(first, small, select, value, out, rows):
@@ -966,15 +961,14 @@
     rows[...] = nt(spots.astype(FULL_TYPE).astype(HALF_TYPE), low)
 
 
-def place_experts_kernel(spots, *refs):
-    up, down = refs[4:]
-    step = pl.program_id(0)
-    for i in range(4):
-
-        @pl.when(step == i)
-        def _(i=i):
-            up[...] = refs[i][0].astype(FULL_TYPE)
-            down[...] = jnp.transpose(refs[i][1].astype(FULL_TYPE))
+def place_experts_kernel(spots, mine, mine_y, *rest):
+    up, down = rest[-2:]
+    for i, ref in enumerate((mine, mine_y)):
+
+        @pl.when(pl.program_id(0) == i)
+        def _(ref=ref):
+            up[...] = ref[0].astype(FULL_TYPE)
+            down[...] = jnp.transpose(ref[1].astype(FULL_TYPE))
 
 
 def output_kernel(after, b0, b1, b2, b3, out):
@@ -1046,6 +1040,38 @@
 
 def halve(bit, swap, value):
     return add(pick(value, bit), swap(pick(value, 1 - bit)))
+
+
+def place_out(place, half, core, heads, begun):
+    rows, cols = half.shape
+    size = 2 * rows // heads
+    more = begun or ()
+    return call(
+        place_out_kernel,
+        shaped((heads, size, cols), FULL_TYPE),
+        (place.c ^ core).reshape(1).astype(jnp.int32), half, *more,
+        grid=(heads // 2,), prefetch=1,
+        in_specs=[pl.BlockSpec((size, cols), lambda s, spot: (s, 0))] + [pl.BlockSpec(memory_space=pl.ANY)] * len(more),
+        out_specs=pl.BlockSpec((1, size, cols), lambda s, spot: (spot[0] * (heads // 2) + s, 0, 0)),
+        aliases={2 + i: i for i in range(len(more))},
+    )
+
+
+def place_experts(place, mine, mine_y, core, begun):
+    width, local = mine.shape[1:]
+    more = begun or ()
+    return call(
+        place_experts_kernel,
+        (shaped((width, 4 * local), FULL_TYPE), shaped((4 * local, width), FULL_TYPE)),
+        jnp.stack([place.narrow ^ core, place.narrow ^ core ^ 2]).astype(jnp.int32), mine, mine_y, *more,
+        grid=(2,), prefetch=1,
+        in_specs=[full(mine.shape)] * 2 + [pl.BlockSpec(memory_space=pl.ANY)] * len(more),
+        out_specs=(
+            pl.BlockSpec((width, local), lambda s, spots: (0, spots[s])),
+            pl.BlockSpec((local, width), lambda s, spots: (spots[s], 0)),
+        ),
+        aliases={3 + i: i for i in range(len(more))},
+    )
 
 
 def place_heads(place, sources, core, heads, rows, begun):
@@ -1129,22 +1155,22 @@
 
     own_select = jnp.transpose(w_select).reshape(own_count, 8, -1).swapaxes(0, 1).reshape(-1, LANES)
 
-    own_weights = call(
+    mine_peer = jnp.stack([place.narrow, place.narrow + 1 - 2 * place.c]).astype(jnp.int32)
+    weights_mine, weights_peer = call(
         weights_kernel,
-        shaped((2, 2, width, local)),
-        jnp.stack([place.narrow, place.narrow + 1 - 2 * place.c]).astype(jnp.int32), w_up, w_down,
+        (shaped((2, width, local)), shaped((2, width, local))),
+        mine_peer, w_up, w_down,
         grid=(2,), prefetch=1,
         in_specs=[
             pl.BlockSpec((width, local), lambda s, spots: (0, spots[s])),
             pl.BlockSpec((local, width), lambda s, spots: (spots[s], 0)),
         ],
-        out_specs=pl.BlockSpec((1, 2, width, local), lambda s, spots: (s, 0, 0, 0)),
-    )
-    weights_far = place.swap_high(own_weights[0])
-    weights_near = place.swap_low(own_weights[0])
+        out_specs=(full((2, width, local)), full((2, width, local))),
+    )
 
     cot_own = cotangent.reshape(all_rows, width)
-    cots = [cot_own, place.swap_y(cot_own), place.swap_x(cot_own), place.swap_xy(cot_own)]
+    cots = [cot_own, place.swap_y(cot_own)]
+    tokens_x = place.swap_x(tokens)
 
     cosine, sine = turn_tables(span, head_dim)
     here = lambda t: lax.dynamic_slice_in_dim(t, first_row, row_count, 0)
@@ -1181,11 +1207,10 @@
         flops=2 * all_rows * width * 3712,
     )
     qkv = lax.all_to_all(qkv, "wide", 0, 0, tiled=True)
-    qkv, weights_far, weights_near, cots[1], cots[2], cots[3] = lax.optimization_barrier(
-        (qkv, weights_far, weights_near, cots[1], cots[2], cots[3])
-    )
-    tokens_x = place.swap_x(tie(tokens, qkv))
-    weights_last = place.swap_low(weights_far)
+    qkv, cots[1], tokens_x, weights_mine = lax.optimization_barrier((qkv, cots[1], tokens_x, weights_mine))
+    weights_far, weights_near = place.swap_high(weights_mine), place.swap_low(weights_mine)
+    cot_later = tie(cot_own, qkv)
+    cots += [place.swap_x(cot_later), place.swap_xy(cot_later)]
     seq_here = place.wide // heads
     length = pick(lengths, seq_here).reshape(1)
     mixed, out_t, lse = call(
@@ -1198,7 +1223,10 @@
         flops=2 * span * span * head_dim,
     )
     mixed = lax.all_to_all(mixed, "wide", 0, 0, tiled=True)
-    mixed, weights_last, tokens_x = lax.optimization_barrier((mixed, weights_last, tokens_x))
+    mixed, weights_far, weights_near, cots[2], cots[3] = lax.optimization_barrier(
+        (mixed, weights_far, weights_near, cots[2], cots[3])
+    )
+    weights_last = place.swap_low(weights_far)
 
     kinds = (place.x * 2 + place.y) ^ jnp.arange(4)
     kx, ky = (kinds // 2)[:, None, None, None], (kinds % 2)[:, None, None, None]
@@ -1232,49 +1260,46 @@
     rows_y, rows_x = place.swap_y(rows_own), place.swap_x(rows_own)
     rows_d = (place.swap_x(rows_y[0]), place.swap_y(rows_x[1]))
     rows_in = [(rows_own,), (rows_y,), (rows_x,), rows_d]
-    weights = [own_weights]
+    weights = [weights_mine, weights_peer]
     for piece in (weights_near, weights_far, weights_last):
         weights += [piece, place.swap_c(piece)]
-    results = []
-    for i in range(4):
-        if i:
-            cots[i] = tie(cots[i], results[-1][1])
-        results.append(
-            call(
+    own_two = jnp.stack([pick(tokens, seq_here), pick(tokens_x, seq_here)])
+    other_two = jnp.stack([pick(tokens, 1 - seq_here), pick(tokens_x, 1 - seq_here)])
+    other_two = place.swap_high(tie(other_two, rows_own))
+    results = {}
+    for i, before in ((1, None), (2, 1), (3, 2), (0, 3)):
+        if before is not None:
+            cots[i] = tie(cots[i], results[before][1])
+        results[i] = call(
                 functools.partial(experts_kernel, i, len(rows_in[i])),
                 (
                     shaped((seqs, tall, width)), shaped((8, all_rows, local)), shaped((8, all_rows, local)),
                 ),
                 *rows_in[i], cots[i], *weights,
-                flops=6 * all_rows * width * hidden,
+                flops=8 * all_rows * width * hidden,
             )
-        )
     swaps = (lambda v: v, place.swap_y, place.swap_x, place.swap_xy)
     d_rows = [swaps[i](results[i][0]) for i in range(4)]
-    inners = [r[1] for r in results]
-
-    own_two = jnp.stack([pick(tokens, seq_here), pick(tokens_x, seq_here)])
-    other_two = jnp.stack([pick(tokens, 1 - seq_here), pick(tokens_x, 1 - seq_here)])
-    near_four = jnp.concatenate([own_two, tie(place.swap_high(tie(other_two, rows_own)), results[1][1])])
+    inners = [results[i][1] for i in range(4)]
+    near_four = jnp.concatenate([own_two, tie(other_two, results[2][1])])
     far_four = place.swap_low(near_four)
 
     whole = lambda shape: pl.BlockSpec(tuple(shape), lambda p: (0,) * len(shape))
     piece = lambda: pl.BlockSpec((1, all_rows, local), lambda p: (2 * (2 * (p % 2) + (p // 2) % 2) + p // 4, 0, 0))
-    grads_out = [
-        pl.BlockSpec((1, 2, width, local), lambda p, j=j: (jnp.clip(p - 2 * j, 0, 1), 0, 0, 0)) for j in range(4)
-    ]
     grad_near, grad_far, peer_near, peer_far = call(
         expert_grads_kernel,
         (shaped((2, 2, width, local)),) * 4,
-        tie(rows_own, d_rows[1], d_rows[2]), rows_y, rows_x, *rows_d, *cots, *[r[2] for r in results], *inners,
+        rows_own, rows_y, rows_x, *rows_d, *cots, *[results[i][2] for i in range(4)], *inners,
         grid=(8,),
         in_specs=[whole((seqs, tall, width))] * 3 + [whole((tall, width))] * 2 + [whole((all_rows, width))] * 4
         + [piece() for _ in range(8)],
-        out_specs=tuple(grads_out),
+        out_specs=tuple(
+            pl.BlockSpec((1, 2, width, local), lambda p, j=j: (jnp.clip(p - 2 * j, 0, 1), 0, 0, 0)) for j in range(4)
+        ),
         flops=16 * all_rows * width * hidden,
     )
-    d_rows[3], peer_far, peer_near, far_four = lax.optimization_barrier(
-        (tie(d_rows[3], grad_near), peer_far, peer_near, far_four)
+    d_rows[1], d_rows[2], d_rows[3], peer_far, peer_near, far_four = lax.optimization_barrier(
+        (d_rows[1], d_rows[2], tie(d_rows[3], grad_near), peer_far, peer_near, far_four)
     )
     came_far, came_near = place.swap_c(peer_far), place.swap_c(peer_near)
 
@@ -1302,9 +1327,10 @@
     )
     d_att_all = lax.all_to_all(d_att, "wide", 0, 0, tiled=True)
 
-    to_low = add(grad_far, came_far)
-    passed = place.swap_low(to_low)
-    near_four = tie(near_four, d_att, to_low)
+    to_low = [add(grad_far[a], came_far[a]) for a in range(2)]
+    passed = [None, place.swap_low(to_low[1])]
+    passed[0] = place.swap_low(to_low[0])
+    near_four = tie(near_four, d_att, *to_low)
     tok_t, norm_t = call(
         turn_kernel,
         (shaped((8, width, row_count)), shaped((8, width, row_count))),
@@ -1321,7 +1347,7 @@
         ),
     )
     grad_out = call(
-        out_grad_kernel, shaped((heads * head_dim, experts * width)), tie(mixed, d_att, came_far, came_near), gate, d_after,
+        out_grad_kernel, shaped((heads * head_dim, experts * width)), tie(mixed, d_att, came_near, came_far), gate, d_after,
         flops=2 * all_rows * width * wide_out,
     )
     rows_out, cols_out = grad_out.shape
@@ -1362,28 +1388,24 @@
     d_qkv_rows = lax.all_to_all(d_qkv, "wide", 0, 0, tiled=True)
     bits = ((place.y, place.swap_y), (place.high, place.swap_high))
     rows_head = width // 16
-    head_grads, out_sum, passed = lax.optimization_barrier((head_grads, jnp.stack(out_parts, axis=2), passed))
+    head_grads, out_sum, passed[0], passed[1] = lax.optimization_barrier((head_grads, jnp.stack(out_parts, axis=2), *passed))
+    kept = halve(place.c, place.swap_c, head_grads.reshape(2, 2, 2, 2, rows_head, head_cols))
+    out_sum = halve(place.low, place.swap_low, out_sum)
+    kept = tie(kept, d_qkv)
     branches = call(
         branch_kernel,
         (shaped((all_rows, width)),) * 4,
-        tie(inners[0], head_grads), *inners[1:], *weights,
+        tie(inners[0], kept), *inners[1:], *weights,
         flops=8 * all_rows * width * hidden,
     )
     b0, b1, b2, b3 = branches
+    value = [halve(*bits[i], kept[i]) for i in range(2)]
+    value[0], value[1], d_qkv_rows, out_sum, b1, b2, b3 = lax.optimization_barrier(
+        (value[0], value[1], d_qkv_rows, out_sum, b1, b2, b3)
+    )
     b1, b2 = place.swap_y(b1), place.swap_x(b2)
-    mine = add(grad_near[0], came_near[0], passed[0])
-    mine_far = place.swap_high(add(grad_near[1], came_near[1], passed[1]))
-    kept = halve(place.c, place.swap_c, head_grads.reshape(2, 2, 2, 2, rows_head, head_cols))
-    out_sum = halve(place.low, place.swap_low, out_sum)
-    kept, out_sum, b3 = lax.optimization_barrier((kept, out_sum, b3))
-    value = [halve(*bits[i], kept[i]) for i in range(2)]
+    value = [halve(*bits[1 - i], value[i]) for i in range(2)]
     out_sum = halve(place.high, place.swap_high, out_sum)
-    value[0], value[1], out_sum, d_qkv_rows, b1, b2 = lax.optimization_barrier(
-        (value[0], value[1], out_sum, d_qkv_rows, b1, b2)
-    )
-    b3 = place.swap_xy(tie(b3, b1))
-    value = [halve(*bits[1 - i], value[i]) for i in range(2)]
-    out_sum = in_order(place.high, out_sum, place.swap_high(out_sum))
     grad_tokens, small = call(
         last_kernel,
         (shaped((all_rows, width)), shaped((width, LANES))),
@@ -1400,53 +1422,33 @@
         flops=2 * all_rows * width * 3712,
     )
     done, small, out_sum = lax.optimization_barrier((jnp.stack(value), small, out_sum))
+    mine = add(grad_near[0], came_near[0], passed[0])
     far = place.swap_high(done)
-    out_sum = in_order(place.low, out_sum, place.swap_low(out_sum))
+    out_sum = in_order(place.high, out_sum, place.swap_high(out_sum))
     everywhere = ("wide", "narrow")
     small = lax.all_to_all(small, everywhere, 0, 0, tiled=True).reshape(32, -1, LANES)
-    far, small, out_sum, mine_far, b3 = lax.optimization_barrier((far, small, out_sum, mine_far, b3))
-    mine = add(mine, mine_far)
-    mine_y = place.swap_y(mine)
+    far, out_sum, b1, b2, b3 = lax.optimization_barrier((far, out_sum, b1, b2, b3))
+    b3 = place.swap_xy(b3)
+    out_sum = in_order(place.low, out_sum, place.swap_low(out_sum))
     near = [place.swap_low(done), place.swap_low(far)]
     sets = [
         jnp.stack([jnp.stack([done[i], far[i]]), jnp.stack([near[0][i], near[1][i]])]) for i in range(2)
     ]
+    to_high = add(grad_near[1], came_near[1], passed[1])
+    sets[0], sets[1], small, out_sum, b3, to_high = lax.optimization_barrier(
+        (sets[0], sets[1], small, out_sum, b3, to_high)
+    )
+    mine_far = place.swap_high(to_high)
     small = jnp.sum(small.astype(FULL_TYPE), axis=0).astype(HALF_TYPE)
     small = lax.all_to_all(jnp.broadcast_to(small[None], (32,) + small.shape), everywhere, 0, 0, tiled=True)
     back = [in_order(flat[1 - i][0], out_sum[:, :, i], flat[1 - i][1](out_sum[:, :, i])) for i in range(2)]
-    sets[0], sets[1], small, back[0], back[1] = lax.optimization_barrier((sets[0], sets[1], small, back[0], back[1]))
-    back = [in_order(flat[i][0], back[i], flat[i][1](back[i])) for i in range(2)]
     first = jnp.stack([sets[0], place.swap_x(sets[0])])
     second = jnp.stack([sets[1], place.swap_y(sets[1])])
+    first, second, back[0], back[1] = lax.optimization_barrier((first, second, *back))
+    sources = [first, place.swap_y(first), second, place.swap_x(second)]
+    back = [in_order(flat[i][0], back[i], flat[i][1](back[i])) for i in range(2)]
     out_half = jnp.stack(back).reshape(rows_out // 2, cols_out)
-    first, second, out_half, mine_y = lax.optimization_barrier((first, second, out_half, mine_y))
-    sources = [first, place.swap_y(first), second, place.swap_x(second)]
-    out_peer = place.swap_c(out_half)
-    mine_c, mine_yc = place.swap_c(mine), place.swap_c(mine_y)
     output = call(output_kernel, shaped((all_rows, width)), after, b0, b1, b2, b3)
-    spots = jnp.stack(
-        [place.narrow, place.narrow ^ 2, place.narrow ^ 1, place.narrow ^ 3]
-    ).astype(jnp.int32)
-    grad_up, grad_down = call(
-        place_experts_kernel,
-        (shaped((width, 4 * local), FULL_TYPE), shaped((4 * local, width), FULL_TYPE)),
-        spots, mine, mine_y, mine_c, mine_yc,
-        grid=(4,), prefetch=1,
-        in_specs=[full((2, width, local))] * 4,
-        out_specs=(
-            pl.BlockSpec((width, local), lambda s, spots: (0, spots[s])),
-            pl.BlockSpec((local, width), lambda s, spots: (spots[s], 0)),
-        ),
-    )
-    half_spec = lambda mine: pl.BlockSpec((head_dim, cols_out), lambda s, spot: (jnp.where((s < 2) == mine, s % 2, 1), 0))
-    grad_out = call(
-        place_out_kernel,
-        shaped((heads, head_dim, cols_out), FULL_TYPE),
-        place.c.reshape(1).astype(jnp.int32), out_half, out_peer,
-        grid=(4,), prefetch=1,
-        in_specs=[half_spec(True), half_spec(False)],
-        out_specs=pl.BlockSpec((1, head_dim, cols_out), lambda s, spot: (2 * (spot[0] ^ (s // 2)) + s % 2, 0, 0)),
-    )
     small = small.reshape(width, LANES)
     grad_select, grad_sel_value, grad_sel_out, rows_four = call(
         place_small_kernel,
@@ -1458,14 +1460,26 @@
         in_specs=[smem, vmem],
     )
     peers = [place.swap_c(first), None, place.swap_c(second), None]
-    (sources[1], sources[3], peers[0], peers[2], output, grad_up, grad_down, grad_out, grad_select, grad_sel_value,
+    (sources[1], sources[3], peers[0], peers[2], output, out_half, mine_far, grad_select, grad_sel_value,
      grad_sel_out, rows_four) = lax.optimization_barrier(
-        (sources[1], sources[3], peers[0], peers[2], output, grad_up, grad_down, grad_out, grad_select, grad_sel_value,
+        (sources[1], sources[3], peers[0], peers[2], output, out_half, mine_far, grad_select, grad_sel_value,
          grad_sel_out, rows_four)
     )
+    mine = add(mine, mine_far)
+    mine_y = place.swap_y(mine)
     peers[1], peers[3] = place.swap_c(sources[1]), place.swap_c(sources[3])
+    out_peer = place.swap_c(out_half)
     grad_heads = place_heads(place, sources, 0, heads, width, None)
-    grad_query, grad_key, grad_value = place_heads(place, peers, 1, heads, width, grad_heads)
+    grad_out = place_out(place, out_half, 0, heads, None)
+    grad_heads = lax.optimization_barrier((*grad_heads, grad_out, *peers, out_peer, mine_y))
+    grad_heads, grad_out, peers, out_peer, mine_y = (
+        grad_heads[:3], grad_heads[3], grad_heads[4:8], grad_heads[8], grad_heads[9]
+    )
+    mine_c, mine_yc = place.swap_c(mine), place.swap_c(mine_y)
+    grad_experts = place_experts(place, mine, mine_y, 0, None)
+    grad_query, grad_key, grad_value = place_heads(place, list(peers), 1, heads, width, grad_heads)
+    grad_out = place_out(place, out_peer, 1, heads, (grad_out,))
+    grad_up, grad_down = place_experts(place, mine_c, mine_yc, 1, grad_experts)
     grad_select, grad_sel_value, grad_sel_out = grad_select.T, grad_sel_value.T, grad_sel_out.T
     grad_gain_two, grad_bias_two, grad_gain_one, grad_bias_one = (rows_four[i] for i in range(4))
     return (

time: 660 us -> 627 us (0.950)
  waiting for transfers between devices: 260 us -> 228 us
    ppermute x59 -> x60, waiting for transfers between devices: 242 us -> 166 us  [send(): return lax.ppermute(value, ('wide', 'narrow'), self.pairs(move))]
    all_to_all x1, waiting for transfers between devices: 0.01 us -> 23.2 us  [tuned_device(): lax.all_to_all(jnp.broadcast_to(small[None], (32,) + small.shape), everyw...]
    all_to_all x1, waiting for transfers between devices: 17.2 us -> 39.1 us  [tuned_device(): mixed = lax.all_to_all(mixed, 'wide', 0, 0, tiled=True)]
    ppermute x59 -> x60, starting transfers between devices: 56.6 us -> 59.5 us  [send(): return lax.ppermute(value, ('wide', 'narrow'), self.pairs(move))]
    pallas_call x22 -> x24, Pallas kernels: 250 us -> 253 us  [call(): pl.pallas_call(kernel, out_shape=out_shape, input_output_aliases=aliases...]
  transfers between devices with their start and end apart: 65 -> 66, of which waited for: 20 -> 24; matrix products, arithmetic and copies ran while one was open for 5% -> 5% of each run, Pallas kernels for 34% -> 37%
where the time goes in v3:
time: 627 us; the launch traced here: 618 us
  Pallas kernels  253 us (40%)
  waiting for transfers between devices  228 us (36%)
  starting transfers between devices  84.9 us (14%)
  other arithmetic  25.7 us (4%)
  local copies, waits for them, and re-layouts  23.6 us (4%)
    pallas_call x24, Pallas kernels, call(): pl.pallas_call(kernel, out_shape=out_shape, input_output_aliases=aliases...  253 us
    ppermute x60, waiting for transfers between devices, send(): return lax.ppermute(value, ('wide', 'narrow'), self.pairs(move))  166 us
    ppermute x60, starting transfers between devices, send(): return lax.ppermute(value, ('wide', 'narrow'), self.pairs(move))  59.5 us
    all_to_all x1, waiting for transfers between devices, tuned_device(): mixed = lax.all_to_all(mixed, 'wide', 0, 0, tiled=True)  39.1 us
    all_to_all x1, waiting for transfers between devices, tuned_device(): lax.all_to_all(jnp.broadcast_to(small[None], (32,) + small.shape), everyw...  23.2 us
    convert_element_type x11, other arithmetic, add(): return total.astype(HALF_TYPE)  14.8 us
  transfers between devices with their start and end apart: 66, of which 24 were waited for; matrix products, arithmetic and copies ran while one was open for 5% of the time, Pallas kernels for 37%

profile of v3, /device:TPU:0, one launch (start us, length us, event | category | flops | bytes accessed | tf_op | source)
XLA Modules:
  0.0 617.5 jit_solution(12815323437325371501)
XLA Ops:
  8.6 10.9 %shard_map.316 = (bf16[8,848,128]{2,1,0:T(8,128)(2,1)}, bf16[2,256,2560]{2,1,0:T(8,128)(2,1)}, f32[2,256,128]{2,1,0:T(8,128)}) custom-call(bf16[2,256,1024]{2,1,0:T(8,128)(2,1)} %tok.5, f32[1,1024]{1,0:T(1,128)} %bitcast.208, f32[1,1024]{1,0:T(1,128)} %bitcast.211, bf16[1024,512]{1,0:T(8,128)(2,1)} %wq.3, bf16[1024,512]{1,0:T(8,128)(2,1)} %wk.3, ...), custom_call_target="tpu_custom_call" | custom-call | flops 3892314112 | bytes 13590528 | tf_op jit(solution)/shard_map/pallas_call | solution.py:467
  19.5 7.4 %all-to-all-start = ((bf16[8,848,128]{2,1,0:T(8,128)(2,1)}), bf16[8,848,128]{2,1,0:T(8,128)(2,1)S(1)}, u32[]{:S(2)}, u32[]{:S(2)}) async-start(bf16[8,848,128]{2,1,0:T(8,128)(2,1)} %get-tuple-element.151), calls=%async_computation | async-start | bytes 3473408 | tf_op jit(solution)/shard_map/all_to_all | solution.py:1209
  35.3 16.5 %collective-permute-done.refs_1_.refs_6_ = bf16[512,1024]{1,0:T(8,128)(2,1)} collective-permute-done((bf16[512,1024]{1,0:T(8,128)(2,1)}, bf16[512,1024]{1,0:T(8,128)(2,1)}, u32[]{:S(2)}, u32[]{:S(2)}) %collective-permute-start) | collective-permute-done | bytes 1048608 | tf_op jit(solution)/shard_map/ppermute | solution.py:1001
  51.8 18.6 %collective-permute-done.1 = bf16[2,256,1024]{2,1,0:T(8,128)(2,1)} collective-permute-done((bf16[2,256,1024]{2,1,0:T(8,128)(2,1)S(1)}, bf16[2,256,1024]{2,1,0:T(8,128)(2,1)}, u32[]{:S(2)}, u32[]{:S(2)}) %collective-permute-start.1) | collective-permute-done | bytes 1048608 | tf_op jit(solution)/shard_map/ppermute | solution.py:1001
  77.2 9.6 %shard_map.318 = (bf16[8,256,128]{2,1,0:T(8,128)(2,1)}, f32[128,2048]{1,0:T(8,128)}, f32[1,2048]{1,0:T(1,128)}) custom-call(s32[1]{0:T(128)} %dynamic_slice.105.length, bf16[8,848,128]{2,1,0:T(8,128)(2,1)} %copy-done.13), custom_call_target="tpu_custom_call" | custom-call | flops 1073741824 | bytes 3317764 | tf_op jit(solution)/shard_map/pallas_call | solution.py:467
  90.8 39.1 %all-to-all-done.1.mixed = bf16[8,256,128]{2,1,0:T(8,128)(2,1)S(1)} async-done(((bf16[8,256,128]{2,1,0:T(8,128)(2,1)}), bf16[8,256,128]{2,1,0:T(8,128)(2,1)S(1)}, u32[]{:S(2)}, u32[]{:S(2)}) %all-to-all-start.1) | async-done | bytes 524320 | tf_op jit(solution)/shard_map/all_to_all | solution.py:1225
  131.6 8.8 %shard_map.319 = (f32[512,1024]{1,0:T(8,128)}, f32[64,512]{1,0:T(8,128)}, bf16[2,272,1024]{2,1,0:T(8,128)(2,1)}, bf16[64,1024]{1,0:T(8,128)(2,1)}) custom-call(bf16[8,256,128]{2,1,0:T(8,128)(2,1)} %copy-done.8, f32[2,256,128]{2,1,0:T(8,128)} %get-tuple-element.158.gate, bf16[4,128,5120]{2,1,0:T(8,128)(2,1)} %w_out.3, bf16[2,256,1024]{2,1,0:T(8,128)(2,1)} %tok.5, ...), custom_call_target="tpu_custom_call" | custom-call | flops 2684354560 | bytes 12337152 | tf_op jit(solution)/shard_map/pallas_call | solution.py:467
  143.0 12.4 %collective-permute-done.12.refs_8_.refs_9_.refs_10_ = bf16[2,1024,256]{2,1,0:T(8,128)(2,1)} collective-permute-done((bf16[2,1024,256]{2,1,0:T(8,128)(2,1)}, bf16[2,1024,256]{2,1,0:T(8,128)(2,1)}, u32[]{:S(2)}, u32[]{:S(2)}) %collective-permute-start.12) | collective-permute-done | bytes 1048608 | tf_op jit(solution)/shard_map/ppermute | solution.py:1001
  156.9 10.3 %collective-permute-done.6.refs_0_.refs_1_ = bf16[2,272,1024]{2,1,0:T(8,128)(2,1)S(1)} collective-permute-done((bf16[2,272,1024]{2,1,0:T(8,128)(2,1)}, bf16[2,272,1024]{2,1,0:T(8,128)(2,1)S(1)}, u32[]{:S(2)}, u32[]{:S(2)}) %collective-permute-start.6) | collective-permute-done | bytes 1114144 | tf_op jit(solution)/shard_map/ppermute | solution.py:1001
  173.5 14.2 %shard_map.320 = (bf16[2,272,1024]{2,1,0:T(8,128)(2,1)}, bf16[8,512,256]{2,1,0:T(8,128)(2,1)}, bf16[8,512,256]{2,1,0:T(8,128)(2,1)}) custom-call(bf16[2,272,1024]{2,1,0:T(8,128)(2,1)} %copy-done.23, bf16[512,1024]{1,0:T(8,128)(2,1)} %collective-permute-done.refs_1_.refs_6_, bf16[2,1024,256]{2,1,0:T(8,128)(2,1)} %get-tuple-element.155.refs_2_.refs_3_.refs_4_, ...), custom_call_target="tpu_custom_call" | custom-call | flops 8589934592 | bytes 15859712 | tf_op jit(solution)/shard_map/pallas_call | solution.py:467
  187.7 22.9 %shard_map.321 = (bf16[2,272,1024]{2,1,0:T(8,128)(2,1)}, bf16[8,512,256]{2,1,0:T(8,128)(2,1)}, bf16[8,512,256]{2,1,0:T(8,128)(2,1)}) custom-call(bf16[2,272,1024]{2,1,0:T(8,128)(2,1)} %collective-permute-done.8.refs_0_.refs_2_, bf16[512,1024]{1,0:T(8,128)(2,1)} %collective-permute-done.4.refs_1_.refs_7_, ...), custom_call_target="tpu_custom_call" | custom-call | flops 8589934592 | bytes 15859712 | tf_op jit(solution)/shard_map/pallas_call | solution.py:467
  212.3 14.2 %shard_map.322 = (bf16[2,272,1024]{2,1,0:T(8,128)(2,1)}, bf16[8,512,256]{2,1,0:T(8,128)(2,1)}, bf16[8,512,256]{2,1,0:T(8,128)(2,1)}) custom-call(bf16[272,1024]{1,0:T(8,128)(2,1)} %copy-done.27, bf16[272,1024]{1,0:T(8,128)(2,1)} %copy-done.28, bf16[512,1024]{1,0:T(8,128)(2,1)} %collective-permute-done.5.refs_2_.refs_8_, ...), custom_call_target="tpu_custom_call" | custom-call | flops 8589934592 | bytes 15859712 | tf_op jit(solution)/shard_map/pallas_call | solution.py:467
  232.9 14.6 %shard_map.323 = (bf16[2,272,1024]{2,1,0:T(8,128)(2,1)}, bf16[8,512,256]{2,1,0:T(8,128)(2,1)}, bf16[8,512,256]{2,1,0:T(8,128)(2,1)}) custom-call(bf16[2,272,1024]{2,1,0:T(8,128)(2,1)} %get-tuple-element.159.refs_0_, bf16[512,1024]{1,0:T(8,128)(2,1)} %bitcast.199, bf16[2,1024,256]{2,1,0:T(8,128)(2,1)} %get-tuple-element.155.refs_2_.refs_3_.refs_4_, ...), custom_call_target="tpu_custom_call" | custom-call | flops 8589934592 | bytes 15859712 | tf_op jit(solution)/shard_map/pallas_call | solution.py:467
  247.6 28.0 %shard_map.324 = (bf16[2,2,1024,256]{3,2,1,0:T(8,128)(2,1)}, bf16[2,2,1024,256]{3,2,1,0:T(8,128)(2,1)}, bf16[2,2,1024,256]{3,2,1,0:T(8,128)(2,1)}, bf16[2,2,1024,256]{3,2,1,0:T(8,128)(2,1)}) custom-call(bf16[2,272,1024]{2,1,0:T(8,128)(2,1)} %get-tuple-element.159.refs_0_, bf16[2,272,1024]{2,1,0:T(8,128)(2,1)} %copy-done.23, ...), custom_call_target="tpu_custom_call" | custom-call | flops 17179869184 | bytes 33816576 | tf_op jit(solution)/shard_map/pallas_call | solution.py:467
  279.9 16.9 %shard_map.325 = (f32[512,1024]{1,0:T(8,128)}, bf16[8,256,128]{2,1,0:T(8,128)(2,1)}, f32[2,256,128]{2,1,0:T(8,128)}, f32[1024,128]{1,0:T(8,128)}) custom-call(s32[4]{0:T(128)} %pad_add_fusion.length, bf16[2,272,1024]{2,1,0:T(8,128)(2,1)} %get-tuple-element.172.r0, bf16[2,272,1024]{2,1,0:T(8,128)(2,1)} %copy-done.14, bf16[2,272,1024]{2,1,0:T(8,128)(2,1)} %copy-done.15, ...), custom_call_target="tpu_custom_call" | custom-call | flops 2684354560 | bytes 17317904 | tf_op jit(solution)/shard_map/pallas_call | solution.py:467
  296.9 8.1 %shard_map.327 = bf16[512,5120]{1,0:T(8,128)(2,1)} custom-call(bf16[8,256,128]{2,1,0:T(8,128)(2,1)} %copy-done.8, f32[2,256,128]{2,1,0:T(8,128)} %get-tuple-element.158.gate, f32[512,1024]{1,0:T(8,128)} %get-tuple-element.202.d_after), custom_call_target="tpu_custom_call" | custom-call | flops 2684354560 | bytes 8126464 | tf_op jit(solution)/shard_map/pallas_call | solution.py:467
  316.8 9.6 %shard_map.326 = (bf16[8,1024,256]{2,1,0:T(8,128)(2,1)}, bf16[8,1024,256]{2,1,0:T(8,128)(2,1)}) custom-call(bf16[4,256,1024]{2,1,0:T(8,128)(2,1)} %copy-done.3, bf16[4,256,1024]{2,1,0:T(8,128)(2,1)} %copy-done.11, f32[1,1024]{1,0:T(1,128)} %bitcast.209, f32[1,1024]{1,0:T(1,128)} %bitcast.212), custom_call_target="tpu_custom_call" | custom-call | bytes 12591104 | tf_op jit(solution)/shard_map/pallas_call | solution.py:467
  333.3 11.4 %shard_map.328.d_qkv = bf16[8,768,128]{2,1,0:T(8,128)(2,1)} custom-call(s32[1]{0:T(128)} %dynamic_slice.105.length, bf16[8,848,128]{2,1,0:T(8,128)(2,1)} %copy-done.13, bf16[8,256,128]{2,1,0:T(8,128)(2,1)} %copy-done.22, f32[128,2048]{1,0:T(8,128)} %get-tuple-element.206.out_t, f32[1,2048]{1,0:T(1,128)} %get-tuple-element.207.lse, ...), custom_call_target="tpu_custom_call" | custom-call | flops 2684354560 | bytes 6987780 | tf_op jit(solution)/shard_map/pallas_call | solution.py:467
  357.2 13.0 %shard_map.329 = bf16[1024,896]{1,0:T(8,128)(2,1)} custom-call(s32[1]{0:T(128)} %bitcast.spot, bf16[8,1024,256]{2,1,0:T(8,128)(2,1)} %get-tuple-element.203.tok_t, bf16[8,1024,256]{2,1,0:T(8,128)(2,1)} %get-tuple-element.204.norm_t, bf16[8,768,128]{2,1,0:T(8,128)(2,1)} %shard_map.328.d_qkv, bf16[8,848,128]{2,1,0:T(8,128)(2,1)} %copy-done.13), custom_call_target="tpu_custom_call" | custom-call | flops 3758096384 | bytes 13533188 | tf_op jit(solution)/shard_map/pallas_call | solution.py:467
  371.6 8.8 %collective-permute-done.27 = bf16[2,1024,256]{2,1,0:T(8,128)(2,1)} collective-permute-done((bf16[2,1024,256]{2,1,0:T(8,128)(2,1)}, bf16[2,1024,256]{2,1,0:T(8,128)(2,1)}, u32[]{:S(2)}, u32[]{:S(2)}) %collective-permute-start.27) | collective-permute-done | bytes 1048608 | tf_op jit(solution)/shard_map/ppermute | solution.py:1001
  383.8 16.2 %collective-permute-done.31 = bf16[2,2,8,5120]{3,2,1,0:T(8,128)(2,1)S(1)} collective-permute-done((bf16[2,2,8,5120]{3,2,1,0:T(8,128)(2,1)S(1)}, bf16[2,2,8,5120]{3,2,1,0:T(8,128)(2,1)S(1)}, u32[]{:S(2)}, u32[]{:S(2)}) %collective-permute-start.31) | collective-permute-done | bytes 327712 | tf_op jit(solution)/shard_map/ppermute | solution.py:1001
  403.1 15.6 %shard_map.330 = (bf16[512,1024]{1,0:T(8,128)(2,1)}, bf16[512,1024]{1,0:T(8,128)(2,1)}, bf16[512,1024]{1,0:T(8,128)(2,1)}, bf16[512,1024]{1,0:T(8,128)(2,1)}) custom-call(bf16[8,512,256]{2,1,0:T(8,128)(2,1)} %get-tuple-element.215.refs_13_.refs_0_, bf16[8,512,256]{2,1,0:T(8,128)(2,1)} %get-tuple-element.166.refs_14_.refs_1_, ...), custom_call_target="tpu_custom_call" | custom-call | flops 8589934592 | bytes 20971520 | tf_op jit(solution)/shard_map/pallas_call | solution.py:467
  425.6 11.9 %shard_map.331 = (bf16[512,1024]{1,0:T(8,128)(2,1)}, bf16[1024,128]{1,0:T(8,128)(2,1)}) custom-call(bf16[8,768,128]{2,1,0:T(8,128)(2,1)} %copy-done.4, bf16[2,256,1024]{2,1,0:T(8,128)(2,1)} %tok.5, f32[1,1024]{1,0:T(1,128)} %bitcast.210, f32[1,1024]{1,0:T(1,128)} %bitcast.213, bf16[1024,512]{1,0:T(8,128)(2,1)} %wq.3, bf16[1024,512]{1,0:T(8,128)(2,1)} %wk.3, ...), custom_call_target="tpu_custom_call" | custom-call | flops 3892314112 | bytes 17309696 | tf_op jit(solution)/shard_map/pallas_call | solution.py:467
  444.4 15.1 %collective-permute-done.36 = bf16[2,8,5120]{2,1,0:T(8,128)(2,1)S(1)} collective-permute-done((bf16[2,8,5120]{2,1,0:T(8,128)(2,1)S(1)}, bf16[2,8,5120]{2,1,0:T(8,128)(2,1)S(1)}, u32[]{:S(2)}, u32[]{:S(2)}) %collective-permute-start.36) | collective-permute-done | bytes 163872 | tf_op jit(solution)/shard_map/ppermute | solution.py:1001
  463.3 4.9 collective-permute-done.40
  473.0 12.8 %collective-permute-done.42.b3 = bf16[512,1024]{1,0:T(8,128)(2,1)} collective-permute-done((bf16[512,1024]{1,0:T(8,128)(2,1)}, bf16[512,1024]{1,0:T(8,128)(2,1)}, u32[]{:S(2)}, u32[]{:S(2)}) %collective-permute-start.42) | collective-permute-done | bytes 1048608 | tf_op jit(solution)/shard_map/ppermute | solution.py:1001
  489.9 6.6 %collective-permute-done.46 = bf16[2,2,8,5120]{3,2,1,0:T(8,128)(2,1)S(1)} collective-permute-done((bf16[2,2,8,5120]{3,2,1,0:T(8,128)(2,1)S(1)}, bf16[2,2,8,5120]{3,2,1,0:T(8,128)(2,1)S(1)}, u32[]{:S(2)}, u32[]{:S(2)}) %collective-permute-start.46) | collective-permute-done | bytes 327712 | tf_op jit(solution)/shard_map/ppermute | solution.py:1001
  518.9 23.2 %all-to-all-done.5 = bf16[32,32,128]{2,1,0:T(8,128)(2,1)S(1)} async-done(((bf16[32,32,128]{2,1,0:T(8,128)(2,1)}), bf16[32,32,128]{2,1,0:T(8,128)(2,1)S(1)}, u32[]{:S(2)}, u32[]{:S(2)}) %all-to-all-start.5) | async-done | bytes 262176 | tf_op jit(solution)/shard_map/all_to_all | solution.py:1443
  545.6 15.4 %collective-permute-done.51 = bf16[2,2,2,8,5120]{4,3,2,1,0:T(8,128)(2,1)S(1)} collective-permute-done((bf16[2,2,2,8,5120]{4,3,2,1,0:T(8,128)(2,1)S(1)}, bf16[2,2,2,8,5120]{4,3,2,1,0:T(8,128)(2,1)S(1)}, u32[]{:S(2)}, u32[]{:S(2)}) %collective-permute-start.51) | collective-permute-done | bytes 655392 | tf_op jit(solution)/shard_map/ppermute | solution.py:1001
  573.8 8.3 %shard_map.334 = (f32[1024,512]{1,0:T(8,128)}, f32[1024,512]{1,0:T(8,128)}, f32[1024,2560]{1,0:T(8,128)}) custom-call(s32[5]{0:T(128)} %stack.237.bits, bf16[2,2,2,64,896]{4,3,2,1,0:T(8,128)(2,1)} %pad_maximum_fusion.3.refs_0_, bf16[2,2,2,64,896]{4,3,2,1,0:T(8,128)(2,1)} %collective-permute-done.47.refs_1_, ...), custom_call_target="tpu_custom_call" | custom-call | bytes 18350100 | tf_op jit(solution)/shard_map/pallas_call | solution.py:467
  582.1 11.0 %collective-permute-done.57.mine_y = bf16[2,1024,256]{2,1,0:T(8,128)(2,1)} collective-permute-done((bf16[2,1024,256]{2,1,0:T(8,128)(2,1)}, bf16[2,1024,256]{2,1,0:T(8,128)(2,1)}, u32[]{:S(2)}, u32[]{:S(2)}) %collective-permute-start.57) | collective-permute-done | bytes 1048608 | tf_op jit(solution)/shard_map/ppermute | solution.py:1001
  603.3 8.2 %shard_map.336 = (f32[1024,512]{1,0:T(8,128)}, f32[1024,512]{1,0:T(8,128)}, f32[1024,2560]{1,0:T(8,128)}) custom-call(s32[5]{0:T(128)} %stack.237.bits, bf16[2,2,2,64,896]{4,3,2,1,0:T(8,128)(2,1)} %collective-permute-done.49.refs_0_, ...), custom_call_target="tpu_custom_call", output_to_operand_aliasing={{0}: (5, {}), {1}: (6, {}), {2}: (7, {})} | custom-call | bytes 33030164 | tf_op jit(solution)/shard_map/pallas_call | solution.py:467
  (274 shorter events, 171.1 us)
Async XLA Ops:
  19.5 50.9 %all-to-all-start = ((bf16[8,848,128]{2,1,0:T(8,128)(2,1)}), bf16[8,848,128]{2,1,0:T(8,128)(2,1)S(1)}, u32[]{:S(2)}, u32[]{:S(2)}) async-start(bf16[8,848,128]{2,1,0:T(8,128)(2,1)} %get-tuple-element.151), calls=%async_computation | async-start | bytes 3473408 | tf_op jit(solution)/shard_map/all_to_all | solution.py:1209
  28.4 42.0 %collective-permute-start.1 = (bf16[2,256,1024]{2,1,0:T(8,128)(2,1)S(1)}, bf16[2,256,1024]{2,1,0:T(8,128)(2,1)}, u32[]{:S(2)}, u32[]{:S(2)}) collective-permute-start(bf16[2,256,1024]{2,1,0:T(8,128)(2,1)S(1)} %copy-done.5), channel_id=1, source_target_pairs={{0,4},{1,5},{2,6},{3,7},{4,0},{5,1},{6,2},{7,3},{8,12},{9,13},{10,... | collective-permute-start | bytes 3145736 | tf_op jit(solution)/shard_map/ppermute | solution.py:1001
  70.4 59.5 %collective-permute-start.2 = (bf16[2,1024,256]{2,1,0:T(8,128)(2,1)}, bf16[2,1024,256]{2,1,0:T(8,128)(2,1)}, u32[]{:S(2)}, u32[]{:S(2)}) collective-permute-start(bf16[2,1024,256]{2,1,0:T(8,128)(2,1)} %get-tuple-element.155.refs_2_.refs_3_.refs_4_), channel_id=1, source_target_pairs={{0,16},{1,17},{2,18},{3,19},{4,20},{5,21},{6,22},{7,23},{8,24},{9,... | collective-permute-start | bytes 3145736 | tf_op jit(solution)/shard_map/ppermute | solution.py:1001
  72.8 57.2 %collective-permute-start.3 = (bf16[2,1024,256]{2,1,0:T(8,128)(2,1)}, bf16[2,1024,256]{2,1,0:T(8,128)(2,1)S(1)}, u32[]{:S(2)}, u32[]{:S(2)}) collective-permute-start(bf16[2,1024,256]{2,1,0:T(8,128)(2,1)} %get-tuple-element.155.refs_2_.refs_3_.refs_4_), channel_id=1, source_target_pairs={{0,8},{1,9},{2,10},{3,11},{4,12},{5,13},{6,14},{7,15},{8,0},{9,1},... | collective-permute-start | bytes 3145736 | tf_op jit(solution)/shard_map/ppermute | solution.py:1001
  74.2 55.7 %collective-permute-start.4 = (bf16[512,1024]{1,0:T(8,128)(2,1)}, bf16[512,1024]{1,0:T(8,128)(2,1)}, u32[]{:S(2)}, u32[]{:S(2)}) collective-permute-start(bf16[512,1024]{1,0:T(8,128)(2,1)} %bitcast.197), channel_id=1, source_target_pairs={{0,4},{1,5},{2,6},{3,7},{4,0},{5,1},{6,2},{7,3},{8,12},{9,13},{10,... | collective-permute-start | bytes 3145736 | tf_op jit(solution)/shard_map/ppermute | solution.py:1001
  74.5 55.4 %collective-permute-start.5 = (bf16[512,1024]{1,0:T(8,128)(2,1)}, bf16[512,1024]{1,0:T(8,128)(2,1)}, u32[]{:S(2)}, u32[]{:S(2)}) collective-permute-start(bf16[512,1024]{1,0:T(8,128)(2,1)} %bitcast.198), channel_id=1, source_target_pairs={{0,6},{1,7},{2,4},{3,5},{4,2},{5,3},{6,0},{7,1},{8,14},{9,15},{10,... | collective-permute-start | bytes 3145736 | tf_op jit(solution)/shard_map/ppermute | solution.py:1001
  86.8 43.1 %all-to-all-start.1 = ((bf16[8,256,128]{2,1,0:T(8,128)(2,1)}), bf16[8,256,128]{2,1,0:T(8,128)(2,1)S(1)}, u32[]{:S(2)}, u32[]{:S(2)}) async-start(bf16[8,256,128]{2,1,0:T(8,128)(2,1)} %get-tuple-element.154), calls=%async_computation.1 | async-start | bytes 1048576 | tf_op jit(solution)/shard_map/all_to_all | solution.py:1225
  140.4 26.8 %collective-permute-start.6 = (bf16[2,272,1024]{2,1,0:T(8,128)(2,1)}, bf16[2,272,1024]{2,1,0:T(8,128)(2,1)S(1)}, u32[]{:S(2)}, u32[]{:S(2)}) collective-permute-start(bf16[2,272,1024]{2,1,0:T(8,128)(2,1)} %get-tuple-element.159.refs_0_), channel_id=1, source_target_pairs={{0,2},{1,3},{2,0},{3,1},{4,6},{5,7},{6,4},{7,5},{8,10},{9,11},{10,... | collective-permute-start | bytes 3342344 | tf_op jit(solution)/shard_map/ppermute | solution.py:1001
  142.0 26.5 %collective-permute-start.8 = (bf16[2,272,1024]{2,1,0:T(8,128)(2,1)}, bf16[2,272,1024]{2,1,0:T(8,128)(2,1)}, u32[]{:S(2)}, u32[]{:S(2)}) collective-permute-start(bf16[2,272,1024]{2,1,0:T(8,128)(2,1)} %get-tuple-element.159.refs_0_), channel_id=1, source_target_pairs={{0,4},{1,5},{2,6},{3,7},{4,0},{5,1},{6,2},{7,3},{8,12},{9,13},{10,... | collective-permute-start | bytes 3342344 | tf_op jit(solution)/shard_map/ppermute | solution.py:1001
  142.5 29.4 %collective-permute-start.10 = (bf16[2,1024,256]{2,1,0:T(8,128)(2,1)}, bf16[2,1024,256]{2,1,0:T(8,128)(2,1)}, u32[]{:S(2)}, u32[]{:S(2)}) collective-permute-start(bf16[2,1024,256]{2,1,0:T(8,128)(2,1)} %copy-done.26), channel_id=1, source_target_pairs={{0,1},{1,0},{2,3},{3,2},{4,5},{5,4},{6,7},{7,6},{8,9},{9,8},{10,11... | collective-permute-start | bytes 3145736 | tf_op jit(solution)/shard_map/ppermute | solution.py:1001
  142.5 31.0 %collective-permute-start.11 = (bf16[2,1024,256]{2,1,0:T(8,128)(2,1)}, bf16[2,1024,256]{2,1,0:T(8,128)(2,1)}, u32[]{:S(2)}, u32[]{:S(2)}) collective-permute-start(bf16[2,1024,256]{2,1,0:T(8,128)(2,1)} %collective-permute-done.2.refs_6_.refs_7_.refs_8_), channel_id=1, source_target_pairs={{0,1},{1,0},{2,3},{3,2},{4,5},{5,4},{6,7},{7,6},{8,9},{9,8},{10,11... | collective-permute-start | bytes 3145736 | tf_op jit(solution)/shard_map/ppermute | solution.py:1001
  167.2 62.8 %collective-permute-start.17 = (bf16[2,256,1024]{2,1,0:T(8,128)(2,1)S(1)}, bf16[2,256,1024]{2,1,0:T(8,128)(2,1)S(1)}, u32[]{:S(2)}, u32[]{:S(2)}) collective-permute-start(bf16[2,256,1024]{2,1,0:T(8,128)(2,1)S(1)} %pad_maximum_fusion.2), channel_id=1, source_target_pairs={{0,16},{1,17},{2,18},{3,19},{4,20},{5,21},{6,22},{7,23},{8,24},{9,... | collective-permute-start | bytes 3145736 | tf_op jit(solution)/shard_map/ppermute | solution.py:1001
  168.5 42.1 %collective-permute-start.7 = (bf16[272,1024]{1,0:T(8,128)(2,1)S(1)}, bf16[272,1024]{1,0:T(8,128)(2,1)S(1)}, u32[]{:S(2)}, u32[]{:S(2)}) collective-permute-start(bf16[272,1024]{1,0:T(8,128)(2,1)S(1)} %slice_bitcast_fusion.1), channel_id=1, source_target_pairs={{0,4},{1,5},{2,6},{3,7},{4,0},{5,1},{6,2},{7,3},{8,12},{9,13},{10,... | collective-permute-start | bytes 1671176 | tf_op jit(solution)/shard_map/ppermute | solution.py:1001
  171.9 38.7 %collective-permute-start.9 = (bf16[272,1024]{1,0:T(8,128)(2,1)S(1)}, bf16[272,1024]{1,0:T(8,128)(2,1)S(1)}, u32[]{:S(2)}, u32[]{:S(2)}) collective-permute-start(bf16[272,1024]{1,0:T(8,128)(2,1)S(1)} %slice_bitcast_fusion), channel_id=1, source_target_pairs={{0,2},{1,3},{2,0},{3,1},{4,6},{5,7},{6,4},{7,5},{8,10},{9,11},{10,... | collective-permute-start | bytes 1671176 | tf_op jit(solution)/shard_map/ppermute | solution.py:1001
  226.5 49.9 %collective-permute-start.14 = (bf16[2,272,1024]{2,1,0:T(8,128)(2,1)}, bf16[2,272,1024]{2,1,0:T(8,128)(2,1)S(1)}, u32[]{:S(2)}, u32[]{:S(2)}) collective-permute-start(bf16[2,272,1024]{2,1,0:T(8,128)(2,1)} %get-tuple-element.173), channel_id=1, source_target_pairs={{0,2},{1,3},{2,0},{3,1},{4,6},{5,7},{6,4},{7,5},{8,10},{9,11},{10,... | collective-permute-start | bytes 3342344 | tf_op jit(solution)/shard_map/ppermute | solution.py:1001
  227.0 49.4 %collective-permute-start.15 = (bf16[2,272,1024]{2,1,0:T(8,128)(2,1)}, bf16[2,272,1024]{2,1,0:T(8,128)(2,1)S(1)}, u32[]{:S(2)}, u32[]{:S(2)}) collective-permute-start(bf16[2,272,1024]{2,1,0:T(8,128)(2,1)} %get-tuple-element.174), channel_id=1, source_target_pairs={{0,4},{1,5},{2,6},{3,7},{4,0},{5,1},{6,2},{7,3},{8,12},{9,13},{10,... | collective-permute-start | bytes 3342344 | tf_op jit(solution)/shard_map/ppermute | solution.py:1001
  227.0 49.3 %collective-permute-start.16 = (bf16[2,272,1024]{2,1,0:T(8,128)(2,1)}, bf16[2,272,1024]{2,1,0:T(8,128)(2,1)S(1)}, u32[]{:S(2)}, u32[]{:S(2)}) collective-permute-start(bf16[2,272,1024]{2,1,0:T(8,128)(2,1)} %get-tuple-element.175), channel_id=1, source_target_pairs={{0,6},{1,7},{2,4},{3,5},{4,2},{5,3},{6,0},{7,1},{8,14},{9,15},{10,... | collective-permute-start | bytes 3342344 | tf_op jit(solution)/shard_map/ppermute | solution.py:1001
  232.4 44.9 %collective-permute-start.18 = (bf16[4,256,1024]{2,1,0:T(8,128)(2,1)S(1)}, bf16[4,256,1024]{2,1,0:T(8,128)(2,1)S(1)}, u32[]{:S(2)}, u32[]{:S(2)}) collective-permute-start(bf16[4,256,1024]{2,1,0:T(8,128)(2,1)S(1)} %pad_maximum_fusion.1.near), channel_id=1, source_target_pairs={{0,8},{1,9},{2,10},{3,11},{4,12},{5,13},{6,14},{7,15},{8,0},{9,1},... | collective-permute-start | bytes 6291464 | tf_op jit(solution)/shard_map/ppermute | solution.py:1001
  314.7 56.9 %collective-permute-start.26 = (bf16[2,1024,256]{2,1,0:T(8,128)(2,1)}, bf16[2,1024,256]{2,1,0:T(8,128)(2,1)}, u32[]{:S(2)}, u32[]{:S(2)}) collective-permute-start(bf16[2,1024,256]{2,1,0:T(8,128)(2,1)} %get-tuple-element.288), channel_id=1, source_target_pairs={{0,8},{1,9},{2,10},{3,11},{4,12},{5,13},{6,14},{7,15},{8,0},{9,1},... | collective-permute-start | bytes 3145736 | tf_op jit(solution)/shard_map/ppermute | solution.py:1001
  316.7 63.8 %collective-permute-start.27 = (bf16[2,1024,256]{2,1,0:T(8,128)(2,1)}, bf16[2,1024,256]{2,1,0:T(8,128)(2,1)}, u32[]{:S(2)}, u32[]{:S(2)}) collective-permute-start(bf16[2,1024,256]{2,1,0:T(8,128)(2,1)} %get-tuple-element.287), channel_id=1, source_target_pairs={{0,8},{1,9},{2,10},{3,11},{4,12},{5,13},{6,14},{7,15},{8,0},{9,1},... | collective-permute-start | bytes 3145736 | tf_op jit(solution)/shard_map/ppermute | solution.py:1001
  352.4 66.5 %all-to-all-start.3 = ((bf16[8,768,128]{2,1,0:T(8,128)(2,1)}), bf16[8,768,128]{2,1,0:T(8,128)(2,1)S(1)}, u32[]{:S(2)}, u32[]{:S(2)}) async-start(bf16[8,768,128]{2,1,0:T(8,128)(2,1)} %shard_map.328.d_qkv), calls=%async_computation.3 | async-start | bytes 3145728 | tf_op jit(solution)/shard_map/all_to_all | solution.py:1388
  423.6 36.0 %collective-permute-start.37 = (bf16[512,1024]{1,0:T(8,128)(2,1)}, bf16[512,1024]{1,0:T(8,128)(2,1)S(1)}, u32[]{:S(2)}, u32[]{:S(2)}) collective-permute-start(bf16[512,1024]{1,0:T(8,128)(2,1)} %get-tuple-element.229), channel_id=1, source_target_pairs={{0,2},{1,3},{2,0},{3,1},{4,6},{5,7},{6,4},{7,5},{8,10},{9,11},{10,... | collective-permute-start | bytes 3145736 | tf_op jit(solution)/shard_map/ppermute | solution.py:1001
  424.1 35.5 %collective-permute-start.38 = (bf16[512,1024]{1,0:T(8,128)(2,1)}, bf16[512,1024]{1,0:T(8,128)(2,1)}, u32[]{:S(2)}, u32[]{:S(2)}) collective-permute-start(bf16[512,1024]{1,0:T(8,128)(2,1)} %get-tuple-element.230), channel_id=1, source_target_pairs={{0,4},{1,5},{2,6},{3,7},{4,0},{5,1},{6,2},{7,3},{8,12},{9,13},{10,... | collective-permute-start | bytes 3145736 | tf_op jit(solution)/shard_map/ppermute | solution.py:1001
  441.2 31.8 %all-to-all-start.4 = ((bf16[32,32,128]{2,1,0:T(8,128)(2,1)}), bf16[32,32,128]{2,1,0:T(8,128)(2,1)S(1)}, u32[]{:S(2)}, u32[]{:S(2)}) async-start(bf16[32,32,128]{2,1,0:T(8,128)(2,1)} %bitcast.205), calls=%async_computation.4 | async-start | bytes 524288 | tf_op jit(solution)/shard_map/all_to_all | solution.py:1429
  505.2 39.6 %collective-permute-start.52 = (bf16[2,2,2,8,5120]{4,3,2,1,0:T(8,128)(2,1)S(1)}, bf16[2,2,2,8,5120]{4,3,2,1,0:T(8,128)(2,1)S(1)}, u32[]{:S(2)}, u32[]{:S(2)}) collective-permute-start(bf16[2,2,2,8,5120]{4,3,2,1,0:T(8,128)(2,1)S(1)} %pad_maximum_fusion.8), channel_id=1, source_target_pairs={{0,4},{1,5},{2,6},{3,7},{4,0},{5,1},{6,2},{7,3},{8,12},{9,13},{10,... | collective-permute-start | bytes 1966088 | tf_op jit(solution)/shard_map/ppermute | solution.py:1001
  506.3 35.9 %all-to-all-start.5 = ((bf16[32,32,128]{2,1,0:T(8,128)(2,1)}), bf16[32,32,128]{2,1,0:T(8,128)(2,1)S(1)}, u32[]{:S(2)}, u32[]{:S(2)}) async-start(bf16[32,32,128]{2,1,0:T(8,128)(2,1)} %broadcast_in_dim.8), calls=%async_computation.5 | async-start | bytes 524288 | tf_op jit(solution)/shard_map/all_to_all | solution.py:1443
  508.9 54.4 %collective-permute-start.53 = (bf16[2,1024,256]{2,1,0:T(8,128)(2,1)}, bf16[2,1024,256]{2,1,0:T(8,128)(2,1)}, u32[]{:S(2)}, u32[]{:S(2)}) collective-permute-start(bf16[2,1024,256]{2,1,0:T(8,128)(2,1)} %fusion.2), channel_id=1, source_target_pairs={{0,16},{1,17},{2,18},{3,19},{4,20},{5,21},{6,22},{7,23},{8,24},{9,... | collective-permute-start | bytes 3145736 | tf_op jit(solution)/shard_map/ppermute | solution.py:1001
  515.9 47.3 %collective-permute-start.47 = (bf16[2,2,2,64,896]{4,3,2,1,0:T(8,128)(2,1)}, bf16[2,2,2,64,896]{4,3,2,1,0:T(8,128)(2,1)}, u32[]{:S(2)}, u32[]{:S(2)}) collective-permute-start(bf16[2,2,2,64,896]{4,3,2,1,0:T(8,128)(2,1)} %pad_maximum_fusion.3.refs_0_), channel_id=1, source_target_pairs={{0,2},{1,3},{2,0},{3,1},{4,6},{5,7},{6,4},{7,5},{8,10},{9,11},{10,... | collective-permute-start | bytes 2752520 | tf_op jit(solution)/shard_map/ppermute | solution.py:1001
  517.4 45.9 %collective-permute-start.49 = (bf16[2,2,2,64,896]{4,3,2,1,0:T(8,128)(2,1)}, bf16[2,2,2,64,896]{4,3,2,1,0:T(8,128)(2,1)}, u32[]{:S(2)}, u32[]{:S(2)}) collective-permute-start(bf16[2,2,2,64,896]{4,3,2,1,0:T(8,128)(2,1)} %pad_maximum_fusion.3.refs_0_), channel_id=1, source_target_pairs={{0,1},{1,0},{2,3},{3,2},{4,5},{5,4},{6,7},{7,6},{8,9},{9,8},{10,11... | collective-permute-start | bytes 2752520 | tf_op jit(solution)/shard_map/ppermute | solution.py:1001
  517.4 45.8 %collective-permute-start.48 = (bf16[2,2,2,64,896]{4,3,2,1,0:T(8,128)(2,1)}, bf16[2,2,2,64,896]{4,3,2,1,0:T(8,128)(2,1)}, u32[]{:S(2)}, u32[]{:S(2)}) collective-permute-start(bf16[2,2,2,64,896]{4,3,2,1,0:T(8,128)(2,1)} %pad_maximum_fusion.4.refs_2_), channel_id=1, source_target_pairs={{0,4},{1,5},{2,6},{3,7},{4,0},{5,1},{6,2},{7,3},{8,12},{9,13},{10,... | collective-permute-start | bytes 2752520 | tf_op jit(solution)/shard_map/ppermute | solution.py:1001
  563.7 29.4 %collective-permute-start.56 = (bf16[256,5120]{1,0:T(8,128)(2,1)S(1)}, bf16[256,5120]{1,0:T(8,128)(2,1)}, u32[]{:S(2)}, u32[]{:S(2)}) collective-permute-start(bf16[256,5120]{1,0:T(8,128)(2,1)S(1)} %bitcast.188), channel_id=1, source_target_pairs={{0,1},{1,0},{2,3},{3,2},{4,5},{5,4},{6,7},{7,6},{8,9},{9,8},{10,11... | collective-permute-start | bytes 7864328 | tf_op jit(solution)/shard_map/ppermute | solution.py:1001
  573.8 37.7 %collective-permute-start.58 = (bf16[2,1024,256]{2,1,0:T(8,128)(2,1)}, bf16[2,1024,256]{2,1,0:T(8,128)(2,1)}, u32[]{:S(2)}, u32[]{:S(2)}) collective-permute-start(bf16[2,1024,256]{2,1,0:T(8,128)(2,1)} %add_convert_fusion.mine), channel_id=1, source_target_pairs={{0,1},{1,0},{2,3},{3,2},{4,5},{5,4},{6,7},{7,6},{8,9},{9,8},{10,11... | collective-permute-start | bytes 3145736 | tf_op jit(solution)/shard_map/ppermute | solution.py:1001
  (63 other events, 905.9 us)

commit v4 on v3

--- a/solution.py
+++ b/solution.py
@@ -971,10 +971,9 @@
             down[...] = jnp.transpose(ref[1].astype(FULL_TYPE))
 
 
-def output_kernel(after, b0, b1, b2, b3, out):
+def output_kernel(after, own, first, last, out):
     out[...] = (
-        after[...] + b0[...].astype(FULL_TYPE) + b1[...].astype(FULL_TYPE)
-        + b2[...].astype(FULL_TYPE) + b3[...].astype(FULL_TYPE)
+        after[...] + own[...].astype(FULL_TYPE) + first[...].astype(FULL_TYPE) + last[...].astype(FULL_TYPE)
     ).astype(HALF_TYPE)
 
 
@@ -1329,7 +1328,6 @@
 
     to_low = [add(grad_far[a], came_far[a]) for a in range(2)]
     passed = [None, place.swap_low(to_low[1])]
-    passed[0] = place.swap_low(to_low[0])
     near_four = tie(near_four, d_att, *to_low)
     tok_t, norm_t = call(
         turn_kernel,
@@ -1347,15 +1345,14 @@
         ),
     )
     grad_out = call(
-        out_grad_kernel, shaped((heads * head_dim, experts * width)), tie(mixed, d_att, came_near, came_far), gate, d_after,
+        out_grad_kernel, shaped((heads * head_dim, experts * width)), tie(mixed, d_att, tok_t), gate, d_after,
         flops=2 * all_rows * width * wide_out,
     )
     rows_out, cols_out = grad_out.shape
     flat = ((place.y, place.swap_y), (place.x, place.swap_x))
+    d_att_all, tok_t, grad_out = lax.optimization_barrier((d_att_all, tok_t, grad_out))
     out_parts = halve(place.c, place.swap_c, grad_out.reshape(2, 2, 2, 2, 2, 2, rows_out // 64, cols_out))
 
-    d_att_all, tok_t, out_parts = lax.optimization_barrier((d_att_all, tok_t, out_parts))
-    out_parts = [halve(*flat[i], out_parts[i]) for i in range(2)]
     d_qkv = call(
         attend_back_kernel,
         shaped((8, 3 * row_count, head_dim)),
@@ -1365,8 +1362,8 @@
         flops=5 * span * span * head_dim,
     )
 
-    d_qkv, out_parts[0], out_parts[1] = lax.optimization_barrier((d_qkv, *out_parts))
-    out_parts = [halve(*flat[1 - i], out_parts[i]) for i in range(2)]
+    d_qkv, out_parts = lax.optimization_barrier((d_qkv, out_parts))
+    out_parts = [halve(*flat[i], out_parts[i]) for i in range(2)]
 
     block_of = lambda i, spot: spot[0] ^ ((i & 1) | ((i & 2) << 1) | ((i & 4) >> 1))
     head_cols = (2 + experts) * LANES
@@ -1388,22 +1385,21 @@
     d_qkv_rows = lax.all_to_all(d_qkv, "wide", 0, 0, tiled=True)
     bits = ((place.y, place.swap_y), (place.high, place.swap_high))
     rows_head = width // 16
-    head_grads, out_sum, passed[0], passed[1] = lax.optimization_barrier((head_grads, jnp.stack(out_parts, axis=2), *passed))
+    head_grads, out_parts[0], out_parts[1] = lax.optimization_barrier((head_grads, *out_parts))
+    out_parts = [halve(*flat[1 - i], out_parts[i]) for i in range(2)]
     kept = halve(place.c, place.swap_c, head_grads.reshape(2, 2, 2, 2, rows_head, head_cols))
-    out_sum = halve(place.low, place.swap_low, out_sum)
-    kept = tie(kept, d_qkv)
     branches = call(
         branch_kernel,
         (shaped((all_rows, width)),) * 4,
-        tie(inners[0], kept), *inners[1:], *weights,
+        tie(inners[0], head_grads), *inners[1:], *weights,
         flops=8 * all_rows * width * hidden,
     )
     b0, b1, b2, b3 = branches
+    kept, out_sum, b1, b2, b3 = lax.optimization_barrier((kept, jnp.stack(out_parts, axis=2), b1, b2, b3))
+    b3 = place.swap_x(b3)
+    out_sum = halve(place.low, place.swap_low, out_sum)
     value = [halve(*bits[i], kept[i]) for i in range(2)]
-    value[0], value[1], d_qkv_rows, out_sum, b1, b2, b3 = lax.optimization_barrier(
-        (value[0], value[1], d_qkv_rows, out_sum, b1, b2, b3)
-    )
-    b1, b2 = place.swap_y(b1), place.swap_x(b2)
+    value[0], value[1], d_qkv_rows, out_sum = lax.optimization_barrier((value[0], value[1], d_qkv_rows, out_sum))
     value = [halve(*bits[1 - i], value[i]) for i in range(2)]
     out_sum = halve(place.high, place.swap_high, out_sum)
     grad_tokens, small = call(
@@ -1421,22 +1417,23 @@
         scratch=[pltpu.VMEM((row_count, wide_out), HALF_TYPE), pltpu.VMEM((width, LANES), FULL_TYPE)],
         flops=2 * all_rows * width * 3712,
     )
-    done, small, out_sum = lax.optimization_barrier((jnp.stack(value), small, out_sum))
-    mine = add(grad_near[0], came_near[0], passed[0])
+    done, small, out_sum, b3 = lax.optimization_barrier((jnp.stack(value), small, out_sum, b3))
+    b1 = place.swap_y(add(b1, b3))
+    b2 = place.swap_x(tie(b2, b3))
     far = place.swap_high(done)
     out_sum = in_order(place.high, out_sum, place.swap_high(out_sum))
     everywhere = ("wide", "narrow")
     small = lax.all_to_all(small, everywhere, 0, 0, tiled=True).reshape(32, -1, LANES)
-    far, out_sum, b1, b2, b3 = lax.optimization_barrier((far, out_sum, b1, b2, b3))
-    b3 = place.swap_xy(b3)
+    far, out_sum = lax.optimization_barrier((far, out_sum))
     out_sum = in_order(place.low, out_sum, place.swap_low(out_sum))
     near = [place.swap_low(done), place.swap_low(far)]
     sets = [
         jnp.stack([jnp.stack([done[i], far[i]]), jnp.stack([near[0][i], near[1][i]])]) for i in range(2)
     ]
-    to_high = add(grad_near[1], came_near[1], passed[1])
-    sets[0], sets[1], small, out_sum, b3, to_high = lax.optimization_barrier(
-        (sets[0], sets[1], small, out_sum, b3, to_high)
+    passed[0] = place.swap_low(tie(to_low[0], near[1]))
+    to_high = add(grad_near[1], came_near[1], tie(passed[1], done))
+    sets[0], sets[1], small, out_sum, b1, b2, to_high = lax.optimization_barrier(
+        (sets[0], sets[1], small, out_sum, b1, b2, to_high)
     )
     mine_far = place.swap_high(to_high)
     small = jnp.sum(small.astype(FULL_TYPE), axis=0).astype(HALF_TYPE)
@@ -1448,7 +1445,19 @@
     sources = [first, place.swap_y(first), second, place.swap_x(second)]
     back = [in_order(flat[i][0], back[i], flat[i][1](back[i])) for i in range(2)]
     out_half = jnp.stack(back).reshape(rows_out // 2, cols_out)
-    output = call(output_kernel, shaped((all_rows, width)), after, b0, b1, b2, b3)
+    output = call(output_kernel, shaped((all_rows, width)), after, b0, b2, b1)
+    sources[1], sources[3], output, out_half, mine_far, small, passed[0] = lax.optimization_barrier(
+        (sources[1], sources[3], output, out_half, mine_far, small, passed[0])
+    )
+    mine = add(grad_near[0], came_near[0], passed[0], mine_far)
+    mine_y = place.swap_y(mine)
+    peers = [place.swap_c(first), None, place.swap_c(second), None]
+    peers[1], peers[3] = place.swap_c(sources[1]), place.swap_c(sources[3])
+    out_peer = place.swap_c(out_half)
+    grad_heads = place_heads(place, sources, 0, heads, width, None)
+    grad_out = place_out(place, out_half, 0, heads, None)
+    grad_heads = lax.optimization_barrier((*grad_heads, grad_out, *peers, out_peer))
+    grad_heads, grad_out, peers, out_peer = grad_heads[:3], grad_heads[3], grad_heads[4:8], grad_heads[8]
     small = small.reshape(width, LANES)
     grad_select, grad_sel_value, grad_sel_out, rows_four = call(
         place_small_kernel,
@@ -1459,26 +1468,11 @@
         (place.wide * own_count).reshape(1).astype(jnp.int32), small,
         in_specs=[smem, vmem],
     )
-    peers = [place.swap_c(first), None, place.swap_c(second), None]
-    (sources[1], sources[3], peers[0], peers[2], output, out_half, mine_far, grad_select, grad_sel_value,
-     grad_sel_out, rows_four) = lax.optimization_barrier(
-        (sources[1], sources[3], peers[0], peers[2], output, out_half, mine_far, grad_select, grad_sel_value,
-         grad_sel_out, rows_four)
-    )
-    mine = add(mine, mine_far)
-    mine_y = place.swap_y(mine)
-    peers[1], peers[3] = place.swap_c(sources[1]), place.swap_c(sources[3])
-    out_peer = place.swap_c(out_half)
-    grad_heads = place_heads(place, sources, 0, heads, width, None)
-    grad_out = place_out(place, out_half, 0, heads, None)
-    grad_heads = lax.optimization_barrier((*grad_heads, grad_out, *peers, out_peer, mine_y))
-    grad_heads, grad_out, peers, out_peer, mine_y = (
-        grad_heads[:3], grad_heads[3], grad_heads[4:8], grad_heads[8], grad_heads[9]
-    )
+    grad_query, grad_key, grad_value = place_heads(place, list(peers), 1, heads, width, grad_heads)
+    grad_out = place_out(place, out_peer, 1, heads, (grad_out,))
+    mine, mine_y, grad_query, grad_out, rows_four = lax.optimization_barrier((mine, mine_y, grad_query, grad_out, rows_four))
     mine_c, mine_yc = place.swap_c(mine), place.swap_c(mine_y)
     grad_experts = place_experts(place, mine, mine_y, 0, None)
-    grad_query, grad_key, grad_value = place_heads(place, list(peers), 1, heads, width, grad_heads)
-    grad_out = place_out(place, out_peer, 1, heads, (grad_out,))
     grad_up, grad_down = place_experts(place, mine_c, mine_yc, 1, grad_experts)
     grad_select, grad_sel_value, grad_sel_out = grad_select.T, grad_sel_value.T, grad_sel_out.T
     grad_gain_two, grad_bias_two, grad_gain_one, grad_bias_one = (rows_four[i] for i in range(4))

time: 627 us -> 604 us (0.963)
  waiting for transfers between devices: 228 us -> 194 us
    all_to_all x1, waiting for transfers between devices: 23.2 us -> 3.19 us  [tuned_device(): lax.all_to_all(jnp.broadcast_to(small[None], (32,) + small.shape), everyw...]
    ppermute x60, waiting for transfers between devices: 166 us -> 152 us  [send(): return lax.ppermute(value, ('wide', 'narrow'), self.pairs(move))]
    convert_element_type x11 -> x12, other arithmetic: 14.8 us -> 18.3 us  [add(): return total.astype(HALF_TYPE)]
  transfers between devices with their start and end apart: 66 -> 66, of which waited for: 24 -> 22; matrix products, arithmetic and copies ran while one was open for 5% -> 6% of each run, Pallas kernels for 37% -> 40%
where the time goes in v4:
time: 604 us; the launch traced here: 594 us
  Pallas kernels  252 us (42%)
  waiting for transfers between devices  194 us (32%)
  starting transfers between devices  89.7 us (15%)
  other arithmetic  29.1 us (5%)
  local copies, waits for them, and re-layouts  26.9 us (4%)
    pallas_call x24, Pallas kernels, call(): pl.pallas_call(kernel, out_shape=out_shape, input_output_aliases=aliases...  252 us
    ppermute x60, waiting for transfers between devices, send(): return lax.ppermute(value, ('wide', 'narrow'), self.pairs(move))  152 us
    ppermute x60, starting transfers between devices, send(): return lax.ppermute(value, ('wide', 'narrow'), self.pairs(move))  64.5 us
    all_to_all x1, waiting for transfers between devices, tuned_device(): mixed = lax.all_to_all(mixed, 'wide', 0, 0, tiled=True)  39.1 us
    convert_element_type x12, other arithmetic, add(): return total.astype(HALF_TYPE)  18.3 us
  transfers between devices with their start and end apart: 66, of which 22 were waited for; matrix products, arithmetic and copies ran while one was open for 6% of the time, Pallas kernels for 40%

profile of v4, /device:TPU:0, one launch (start us, length us, event | category | flops | bytes accessed | tf_op | source)
XLA Modules:
  0.0 594.2 jit_solution(1054891767117364749)
XLA Ops:
  8.6 10.9 %shard_map.316 = (bf16[8,848,128]{2,1,0:T(8,128)(2,1)}, bf16[2,256,2560]{2,1,0:T(8,128)(2,1)}, f32[2,256,128]{2,1,0:T(8,128)}) custom-call(bf16[2,256,1024]{2,1,0:T(8,128)(2,1)} %tok.5, f32[1,1024]{1,0:T(1,128)} %bitcast.210, f32[1,1024]{1,0:T(1,128)} %bitcast.213, bf16[1024,512]{1,0:T(8,128)(2,1)} %wq.3, bf16[1024,512]{1,0:T(8,128)(2,1)} %wk.3, ...), custom_call_target="tpu_custom_call" | custom-call | flops 3892314112 | bytes 13590528 | tf_op jit(solution)/shard_map/pallas_call | solution.py:467
  19.5 7.4 %all-to-all-start = ((bf16[8,848,128]{2,1,0:T(8,128)(2,1)}), bf16[8,848,128]{2,1,0:T(8,128)(2,1)S(1)}, u32[]{:S(2)}, u32[]{:S(2)}) async-start(bf16[8,848,128]{2,1,0:T(8,128)(2,1)} %get-tuple-element.152), calls=%async_computation | async-start | bytes 3473408 | tf_op jit(solution)/shard_map/all_to_all | solution.py:1208
  35.4 16.4 %collective-permute-done.refs_1_.refs_6_ = bf16[512,1024]{1,0:T(8,128)(2,1)} collective-permute-done((bf16[512,1024]{1,0:T(8,128)(2,1)}, bf16[512,1024]{1,0:T(8,128)(2,1)}, u32[]{:S(2)}, u32[]{:S(2)}) %collective-permute-start) | collective-permute-done | bytes 1048608 | tf_op jit(solution)/shard_map/ppermute | solution.py:1000
  51.8 18.6 %collective-permute-done.1 = bf16[2,256,1024]{2,1,0:T(8,128)(2,1)} collective-permute-done((bf16[2,256,1024]{2,1,0:T(8,128)(2,1)S(1)}, bf16[2,256,1024]{2,1,0:T(8,128)(2,1)}, u32[]{:S(2)}, u32[]{:S(2)}) %collective-permute-start.1) | collective-permute-done | bytes 1048608 | tf_op jit(solution)/shard_map/ppermute | solution.py:1000
  77.2 9.6 %shard_map.318 = (bf16[8,256,128]{2,1,0:T(8,128)(2,1)}, f32[128,2048]{1,0:T(8,128)}, f32[1,2048]{1,0:T(1,128)}) custom-call(s32[1]{0:T(128)} %dynamic_slice.105.length, bf16[8,848,128]{2,1,0:T(8,128)(2,1)} %copy-done.14), custom_call_target="tpu_custom_call" | custom-call | flops 1073741824 | bytes 3317764 | tf_op jit(solution)/shard_map/pallas_call | solution.py:467
  90.9 39.1 %all-to-all-done.1.mixed = bf16[8,256,128]{2,1,0:T(8,128)(2,1)S(1)} async-done(((bf16[8,256,128]{2,1,0:T(8,128)(2,1)}), bf16[8,256,128]{2,1,0:T(8,128)(2,1)S(1)}, u32[]{:S(2)}, u32[]{:S(2)}) %all-to-all-start.1) | async-done | bytes 524320 | tf_op jit(solution)/shard_map/all_to_all | solution.py:1224
  131.6 8.7 %shard_map.319 = (f32[512,1024]{1,0:T(8,128)}, f32[64,512]{1,0:T(8,128)}, bf16[2,272,1024]{2,1,0:T(8,128)(2,1)}, bf16[64,1024]{1,0:T(8,128)(2,1)}) custom-call(bf16[8,256,128]{2,1,0:T(8,128)(2,1)} %copy-done.10, f32[2,256,128]{2,1,0:T(8,128)} %get-tuple-element.159.gate, bf16[4,128,5120]{2,1,0:T(8,128)(2,1)} %w_out.3, bf16[2,256,1024]{2,1,0:T(8,128)(2,1)} %tok.5, ...), custom_call_target="tpu_custom_call" | custom-call | flops 2684354560 | bytes 12337152 | tf_op jit(solution)/shard_map/pallas_call | solution.py:467
  143.0 12.4 %collective-permute-done.12.refs_8_.refs_9_.refs_10_ = bf16[2,1024,256]{2,1,0:T(8,128)(2,1)} collective-permute-done((bf16[2,1024,256]{2,1,0:T(8,128)(2,1)}, bf16[2,1024,256]{2,1,0:T(8,128)(2,1)}, u32[]{:S(2)}, u32[]{:S(2)}) %collective-permute-start.12) | collective-permute-done | bytes 1048608 | tf_op jit(solution)/shard_map/ppermute | solution.py:1000
  156.9 10.2 %collective-permute-done.6.refs_0_.refs_1_ = bf16[2,272,1024]{2,1,0:T(8,128)(2,1)S(1)} collective-permute-done((bf16[2,272,1024]{2,1,0:T(8,128)(2,1)}, bf16[2,272,1024]{2,1,0:T(8,128)(2,1)S(1)}, u32[]{:S(2)}, u32[]{:S(2)}) %collective-permute-start.6) | collective-permute-done | bytes 1114144 | tf_op jit(solution)/shard_map/ppermute | solution.py:1000
  173.5 14.2 %shard_map.320 = (bf16[2,272,1024]{2,1,0:T(8,128)(2,1)}, bf16[8,512,256]{2,1,0:T(8,128)(2,1)}, bf16[8,512,256]{2,1,0:T(8,128)(2,1)}) custom-call(bf16[2,272,1024]{2,1,0:T(8,128)(2,1)} %copy-done.23, bf16[512,1024]{1,0:T(8,128)(2,1)} %collective-permute-done.refs_1_.refs_6_, bf16[2,1024,256]{2,1,0:T(8,128)(2,1)} %get-tuple-element.156.refs_2_.refs_3_.refs_4_, ...), custom_call_target="tpu_custom_call" | custom-call | flops 8589934592 | bytes 15859712 | tf_op jit(solution)/shard_map/pallas_call | solution.py:467
  187.6 23.0 %shard_map.321 = (bf16[2,272,1024]{2,1,0:T(8,128)(2,1)}, bf16[8,512,256]{2,1,0:T(8,128)(2,1)}, bf16[8,512,256]{2,1,0:T(8,128)(2,1)}) custom-call(bf16[2,272,1024]{2,1,0:T(8,128)(2,1)} %collective-permute-done.8.refs_0_.refs_2_, bf16[512,1024]{1,0:T(8,128)(2,1)} %collective-permute-done.4.refs_1_.refs_7_, ...), custom_call_target="tpu_custom_call" | custom-call | flops 8589934592 | bytes 15859712 | tf_op jit(solution)/shard_map/pallas_call | solution.py:467
  212.2 14.2 %shard_map.322 = (bf16[2,272,1024]{2,1,0:T(8,128)(2,1)}, bf16[8,512,256]{2,1,0:T(8,128)(2,1)}, bf16[8,512,256]{2,1,0:T(8,128)(2,1)}) custom-call(bf16[272,1024]{1,0:T(8,128)(2,1)} %copy-done.27, bf16[272,1024]{1,0:T(8,128)(2,1)} %copy-done.28, bf16[512,1024]{1,0:T(8,128)(2,1)} %collective-permute-done.5.refs_2_.refs_8_, ...), custom_call_target="tpu_custom_call" | custom-call | flops 8589934592 | bytes 15859712 | tf_op jit(solution)/shard_map/pallas_call | solution.py:467
  232.9 14.8 %shard_map.323 = (bf16[2,272,1024]{2,1,0:T(8,128)(2,1)}, bf16[8,512,256]{2,1,0:T(8,128)(2,1)}, bf16[8,512,256]{2,1,0:T(8,128)(2,1)}) custom-call(bf16[2,272,1024]{2,1,0:T(8,128)(2,1)} %get-tuple-element.160.refs_0_, bf16[512,1024]{1,0:T(8,128)(2,1)} %bitcast.201, bf16[2,1024,256]{2,1,0:T(8,128)(2,1)} %get-tuple-element.156.refs_2_.refs_3_.refs_4_, ...), custom_call_target="tpu_custom_call" | custom-call | flops 8589934592 | bytes 15859712 | tf_op jit(solution)/shard_map/pallas_call | solution.py:467
  247.6 28.0 %shard_map.324 = (bf16[2,2,1024,256]{3,2,1,0:T(8,128)(2,1)}, bf16[2,2,1024,256]{3,2,1,0:T(8,128)(2,1)}, bf16[2,2,1024,256]{3,2,1,0:T(8,128)(2,1)}, bf16[2,2,1024,256]{3,2,1,0:T(8,128)(2,1)}) custom-call(bf16[2,272,1024]{2,1,0:T(8,128)(2,1)} %get-tuple-element.160.refs_0_, bf16[2,272,1024]{2,1,0:T(8,128)(2,1)} %copy-done.23, ...), custom_call_target="tpu_custom_call" | custom-call | flops 17179869184 | bytes 33816576 | tf_op jit(solution)/shard_map/pallas_call | solution.py:467
  278.0 16.5 %shard_map.325 = (f32[512,1024]{1,0:T(8,128)}, bf16[8,256,128]{2,1,0:T(8,128)(2,1)}, f32[2,256,128]{2,1,0:T(8,128)}, f32[1024,128]{1,0:T(8,128)}) custom-call(s32[4]{0:T(128)} %pad_add_fusion.length, bf16[2,272,1024]{2,1,0:T(8,128)(2,1)} %get-tuple-element.173.r0, bf16[2,272,1024]{2,1,0:T(8,128)(2,1)} %copy-done.15, bf16[2,272,1024]{2,1,0:T(8,128)(2,1)} %copy-done.16, ...), custom_call_target="tpu_custom_call" | custom-call | flops 2684354560 | bytes 17317904 | tf_op jit(solution)/shard_map/pallas_call | solution.py:467
  301.4 9.7 %shard_map.326 = (bf16[8,1024,256]{2,1,0:T(8,128)(2,1)}, bf16[8,1024,256]{2,1,0:T(8,128)(2,1)}) custom-call(bf16[4,256,1024]{2,1,0:T(8,128)(2,1)} %copy-done.3, bf16[4,256,1024]{2,1,0:T(8,128)(2,1)} %copy-done.12, f32[1,1024]{1,0:T(1,128)} %bitcast.211, f32[1,1024]{1,0:T(1,128)} %bitcast.214), custom_call_target="tpu_custom_call" | custom-call | bytes 12591104 | tf_op jit(solution)/shard_map/pallas_call | solution.py:467
  311.1 7.3 %shard_map.327 = bf16[512,5120]{1,0:T(8,128)(2,1)} custom-call(bf16[8,256,128]{2,1,0:T(8,128)(2,1)} %copy-done.10, f32[2,256,128]{2,1,0:T(8,128)} %get-tuple-element.159.gate, f32[512,1024]{1,0:T(8,128)} %get-tuple-element.202.d_after), custom_call_target="tpu_custom_call" | custom-call | flops 2684354560 | bytes 8126464 | tf_op jit(solution)/shard_map/pallas_call | solution.py:467
  324.5 11.7 %shard_map.328.d_qkv = bf16[8,768,128]{2,1,0:T(8,128)(2,1)} custom-call(s32[1]{0:T(128)} %dynamic_slice.105.length, bf16[8,848,128]{2,1,0:T(8,128)(2,1)} %copy-done.14, bf16[8,256,128]{2,1,0:T(8,128)(2,1)} %copy-done.22, f32[128,2048]{1,0:T(8,128)} %get-tuple-element.206.out_t, f32[1,2048]{1,0:T(1,128)} %get-tuple-element.207.lse, ...), custom_call_target="tpu_custom_call" | custom-call | flops 2684354560 | bytes 6987780 | tf_op jit(solution)/shard_map/pallas_call | solution.py:467
  347.9 13.1 %shard_map.329 = bf16[1024,896]{1,0:T(8,128)(2,1)} custom-call(s32[1]{0:T(128)} %bitcast.spot, bf16[8,1024,256]{2,1,0:T(8,128)(2,1)} %get-tuple-element.203.tok_t, bf16[8,1024,256]{2,1,0:T(8,128)(2,1)} %get-tuple-element.204.norm_t, bf16[8,768,128]{2,1,0:T(8,128)(2,1)} %shard_map.328.d_qkv, bf16[8,848,128]{2,1,0:T(8,128)(2,1)} %copy-done.14), custom_call_target="tpu_custom_call" | custom-call | flops 3758096384 | bytes 13533188 | tf_op jit(solution)/shard_map/pallas_call | solution.py:467
  362.4 8.0 %collective-permute-done.22 = bf16[2,2,2,8,5120]{4,3,2,1,0:T(8,128)(2,1)} collective-permute-done((bf16[2,2,2,8,5120]{4,3,2,1,0:T(8,128)(2,1)}, bf16[2,2,2,8,5120]{4,3,2,1,0:T(8,128)(2,1)}, u32[]{:S(2)}, u32[]{:S(2)}) %collective-permute-start.22) | collective-permute-done | bytes 655392 | tf_op jit(solution)/shard_map/ppermute | solution.py:1000
  375.0 15.6 %shard_map.330 = (bf16[512,1024]{1,0:T(8,128)(2,1)}, bf16[512,1024]{1,0:T(8,128)(2,1)}, bf16[512,1024]{1,0:T(8,128)(2,1)}, bf16[512,1024]{1,0:T(8,128)(2,1)}) custom-call(bf16[8,512,256]{2,1,0:T(8,128)(2,1)} %get-tuple-element.214.refs_13_.refs_0_, bf16[8,512,256]{2,1,0:T(8,128)(2,1)} %get-tuple-element.167.refs_14_.refs_1_, ...), custom_call_target="tpu_custom_call" | custom-call | flops 8589934592 | bytes 20971520 | tf_op jit(solution)/shard_map/pallas_call | solution.py:467
  391.8 5.2 collective-permute-start.27
  399.3 7.0 %collective-permute-done.27 = bf16[2,64,896]{2,1,0:T(8,128)(2,1)S(1)} collective-permute-done((bf16[2,64,896]{2,1,0:T(8,128)(2,1)S(1)}, bf16[2,64,896]{2,1,0:T(8,128)(2,1)S(1)}, u32[]{:S(2)}, u32[]{:S(2)}) %collective-permute-start.27) | collective-permute-done | bytes 229408 | tf_op jit(solution)/shard_map/ppermute | solution.py:1000
  412.8 11.9 %shard_map.331 = (bf16[512,1024]{1,0:T(8,128)(2,1)}, bf16[1024,128]{1,0:T(8,128)(2,1)}) custom-call(bf16[8,768,128]{2,1,0:T(8,128)(2,1)} %copy-done.4, bf16[2,256,1024]{2,1,0:T(8,128)(2,1)} %tok.5, f32[1,1024]{1,0:T(1,128)} %bitcast.212, f32[1,1024]{1,0:T(1,128)} %bitcast.215, bf16[1024,512]{1,0:T(8,128)(2,1)} %wq.3, bf16[1024,512]{1,0:T(8,128)(2,1)} %wk.3, ...), custom_call_target="tpu_custom_call" | custom-call | flops 3892314112 | bytes 17309696 | tf_op jit(solution)/shard_map/pallas_call | solution.py:467
  428.5 5.3 collective-permute-done.31
  450.0 6.8 %collective-permute-done.34 = bf16[2,8,5120]{2,1,0:T(8,128)(2,1)} collective-permute-done((bf16[2,8,5120]{2,1,0:T(8,128)(2,1)}, bf16[2,8,5120]{2,1,0:T(8,128)(2,1)}, u32[]{:S(2)}, u32[]{:S(2)}) %collective-permute-start.34) | collective-permute-done | bytes 163872 | tf_op jit(solution)/shard_map/ppermute | solution.py:1000
  466.9 5.8 collective-permute-done.37
  477.0 6.6 %collective-permute-done.45 = bf16[2,2,8,5120]{3,2,1,0:T(8,128)(2,1)S(1)} collective-permute-done((bf16[2,2,8,5120]{3,2,1,0:T(8,128)(2,1)S(1)}, bf16[2,2,8,5120]{3,2,1,0:T(8,128)(2,1)S(1)}, u32[]{:S(2)}, u32[]{:S(2)}) %collective-permute-start.45) | collective-permute-done | bytes 327712 | tf_op jit(solution)/shard_map/ppermute | solution.py:1000
  484.3 7.5 %collective-permute-done.42 = bf16[2,2,64,896]{3,2,1,0:T(8,128)(2,1)S(1)} collective-permute-done((bf16[2,2,64,896]{3,2,1,0:T(8,128)(2,1)S(1)}, bf16[2,2,64,896]{3,2,1,0:T(8,128)(2,1)S(1)}, u32[]{:S(2)}, u32[]{:S(2)}) %collective-permute-start.42) | collective-permute-done | bytes 458784 | tf_op jit(solution)/shard_map/ppermute | solution.py:1000
  510.5 33.9 %collective-permute-done.48 = bf16[2,2,2,8,5120]{4,3,2,1,0:T(8,128)(2,1)S(1)} collective-permute-done((bf16[2,2,2,8,5120]{4,3,2,1,0:T(8,128)(2,1)S(1)}, bf16[2,2,2,8,5120]{4,3,2,1,0:T(8,128)(2,1)S(1)}, u32[]{:S(2)}, u32[]{:S(2)}) %collective-permute-start.48) | collective-permute-done | bytes 655392 | tf_op jit(solution)/shard_map/ppermute | solution.py:1000
  559.3 8.2 %shard_map.333 = (f32[1024,512]{1,0:T(8,128)}, f32[1024,512]{1,0:T(8,128)}, f32[1024,2560]{1,0:T(8,128)}) custom-call(s32[5]{0:T(128)} %stack.237.bits, bf16[2,2,2,64,896]{4,3,2,1,0:T(8,128)(2,1)} %pad_maximum_fusion.3.refs_0_, bf16[2,2,2,64,896]{4,3,2,1,0:T(8,128)(2,1)} %collective-permute-done.46.refs_1_, ...), custom_call_target="tpu_custom_call" | custom-call | bytes 18350100 | tf_op jit(solution)/shard_map/pallas_call | solution.py:467
  573.3 8.2 %shard_map.335 = (f32[1024,512]{1,0:T(8,128)}, f32[1024,512]{1,0:T(8,128)}, f32[1024,2560]{1,0:T(8,128)}) custom-call(s32[5]{0:T(128)} %stack.237.bits, bf16[2,2,2,64,896]{4,3,2,1,0:T(8,128)(2,1)} %collective-permute-done.53.refs_0_, ...), custom_call_target="tpu_custom_call", output_to_operand_aliasing={{0}: (5, {}), {1}: (6, {}), {2}: (7, {})} | custom-call | bytes 33030164 | tf_op jit(solution)/shard_map/pallas_call | solution.py:467
  (279 shorter events, 176.6 us)
Async XLA Ops:
  19.5 50.9 %all-to-all-start = ((bf16[8,848,128]{2,1,0:T(8,128)(2,1)}), bf16[8,848,128]{2,1,0:T(8,128)(2,1)S(1)}, u32[]{:S(2)}, u32[]{:S(2)}) async-start(bf16[8,848,128]{2,1,0:T(8,128)(2,1)} %get-tuple-element.152), calls=%async_computation | async-start | bytes 3473408 | tf_op jit(solution)/shard_map/all_to_all | solution.py:1208
  28.4 42.0 %collective-permute-start.1 = (bf16[2,256,1024]{2,1,0:T(8,128)(2,1)S(1)}, bf16[2,256,1024]{2,1,0:T(8,128)(2,1)}, u32[]{:S(2)}, u32[]{:S(2)}) collective-permute-start(bf16[2,256,1024]{2,1,0:T(8,128)(2,1)S(1)} %copy-done.7), channel_id=1, source_target_pairs={{0,4},{1,5},{2,6},{3,7},{4,0},{5,1},{6,2},{7,3},{8,12},{9,13},{10,... | collective-permute-start | bytes 3145736 | tf_op jit(solution)/shard_map/ppermute | solution.py:1000
  70.4 59.5 %collective-permute-start.2 = (bf16[2,1024,256]{2,1,0:T(8,128)(2,1)}, bf16[2,1024,256]{2,1,0:T(8,128)(2,1)}, u32[]{:S(2)}, u32[]{:S(2)}) collective-permute-start(bf16[2,1024,256]{2,1,0:T(8,128)(2,1)} %get-tuple-element.156.refs_2_.refs_3_.refs_4_), channel_id=1, source_target_pairs={{0,16},{1,17},{2,18},{3,19},{4,20},{5,21},{6,22},{7,23},{8,24},{9,... | collective-permute-start | bytes 3145736 | tf_op jit(solution)/shard_map/ppermute | solution.py:1000
  72.8 57.2 %collective-permute-start.3 = (bf16[2,1024,256]{2,1,0:T(8,128)(2,1)}, bf16[2,1024,256]{2,1,0:T(8,128)(2,1)S(1)}, u32[]{:S(2)}, u32[]{:S(2)}) collective-permute-start(bf16[2,1024,256]{2,1,0:T(8,128)(2,1)} %get-tuple-element.156.refs_2_.refs_3_.refs_4_), channel_id=1, source_target_pairs={{0,8},{1,9},{2,10},{3,11},{4,12},{5,13},{6,14},{7,15},{8,0},{9,1},... | collective-permute-start | bytes 3145736 | tf_op jit(solution)/shard_map/ppermute | solution.py:1000
  74.2 55.7 %collective-permute-start.4 = (bf16[512,1024]{1,0:T(8,128)(2,1)}, bf16[512,1024]{1,0:T(8,128)(2,1)}, u32[]{:S(2)}, u32[]{:S(2)}) collective-permute-start(bf16[512,1024]{1,0:T(8,128)(2,1)} %bitcast.199), channel_id=1, source_target_pairs={{0,4},{1,5},{2,6},{3,7},{4,0},{5,1},{6,2},{7,3},{8,12},{9,13},{10,... | collective-permute-start | bytes 3145736 | tf_op jit(solution)/shard_map/ppermute | solution.py:1000
  74.5 55.4 %collective-permute-start.5 = (bf16[512,1024]{1,0:T(8,128)(2,1)}, bf16[512,1024]{1,0:T(8,128)(2,1)}, u32[]{:S(2)}, u32[]{:S(2)}) collective-permute-start(bf16[512,1024]{1,0:T(8,128)(2,1)} %bitcast.200), channel_id=1, source_target_pairs={{0,6},{1,7},{2,4},{3,5},{4,2},{5,3},{6,0},{7,1},{8,14},{9,15},{10,... | collective-permute-start | bytes 3145736 | tf_op jit(solution)/shard_map/ppermute | solution.py:1000
  86.8 43.1 %all-to-all-start.1 = ((bf16[8,256,128]{2,1,0:T(8,128)(2,1)}), bf16[8,256,128]{2,1,0:T(8,128)(2,1)S(1)}, u32[]{:S(2)}, u32[]{:S(2)}) async-start(bf16[8,256,128]{2,1,0:T(8,128)(2,1)} %get-tuple-element.155), calls=%async_computation.1 | async-start | bytes 1048576 | tf_op jit(solution)/shard_map/all_to_all | solution.py:1224
  140.4 26.8 %collective-permute-start.6 = (bf16[2,272,1024]{2,1,0:T(8,128)(2,1)}, bf16[2,272,1024]{2,1,0:T(8,128)(2,1)S(1)}, u32[]{:S(2)}, u32[]{:S(2)}) collective-permute-start(bf16[2,272,1024]{2,1,0:T(8,128)(2,1)} %get-tuple-element.160.refs_0_), channel_id=1, source_target_pairs={{0,2},{1,3},{2,0},{3,1},{4,6},{5,7},{6,4},{7,5},{8,10},{9,11},{10,... | collective-permute-start | bytes 3342344 | tf_op jit(solution)/shard_map/ppermute | solution.py:1000
  142.5 29.4 %collective-permute-start.10 = (bf16[2,1024,256]{2,1,0:T(8,128)(2,1)}, bf16[2,1024,256]{2,1,0:T(8,128)(2,1)}, u32[]{:S(2)}, u32[]{:S(2)}) collective-permute-start(bf16[2,1024,256]{2,1,0:T(8,128)(2,1)} %copy-done.26), channel_id=1, source_target_pairs={{0,1},{1,0},{2,3},{3,2},{4,5},{5,4},{6,7},{7,6},{8,9},{9,8},{10,11... | collective-permute-start | bytes 3145736 | tf_op jit(solution)/shard_map/ppermute | solution.py:1000
  142.5 31.0 %collective-permute-start.11 = (bf16[2,1024,256]{2,1,0:T(8,128)(2,1)}, bf16[2,1024,256]{2,1,0:T(8,128)(2,1)}, u32[]{:S(2)}, u32[]{:S(2)}) collective-permute-start(bf16[2,1024,256]{2,1,0:T(8,128)(2,1)} %collective-permute-done.2.refs_6_.refs_7_.refs_8_), channel_id=1, source_target_pairs={{0,1},{1,0},{2,3},{3,2},{4,5},{5,4},{6,7},{7,6},{8,9},{9,8},{10,11... | collective-permute-start | bytes 3145736 | tf_op jit(solution)/shard_map/ppermute | solution.py:1000
  167.1 62.8 %collective-permute-start.17 = (bf16[2,256,1024]{2,1,0:T(8,128)(2,1)S(1)}, bf16[2,256,1024]{2,1,0:T(8,128)(2,1)S(1)}, u32[]{:S(2)}, u32[]{:S(2)}) collective-permute-start(bf16[2,256,1024]{2,1,0:T(8,128)(2,1)S(1)} %pad_maximum_fusion.2), channel_id=1, source_target_pairs={{0,16},{1,17},{2,18},{3,19},{4,20},{5,21},{6,22},{7,23},{8,24},{9,... | collective-permute-start | bytes 3145736 | tf_op jit(solution)/shard_map/ppermute | solution.py:1000
  168.5 42.1 %collective-permute-start.7 = (bf16[272,1024]{1,0:T(8,128)(2,1)S(1)}, bf16[272,1024]{1,0:T(8,128)(2,1)S(1)}, u32[]{:S(2)}, u32[]{:S(2)}) collective-permute-start(bf16[272,1024]{1,0:T(8,128)(2,1)S(1)} %slice_bitcast_fusion.1), channel_id=1, source_target_pairs={{0,4},{1,5},{2,6},{3,7},{4,0},{5,1},{6,2},{7,3},{8,12},{9,13},{10,... | collective-permute-start | bytes 1671176 | tf_op jit(solution)/shard_map/ppermute | solution.py:1000
  171.8 38.8 %collective-permute-start.9 = (bf16[272,1024]{1,0:T(8,128)(2,1)S(1)}, bf16[272,1024]{1,0:T(8,128)(2,1)S(1)}, u32[]{:S(2)}, u32[]{:S(2)}) collective-permute-start(bf16[272,1024]{1,0:T(8,128)(2,1)S(1)} %slice_bitcast_fusion), channel_id=1, source_target_pairs={{0,2},{1,3},{2,0},{3,1},{4,6},{5,7},{6,4},{7,5},{8,10},{9,11},{10,... | collective-permute-start | bytes 1671176 | tf_op jit(solution)/shard_map/ppermute | solution.py:1000
  226.4 49.9 %collective-permute-start.14 = (bf16[2,272,1024]{2,1,0:T(8,128)(2,1)}, bf16[2,272,1024]{2,1,0:T(8,128)(2,1)S(1)}, u32[]{:S(2)}, u32[]{:S(2)}) collective-permute-start(bf16[2,272,1024]{2,1,0:T(8,128)(2,1)} %get-tuple-element.174), channel_id=1, source_target_pairs={{0,2},{1,3},{2,0},{3,1},{4,6},{5,7},{6,4},{7,5},{8,10},{9,11},{10,... | collective-permute-start | bytes 3342344 | tf_op jit(solution)/shard_map/ppermute | solution.py:1000
  226.9 49.4 %collective-permute-start.15 = (bf16[2,272,1024]{2,1,0:T(8,128)(2,1)}, bf16[2,272,1024]{2,1,0:T(8,128)(2,1)S(1)}, u32[]{:S(2)}, u32[]{:S(2)}) collective-permute-start(bf16[2,272,1024]{2,1,0:T(8,128)(2,1)} %get-tuple-element.175), channel_id=1, source_target_pairs={{0,4},{1,5},{2,6},{3,7},{4,0},{5,1},{6,2},{7,3},{8,12},{9,13},{10,... | collective-permute-start | bytes 3342344 | tf_op jit(solution)/shard_map/ppermute | solution.py:1000
  226.9 49.3 %collective-permute-start.16 = (bf16[2,272,1024]{2,1,0:T(8,128)(2,1)}, bf16[2,272,1024]{2,1,0:T(8,128)(2,1)S(1)}, u32[]{:S(2)}, u32[]{:S(2)}) collective-permute-start(bf16[2,272,1024]{2,1,0:T(8,128)(2,1)} %get-tuple-element.176), channel_id=1, source_target_pairs={{0,6},{1,7},{2,4},{3,5},{4,2},{5,3},{6,0},{7,1},{8,14},{9,15},{10,... | collective-permute-start | bytes 3342344 | tf_op jit(solution)/shard_map/ppermute | solution.py:1000
  232.3 44.9 %collective-permute-start.18 = (bf16[4,256,1024]{2,1,0:T(8,128)(2,1)S(1)}, bf16[4,256,1024]{2,1,0:T(8,128)(2,1)S(1)}, u32[]{:S(2)}, u32[]{:S(2)}) collective-permute-start(bf16[4,256,1024]{2,1,0:T(8,128)(2,1)S(1)} %pad_maximum_fusion.1.near), channel_id=1, source_target_pairs={{0,8},{1,9},{2,10},{3,11},{4,12},{5,13},{6,14},{7,15},{8,0},{9,1},... | collective-permute-start | bytes 6291464 | tf_op jit(solution)/shard_map/ppermute | solution.py:1000
  322.4 122.2 %collective-permute-start.40 = (bf16[2,2,1024,256]{3,2,1,0:T(8,128)(2,1)}, bf16[2,2,1024,256]{3,2,1,0:T(8,128)(2,1)}, u32[]{:S(2)}, u32[]{:S(2)}) collective-permute-start(bf16[2,2,1024,256]{3,2,1,0:T(8,128)(2,1)} %get-tuple-element.238), channel_id=1, source_target_pairs={{0,1},{1,0},{2,3},{3,2},{4,5},{5,4},{6,7},{7,6},{8,9},{9,8},{10,11... | collective-permute-start | bytes 6291464 | tf_op jit(solution)/shard_map/ppermute | solution.py:1000
  322.6 120.2 %collective-permute-start.41 = (bf16[2,1024,256]{2,1,0:T(8,128)(2,1)}, bf16[2,1024,256]{2,1,0:T(8,128)(2,1)}, u32[]{:S(2)}, u32[]{:S(2)}) collective-permute-start(bf16[2,1024,256]{2,1,0:T(8,128)(2,1)} %get-tuple-element.289), channel_id=1, source_target_pairs={{0,8},{1,9},{2,10},{3,11},{4,12},{5,13},{6,14},{7,15},{8,0},{9,1},... | collective-permute-start | bytes 3145736 | tf_op jit(solution)/shard_map/ppermute | solution.py:1000
  342.5 27.8 %collective-permute-start.22 = (bf16[2,2,2,8,5120]{4,3,2,1,0:T(8,128)(2,1)}, bf16[2,2,2,8,5120]{4,3,2,1,0:T(8,128)(2,1)}, u32[]{:S(2)}, u32[]{:S(2)}) collective-permute-start(bf16[2,2,2,8,5120]{4,3,2,1,0:T(8,128)(2,1)} %dynamic-slice_bitcast_fusion.2), channel_id=1, source_target_pairs={{0,4},{1,5},{2,6},{3,7},{4,0},{5,1},{6,2},{7,3},{8,12},{9,13},{10,... | collective-permute-start | bytes 1966088 | tf_op jit(solution)/shard_map/ppermute | solution.py:1000
  344.0 67.0 %all-to-all-start.3 = ((bf16[8,768,128]{2,1,0:T(8,128)(2,1)}), bf16[8,768,128]{2,1,0:T(8,128)(2,1)S(1)}, u32[]{:S(2)}, u32[]{:S(2)}) async-start(bf16[8,768,128]{2,1,0:T(8,128)(2,1)} %shard_map.328.d_qkv), calls=%async_computation.3 | async-start | bytes 3145728 | tf_op jit(solution)/shard_map/all_to_all | solution.py:1385
  398.7 35.8 %collective-permute-start.32 = (bf16[512,1024]{1,0:T(8,128)(2,1)}, bf16[512,1024]{1,0:T(8,128)(2,1)}, u32[]{:S(2)}, u32[]{:S(2)}) collective-permute-start(bf16[512,1024]{1,0:T(8,128)(2,1)} %get-tuple-element.228), channel_id=1, source_target_pairs={{0,4},{1,5},{2,6},{3,7},{4,0},{5,1},{6,2},{7,3},{8,12},{9,13},{10,... | collective-permute-start | bytes 3145736 | tf_op jit(solution)/shard_map/ppermute | solution.py:1000
  437.6 35.2 %all-to-all-start.4 = ((bf16[32,32,128]{2,1,0:T(8,128)(2,1)}), bf16[32,32,128]{2,1,0:T(8,128)(2,1)S(1)}, u32[]{:S(2)}, u32[]{:S(2)}) async-start(bf16[32,32,128]{2,1,0:T(8,128)(2,1)} %bitcast.207), calls=%async_computation.4 | async-start | bytes 524288 | tf_op jit(solution)/shard_map/all_to_all | solution.py:1426
  442.8 30.0 %collective-permute-start.38 = (bf16[512,1024]{1,0:T(8,128)(2,1)S(1)}, bf16[512,1024]{1,0:T(8,128)(2,1)}, u32[]{:S(2)}, u32[]{:S(2)}) collective-permute-start(bf16[512,1024]{1,0:T(8,128)(2,1)S(1)} %add_convert_fusion), channel_id=1, source_target_pairs={{0,2},{1,3},{2,0},{3,1},{4,6},{5,7},{6,4},{7,5},{8,10},{9,11},{10,... | collective-permute-start | bytes 3145736 | tf_op jit(solution)/shard_map/ppermute | solution.py:1000
  444.7 28.1 %collective-permute-start.39 = (bf16[512,1024]{1,0:T(8,128)(2,1)}, bf16[512,1024]{1,0:T(8,128)(2,1)}, u32[]{:S(2)}, u32[]{:S(2)}) collective-permute-start(bf16[512,1024]{1,0:T(8,128)(2,1)} %get-tuple-element.237), channel_id=1, source_target_pairs={{0,4},{1,5},{2,6},{3,7},{4,0},{5,1},{6,2},{7,3},{8,12},{9,13},{10,... | collective-permute-start | bytes 3145736 | tf_op jit(solution)/shard_map/ppermute | solution.py:1000
  495.0 50.0 %collective-permute-start.51 = (bf16[2,1024,256]{2,1,0:T(8,128)(2,1)}, bf16[2,1024,256]{2,1,0:T(8,128)(2,1)}, u32[]{:S(2)}, u32[]{:S(2)}) collective-permute-start(bf16[2,1024,256]{2,1,0:T(8,128)(2,1)} %get-tuple-element.252), channel_id=1, source_target_pairs={{0,8},{1,9},{2,10},{3,11},{4,12},{5,13},{6,14},{7,15},{8,0},{9,1},... | collective-permute-start | bytes 3145736 | tf_op jit(solution)/shard_map/ppermute | solution.py:1000
  496.0 52.2 %collective-permute-start.50 = (bf16[2,1024,256]{2,1,0:T(8,128)(2,1)}, bf16[2,1024,256]{2,1,0:T(8,128)(2,1)}, u32[]{:S(2)}, u32[]{:S(2)}) collective-permute-start(bf16[2,1024,256]{2,1,0:T(8,128)(2,1)} %fusion.3), channel_id=1, source_target_pairs={{0,16},{1,17},{2,18},{3,19},{4,20},{5,21},{6,22},{7,23},{8,24},{9,... | collective-permute-start | bytes 3145736 | tf_op jit(solution)/shard_map/ppermute | solution.py:1000
  498.8 49.4 %all-to-all-start.5 = ((bf16[32,32,128]{2,1,0:T(8,128)(2,1)}), bf16[32,32,128]{2,1,0:T(8,128)(2,1)S(1)}, u32[]{:S(2)}, u32[]{:S(2)}) async-start(bf16[32,32,128]{2,1,0:T(8,128)(2,1)} %broadcast_in_dim.8), calls=%async_computation.5 | async-start | bytes 524288 | tf_op jit(solution)/shard_map/all_to_all | solution.py:1440
  506.0 42.1 %collective-permute-start.46 = (bf16[2,2,2,64,896]{4,3,2,1,0:T(8,128)(2,1)}, bf16[2,2,2,64,896]{4,3,2,1,0:T(8,128)(2,1)}, u32[]{:S(2)}, u32[]{:S(2)}) collective-permute-start(bf16[2,2,2,64,896]{4,3,2,1,0:T(8,128)(2,1)} %pad_maximum_fusion.3.refs_0_), channel_id=1, source_target_pairs={{0,2},{1,3},{2,0},{3,1},{4,6},{5,7},{6,4},{7,5},{8,10},{9,11},{10,... | collective-permute-start | bytes 2752520 | tf_op jit(solution)/shard_map/ppermute | solution.py:1000
  507.9 40.3 %collective-permute-start.47 = (bf16[2,2,2,64,896]{4,3,2,1,0:T(8,128)(2,1)}, bf16[2,2,2,64,896]{4,3,2,1,0:T(8,128)(2,1)}, u32[]{:S(2)}, u32[]{:S(2)}) collective-permute-start(bf16[2,2,2,64,896]{4,3,2,1,0:T(8,128)(2,1)} %pad_maximum_fusion.4.refs_2_), channel_id=1, source_target_pairs={{0,4},{1,5},{2,6},{3,7},{4,0},{5,1},{6,2},{7,3},{8,12},{9,13},{10,... | collective-permute-start | bytes 2752520 | tf_op jit(solution)/shard_map/ppermute | solution.py:1000
  509.4 35.1 %collective-permute-start.48 = (bf16[2,2,2,8,5120]{4,3,2,1,0:T(8,128)(2,1)S(1)}, bf16[2,2,2,8,5120]{4,3,2,1,0:T(8,128)(2,1)S(1)}, u32[]{:S(2)}, u32[]{:S(2)}) collective-permute-start(bf16[2,2,2,8,5120]{4,3,2,1,0:T(8,128)(2,1)S(1)} %pad_maximum_fusion.7), channel_id=1, source_target_pairs={{0,2},{1,3},{2,0},{3,1},{4,6},{5,7},{6,4},{7,5},{8,10},{9,11},{10,... | collective-permute-start | bytes 1966088 | tf_op jit(solution)/shard_map/ppermute | solution.py:1000
  552.4 29.0 %collective-permute-start.52 = (bf16[2,1024,256]{2,1,0:T(8,128)(2,1)}, bf16[2,1024,256]{2,1,0:T(8,128)(2,1)}, u32[]{:S(2)}, u32[]{:S(2)}) collective-permute-start(bf16[2,1024,256]{2,1,0:T(8,128)(2,1)} %fusion.2.mine), channel_id=1, source_target_pairs={{0,2},{1,3},{2,0},{3,1},{4,6},{5,7},{6,4},{7,5},{8,10},{9,11},{10,... | collective-permute-start | bytes 3145736 | tf_op jit(solution)/shard_map/ppermute | solution.py:1000
  (65 other events, 912.9 us)

commit v5 on v4

--- a/solution.py
+++ b/solution.py
@@ -509,7 +509,7 @@
     return lax.broadcasted_iota(jnp.int32, shape, dim)
 
 
-def pre_kernel(tok, gain, bias, wq, wk, wv, sel, vid, oid, cos, sin, select, qkv, proj, gate):
+def pre_kernel(spot, tok, gain, bias, wq, wk, wv, sel, vid, oid, cos, sin, select, qkv, proj, gate):
     heads = qkv.shape[0]
     experts = wv.shape[1] // (heads * LANES)
     low = tok[0]
@@ -521,15 +521,15 @@
         for h in range(heads):
             head = turned(pre[:, h * LANES:(h + 1) * LANES], cos[...], sin[...])
             qkv[h, part * rows:(part + 1) * rows] = head.astype(HALF_TYPE)
-    lanes = lane_ids((rows, LANES), 1)
-    chosen = jnp.zeros((rows, LANES), FULL_TYPE)
-    tops = vid.shape[2] // heads
+    ids = lane_ids((LANES, rows), 0)
+    chosen = jnp.zeros((LANES, rows), FULL_TYPE)
+    tops = vid.shape[1] // heads
     for h in range(heads):
         for k in range(tops):
             j = h * tops + k
-            chosen += (lanes == vid[0, :, j:j + 1] + (SELV + experts * h)).astype(FULL_TYPE)
-            chosen += (lanes == oid[0, :, j:j + 1] + (SELO + experts * h)).astype(FULL_TYPE)
-    gates = jax.nn.sigmoid(nn(normed, sel[...])) * chosen
+            chosen += (ids == vid[0, j:j + 1, :] + (SELV + experts * h)).astype(FULL_TYPE)
+            chosen += (ids == oid[0, j:j + 1, :] + (SELO + experts * h)).astype(FULL_TYPE)
+    gates = jax.nn.sigmoid(nt(normed, sel[...])) * jnp.transpose(chosen)
     gate[0] = gates
     gates_low = gates.astype(HALF_TYPE)
     for h in range(heads):
@@ -846,7 +846,7 @@
             product = (proj[0, :, at:at + LANES].astype(FULL_TYPE) * d_value).astype(HALF_TYPE)
             d_gates += nn(product, hit)
     d_logit = (d_gates * gate_here * (1.0 - gate_here)).astype(HALF_TYPE)
-    d_normed = nt(d_query, wq[...]) + nt(d_key, wk[...]) + nt(d_logit, sel[...])
+    d_normed = nt(d_query, wq[...]) + nt(d_key, wk[...]) + nn(d_logit, sel[...])
     total = d_after[...] + norm_back(d_normed, normal, inv, gain[...]) + nt(d_proj[...], wv[...])
     out[...] = total.astype(HALF_TYPE)
     gain_sum = jnp.sum(d_normed * normal, axis=0, keepdims=True)
@@ -918,29 +918,32 @@
     sources = refs[:4]
     query, key, value = refs[-3:]
     step = pl.program_id(0)
-    part = step // 4
-    x, low = bits[1], bits[3]
+    y, x, high, low = bits[0], bits[1], bits[2], bits[3]
     wide = value.shape[1] // 4
-
-    def put(block, head):
+    size = value.shape[0] // 2
+
+    def put(block, head, place):
+        here = pl.ds(pl.multiple_of(place * size, size), size)
         at = pl.multiple_of(head * LANES, LANES)
-        query[:, pl.ds(at, LANES)] = block[:, 0:LANES].astype(FULL_TYPE)
-        key[:, pl.ds(at, LANES)] = block[:, LANES:2 * LANES].astype(FULL_TYPE)
-        value[:, pl.ds(pl.multiple_of(head * wide, LANES), wide)] = block[:, 2 * LANES:].astype(FULL_TYPE)
-
-    for y in range(2):
-
-        @pl.when((part == 0) & ((step // 2) % 2 == y))
-        def _(y=y):
+        query[here, pl.ds(at, LANES)] = block[:, 0:LANES].astype(FULL_TYPE)
+        key[here, pl.ds(at, LANES)] = block[:, LANES:2 * LANES].astype(FULL_TYPE)
+        value[here, pl.ds(pl.multiple_of(head * wide, LANES), wide)] = block[:, 2 * LANES:].astype(FULL_TYPE)
+
+    for j in range(2):
+
+        @pl.when(step == j)
+        def _(j=j):
             for i in range(2):
                 for b in range(2):
-                    put(sources[y][i, b, 0], (low ^ b) * 2 + (x ^ i))
-
-    @pl.when(part == 1)
+                    for a in range(2):
+                        put(sources[j][i, b, a], (low ^ b) * 2 + (x ^ i), high ^ a)
+
+    @pl.when(step >= 2)
     def _():
-        for i in range(2):
-            for b in range(2):
-                put(sources[2 + i][0, b, 0], (low ^ b) * 2 + (x ^ i))
+        for j in range(2):
+            for i in range(2):
+                for b in range(2):
+                    put(sources[2 + j][i, b, 0], (low ^ b) * 2 + (x ^ j), y ^ i)
 
 
 def place_out_kernel(spot, mine, *rest):
@@ -1077,23 +1080,13 @@
     size, cols = sources[0].shape[3:]
 
     def block(j):
-        part, y = j // 2, j % 2
-
-        def at(s, bits):
-            a = s % 2
-            active = (s // 4) == part
-            if part == 0:
-                active = active & ((s // 2) % 2 == y)
-                return (0, 0, jnp.where(active, a, 0), 0, 0)
-            return (jnp.where(active, (s // 2) % 2, 0), 0, jnp.where(active, a, 0), 0, 0)
-
-        return pl.BlockSpec((2 if part == 0 else 1, 2, 1, size, cols), at)
+        if j < 2:
+            return pl.BlockSpec((2, 2, 2, size, cols), lambda s, bits: (0, 0, 0, 0, 0))
+        return pl.BlockSpec((2, 2, 1, size, cols), lambda s, bits: (0, 0, jnp.where(s < 2, 0, s % 2), 0, 0))
 
     def row_block(s, bits):
-        part, i, a = s // 4, (s // 2) % 2, s % 2
-        y, high = bits[0] ^ i, bits[2] ^ a
-        inside = jnp.where(part == 0, y * 2 + high, high * 2 + y)
-        return (((bits[4] ^ core) * 2 + part) * 4 + inside, 0)
+        inside = jnp.where(s < 2, bits[0], bits[2]) ^ (s % 2)
+        return (((bits[4] ^ core) * 2 + s // 2) * 2 + inside, 0)
 
     wide = cols - 2 * LANES
     more = () if begun is None else tuple(begun)
@@ -1104,11 +1097,11 @@
             shaped((rows, heads * wide), FULL_TYPE),
         ),
         jnp.stack([place.y, place.x, place.high, place.low, place.c]).astype(jnp.int32), *sources, *more,
-        grid=(8,), prefetch=1,
+        grid=(4,), prefetch=1,
         in_specs=[block(j) for j in range(4)] + [pl.BlockSpec(memory_space=pl.ANY)] * len(more),
         out_specs=(
-            pl.BlockSpec((size, heads * LANES), row_block), pl.BlockSpec((size, heads * LANES), row_block),
-            pl.BlockSpec((size, heads * wide), row_block),
+            pl.BlockSpec((2 * size, heads * LANES), row_block), pl.BlockSpec((2 * size, heads * LANES), row_block),
+            pl.BlockSpec((2 * size, heads * wide), row_block),
         ),
         aliases={5 + i: i for i in range(len(more))},
     )
@@ -1148,8 +1141,8 @@
     smem = pl.BlockSpec(memory_space=pltpu.SMEM)
     vmem = pl.BlockSpec(memory_space=pltpu.VMEM)
     hbm = pl.BlockSpec(memory_space=pl.ANY)
-    by_seq = lambda shape: pl.BlockSpec((1,) + tuple(shape[1:]), lambda s: (s,) + (0,) * (len(shape) - 1))
-    split = lambda shape: pl.BlockSpec((shape[0] // seqs,) + tuple(shape[1:]), lambda s: (s,) + (0,) * (len(shape) - 1))
+    by_seq = lambda shape: pl.BlockSpec((1,) + tuple(shape[1:]), lambda s, *_: (s,) + (0,) * (len(shape) - 1))
+    split = lambda shape: pl.BlockSpec((shape[0] // seqs,) + tuple(shape[1:]), lambda s, *_: (s,) + (0,) * (len(shape) - 1))
     token_cols = lambda n: pl.BlockSpec((n, row_count), lambda s: (0, s))
 
     own_select = jnp.transpose(w_select).reshape(own_count, 8, -1).swapaxes(0, 1).reshape(-1, LANES)
@@ -1172,16 +1165,15 @@
     tokens_x = place.swap_x(tokens)
 
     cosine, sine = turn_tables(span, head_dim)
-    here = lambda t: lax.dynamic_slice_in_dim(t, first_row, row_count, 0)
     sel = jnp.concatenate(
         [
-            jnp.zeros((width, SELV), HALF_TYPE), sel_value, sel_out,
-            jnp.zeros((width, LANES - SELO - heads * experts), HALF_TYPE),
+            jnp.zeros((SELV, width), HALF_TYPE), sel_value.T, sel_out.T,
+            jnp.zeros((LANES - SELO - heads * experts, width), HALF_TYPE),
         ],
-        axis=1,
-    )
-    value_flat = value_ids.reshape(seqs, row_count, -1)
-    out_flat = out_ids.reshape(seqs, row_count, -1)
+        axis=0,
+    )
+    value_flat = jnp.transpose(value_ids, (0, 2, 3, 1)).reshape(seqs, -1, row_count)
+    out_flat = jnp.transpose(out_ids, (0, 2, 3, 1)).reshape(seqs, -1, row_count)
     payload = 3 * row_count + own_select.shape[0] + 16
     qkv, projected, gate = call(
         pre_kernel,
@@ -1190,13 +1182,14 @@
             shaped((seqs, row_count, wide_out)),
             shaped((seqs, row_count, LANES), FULL_TYPE),
         ),
-        tokens, row(gain_one), row(bias_one), w_query, w_key, w_value, sel, value_flat, out_flat,
-        here(cosine), here(sine), own_select,
-        grid=(seqs,),
+        place.wide.reshape(1).astype(jnp.int32), tokens, row(gain_one), row(bias_one), w_query, w_key, w_value, sel,
+        value_flat, out_flat, cosine, sine, own_select,
+        grid=(seqs,), prefetch=1,
         in_specs=[
             by_seq(tokens.shape), full((1, width)), full((1, width)), full(w_query.shape), full(w_key.shape),
             full(w_value.shape), full(sel.shape), by_seq(value_flat.shape), by_seq(out_flat.shape),
-            full((row_count, head_dim)), full((row_count, head_dim)),
+            pl.BlockSpec((row_count, head_dim), lambda s, spot: (spot[0], 0)),
+            pl.BlockSpec((row_count, head_dim), lambda s, spot: (spot[0], 0)),
             full(own_select.shape),
         ],
         out_specs=(
@@ -1441,11 +1434,11 @@
     back = [in_order(flat[1 - i][0], out_sum[:, :, i], flat[1 - i][1](out_sum[:, :, i])) for i in range(2)]
     first = jnp.stack([sets[0], place.swap_x(sets[0])])
     second = jnp.stack([sets[1], place.swap_y(sets[1])])
-    first, second, back[0], back[1] = lax.optimization_barrier((first, second, *back))
+    output = call(output_kernel, shaped((all_rows, width)), after, b0, b2, b1)
+    first, second, back[0], back[1], output = lax.optimization_barrier((first, second, *back, output))
     sources = [first, place.swap_y(first), second, place.swap_x(second)]
     back = [in_order(flat[i][0], back[i], flat[i][1](back[i])) for i in range(2)]
     out_half = jnp.stack(back).reshape(rows_out // 2, cols_out)
-    output = call(output_kernel, shaped((all_rows, width)), after, b0, b2, b1)
     sources[1], sources[3], output, out_half, mine_far, small, passed[0] = lax.optimization_barrier(
         (sources[1], sources[3], output, out_half, mine_far, small, passed[0])
     )

time: 604 us -> 597 us (0.988)
  transfers between devices with their start and end apart: 66 -> 66, of which waited for: 22 -> 24; matrix products, arithmetic and copies ran while one was open for 6% -> 7% of each run, Pallas kernels for 40% -> 40%
where the time goes in v5:
time: 597 us; the launch traced here: 588 us
  Pallas kernels  249 us (42%)
  waiting for transfers between devices  193 us (32%)
  starting transfers between devices  91 us (15%)
  other arithmetic  29.9 us (5%)
  local copies, waits for them, and re-layouts  22.7 us (4%)
    pallas_call x24, Pallas kernels, call(): pl.pallas_call(kernel, out_shape=out_shape, input_output_aliases=aliases...  249 us
    ppermute x60, waiting for transfers between devices, send(): return lax.ppermute(value, ('wide', 'narrow'), self.pairs(move))  147 us
    ppermute x60, starting transfers between devices, send(): return lax.ppermute(value, ('wide', 'narrow'), self.pairs(move))  65.8 us
    all_to_all x1, waiting for transfers between devices, tuned_device(): mixed = lax.all_to_all(mixed, 'wide', 0, 0, tiled=True)  39.1 us
    convert_element_type x12, other arithmetic, add(): return total.astype(HALF_TYPE)  18.3 us
  transfers between devices with their start and end apart: 66, of which 24 were waited for; matrix products, arithmetic and copies ran while one was open for 7% of the time, Pallas kernels for 40%

profile of v5, /device:TPU:0, one launch (start us, length us, event | category | flops | bytes accessed | tf_op | source)
XLA Modules:
  0.0 588.0 jit_solution(2553783214000046095)
XLA Ops:
  5.1 11.1 %shard_map.316 = (bf16[8,848,128]{2,1,0:T(8,128)(2,1)}, bf16[2,256,2560]{2,1,0:T(8,128)(2,1)}, f32[2,256,128]{2,1,0:T(8,128)}) custom-call(s32[1]{0:T(128)} %bitcast.spot, bf16[2,256,1024]{2,1,0:T(8,128)(2,1)} %tok.5, f32[1,1024]{1,0:T(1,128)} %bitcast.214, f32[1,1024]{1,0:T(1,128)} %bitcast.217, bf16[1024,512]{1,0:T(8,128)(2,1)} %wq.3, ...), custom_call_target="tpu_custom_call" | custom-call | flops 3892314112 | bytes 15425540 | tf_op jit(solution)/shard_map/pallas_call | solution.py:467
  16.2 7.4 %all-to-all-start = ((bf16[8,848,128]{2,1,0:T(8,128)(2,1)}), bf16[8,848,128]{2,1,0:T(8,128)(2,1)S(1)}, u32[]{:S(2)}, u32[]{:S(2)}) async-start(bf16[8,848,128]{2,1,0:T(8,128)(2,1)} %get-tuple-element.153), calls=%async_computation | async-start | bytes 3473408 | tf_op jit(solution)/shard_map/all_to_all | solution.py:1201
  32.1 16.4 %collective-permute-done.refs_1_.refs_6_ = bf16[512,1024]{1,0:T(8,128)(2,1)} collective-permute-done((bf16[512,1024]{1,0:T(8,128)(2,1)}, bf16[512,1024]{1,0:T(8,128)(2,1)}, u32[]{:S(2)}, u32[]{:S(2)}) %collective-permute-start) | collective-permute-done | bytes 1048608 | tf_op jit(solution)/shard_map/ppermute | solution.py:1003
  48.5 18.6 %collective-permute-done.1 = bf16[2,256,1024]{2,1,0:T(8,128)(2,1)} collective-permute-done((bf16[2,256,1024]{2,1,0:T(8,128)(2,1)S(1)}, bf16[2,256,1024]{2,1,0:T(8,128)(2,1)}, u32[]{:S(2)}, u32[]{:S(2)}) %collective-permute-start.1) | collective-permute-done | bytes 1048608 | tf_op jit(solution)/shard_map/ppermute | solution.py:1003
  73.9 9.6 %shard_map.318 = (bf16[8,256,128]{2,1,0:T(8,128)(2,1)}, f32[128,2048]{1,0:T(8,128)}, f32[1,2048]{1,0:T(1,128)}) custom-call(s32[1]{0:T(128)} %dynamic_slice.99.length, bf16[8,848,128]{2,1,0:T(8,128)(2,1)} %copy-done.14), custom_call_target="tpu_custom_call" | custom-call | flops 1073741824 | bytes 3317764 | tf_op jit(solution)/shard_map/pallas_call | solution.py:467
  87.6 39.1 %all-to-all-done.1.mixed = bf16[8,256,128]{2,1,0:T(8,128)(2,1)S(1)} async-done(((bf16[8,256,128]{2,1,0:T(8,128)(2,1)}), bf16[8,256,128]{2,1,0:T(8,128)(2,1)S(1)}, u32[]{:S(2)}, u32[]{:S(2)}) %all-to-all-start.1) | async-done | bytes 524320 | tf_op jit(solution)/shard_map/all_to_all | solution.py:1217
  128.4 8.7 %shard_map.319 = (f32[512,1024]{1,0:T(8,128)}, f32[64,512]{1,0:T(8,128)}, bf16[2,272,1024]{2,1,0:T(8,128)(2,1)}, bf16[64,1024]{1,0:T(8,128)(2,1)}) custom-call(bf16[8,256,128]{2,1,0:T(8,128)(2,1)} %copy-done.10, f32[2,256,128]{2,1,0:T(8,128)} %get-tuple-element.160.gate, bf16[4,128,5120]{2,1,0:T(8,128)(2,1)} %w_out.3, bf16[2,256,1024]{2,1,0:T(8,128)(2,1)} %tok.5, ...), custom_call_target="tpu_custom_call" | custom-call | flops 2684354560 | bytes 12337152 | tf_op jit(solution)/shard_map/pallas_call | solution.py:467
  139.7 12.5 %collective-permute-done.12.refs_8_.refs_9_.refs_10_ = bf16[2,1024,256]{2,1,0:T(8,128)(2,1)} collective-permute-done((bf16[2,1024,256]{2,1,0:T(8,128)(2,1)}, bf16[2,1024,256]{2,1,0:T(8,128)(2,1)}, u32[]{:S(2)}, u32[]{:S(2)}) %collective-permute-start.12) | collective-permute-done | bytes 1048608 | tf_op jit(solution)/shard_map/ppermute | solution.py:1003
  153.6 10.3 %collective-permute-done.6.refs_0_.refs_1_ = bf16[2,272,1024]{2,1,0:T(8,128)(2,1)S(1)} collective-permute-done((bf16[2,272,1024]{2,1,0:T(8,128)(2,1)}, bf16[2,272,1024]{2,1,0:T(8,128)(2,1)S(1)}, u32[]{:S(2)}, u32[]{:S(2)}) %collective-permute-start.6) | collective-permute-done | bytes 1114144 | tf_op jit(solution)/shard_map/ppermute | solution.py:1003
  170.1 14.2 %shard_map.320 = (bf16[2,272,1024]{2,1,0:T(8,128)(2,1)}, bf16[8,512,256]{2,1,0:T(8,128)(2,1)}, bf16[8,512,256]{2,1,0:T(8,128)(2,1)}) custom-call(bf16[2,272,1024]{2,1,0:T(8,128)(2,1)} %copy-done.23, bf16[512,1024]{1,0:T(8,128)(2,1)} %collective-permute-done.refs_1_.refs_6_, bf16[2,1024,256]{2,1,0:T(8,128)(2,1)} %get-tuple-element.157.refs_2_.refs_3_.refs_4_, ...), custom_call_target="tpu_custom_call" | custom-call | flops 8589934592 | bytes 15859712 | tf_op jit(solution)/shard_map/pallas_call | solution.py:467
  184.3 23.0 %shard_map.321 = (bf16[2,272,1024]{2,1,0:T(8,128)(2,1)}, bf16[8,512,256]{2,1,0:T(8,128)(2,1)}, bf16[8,512,256]{2,1,0:T(8,128)(2,1)}) custom-call(bf16[2,272,1024]{2,1,0:T(8,128)(2,1)} %collective-permute-done.8.refs_0_.refs_2_, bf16[512,1024]{1,0:T(8,128)(2,1)} %collective-permute-done.4.refs_1_.refs_7_, ...), custom_call_target="tpu_custom_call" | custom-call | flops 8589934592 | bytes 15859712 | tf_op jit(solution)/shard_map/pallas_call | solution.py:467
  209.0 14.2 %shard_map.322 = (bf16[2,272,1024]{2,1,0:T(8,128)(2,1)}, bf16[8,512,256]{2,1,0:T(8,128)(2,1)}, bf16[8,512,256]{2,1,0:T(8,128)(2,1)}) custom-call(bf16[272,1024]{1,0:T(8,128)(2,1)} %copy-done.27, bf16[272,1024]{1,0:T(8,128)(2,1)} %copy-done.28, bf16[512,1024]{1,0:T(8,128)(2,1)} %collective-permute-done.5.refs_2_.refs_8_, ...), custom_call_target="tpu_custom_call" | custom-call | flops 8589934592 | bytes 15859712 | tf_op jit(solution)/shard_map/pallas_call | solution.py:467
  229.6 14.8 %shard_map.323 = (bf16[2,272,1024]{2,1,0:T(8,128)(2,1)}, bf16[8,512,256]{2,1,0:T(8,128)(2,1)}, bf16[8,512,256]{2,1,0:T(8,128)(2,1)}) custom-call(bf16[2,272,1024]{2,1,0:T(8,128)(2,1)} %get-tuple-element.161.refs_0_, bf16[512,1024]{1,0:T(8,128)(2,1)} %bitcast.203, bf16[2,1024,256]{2,1,0:T(8,128)(2,1)} %get-tuple-element.157.refs_2_.refs_3_.refs_4_, ...), custom_call_target="tpu_custom_call" | custom-call | flops 8589934592 | bytes 15859712 | tf_op jit(solution)/shard_map/pallas_call | solution.py:467
  244.4 28.0 %shard_map.324 = (bf16[2,2,1024,256]{3,2,1,0:T(8,128)(2,1)}, bf16[2,2,1024,256]{3,2,1,0:T(8,128)(2,1)}, bf16[2,2,1024,256]{3,2,1,0:T(8,128)(2,1)}, bf16[2,2,1024,256]{3,2,1,0:T(8,128)(2,1)}) custom-call(bf16[2,272,1024]{2,1,0:T(8,128)(2,1)} %get-tuple-element.161.refs_0_, bf16[2,272,1024]{2,1,0:T(8,128)(2,1)} %copy-done.23, ...), custom_call_target="tpu_custom_call" | custom-call | flops 17179869184 | bytes 33816576 | tf_op jit(solution)/shard_map/pallas_call | solution.py:467
  274.7 16.5 %shard_map.325 = (f32[512,1024]{1,0:T(8,128)}, bf16[8,256,128]{2,1,0:T(8,128)(2,1)}, f32[2,256,128]{2,1,0:T(8,128)}, f32[1024,128]{1,0:T(8,128)}) custom-call(s32[4]{0:T(128)} %pad_add_fusion.length, bf16[2,272,1024]{2,1,0:T(8,128)(2,1)} %get-tuple-element.174.r0, bf16[2,272,1024]{2,1,0:T(8,128)(2,1)} %copy-done.15, bf16[2,272,1024]{2,1,0:T(8,128)(2,1)} %copy-done.16, ...), custom_call_target="tpu_custom_call" | custom-call | flops 2684354560 | bytes 17317904 | tf_op jit(solution)/shard_map/pallas_call | solution.py:467
  298.1 9.7 %shard_map.326 = (bf16[8,1024,256]{2,1,0:T(8,128)(2,1)}, bf16[8,1024,256]{2,1,0:T(8,128)(2,1)}) custom-call(bf16[4,256,1024]{2,1,0:T(8,128)(2,1)} %copy-done.3, bf16[4,256,1024]{2,1,0:T(8,128)(2,1)} %copy-done.12, f32[1,1024]{1,0:T(1,128)} %bitcast.215, f32[1,1024]{1,0:T(1,128)} %bitcast.218), custom_call_target="tpu_custom_call" | custom-call | bytes 12591104 | tf_op jit(solution)/shard_map/pallas_call | solution.py:467
  307.8 7.3 %shard_map.327 = bf16[512,5120]{1,0:T(8,128)(2,1)} custom-call(bf16[8,256,128]{2,1,0:T(8,128)(2,1)} %copy-done.10, f32[2,256,128]{2,1,0:T(8,128)} %get-tuple-element.160.gate, f32[512,1024]{1,0:T(8,128)} %get-tuple-element.203.d_after), custom_call_target="tpu_custom_call" | custom-call | flops 2684354560 | bytes 8126464 | tf_op jit(solution)/shard_map/pallas_call | solution.py:467
  321.3 11.7 %shard_map.328.d_qkv = bf16[8,768,128]{2,1,0:T(8,128)(2,1)} custom-call(s32[1]{0:T(128)} %dynamic_slice.99.length, bf16[8,848,128]{2,1,0:T(8,128)(2,1)} %copy-done.14, bf16[8,256,128]{2,1,0:T(8,128)(2,1)} %copy-done.22, f32[128,2048]{1,0:T(8,128)} %get-tuple-element.207.out_t, f32[1,2048]{1,0:T(1,128)} %get-tuple-element.208.lse, ...), custom_call_target="tpu_custom_call" | custom-call | flops 2684354560 | bytes 6987780 | tf_op jit(solution)/shard_map/pallas_call | solution.py:467
  344.6 13.1 %shard_map.329 = bf16[1024,896]{1,0:T(8,128)(2,1)} custom-call(s32[1]{0:T(128)} %bitcast.spot, bf16[8,1024,256]{2,1,0:T(8,128)(2,1)} %get-tuple-element.204.tok_t, bf16[8,1024,256]{2,1,0:T(8,128)(2,1)} %get-tuple-element.205.norm_t, bf16[8,768,128]{2,1,0:T(8,128)(2,1)} %shard_map.328.d_qkv, bf16[8,848,128]{2,1,0:T(8,128)(2,1)} %copy-done.14), custom_call_target="tpu_custom_call" | custom-call | flops 3758096384 | bytes 13533188 | tf_op jit(solution)/shard_map/pallas_call | solution.py:467
  359.1 8.0 %collective-permute-done.22 = bf16[2,2,2,8,5120]{4,3,2,1,0:T(8,128)(2,1)} collective-permute-done((bf16[2,2,2,8,5120]{4,3,2,1,0:T(8,128)(2,1)}, bf16[2,2,2,8,5120]{4,3,2,1,0:T(8,128)(2,1)}, u32[]{:S(2)}, u32[]{:S(2)}) %collective-permute-start.22) | collective-permute-done | bytes 655392 | tf_op jit(solution)/shard_map/ppermute | solution.py:1003
  371.7 15.6 %shard_map.330 = (bf16[512,1024]{1,0:T(8,128)(2,1)}, bf16[512,1024]{1,0:T(8,128)(2,1)}, bf16[512,1024]{1,0:T(8,128)(2,1)}, bf16[512,1024]{1,0:T(8,128)(2,1)}) custom-call(bf16[8,512,256]{2,1,0:T(8,128)(2,1)} %get-tuple-element.215.refs_13_.refs_0_, bf16[8,512,256]{2,1,0:T(8,128)(2,1)} %get-tuple-element.168.refs_14_.refs_1_, ...), custom_call_target="tpu_custom_call" | custom-call | flops 8589934592 | bytes 20971520 | tf_op jit(solution)/shard_map/pallas_call | solution.py:467
  396.1 6.9 %collective-permute-done.27 = bf16[2,64,896]{2,1,0:T(8,128)(2,1)S(1)} collective-permute-done((bf16[2,64,896]{2,1,0:T(8,128)(2,1)S(1)}, bf16[2,64,896]{2,1,0:T(8,128)(2,1)S(1)}, u32[]{:S(2)}, u32[]{:S(2)}) %collective-permute-start.27) | collective-permute-done | bytes 229408 | tf_op jit(solution)/shard_map/ppermute | solution.py:1003
  409.5 11.9 %shard_map.331 = (bf16[512,1024]{1,0:T(8,128)(2,1)}, bf16[1024,128]{1,0:T(8,128)(2,1)}) custom-call(bf16[8,768,128]{2,1,0:T(8,128)(2,1)} %copy-done.4, bf16[2,256,1024]{2,1,0:T(8,128)(2,1)} %tok.5, f32[1,1024]{1,0:T(1,128)} %bitcast.216, f32[1,1024]{1,0:T(1,128)} %bitcast.219, bf16[1024,512]{1,0:T(8,128)(2,1)} %wq.3, bf16[1024,512]{1,0:T(8,128)(2,1)} %wk.3, ...), custom_call_target="tpu_custom_call" | custom-call | flops 3892314112 | bytes 17309696 | tf_op jit(solution)/shard_map/pallas_call | solution.py:467
  425.2 5.3 collective-permute-done.31
  446.8 6.8 %collective-permute-done.34 = bf16[2,8,5120]{2,1,0:T(8,128)(2,1)} collective-permute-done((bf16[2,8,5120]{2,1,0:T(8,128)(2,1)}, bf16[2,8,5120]{2,1,0:T(8,128)(2,1)}, u32[]{:S(2)}, u32[]{:S(2)}) %collective-permute-start.34) | collective-permute-done | bytes 163872 | tf_op jit(solution)/shard_map/ppermute | solution.py:1003
  463.6 5.8 collective-permute-done.37
  481.1 7.5 %collective-permute-done.42 = bf16[2,2,64,896]{3,2,1,0:T(8,128)(2,1)S(1)} collective-permute-done((bf16[2,2,64,896]{3,2,1,0:T(8,128)(2,1)S(1)}, bf16[2,2,64,896]{3,2,1,0:T(8,128)(2,1)S(1)}, u32[]{:S(2)}, u32[]{:S(2)}) %collective-permute-start.42) | collective-permute-done | bytes 458784 | tf_op jit(solution)/shard_map/ppermute | solution.py:1003
  502.3 5.2 collective-permute-done.49
  510.0 27.1 %collective-permute-done.48 = bf16[2,2,2,8,5120]{4,3,2,1,0:T(8,128)(2,1)S(1)} collective-permute-done((bf16[2,2,2,8,5120]{4,3,2,1,0:T(8,128)(2,1)S(1)}, bf16[2,2,2,8,5120]{4,3,2,1,0:T(8,128)(2,1)S(1)}, u32[]{:S(2)}, u32[]{:S(2)}) %collective-permute-start.48) | collective-permute-done | bytes 655392 | tf_op jit(solution)/shard_map/ppermute | solution.py:1003
  538.0 6.9 %all-to-all-done.5 = bf16[32,32,128]{2,1,0:T(8,128)(2,1)S(1)} async-done(((bf16[32,32,128]{2,1,0:T(8,128)(2,1)}), bf16[32,32,128]{2,1,0:T(8,128)(2,1)S(1)}, u32[]{:S(2)}, u32[]{:S(2)}) %all-to-all-start.5) | async-done | bytes 262176 | tf_op jit(solution)/shard_map/all_to_all | solution.py:1433
  556.0 6.7 %shard_map.333 = (f32[1024,512]{1,0:T(8,128)}, f32[1024,512]{1,0:T(8,128)}, f32[1024,2560]{1,0:T(8,128)}) custom-call(s32[5]{0:T(128)} %stack.237.bits, bf16[2,2,2,64,896]{4,3,2,1,0:T(8,128)(2,1)} %pad_maximum_fusion.3.refs_0_, bf16[2,2,2,64,896]{4,3,2,1,0:T(8,128)(2,1)} %collective-permute-done.46.refs_1_, ...), custom_call_target="tpu_custom_call" | custom-call | bytes 18350100 | tf_op jit(solution)/shard_map/pallas_call | solution.py:467
  568.5 6.7 %shard_map.335 = (f32[1024,512]{1,0:T(8,128)}, f32[1024,512]{1,0:T(8,128)}, f32[1024,2560]{1,0:T(8,128)}) custom-call(s32[5]{0:T(128)} %stack.237.bits, bf16[2,2,2,64,896]{4,3,2,1,0:T(8,128)(2,1)} %collective-permute-done.53.refs_0_, ...), custom_call_target="tpu_custom_call", output_to_operand_aliasing={{0}: (5, {}), {1}: (6, {}), {2}: (7, {})} | custom-call | bytes 33030164 | tf_op jit(solution)/shard_map/pallas_call | solution.py:467
  (274 shorter events, 179.5 us)
Async XLA Ops:
  16.2 50.9 %all-to-all-start = ((bf16[8,848,128]{2,1,0:T(8,128)(2,1)}), bf16[8,848,128]{2,1,0:T(8,128)(2,1)S(1)}, u32[]{:S(2)}, u32[]{:S(2)}) async-start(bf16[8,848,128]{2,1,0:T(8,128)(2,1)} %get-tuple-element.153), calls=%async_computation | async-start | bytes 3473408 | tf_op jit(solution)/shard_map/all_to_all | solution.py:1201
  25.1 42.0 %collective-permute-start.1 = (bf16[2,256,1024]{2,1,0:T(8,128)(2,1)S(1)}, bf16[2,256,1024]{2,1,0:T(8,128)(2,1)}, u32[]{:S(2)}, u32[]{:S(2)}) collective-permute-start(bf16[2,256,1024]{2,1,0:T(8,128)(2,1)S(1)} %copy-done.7), channel_id=1, source_target_pairs={{0,4},{1,5},{2,6},{3,7},{4,0},{5,1},{6,2},{7,3},{8,12},{9,13},{10,... | collective-permute-start | bytes 3145736 | tf_op jit(solution)/shard_map/ppermute | solution.py:1003
  67.1 59.5 %collective-permute-start.2 = (bf16[2,1024,256]{2,1,0:T(8,128)(2,1)}, bf16[2,1024,256]{2,1,0:T(8,128)(2,1)}, u32[]{:S(2)}, u32[]{:S(2)}) collective-permute-start(bf16[2,1024,256]{2,1,0:T(8,128)(2,1)} %get-tuple-element.157.refs_2_.refs_3_.refs_4_), channel_id=1, source_target_pairs={{0,16},{1,17},{2,18},{3,19},{4,20},{5,21},{6,22},{7,23},{8,24},{9,... | collective-permute-start | bytes 3145736 | tf_op jit(solution)/shard_map/ppermute | solution.py:1003
  69.5 57.2 %collective-permute-start.3 = (bf16[2,1024,256]{2,1,0:T(8,128)(2,1)}, bf16[2,1024,256]{2,1,0:T(8,128)(2,1)S(1)}, u32[]{:S(2)}, u32[]{:S(2)}) collective-permute-start(bf16[2,1024,256]{2,1,0:T(8,128)(2,1)} %get-tuple-element.157.refs_2_.refs_3_.refs_4_), channel_id=1, source_target_pairs={{0,8},{1,9},{2,10},{3,11},{4,12},{5,13},{6,14},{7,15},{8,0},{9,1},... | collective-permute-start | bytes 3145736 | tf_op jit(solution)/shard_map/ppermute | solution.py:1003
  70.9 55.7 %collective-permute-start.4 = (bf16[512,1024]{1,0:T(8,128)(2,1)}, bf16[512,1024]{1,0:T(8,128)(2,1)}, u32[]{:S(2)}, u32[]{:S(2)}) collective-permute-start(bf16[512,1024]{1,0:T(8,128)(2,1)} %bitcast.201), channel_id=1, source_target_pairs={{0,4},{1,5},{2,6},{3,7},{4,0},{5,1},{6,2},{7,3},{8,12},{9,13},{10,... | collective-permute-start | bytes 3145736 | tf_op jit(solution)/shard_map/ppermute | solution.py:1003
  71.2 55.4 %collective-permute-start.5 = (bf16[512,1024]{1,0:T(8,128)(2,1)}, bf16[512,1024]{1,0:T(8,128)(2,1)}, u32[]{:S(2)}, u32[]{:S(2)}) collective-permute-start(bf16[512,1024]{1,0:T(8,128)(2,1)} %bitcast.202), channel_id=1, source_target_pairs={{0,6},{1,7},{2,4},{3,5},{4,2},{5,3},{6,0},{7,1},{8,14},{9,15},{10,... | collective-permute-start | bytes 3145736 | tf_op jit(solution)/shard_map/ppermute | solution.py:1003
  83.5 43.1 %all-to-all-start.1 = ((bf16[8,256,128]{2,1,0:T(8,128)(2,1)}), bf16[8,256,128]{2,1,0:T(8,128)(2,1)S(1)}, u32[]{:S(2)}, u32[]{:S(2)}) async-start(bf16[8,256,128]{2,1,0:T(8,128)(2,1)} %get-tuple-element.156), calls=%async_computation.1 | async-start | bytes 1048576 | tf_op jit(solution)/shard_map/all_to_all | solution.py:1217
  137.1 26.8 %collective-permute-start.6 = (bf16[2,272,1024]{2,1,0:T(8,128)(2,1)}, bf16[2,272,1024]{2,1,0:T(8,128)(2,1)S(1)}, u32[]{:S(2)}, u32[]{:S(2)}) collective-permute-start(bf16[2,272,1024]{2,1,0:T(8,128)(2,1)} %get-tuple-element.161.refs_0_), channel_id=1, source_target_pairs={{0,2},{1,3},{2,0},{3,1},{4,6},{5,7},{6,4},{7,5},{8,10},{9,11},{10,... | collective-permute-start | bytes 3342344 | tf_op jit(solution)/shard_map/ppermute | solution.py:1003
  138.7 26.5 %collective-permute-start.8 = (bf16[2,272,1024]{2,1,0:T(8,128)(2,1)}, bf16[2,272,1024]{2,1,0:T(8,128)(2,1)}, u32[]{:S(2)}, u32[]{:S(2)}) collective-permute-start(bf16[2,272,1024]{2,1,0:T(8,128)(2,1)} %get-tuple-element.161.refs_0_), channel_id=1, source_target_pairs={{0,4},{1,5},{2,6},{3,7},{4,0},{5,1},{6,2},{7,3},{8,12},{9,13},{10,... | collective-permute-start | bytes 3342344 | tf_op jit(solution)/shard_map/ppermute | solution.py:1003
  139.2 29.4 %collective-permute-start.10 = (bf16[2,1024,256]{2,1,0:T(8,128)(2,1)}, bf16[2,1024,256]{2,1,0:T(8,128)(2,1)}, u32[]{:S(2)}, u32[]{:S(2)}) collective-permute-start(bf16[2,1024,256]{2,1,0:T(8,128)(2,1)} %copy-done.26), channel_id=1, source_target_pairs={{0,1},{1,0},{2,3},{3,2},{4,5},{5,4},{6,7},{7,6},{8,9},{9,8},{10,11... | collective-permute-start | bytes 3145736 | tf_op jit(solution)/shard_map/ppermute | solution.py:1003
  139.2 31.0 %collective-permute-start.11 = (bf16[2,1024,256]{2,1,0:T(8,128)(2,1)}, bf16[2,1024,256]{2,1,0:T(8,128)(2,1)}, u32[]{:S(2)}, u32[]{:S(2)}) collective-permute-start(bf16[2,1024,256]{2,1,0:T(8,128)(2,1)} %collective-permute-done.2.refs_6_.refs_7_.refs_8_), channel_id=1, source_target_pairs={{0,1},{1,0},{2,3},{3,2},{4,5},{5,4},{6,7},{7,6},{8,9},{9,8},{10,11... | collective-permute-start | bytes 3145736 | tf_op jit(solution)/shard_map/ppermute | solution.py:1003
  163.9 62.8 %collective-permute-start.17 = (bf16[2,256,1024]{2,1,0:T(8,128)(2,1)S(1)}, bf16[2,256,1024]{2,1,0:T(8,128)(2,1)S(1)}, u32[]{:S(2)}, u32[]{:S(2)}) collective-permute-start(bf16[2,256,1024]{2,1,0:T(8,128)(2,1)S(1)} %pad_maximum_fusion.2), channel_id=1, source_target_pairs={{0,16},{1,17},{2,18},{3,19},{4,20},{5,21},{6,22},{7,23},{8,24},{9,... | collective-permute-start | bytes 3145736 | tf_op jit(solution)/shard_map/ppermute | solution.py:1003
  165.2 42.1 %collective-permute-start.7 = (bf16[272,1024]{1,0:T(8,128)(2,1)S(1)}, bf16[272,1024]{1,0:T(8,128)(2,1)S(1)}, u32[]{:S(2)}, u32[]{:S(2)}) collective-permute-start(bf16[272,1024]{1,0:T(8,128)(2,1)S(1)} %slice_bitcast_fusion.1), channel_id=1, source_target_pairs={{0,4},{1,5},{2,6},{3,7},{4,0},{5,1},{6,2},{7,3},{8,12},{9,13},{10,... | collective-permute-start | bytes 1671176 | tf_op jit(solution)/shard_map/ppermute | solution.py:1003
  168.6 38.8 %collective-permute-start.9 = (bf16[272,1024]{1,0:T(8,128)(2,1)S(1)}, bf16[272,1024]{1,0:T(8,128)(2,1)S(1)}, u32[]{:S(2)}, u32[]{:S(2)}) collective-permute-start(bf16[272,1024]{1,0:T(8,128)(2,1)S(1)} %slice_bitcast_fusion), channel_id=1, source_target_pairs={{0,2},{1,3},{2,0},{3,1},{4,6},{5,7},{6,4},{7,5},{8,10},{9,11},{10,... | collective-permute-start | bytes 1671176 | tf_op jit(solution)/shard_map/ppermute | solution.py:1003
  223.2 49.9 %collective-permute-start.14 = (bf16[2,272,1024]{2,1,0:T(8,128)(2,1)}, bf16[2,272,1024]{2,1,0:T(8,128)(2,1)S(1)}, u32[]{:S(2)}, u32[]{:S(2)}) collective-permute-start(bf16[2,272,1024]{2,1,0:T(8,128)(2,1)} %get-tuple-element.175), channel_id=1, source_target_pairs={{0,2},{1,3},{2,0},{3,1},{4,6},{5,7},{6,4},{7,5},{8,10},{9,11},{10,... | collective-permute-start | bytes 3342344 | tf_op jit(solution)/shard_map/ppermute | solution.py:1003
  223.7 49.4 %collective-permute-start.15 = (bf16[2,272,1024]{2,1,0:T(8,128)(2,1)}, bf16[2,272,1024]{2,1,0:T(8,128)(2,1)S(1)}, u32[]{:S(2)}, u32[]{:S(2)}) collective-permute-start(bf16[2,272,1024]{2,1,0:T(8,128)(2,1)} %get-tuple-element.176), channel_id=1, source_target_pairs={{0,4},{1,5},{2,6},{3,7},{4,0},{5,1},{6,2},{7,3},{8,12},{9,13},{10,... | collective-permute-start | bytes 3342344 | tf_op jit(solution)/shard_map/ppermute | solution.py:1003
  223.7 49.3 %collective-permute-start.16 = (bf16[2,272,1024]{2,1,0:T(8,128)(2,1)}, bf16[2,272,1024]{2,1,0:T(8,128)(2,1)S(1)}, u32[]{:S(2)}, u32[]{:S(2)}) collective-permute-start(bf16[2,272,1024]{2,1,0:T(8,128)(2,1)} %get-tuple-element.177), channel_id=1, source_target_pairs={{0,6},{1,7},{2,4},{3,5},{4,2},{5,3},{6,0},{7,1},{8,14},{9,15},{10,... | collective-permute-start | bytes 3342344 | tf_op jit(solution)/shard_map/ppermute | solution.py:1003
  229.1 44.9 %collective-permute-start.18 = (bf16[4,256,1024]{2,1,0:T(8,128)(2,1)S(1)}, bf16[4,256,1024]{2,1,0:T(8,128)(2,1)S(1)}, u32[]{:S(2)}, u32[]{:S(2)}) collective-permute-start(bf16[4,256,1024]{2,1,0:T(8,128)(2,1)S(1)} %pad_maximum_fusion.1.near), channel_id=1, source_target_pairs={{0,8},{1,9},{2,10},{3,11},{4,12},{5,13},{6,14},{7,15},{8,0},{9,1},... | collective-permute-start | bytes 6291464 | tf_op jit(solution)/shard_map/ppermute | solution.py:1003
  319.2 122.3 %collective-permute-start.40 = (bf16[2,2,1024,256]{3,2,1,0:T(8,128)(2,1)}, bf16[2,2,1024,256]{3,2,1,0:T(8,128)(2,1)}, u32[]{:S(2)}, u32[]{:S(2)}) collective-permute-start(bf16[2,2,1024,256]{3,2,1,0:T(8,128)(2,1)} %get-tuple-element.239), channel_id=1, source_target_pairs={{0,1},{1,0},{2,3},{3,2},{4,5},{5,4},{6,7},{7,6},{8,9},{9,8},{10,11... | collective-permute-start | bytes 6291464 | tf_op jit(solution)/shard_map/ppermute | solution.py:1003
  319.4 120.2 %collective-permute-start.41 = (bf16[2,1024,256]{2,1,0:T(8,128)(2,1)}, bf16[2,1024,256]{2,1,0:T(8,128)(2,1)}, u32[]{:S(2)}, u32[]{:S(2)}) collective-permute-start(bf16[2,1024,256]{2,1,0:T(8,128)(2,1)} %get-tuple-element.291), channel_id=1, source_target_pairs={{0,8},{1,9},{2,10},{3,11},{4,12},{5,13},{6,14},{7,15},{8,0},{9,1},... | collective-permute-start | bytes 3145736 | tf_op jit(solution)/shard_map/ppermute | solution.py:1003
  339.2 27.9 %collective-permute-start.22 = (bf16[2,2,2,8,5120]{4,3,2,1,0:T(8,128)(2,1)}, bf16[2,2,2,8,5120]{4,3,2,1,0:T(8,128)(2,1)}, u32[]{:S(2)}, u32[]{:S(2)}) collective-permute-start(bf16[2,2,2,8,5120]{4,3,2,1,0:T(8,128)(2,1)} %dynamic-slice_bitcast_fusion.2), channel_id=1, source_target_pairs={{0,4},{1,5},{2,6},{3,7},{4,0},{5,1},{6,2},{7,3},{8,12},{9,13},{10,... | collective-permute-start | bytes 1966088 | tf_op jit(solution)/shard_map/ppermute | solution.py:1003
  340.7 67.1 %all-to-all-start.3 = ((bf16[8,768,128]{2,1,0:T(8,128)(2,1)}), bf16[8,768,128]{2,1,0:T(8,128)(2,1)S(1)}, u32[]{:S(2)}, u32[]{:S(2)}) async-start(bf16[8,768,128]{2,1,0:T(8,128)(2,1)} %shard_map.328.d_qkv), calls=%async_computation.3 | async-start | bytes 3145728 | tf_op jit(solution)/shard_map/all_to_all | solution.py:1378
  395.4 35.8 %collective-permute-start.32 = (bf16[512,1024]{1,0:T(8,128)(2,1)}, bf16[512,1024]{1,0:T(8,128)(2,1)}, u32[]{:S(2)}, u32[]{:S(2)}) collective-permute-start(bf16[512,1024]{1,0:T(8,128)(2,1)} %get-tuple-element.229), channel_id=1, source_target_pairs={{0,4},{1,5},{2,6},{3,7},{4,0},{5,1},{6,2},{7,3},{8,12},{9,13},{10,... | collective-permute-start | bytes 3145736 | tf_op jit(solution)/shard_map/ppermute | solution.py:1003
  434.3 35.3 %all-to-all-start.4 = ((bf16[32,32,128]{2,1,0:T(8,128)(2,1)}), bf16[32,32,128]{2,1,0:T(8,128)(2,1)S(1)}, u32[]{:S(2)}, u32[]{:S(2)}) async-start(bf16[32,32,128]{2,1,0:T(8,128)(2,1)} %bitcast.209), calls=%async_computation.4 | async-start | bytes 524288 | tf_op jit(solution)/shard_map/all_to_all | solution.py:1419
  439.6 30.0 %collective-permute-start.38 = (bf16[512,1024]{1,0:T(8,128)(2,1)S(1)}, bf16[512,1024]{1,0:T(8,128)(2,1)}, u32[]{:S(2)}, u32[]{:S(2)}) collective-permute-start(bf16[512,1024]{1,0:T(8,128)(2,1)S(1)} %add_convert_fusion), channel_id=1, source_target_pairs={{0,2},{1,3},{2,0},{3,1},{4,6},{5,7},{6,4},{7,5},{8,10},{9,11},{10,... | collective-permute-start | bytes 3145736 | tf_op jit(solution)/shard_map/ppermute | solution.py:1003
  441.4 28.1 %collective-permute-start.39 = (bf16[512,1024]{1,0:T(8,128)(2,1)}, bf16[512,1024]{1,0:T(8,128)(2,1)}, u32[]{:S(2)}, u32[]{:S(2)}) collective-permute-start(bf16[512,1024]{1,0:T(8,128)(2,1)} %get-tuple-element.238), channel_id=1, source_target_pairs={{0,4},{1,5},{2,6},{3,7},{4,0},{5,1},{6,2},{7,3},{8,12},{9,13},{10,... | collective-permute-start | bytes 3145736 | tf_op jit(solution)/shard_map/ppermute | solution.py:1003
  491.7 46.3 %collective-permute-start.51 = (bf16[2,1024,256]{2,1,0:T(8,128)(2,1)}, bf16[2,1024,256]{2,1,0:T(8,128)(2,1)}, u32[]{:S(2)}, u32[]{:S(2)}) collective-permute-start(bf16[2,1024,256]{2,1,0:T(8,128)(2,1)} %get-tuple-element.254), channel_id=1, source_target_pairs={{0,8},{1,9},{2,10},{3,11},{4,12},{5,13},{6,14},{7,15},{8,0},{9,1},... | collective-permute-start | bytes 3145736 | tf_op jit(solution)/shard_map/ppermute | solution.py:1003
  492.7 52.2 %collective-permute-start.50 = (bf16[2,1024,256]{2,1,0:T(8,128)(2,1)}, bf16[2,1024,256]{2,1,0:T(8,128)(2,1)}, u32[]{:S(2)}, u32[]{:S(2)}) collective-permute-start(bf16[2,1024,256]{2,1,0:T(8,128)(2,1)} %fusion.3), channel_id=1, source_target_pairs={{0,16},{1,17},{2,18},{3,19},{4,20},{5,21},{6,22},{7,23},{8,24},{9,... | collective-permute-start | bytes 3145736 | tf_op jit(solution)/shard_map/ppermute | solution.py:1003
  495.5 49.4 %all-to-all-start.5 = ((bf16[32,32,128]{2,1,0:T(8,128)(2,1)}), bf16[32,32,128]{2,1,0:T(8,128)(2,1)S(1)}, u32[]{:S(2)}, u32[]{:S(2)}) async-start(bf16[32,32,128]{2,1,0:T(8,128)(2,1)} %broadcast_in_dim.8), calls=%async_computation.5 | async-start | bytes 524288 | tf_op jit(solution)/shard_map/all_to_all | solution.py:1433
  498.8 46.1 %collective-permute-start.46 = (bf16[2,2,2,64,896]{4,3,2,1,0:T(8,128)(2,1)}, bf16[2,2,2,64,896]{4,3,2,1,0:T(8,128)(2,1)}, u32[]{:S(2)}, u32[]{:S(2)}) collective-permute-start(bf16[2,2,2,64,896]{4,3,2,1,0:T(8,128)(2,1)} %pad_maximum_fusion.3.refs_0_), channel_id=1, source_target_pairs={{0,2},{1,3},{2,0},{3,1},{4,6},{5,7},{6,4},{7,5},{8,10},{9,11},{10,... | collective-permute-start | bytes 2752520 | tf_op jit(solution)/shard_map/ppermute | solution.py:1003
  500.8 44.1 %collective-permute-start.47 = (bf16[2,2,2,64,896]{4,3,2,1,0:T(8,128)(2,1)}, bf16[2,2,2,64,896]{4,3,2,1,0:T(8,128)(2,1)}, u32[]{:S(2)}, u32[]{:S(2)}) collective-permute-start(bf16[2,2,2,64,896]{4,3,2,1,0:T(8,128)(2,1)} %pad_maximum_fusion.4.refs_2_), channel_id=1, source_target_pairs={{0,4},{1,5},{2,6},{3,7},{4,0},{5,1},{6,2},{7,3},{8,12},{9,13},{10,... | collective-permute-start | bytes 2752520 | tf_op jit(solution)/shard_map/ppermute | solution.py:1003
  507.5 29.6 %collective-permute-start.48 = (bf16[2,2,2,8,5120]{4,3,2,1,0:T(8,128)(2,1)S(1)}, bf16[2,2,2,8,5120]{4,3,2,1,0:T(8,128)(2,1)S(1)}, u32[]{:S(2)}, u32[]{:S(2)}) collective-permute-start(bf16[2,2,2,8,5120]{4,3,2,1,0:T(8,128)(2,1)S(1)} %pad_maximum_fusion.7), channel_id=1, source_target_pairs={{0,2},{1,3},{2,0},{3,1},{4,6},{5,7},{6,4},{7,5},{8,10},{9,11},{10,... | collective-permute-start | bytes 1966088 | tf_op jit(solution)/shard_map/ppermute | solution.py:1003
  (65 other events, 908.6 us)

commit v6 on v5

--- a/solution.py
+++ b/solution.py
@@ -675,6 +675,16 @@
     return hit.astype(FULL_TYPE).astype(HALF_TYPE)
 
 
+def gate_lanes(rows, first):
+    row = lane_ids((rows, LANES), 0)
+    lane = lane_ids((rows, LANES), 1)
+    hit = None
+    for i in range(rows // LANES):
+        inside = (row >= i * LANES) & (row < (i + 1) * LANES) & (lane == first + i)
+        hit = inside if hit is None else hit | inside
+    return hit.astype(FULL_TYPE).astype(HALF_TYPE)
+
+
 def experts_kernel(kind, halves, *refs):
     rows_in, cot, pieces = refs[:halves], refs[halves], refs[halves + 1:halves + 9]
     back, inner, d_pre = refs[halves + 9:]
@@ -703,11 +713,12 @@
         slope = half + act * (1.0 - tanh) * (root + (3 * root * cube) * square)
         d_pre[p] = (slope * gate_wide * d_in).astype(HALF_TYPE)
         inner[p] = (act * gate_wide).astype(HALF_TYPE)
-        g = nt(spread, (d_in * act).astype(HALF_TYPE))
+        g = nn((d_in * act).astype(HALF_TYPE), gate_lanes(cols, p * (cols // LANES)))
         gate_total = g if p == 0 else gate_total + g
     for p in range(8):
         r = nt(d_pre[p], weight(p, 0))
         row_total = r if p == 0 else row_total + r
+    gate_total = jnp.transpose(gate_total)[0:quarter]
     for s in range(seqs):
         here = slice(s * row_count, (s + 1) * row_count)
         back[s, 0:row_count] = row_total[here].astype(HALF_TYPE)

time: 597 us -> 595 us (level)
  transfers between devices with their start and end apart: 66 -> 66, of which waited for: 24 -> 24; matrix products, arithmetic and copies ran while one was open for 7% -> 7% of each run, Pallas kernels for 40% -> 39%
where the time goes in v6:
time: 595 us; the launch traced here: 586 us
  Pallas kernels  245 us (41%)
  waiting for transfers between devices  194 us (33%)
  starting transfers between devices  91.4 us (15%)
  other arithmetic  29.9 us (5%)
  local copies, waits for them, and re-layouts  22.7 us (4%)
    pallas_call x24, Pallas kernels, call(): pl.pallas_call(kernel, out_shape=out_shape, input_output_aliases=aliases...  245 us
    ppermute x60, waiting for transfers between devices, send(): return lax.ppermute(value, ('wide', 'narrow'), self.pairs(move))  148 us
    ppermute x60, starting transfers between devices, send(): return lax.ppermute(value, ('wide', 'narrow'), self.pairs(move))  66.1 us
    all_to_all x1, waiting for transfers between devices, tuned_device(): mixed = lax.all_to_all(mixed, 'wide', 0, 0, tiled=True)  39.1 us
    convert_element_type x12, other arithmetic, add(): return total.astype(HALF_TYPE)  18.3 us
  transfers between devices with their start and end apart: 66, of which 24 were waited for; matrix products, arithmetic and copies ran while one was open for 7% of the time, Pallas kernels for 39%

profile of v6, /device:TPU:0, one launch (start us, length us, event | category | flops | bytes accessed | tf_op | source)
XLA Modules:
  0.0 585.7 jit_solution(13609776750879914929)
XLA Ops:
  5.1 11.1 %shard_map.316 = (bf16[8,848,128]{2,1,0:T(8,128)(2,1)}, bf16[2,256,2560]{2,1,0:T(8,128)(2,1)}, f32[2,256,128]{2,1,0:T(8,128)}) custom-call(s32[1]{0:T(128)} %bitcast.spot, bf16[2,256,1024]{2,1,0:T(8,128)(2,1)} %tok.5, f32[1,1024]{1,0:T(1,128)} %bitcast.214, f32[1,1024]{1,0:T(1,128)} %bitcast.217, bf16[1024,512]{1,0:T(8,128)(2,1)} %wq.3, ...), custom_call_target="tpu_custom_call" | custom-call | flops 3892314112 | bytes 15425540 | tf_op jit(solution)/shard_map/pallas_call | solution.py:467
  16.2 7.4 %all-to-all-start = ((bf16[8,848,128]{2,1,0:T(8,128)(2,1)}), bf16[8,848,128]{2,1,0:T(8,128)(2,1)S(1)}, u32[]{:S(2)}, u32[]{:S(2)}) async-start(bf16[8,848,128]{2,1,0:T(8,128)(2,1)} %get-tuple-element.153), calls=%async_computation | async-start | bytes 3473408 | tf_op jit(solution)/shard_map/all_to_all | solution.py:1212
  32.1 16.4 %collective-permute-done.refs_1_.refs_6_ = bf16[512,1024]{1,0:T(8,128)(2,1)} collective-permute-done((bf16[512,1024]{1,0:T(8,128)(2,1)}, bf16[512,1024]{1,0:T(8,128)(2,1)}, u32[]{:S(2)}, u32[]{:S(2)}) %collective-permute-start) | collective-permute-done | bytes 1048608 | tf_op jit(solution)/shard_map/ppermute | solution.py:1014
  48.5 18.6 %collective-permute-done.1 = bf16[2,256,1024]{2,1,0:T(8,128)(2,1)} collective-permute-done((bf16[2,256,1024]{2,1,0:T(8,128)(2,1)S(1)}, bf16[2,256,1024]{2,1,0:T(8,128)(2,1)}, u32[]{:S(2)}, u32[]{:S(2)}) %collective-permute-start.1) | collective-permute-done | bytes 1048608 | tf_op jit(solution)/shard_map/ppermute | solution.py:1014
  73.9 9.6 %shard_map.318 = (bf16[8,256,128]{2,1,0:T(8,128)(2,1)}, f32[128,2048]{1,0:T(8,128)}, f32[1,2048]{1,0:T(1,128)}) custom-call(s32[1]{0:T(128)} %dynamic_slice.99.length, bf16[8,848,128]{2,1,0:T(8,128)(2,1)} %copy-done.14), custom_call_target="tpu_custom_call" | custom-call | flops 1073741824 | bytes 3317764 | tf_op jit(solution)/shard_map/pallas_call | solution.py:467
  87.6 39.1 %all-to-all-done.1.mixed = bf16[8,256,128]{2,1,0:T(8,128)(2,1)S(1)} async-done(((bf16[8,256,128]{2,1,0:T(8,128)(2,1)}), bf16[8,256,128]{2,1,0:T(8,128)(2,1)S(1)}, u32[]{:S(2)}, u32[]{:S(2)}) %all-to-all-start.1) | async-done | bytes 524320 | tf_op jit(solution)/shard_map/all_to_all | solution.py:1228
  128.4 8.7 %shard_map.319 = (f32[512,1024]{1,0:T(8,128)}, f32[64,512]{1,0:T(8,128)}, bf16[2,272,1024]{2,1,0:T(8,128)(2,1)}, bf16[64,1024]{1,0:T(8,128)(2,1)}) custom-call(bf16[8,256,128]{2,1,0:T(8,128)(2,1)} %copy-done.10, f32[2,256,128]{2,1,0:T(8,128)} %get-tuple-element.160.gate, bf16[4,128,5120]{2,1,0:T(8,128)(2,1)} %w_out.3, bf16[2,256,1024]{2,1,0:T(8,128)(2,1)} %tok.5, ...), custom_call_target="tpu_custom_call" | custom-call | flops 2684354560 | bytes 12337152 | tf_op jit(solution)/shard_map/pallas_call | solution.py:467
  139.7 12.5 %collective-permute-done.12.refs_8_.refs_9_.refs_10_ = bf16[2,1024,256]{2,1,0:T(8,128)(2,1)} collective-permute-done((bf16[2,1024,256]{2,1,0:T(8,128)(2,1)}, bf16[2,1024,256]{2,1,0:T(8,128)(2,1)}, u32[]{:S(2)}, u32[]{:S(2)}) %collective-permute-start.12) | collective-permute-done | bytes 1048608 | tf_op jit(solution)/shard_map/ppermute | solution.py:1014
  153.6 10.3 %collective-permute-done.6.refs_0_.refs_1_ = bf16[2,272,1024]{2,1,0:T(8,128)(2,1)S(1)} collective-permute-done((bf16[2,272,1024]{2,1,0:T(8,128)(2,1)}, bf16[2,272,1024]{2,1,0:T(8,128)(2,1)S(1)}, u32[]{:S(2)}, u32[]{:S(2)}) %collective-permute-start.6) | collective-permute-done | bytes 1114144 | tf_op jit(solution)/shard_map/ppermute | solution.py:1014
  170.1 13.3 %shard_map.320 = (bf16[2,272,1024]{2,1,0:T(8,128)(2,1)}, bf16[8,512,256]{2,1,0:T(8,128)(2,1)}, bf16[8,512,256]{2,1,0:T(8,128)(2,1)}) custom-call(bf16[2,272,1024]{2,1,0:T(8,128)(2,1)} %copy-done.23, bf16[512,1024]{1,0:T(8,128)(2,1)} %collective-permute-done.refs_1_.refs_6_, bf16[2,1024,256]{2,1,0:T(8,128)(2,1)} %get-tuple-element.157.refs_2_.refs_3_.refs_4_, ...), custom_call_target="tpu_custom_call" | custom-call | flops 8589934592 | bytes 15859712 | tf_op jit(solution)/shard_map/pallas_call | solution.py:467
  183.4 22.1 %shard_map.321 = (bf16[2,272,1024]{2,1,0:T(8,128)(2,1)}, bf16[8,512,256]{2,1,0:T(8,128)(2,1)}, bf16[8,512,256]{2,1,0:T(8,128)(2,1)}) custom-call(bf16[2,272,1024]{2,1,0:T(8,128)(2,1)} %collective-permute-done.8.refs_0_.refs_2_, bf16[512,1024]{1,0:T(8,128)(2,1)} %collective-permute-done.4.refs_1_.refs_7_, ...), custom_call_target="tpu_custom_call" | custom-call | flops 8589934592 | bytes 15859712 | tf_op jit(solution)/shard_map/pallas_call | solution.py:467
  207.2 13.3 %shard_map.322 = (bf16[2,272,1024]{2,1,0:T(8,128)(2,1)}, bf16[8,512,256]{2,1,0:T(8,128)(2,1)}, bf16[8,512,256]{2,1,0:T(8,128)(2,1)}) custom-call(bf16[272,1024]{1,0:T(8,128)(2,1)} %copy-done.27, bf16[272,1024]{1,0:T(8,128)(2,1)} %copy-done.28, bf16[512,1024]{1,0:T(8,128)(2,1)} %collective-permute-done.5.refs_2_.refs_8_, ...), custom_call_target="tpu_custom_call" | custom-call | flops 8589934592 | bytes 15859712 | tf_op jit(solution)/shard_map/pallas_call | solution.py:467
  227.3 13.4 %shard_map.323 = (bf16[2,272,1024]{2,1,0:T(8,128)(2,1)}, bf16[8,512,256]{2,1,0:T(8,128)(2,1)}, bf16[8,512,256]{2,1,0:T(8,128)(2,1)}) custom-call(bf16[2,272,1024]{2,1,0:T(8,128)(2,1)} %get-tuple-element.161.refs_0_, bf16[512,1024]{1,0:T(8,128)(2,1)} %bitcast.203, bf16[2,1024,256]{2,1,0:T(8,128)(2,1)} %get-tuple-element.157.refs_2_.refs_3_.refs_4_, ...), custom_call_target="tpu_custom_call" | custom-call | flops 8589934592 | bytes 15859712 | tf_op jit(solution)/shard_map/pallas_call | solution.py:467
  240.8 28.0 %shard_map.324 = (bf16[2,2,1024,256]{3,2,1,0:T(8,128)(2,1)}, bf16[2,2,1024,256]{3,2,1,0:T(8,128)(2,1)}, bf16[2,2,1024,256]{3,2,1,0:T(8,128)(2,1)}, bf16[2,2,1024,256]{3,2,1,0:T(8,128)(2,1)}) custom-call(bf16[2,272,1024]{2,1,0:T(8,128)(2,1)} %get-tuple-element.161.refs_0_, bf16[2,272,1024]{2,1,0:T(8,128)(2,1)} %copy-done.23, ...), custom_call_target="tpu_custom_call" | custom-call | flops 17179869184 | bytes 33816576 | tf_op jit(solution)/shard_map/pallas_call | solution.py:467
  272.5 16.5 %shard_map.325 = (f32[512,1024]{1,0:T(8,128)}, bf16[8,256,128]{2,1,0:T(8,128)(2,1)}, f32[2,256,128]{2,1,0:T(8,128)}, f32[1024,128]{1,0:T(8,128)}) custom-call(s32[4]{0:T(128)} %pad_add_fusion.length, bf16[2,272,1024]{2,1,0:T(8,128)(2,1)} %get-tuple-element.174.r0, bf16[2,272,1024]{2,1,0:T(8,128)(2,1)} %copy-done.15, bf16[2,272,1024]{2,1,0:T(8,128)(2,1)} %copy-done.16, ...), custom_call_target="tpu_custom_call" | custom-call | flops 2684354560 | bytes 17317904 | tf_op jit(solution)/shard_map/pallas_call | solution.py:467
  295.8 9.7 %shard_map.326 = (bf16[8,1024,256]{2,1,0:T(8,128)(2,1)}, bf16[8,1024,256]{2,1,0:T(8,128)(2,1)}) custom-call(bf16[4,256,1024]{2,1,0:T(8,128)(2,1)} %copy-done.3, bf16[4,256,1024]{2,1,0:T(8,128)(2,1)} %copy-done.12, f32[1,1024]{1,0:T(1,128)} %bitcast.215, f32[1,1024]{1,0:T(1,128)} %bitcast.218), custom_call_target="tpu_custom_call" | custom-call | bytes 12591104 | tf_op jit(solution)/shard_map/pallas_call | solution.py:467
  305.6 7.3 %shard_map.327 = bf16[512,5120]{1,0:T(8,128)(2,1)} custom-call(bf16[8,256,128]{2,1,0:T(8,128)(2,1)} %copy-done.10, f32[2,256,128]{2,1,0:T(8,128)} %get-tuple-element.160.gate, f32[512,1024]{1,0:T(8,128)} %get-tuple-element.203.d_after), custom_call_target="tpu_custom_call" | custom-call | flops 2684354560 | bytes 8126464 | tf_op jit(solution)/shard_map/pallas_call | solution.py:467
  319.0 11.7 %shard_map.328.d_qkv = bf16[8,768,128]{2,1,0:T(8,128)(2,1)} custom-call(s32[1]{0:T(128)} %dynamic_slice.99.length, bf16[8,848,128]{2,1,0:T(8,128)(2,1)} %copy-done.14, bf16[8,256,128]{2,1,0:T(8,128)(2,1)} %copy-done.22, f32[128,2048]{1,0:T(8,128)} %get-tuple-element.207.out_t, f32[1,2048]{1,0:T(1,128)} %get-tuple-element.208.lse, ...), custom_call_target="tpu_custom_call" | custom-call | flops 2684354560 | bytes 6987780 | tf_op jit(solution)/shard_map/pallas_call | solution.py:467
  342.3 13.1 %shard_map.329 = bf16[1024,896]{1,0:T(8,128)(2,1)} custom-call(s32[1]{0:T(128)} %bitcast.spot, bf16[8,1024,256]{2,1,0:T(8,128)(2,1)} %get-tuple-element.204.tok_t, bf16[8,1024,256]{2,1,0:T(8,128)(2,1)} %get-tuple-element.205.norm_t, bf16[8,768,128]{2,1,0:T(8,128)(2,1)} %shard_map.328.d_qkv, bf16[8,848,128]{2,1,0:T(8,128)(2,1)} %copy-done.14), custom_call_target="tpu_custom_call" | custom-call | flops 3758096384 | bytes 13533188 | tf_op jit(solution)/shard_map/pallas_call | solution.py:467
  356.8 8.0 %collective-permute-done.22 = bf16[2,2,2,8,5120]{4,3,2,1,0:T(8,128)(2,1)} collective-permute-done((bf16[2,2,2,8,5120]{4,3,2,1,0:T(8,128)(2,1)}, bf16[2,2,2,8,5120]{4,3,2,1,0:T(8,128)(2,1)}, u32[]{:S(2)}, u32[]{:S(2)}) %collective-permute-start.22) | collective-permute-done | bytes 655392 | tf_op jit(solution)/shard_map/ppermute | solution.py:1014
  369.4 15.6 %shard_map.330 = (bf16[512,1024]{1,0:T(8,128)(2,1)}, bf16[512,1024]{1,0:T(8,128)(2,1)}, bf16[512,1024]{1,0:T(8,128)(2,1)}, bf16[512,1024]{1,0:T(8,128)(2,1)}) custom-call(bf16[8,512,256]{2,1,0:T(8,128)(2,1)} %get-tuple-element.215.refs_13_.refs_0_, bf16[8,512,256]{2,1,0:T(8,128)(2,1)} %get-tuple-element.168.refs_14_.refs_1_, ...), custom_call_target="tpu_custom_call" | custom-call | flops 8589934592 | bytes 20971520 | tf_op jit(solution)/shard_map/pallas_call | solution.py:467
  393.7 7.0 %collective-permute-done.27 = bf16[2,64,896]{2,1,0:T(8,128)(2,1)S(1)} collective-permute-done((bf16[2,64,896]{2,1,0:T(8,128)(2,1)S(1)}, bf16[2,64,896]{2,1,0:T(8,128)(2,1)S(1)}, u32[]{:S(2)}, u32[]{:S(2)}) %collective-permute-start.27) | collective-permute-done | bytes 229408 | tf_op jit(solution)/shard_map/ppermute | solution.py:1014
  407.2 11.9 %shard_map.331 = (bf16[512,1024]{1,0:T(8,128)(2,1)}, bf16[1024,128]{1,0:T(8,128)(2,1)}) custom-call(bf16[8,768,128]{2,1,0:T(8,128)(2,1)} %copy-done.4, bf16[2,256,1024]{2,1,0:T(8,128)(2,1)} %tok.5, f32[1,1024]{1,0:T(1,128)} %bitcast.216, f32[1,1024]{1,0:T(1,128)} %bitcast.219, bf16[1024,512]{1,0:T(8,128)(2,1)} %wq.3, bf16[1024,512]{1,0:T(8,128)(2,1)} %wk.3, ...), custom_call_target="tpu_custom_call" | custom-call | flops 3892314112 | bytes 17309696 | tf_op jit(solution)/shard_map/pallas_call | solution.py:467
  422.9 5.3 collective-permute-done.31
  444.5 6.8 %collective-permute-done.34 = bf16[2,8,5120]{2,1,0:T(8,128)(2,1)} collective-permute-done((bf16[2,8,5120]{2,1,0:T(8,128)(2,1)}, bf16[2,8,5120]{2,1,0:T(8,128)(2,1)}, u32[]{:S(2)}, u32[]{:S(2)}) %collective-permute-start.34) | collective-permute-done | bytes 163872 | tf_op jit(solution)/shard_map/ppermute | solution.py:1014
  461.4 5.8 collective-permute-done.37
  478.8 7.5 %collective-permute-done.42 = bf16[2,2,64,896]{3,2,1,0:T(8,128)(2,1)S(1)} collective-permute-done((bf16[2,2,64,896]{3,2,1,0:T(8,128)(2,1)S(1)}, bf16[2,2,64,896]{3,2,1,0:T(8,128)(2,1)S(1)}, u32[]{:S(2)}, u32[]{:S(2)}) %collective-permute-start.42) | collective-permute-done | bytes 458784 | tf_op jit(solution)/shard_map/ppermute | solution.py:1014
  500.0 5.3 collective-permute-done.49
  507.7 27.1 %collective-permute-done.48 = bf16[2,2,2,8,5120]{4,3,2,1,0:T(8,128)(2,1)S(1)} collective-permute-done((bf16[2,2,2,8,5120]{4,3,2,1,0:T(8,128)(2,1)S(1)}, bf16[2,2,2,8,5120]{4,3,2,1,0:T(8,128)(2,1)S(1)}, u32[]{:S(2)}, u32[]{:S(2)}) %collective-permute-start.48) | collective-permute-done | bytes 655392 | tf_op jit(solution)/shard_map/ppermute | solution.py:1014
  535.7 6.9 %all-to-all-done.5 = bf16[32,32,128]{2,1,0:T(8,128)(2,1)S(1)} async-done(((bf16[32,32,128]{2,1,0:T(8,128)(2,1)}), bf16[32,32,128]{2,1,0:T(8,128)(2,1)S(1)}, u32[]{:S(2)}, u32[]{:S(2)}) %all-to-all-start.5) | async-done | bytes 262176 | tf_op jit(solution)/shard_map/all_to_all | solution.py:1444
  553.7 6.7 %shard_map.333 = (f32[1024,512]{1,0:T(8,128)}, f32[1024,512]{1,0:T(8,128)}, f32[1024,2560]{1,0:T(8,128)}) custom-call(s32[5]{0:T(128)} %stack.237.bits, bf16[2,2,2,64,896]{4,3,2,1,0:T(8,128)(2,1)} %pad_maximum_fusion.3.refs_0_, bf16[2,2,2,64,896]{4,3,2,1,0:T(8,128)(2,1)} %collective-permute-done.46.refs_1_, ...), custom_call_target="tpu_custom_call" | custom-call | bytes 18350100 | tf_op jit(solution)/shard_map/pallas_call | solution.py:467
  566.3 6.7 %shard_map.335 = (f32[1024,512]{1,0:T(8,128)}, f32[1024,512]{1,0:T(8,128)}, f32[1024,2560]{1,0:T(8,128)}) custom-call(s32[5]{0:T(128)} %stack.237.bits, bf16[2,2,2,64,896]{4,3,2,1,0:T(8,128)(2,1)} %collective-permute-done.53.refs_0_, ...), custom_call_target="tpu_custom_call", output_to_operand_aliasing={{0}: (5, {}), {1}: (6, {}), {2}: (7, {})} | custom-call | bytes 33030164 | tf_op jit(solution)/shard_map/pallas_call | solution.py:467
  (274 shorter events, 181.2 us)
Async XLA Ops:
  16.2 50.9 %all-to-all-start = ((bf16[8,848,128]{2,1,0:T(8,128)(2,1)}), bf16[8,848,128]{2,1,0:T(8,128)(2,1)S(1)}, u32[]{:S(2)}, u32[]{:S(2)}) async-start(bf16[8,848,128]{2,1,0:T(8,128)(2,1)} %get-tuple-element.153), calls=%async_computation | async-start | bytes 3473408 | tf_op jit(solution)/shard_map/all_to_all | solution.py:1212
  25.1 42.0 %collective-permute-start.1 = (bf16[2,256,1024]{2,1,0:T(8,128)(2,1)S(1)}, bf16[2,256,1024]{2,1,0:T(8,128)(2,1)}, u32[]{:S(2)}, u32[]{:S(2)}) collective-permute-start(bf16[2,256,1024]{2,1,0:T(8,128)(2,1)S(1)} %copy-done.7), channel_id=1, source_target_pairs={{0,4},{1,5},{2,6},{3,7},{4,0},{5,1},{6,2},{7,3},{8,12},{9,13},{10,... | collective-permute-start | bytes 3145736 | tf_op jit(solution)/shard_map/ppermute | solution.py:1014
  67.1 59.5 %collective-permute-start.2 = (bf16[2,1024,256]{2,1,0:T(8,128)(2,1)}, bf16[2,1024,256]{2,1,0:T(8,128)(2,1)}, u32[]{:S(2)}, u32[]{:S(2)}) collective-permute-start(bf16[2,1024,256]{2,1,0:T(8,128)(2,1)} %get-tuple-element.157.refs_2_.refs_3_.refs_4_), channel_id=1, source_target_pairs={{0,16},{1,17},{2,18},{3,19},{4,20},{5,21},{6,22},{7,23},{8,24},{9,... | collective-permute-start | bytes 3145736 | tf_op jit(solution)/shard_map/ppermute | solution.py:1014
  69.5 57.2 %collective-permute-start.3 = (bf16[2,1024,256]{2,1,0:T(8,128)(2,1)}, bf16[2,1024,256]{2,1,0:T(8,128)(2,1)S(1)}, u32[]{:S(2)}, u32[]{:S(2)}) collective-permute-start(bf16[2,1024,256]{2,1,0:T(8,128)(2,1)} %get-tuple-element.157.refs_2_.refs_3_.refs_4_), channel_id=1, source_target_pairs={{0,8},{1,9},{2,10},{3,11},{4,12},{5,13},{6,14},{7,15},{8,0},{9,1},... | collective-permute-start | bytes 3145736 | tf_op jit(solution)/shard_map/ppermute | solution.py:1014
  70.9 55.7 %collective-permute-start.4 = (bf16[512,1024]{1,0:T(8,128)(2,1)}, bf16[512,1024]{1,0:T(8,128)(2,1)}, u32[]{:S(2)}, u32[]{:S(2)}) collective-permute-start(bf16[512,1024]{1,0:T(8,128)(2,1)} %bitcast.201), channel_id=1, source_target_pairs={{0,4},{1,5},{2,6},{3,7},{4,0},{5,1},{6,2},{7,3},{8,12},{9,13},{10,... | collective-permute-start | bytes 3145736 | tf_op jit(solution)/shard_map/ppermute | solution.py:1014
  71.2 55.4 %collective-permute-start.5 = (bf16[512,1024]{1,0:T(8,128)(2,1)}, bf16[512,1024]{1,0:T(8,128)(2,1)}, u32[]{:S(2)}, u32[]{:S(2)}) collective-permute-start(bf16[512,1024]{1,0:T(8,128)(2,1)} %bitcast.202), channel_id=1, source_target_pairs={{0,6},{1,7},{2,4},{3,5},{4,2},{5,3},{6,0},{7,1},{8,14},{9,15},{10,... | collective-permute-start | bytes 3145736 | tf_op jit(solution)/shard_map/ppermute | solution.py:1014
  83.5 43.1 %all-to-all-start.1 = ((bf16[8,256,128]{2,1,0:T(8,128)(2,1)}), bf16[8,256,128]{2,1,0:T(8,128)(2,1)S(1)}, u32[]{:S(2)}, u32[]{:S(2)}) async-start(bf16[8,256,128]{2,1,0:T(8,128)(2,1)} %get-tuple-element.156), calls=%async_computation.1 | async-start | bytes 1048576 | tf_op jit(solution)/shard_map/all_to_all | solution.py:1228
  137.1 26.8 %collective-permute-start.6 = (bf16[2,272,1024]{2,1,0:T(8,128)(2,1)}, bf16[2,272,1024]{2,1,0:T(8,128)(2,1)S(1)}, u32[]{:S(2)}, u32[]{:S(2)}) collective-permute-start(bf16[2,272,1024]{2,1,0:T(8,128)(2,1)} %get-tuple-element.161.refs_0_), channel_id=1, source_target_pairs={{0,2},{1,3},{2,0},{3,1},{4,6},{5,7},{6,4},{7,5},{8,10},{9,11},{10,... | collective-permute-start | bytes 3342344 | tf_op jit(solution)/shard_map/ppermute | solution.py:1014
  138.7 26.5 %collective-permute-start.8 = (bf16[2,272,1024]{2,1,0:T(8,128)(2,1)}, bf16[2,272,1024]{2,1,0:T(8,128)(2,1)}, u32[]{:S(2)}, u32[]{:S(2)}) collective-permute-start(bf16[2,272,1024]{2,1,0:T(8,128)(2,1)} %get-tuple-element.161.refs_0_), channel_id=1, source_target_pairs={{0,4},{1,5},{2,6},{3,7},{4,0},{5,1},{6,2},{7,3},{8,12},{9,13},{10,... | collective-permute-start | bytes 3342344 | tf_op jit(solution)/shard_map/ppermute | solution.py:1014
  139.2 29.4 %collective-permute-start.10 = (bf16[2,1024,256]{2,1,0:T(8,128)(2,1)}, bf16[2,1024,256]{2,1,0:T(8,128)(2,1)}, u32[]{:S(2)}, u32[]{:S(2)}) collective-permute-start(bf16[2,1024,256]{2,1,0:T(8,128)(2,1)} %copy-done.26), channel_id=1, source_target_pairs={{0,1},{1,0},{2,3},{3,2},{4,5},{5,4},{6,7},{7,6},{8,9},{9,8},{10,11... | collective-permute-start | bytes 3145736 | tf_op jit(solution)/shard_map/ppermute | solution.py:1014
  139.2 31.0 %collective-permute-start.11 = (bf16[2,1024,256]{2,1,0:T(8,128)(2,1)}, bf16[2,1024,256]{2,1,0:T(8,128)(2,1)}, u32[]{:S(2)}, u32[]{:S(2)}) collective-permute-start(bf16[2,1024,256]{2,1,0:T(8,128)(2,1)} %collective-permute-done.2.refs_6_.refs_7_.refs_8_), channel_id=1, source_target_pairs={{0,1},{1,0},{2,3},{3,2},{4,5},{5,4},{6,7},{7,6},{8,9},{9,8},{10,11... | collective-permute-start | bytes 3145736 | tf_op jit(solution)/shard_map/ppermute | solution.py:1014
  163.9 60.5 %collective-permute-start.17 = (bf16[2,256,1024]{2,1,0:T(8,128)(2,1)S(1)}, bf16[2,256,1024]{2,1,0:T(8,128)(2,1)S(1)}, u32[]{:S(2)}, u32[]{:S(2)}) collective-permute-start(bf16[2,256,1024]{2,1,0:T(8,128)(2,1)S(1)} %pad_maximum_fusion.2), channel_id=1, source_target_pairs={{0,16},{1,17},{2,18},{3,19},{4,20},{5,21},{6,22},{7,23},{8,24},{9,... | collective-permute-start | bytes 3145736 | tf_op jit(solution)/shard_map/ppermute | solution.py:1014
  165.2 40.3 %collective-permute-start.7 = (bf16[272,1024]{1,0:T(8,128)(2,1)S(1)}, bf16[272,1024]{1,0:T(8,128)(2,1)S(1)}, u32[]{:S(2)}, u32[]{:S(2)}) collective-permute-start(bf16[272,1024]{1,0:T(8,128)(2,1)S(1)} %slice_bitcast_fusion.1), channel_id=1, source_target_pairs={{0,4},{1,5},{2,6},{3,7},{4,0},{5,1},{6,2},{7,3},{8,12},{9,13},{10,... | collective-permute-start | bytes 1671176 | tf_op jit(solution)/shard_map/ppermute | solution.py:1014
  168.6 37.0 %collective-permute-start.9 = (bf16[272,1024]{1,0:T(8,128)(2,1)S(1)}, bf16[272,1024]{1,0:T(8,128)(2,1)S(1)}, u32[]{:S(2)}, u32[]{:S(2)}) collective-permute-start(bf16[272,1024]{1,0:T(8,128)(2,1)S(1)} %slice_bitcast_fusion), channel_id=1, source_target_pairs={{0,2},{1,3},{2,0},{3,1},{4,6},{5,7},{6,4},{7,5},{8,10},{9,11},{10,... | collective-permute-start | bytes 1671176 | tf_op jit(solution)/shard_map/ppermute | solution.py:1014
  220.4 50.3 %collective-permute-start.14 = (bf16[2,272,1024]{2,1,0:T(8,128)(2,1)}, bf16[2,272,1024]{2,1,0:T(8,128)(2,1)S(1)}, u32[]{:S(2)}, u32[]{:S(2)}) collective-permute-start(bf16[2,272,1024]{2,1,0:T(8,128)(2,1)} %get-tuple-element.175), channel_id=1, source_target_pairs={{0,2},{1,3},{2,0},{3,1},{4,6},{5,7},{6,4},{7,5},{8,10},{9,11},{10,... | collective-permute-start | bytes 3342344 | tf_op jit(solution)/shard_map/ppermute | solution.py:1014
  221.0 49.8 %collective-permute-start.15 = (bf16[2,272,1024]{2,1,0:T(8,128)(2,1)}, bf16[2,272,1024]{2,1,0:T(8,128)(2,1)S(1)}, u32[]{:S(2)}, u32[]{:S(2)}) collective-permute-start(bf16[2,272,1024]{2,1,0:T(8,128)(2,1)} %get-tuple-element.176), channel_id=1, source_target_pairs={{0,4},{1,5},{2,6},{3,7},{4,0},{5,1},{6,2},{7,3},{8,12},{9,13},{10,... | collective-permute-start | bytes 3342344 | tf_op jit(solution)/shard_map/ppermute | solution.py:1014
  221.4 49.3 %collective-permute-start.16 = (bf16[2,272,1024]{2,1,0:T(8,128)(2,1)}, bf16[2,272,1024]{2,1,0:T(8,128)(2,1)S(1)}, u32[]{:S(2)}, u32[]{:S(2)}) collective-permute-start(bf16[2,272,1024]{2,1,0:T(8,128)(2,1)} %get-tuple-element.177), channel_id=1, source_target_pairs={{0,6},{1,7},{2,4},{3,5},{4,2},{5,3},{6,0},{7,1},{8,14},{9,15},{10,... | collective-permute-start | bytes 3342344 | tf_op jit(solution)/shard_map/ppermute | solution.py:1014
  226.8 44.9 %collective-permute-start.18 = (bf16[4,256,1024]{2,1,0:T(8,128)(2,1)S(1)}, bf16[4,256,1024]{2,1,0:T(8,128)(2,1)S(1)}, u32[]{:S(2)}, u32[]{:S(2)}) collective-permute-start(bf16[4,256,1024]{2,1,0:T(8,128)(2,1)S(1)} %pad_maximum_fusion.1.near), channel_id=1, source_target_pairs={{0,8},{1,9},{2,10},{3,11},{4,12},{5,13},{6,14},{7,15},{8,0},{9,1},... | collective-permute-start | bytes 6291464 | tf_op jit(solution)/shard_map/ppermute | solution.py:1014
  316.9 122.2 %collective-permute-start.40 = (bf16[2,2,1024,256]{3,2,1,0:T(8,128)(2,1)}, bf16[2,2,1024,256]{3,2,1,0:T(8,128)(2,1)}, u32[]{:S(2)}, u32[]{:S(2)}) collective-permute-start(bf16[2,2,1024,256]{3,2,1,0:T(8,128)(2,1)} %get-tuple-element.239), channel_id=1, source_target_pairs={{0,1},{1,0},{2,3},{3,2},{4,5},{5,4},{6,7},{7,6},{8,9},{9,8},{10,11... | collective-permute-start | bytes 6291464 | tf_op jit(solution)/shard_map/ppermute | solution.py:1014
  317.1 120.2 %collective-permute-start.41 = (bf16[2,1024,256]{2,1,0:T(8,128)(2,1)}, bf16[2,1024,256]{2,1,0:T(8,128)(2,1)}, u32[]{:S(2)}, u32[]{:S(2)}) collective-permute-start(bf16[2,1024,256]{2,1,0:T(8,128)(2,1)} %get-tuple-element.291), channel_id=1, source_target_pairs={{0,8},{1,9},{2,10},{3,11},{4,12},{5,13},{6,14},{7,15},{8,0},{9,1},... | collective-permute-start | bytes 3145736 | tf_op jit(solution)/shard_map/ppermute | solution.py:1014
  336.9 27.8 %collective-permute-start.22 = (bf16[2,2,2,8,5120]{4,3,2,1,0:T(8,128)(2,1)}, bf16[2,2,2,8,5120]{4,3,2,1,0:T(8,128)(2,1)}, u32[]{:S(2)}, u32[]{:S(2)}) collective-permute-start(bf16[2,2,2,8,5120]{4,3,2,1,0:T(8,128)(2,1)} %dynamic-slice_bitcast_fusion.2), channel_id=1, source_target_pairs={{0,4},{1,5},{2,6},{3,7},{4,0},{5,1},{6,2},{7,3},{8,12},{9,13},{10,... | collective-permute-start | bytes 1966088 | tf_op jit(solution)/shard_map/ppermute | solution.py:1014
  338.4 67.0 %all-to-all-start.3 = ((bf16[8,768,128]{2,1,0:T(8,128)(2,1)}), bf16[8,768,128]{2,1,0:T(8,128)(2,1)S(1)}, u32[]{:S(2)}, u32[]{:S(2)}) async-start(bf16[8,768,128]{2,1,0:T(8,128)(2,1)} %shard_map.328.d_qkv), calls=%async_computation.3 | async-start | bytes 3145728 | tf_op jit(solution)/shard_map/all_to_all | solution.py:1389
  393.1 35.8 %collective-permute-start.32 = (bf16[512,1024]{1,0:T(8,128)(2,1)}, bf16[512,1024]{1,0:T(8,128)(2,1)}, u32[]{:S(2)}, u32[]{:S(2)}) collective-permute-start(bf16[512,1024]{1,0:T(8,128)(2,1)} %get-tuple-element.229), channel_id=1, source_target_pairs={{0,4},{1,5},{2,6},{3,7},{4,0},{5,1},{6,2},{7,3},{8,12},{9,13},{10,... | collective-permute-start | bytes 3145736 | tf_op jit(solution)/shard_map/ppermute | solution.py:1014
  432.0 35.3 %all-to-all-start.4 = ((bf16[32,32,128]{2,1,0:T(8,128)(2,1)}), bf16[32,32,128]{2,1,0:T(8,128)(2,1)S(1)}, u32[]{:S(2)}, u32[]{:S(2)}) async-start(bf16[32,32,128]{2,1,0:T(8,128)(2,1)} %bitcast.209), calls=%async_computation.4 | async-start | bytes 524288 | tf_op jit(solution)/shard_map/all_to_all | solution.py:1430
  437.3 30.0 %collective-permute-start.38 = (bf16[512,1024]{1,0:T(8,128)(2,1)S(1)}, bf16[512,1024]{1,0:T(8,128)(2,1)}, u32[]{:S(2)}, u32[]{:S(2)}) collective-permute-start(bf16[512,1024]{1,0:T(8,128)(2,1)S(1)} %add_convert_fusion), channel_id=1, source_target_pairs={{0,2},{1,3},{2,0},{3,1},{4,6},{5,7},{6,4},{7,5},{8,10},{9,11},{10,... | collective-permute-start | bytes 3145736 | tf_op jit(solution)/shard_map/ppermute | solution.py:1014
  439.1 28.1 %collective-permute-start.39 = (bf16[512,1024]{1,0:T(8,128)(2,1)}, bf16[512,1024]{1,0:T(8,128)(2,1)}, u32[]{:S(2)}, u32[]{:S(2)}) collective-permute-start(bf16[512,1024]{1,0:T(8,128)(2,1)} %get-tuple-element.238), channel_id=1, source_target_pairs={{0,4},{1,5},{2,6},{3,7},{4,0},{5,1},{6,2},{7,3},{8,12},{9,13},{10,... | collective-permute-start | bytes 3145736 | tf_op jit(solution)/shard_map/ppermute | solution.py:1014
  489.4 46.3 %collective-permute-start.51 = (bf16[2,1024,256]{2,1,0:T(8,128)(2,1)}, bf16[2,1024,256]{2,1,0:T(8,128)(2,1)}, u32[]{:S(2)}, u32[]{:S(2)}) collective-permute-start(bf16[2,1024,256]{2,1,0:T(8,128)(2,1)} %get-tuple-element.254), channel_id=1, source_target_pairs={{0,8},{1,9},{2,10},{3,11},{4,12},{5,13},{6,14},{7,15},{8,0},{9,1},... | collective-permute-start | bytes 3145736 | tf_op jit(solution)/shard_map/ppermute | solution.py:1014
  490.4 52.2 %collective-permute-start.50 = (bf16[2,1024,256]{2,1,0:T(8,128)(2,1)}, bf16[2,1024,256]{2,1,0:T(8,128)(2,1)}, u32[]{:S(2)}, u32[]{:S(2)}) collective-permute-start(bf16[2,1024,256]{2,1,0:T(8,128)(2,1)} %fusion.3), channel_id=1, source_target_pairs={{0,16},{1,17},{2,18},{3,19},{4,20},{5,21},{6,22},{7,23},{8,24},{9,... | collective-permute-start | bytes 3145736 | tf_op jit(solution)/shard_map/ppermute | solution.py:1014
  493.1 49.5 %all-to-all-start.5 = ((bf16[32,32,128]{2,1,0:T(8,128)(2,1)}), bf16[32,32,128]{2,1,0:T(8,128)(2,1)S(1)}, u32[]{:S(2)}, u32[]{:S(2)}) async-start(bf16[32,32,128]{2,1,0:T(8,128)(2,1)} %broadcast_in_dim.8), calls=%async_computation.5 | async-start | bytes 524288 | tf_op jit(solution)/shard_map/all_to_all | solution.py:1444
  496.6 46.1 %collective-permute-start.46 = (bf16[2,2,2,64,896]{4,3,2,1,0:T(8,128)(2,1)}, bf16[2,2,2,64,896]{4,3,2,1,0:T(8,128)(2,1)}, u32[]{:S(2)}, u32[]{:S(2)}) collective-permute-start(bf16[2,2,2,64,896]{4,3,2,1,0:T(8,128)(2,1)} %pad_maximum_fusion.3.refs_0_), channel_id=1, source_target_pairs={{0,2},{1,3},{2,0},{3,1},{4,6},{5,7},{6,4},{7,5},{8,10},{9,11},{10,... | collective-permute-start | bytes 2752520 | tf_op jit(solution)/shard_map/ppermute | solution.py:1014
  498.5 44.1 %collective-permute-start.47 = (bf16[2,2,2,64,896]{4,3,2,1,0:T(8,128)(2,1)}, bf16[2,2,2,64,896]{4,3,2,1,0:T(8,128)(2,1)}, u32[]{:S(2)}, u32[]{:S(2)}) collective-permute-start(bf16[2,2,2,64,896]{4,3,2,1,0:T(8,128)(2,1)} %pad_maximum_fusion.4.refs_2_), channel_id=1, source_target_pairs={{0,4},{1,5},{2,6},{3,7},{4,0},{5,1},{6,2},{7,3},{8,12},{9,13},{10,... | collective-permute-start | bytes 2752520 | tf_op jit(solution)/shard_map/ppermute | solution.py:1014
  505.2 29.6 %collective-permute-start.48 = (bf16[2,2,2,8,5120]{4,3,2,1,0:T(8,128)(2,1)S(1)}, bf16[2,2,2,8,5120]{4,3,2,1,0:T(8,128)(2,1)S(1)}, u32[]{:S(2)}, u32[]{:S(2)}) collective-permute-start(bf16[2,2,2,8,5120]{4,3,2,1,0:T(8,128)(2,1)S(1)} %pad_maximum_fusion.7), channel_id=1, source_target_pairs={{0,2},{1,3},{2,0},{3,1},{4,6},{5,7},{6,4},{7,5},{8,10},{9,11},{10,... | collective-permute-start | bytes 1966088 | tf_op jit(solution)/shard_map/ppermute | solution.py:1014
  (65 other events, 907.3 us)
